TPU v7x, 32 devices: a whole 2x2x4 slice. The times are simulated.
32 devices in a mesh: elem: 16 (over z, x, core), state: 2 (over y).
Axes of the slice: x: 2, y: 2, z: 4, core: 2. Of those that a mesh axis runs over, the one named last changes fastest.
Arguments:
- orbitals: bfloat16 [192, 160, 256], P(('elem', 'state')), may hold values from -6 to 6
- rotation: bfloat16 [256, 256], replicated, may hold values from -0.375 to 0.375
- counts: int32 [192], P('elem'), may hold values from 96 to 160, as said below
- neighbors: int32 [192, 5], P('elem'), may hold values from 0 to 191, as said below
- blocks: bfloat16 [192, 5, 160, 160], P('elem'), may hold values from -0.21875 to 0.21875
Outputs:
- filtered: bfloat16 [192, 160, 256], P(('elem', 'state'))
Inputs may be any that keep to these rules, and one draw needn't show every extreme that they name: `neighbors`: entry 0 of row e is e; every other entry is (e + d) mod 192 with 1 <= |d| <= 4. The adaptive basis is sized per pair of neighbouring elements: over each aligned block of 6 elements the counts sum to at most 864, and the first block of every index of elem sums to exactly 864.
All inputs are finite; a program needn't handle non-finite values.
Results may differ from a plain program's by a relative error of at most 0.007.
Values may be sent and summed in bfloat16 or wider, within the bound.
No kernel may reach another device: no remote copies, remote signals or barrier semaphores. Data moves between devices by JAX's collectives and lax.ppermute only.
A program may use at most 64 MiB of HBM per device.

v0:
```python
import jax
import jax.numpy as jnp
from jax import lax
from jax.sharding import PartitionSpec as P

DEG = 4


center_shift = 0.2
half_span = 1.1


def with_halo(block, sides, width):
    for axis, dim in sides:
        count = lax.axis_size(axis)
        forward = [(i, i + 1) for i in range(count - 1)]
        forward.append((count - 1, 0))
        backward = [(target, source) for source, target in forward]
        low = lax.ppermute(
            lax.slice_in_dim(block, block.shape[dim] - width, None, axis=dim), axis, forward
        )
        high = lax.ppermute(lax.slice_in_dim(block, 0, width, axis=dim), axis, backward)
        block = jnp.concatenate([low, block, high], axis=dim)
    return block


def padded_rim(current, reach):
    return with_halo(current, (("elem", 0),), reach)


def coupled(block_part, gathered):
    return jnp.einsum("ekij,ekjs->eis", block_part, gathered, preferred_element_type=jnp.float32)


def on_device(orbitals, rotation, counts, neighbors, blocks):
    row_elems = orbitals.shape[0]
    basis_len = orbitals.shape[1]
    elems = counts.shape[0]
    reach = elems // 3
    shard = lax.axis_index("state")
    my_counts = lax.dynamic_slice_in_dim(counts, shard * row_elems, row_elems, 0)
    flat_orbitals = orbitals.reshape(row_elems * basis_len, -1)
    rows_mask = (
        lax.broadcasted_iota(jnp.int32, (row_elems, basis_len, 1), 1) < my_counts[:, None, None]
    ).astype(jnp.float32)
    rotated = jnp.dot(flat_orbitals, rotation, preferred_element_type=jnp.float32)
    rotated = rotated.reshape(row_elems, basis_len, -1)
    start_rows = (rotated * rows_mask).astype(jnp.bfloat16)
    start = lax.all_to_all(start_rows, "state", split_axis=2, concat_axis=0, tiled=True)
    elem_mask = (
        lax.broadcasted_iota(jnp.int32, (elems, basis_len, 1), 1) < counts[:, None, None]
    ).astype(jnp.float32)
    all_elems = elems * lax.axis_size("elem")
    first_global = lax.axis_index("elem") * elems
    local_source = jnp.mod(neighbors - first_global + reach, all_elems)

    def image_of(current):
        padded = padded_rim(current, reach)
        image = coupled(blocks, padded[local_source])
        return image * elem_mask

    def chebyshev(current, previous, factor, with_prev):
        value = (
            factor * (image_of(current) - center_shift * current.astype(jnp.float32)) / half_span
        )
        if with_prev:
            value = value - previous.astype(jnp.float32)
        return value.astype(jnp.bfloat16)

    previous = start
    current = chebyshev(start, start, 1.0, False)
    for degree in range(DEG - 1):
        following = chebyshev(current, previous, 2.0, True)
        previous = current
        current = following
    return lax.all_to_all(current, "state", split_axis=0, concat_axis=2, tiled=True)


def solution(mesh):
    in_specs = (
        P(("elem", "state"), None, None),
        P(),
        P("elem"),
        P("elem", None),
        P("elem", None, None, None),
    )
    out_specs = P(("elem", "state"), None, None)
    return jax.shard_map(
        on_device, mesh=mesh, in_specs=in_specs, out_specs=out_specs, check_vma=False
    )
```

profile of v0, /device:TPU:0, one launch (start us, length us, event | category | flops | bytes accessed | tf_op | source)
XLA Modules:
  0.0 87.1 jit_solution(17012007488805748699)
XLA Ops:
  0.0 0.0 copy-start
  0.0 0.8 dynamic_slice.3
  0.8 0.1 fusion.26
  0.9 0.2 copy-done
  1.0 0.0 copy-start.2
  1.0 1.2 %fusion.23 = bf16[6,160,256]{2,1,0:T(8,128)(2,1)S(1)} fusion(bf16[6,160,256]{2,1,0:T(8,128)(2,1)S(1)} %copy-done, f32[6,160]{1,0:T(8,128)S(1)} %fusion.26, bf16[256,256]{1,0:T(8,128)(2,1)} %param.6), kind=kOutput, calls=%fused_computation.32 | convolution fusion | flops 126320640 | bytes 1117952 | tf_op jit(solution)/shard_map/dot_general | solution.py:46
  2.3 0.9 copy.12
  3.1 2.0 %reshape.97 = bf16[2,2,61440]{2,1,0:T(2,128)(2,1)} reshape(bf16[256,6,160]{2,1,0:T(8,128)(2,1)S(1)} %bitcast.125) | data formatting | bytes 983040
  5.1 0.0 copy-start.1
  5.1 4.4 %all-to-all-start = ((bf16[2,2,61440]{2,1,0:T(2,128)(2,1)}), bf16[2,2,61440]{2,1,0:T(2,128)(2,1)S(1)}, u32[]{:S(2)}, u32[]{:S(2)}) async-start(bf16[2,2,61440]{2,1,0:T(2,128)(2,1)} %reshape.97), calls=%async_computation | async-start | bytes 983040 | tf_op jit(solution)/shard_map/all_to_all | solution.py:49
  9.5 0.0 copy-done.2
  9.5 0.1 fusion.25
  9.6 8.3 %all-to-all-done = bf16[2,2,61440]{2,1,0:T(2,128)(2,1)S(1)} async-done(((bf16[2,2,61440]{2,1,0:T(2,128)(2,1)}), bf16[2,2,61440]{2,1,0:T(2,128)(2,1)S(1)}, u32[]{:S(2)}, u32[]{:S(2)}) %all-to-all-start) | async-done | bytes 491552 | tf_op jit(solution)/shard_map/all_to_all | solution.py:49
  17.9 1.3 %reshape.98 = bf16[256,6,160]{2,1,0:T(8,128)(2,1)S(1)} reshape(bf16[2,2,61440]{2,1,0:T(2,128)(2,1)S(1)} %all-to-all-done) | data formatting | bytes 983040
  19.2 0.6 copy.13
  19.8 0.1 collective-permute-start
  19.9 4.4 %collective-permute-start.1 = (bf16[4,160,128]{2,1,0:T(8,128)(2,1)S(1)}, bf16[4,160,128]{2,1,0:T(8,128)(2,1)S(1)}, u32[]{:S(2)}, u32[]{:S(2)}) collective-permute-start(bf16[4,160,128]{2,1,0:T(8,128)(2,1)S(1)} %get-tuple-element.12), channel_id=1, source_target_pairs={{2,0},{4,2},{6,4},{8,6},{10,8},{12,10},{14,12},{16,14},{18,16},{20... | collective-permute-start | bytes 491528 | tf_op jit(solution)/shard_map/ppermute | solution.py:22
  24.3 0.0 copy-done.1
  24.4 0.1 copy.14
  24.5 0.1 reshape.54
  24.6 2.9 %collective-permute-done = bf16[4,160,128]{2,1,0:T(8,128)(2,1)S(1)} collective-permute-done((bf16[4,160,128]{2,1,0:T(8,128)(2,1)S(1)}, bf16[4,160,128]{2,1,0:T(8,128)(2,1)S(1)}, u32[]{:S(2)}, u32[]{:S(2)}) %collective-permute-start) | collective-permute-done | bytes 163872 | tf_op jit(solution)/shard_map/ppermute | solution.py:19
  27.4 0.0 collective-permute-done.1
  27.4 0.1 pad_maximum_fusion
  27.6 2.4 %gather_fusion = bf16[60,160,128]{2,1,0:T(8,128)(2,1)} fusion(bf16[20,160,128]{2,1,0:T(8,128)(2,1)S(1)} %pad_maximum_fusion, s32[1024]{0:T(1024)S(1)} %pad_clamp_fusion), kind=kCustom, calls=%fused_computation | custom fusion | bytes 4915440 | tf_op jit(solution)/shard_map/gather | solution.py:59
  29.9 4.3 %fusion.22 = bf16[12,160,128]{2,1,0:T(8,128)(2,1)S(1)} fusion(bf16[12,5,160,160]{3,2,1,0:T(8,128)(2,1)} %param.9, bf16[12,5,160,128]{3,2,1,0:T(8,128)(2,1)} %bitcast.134, bf16[12,160,128]{2,1,0:T(8,128)(2,1)S(1)} %bitcast.129, f32[12,160]{1,0:T(8,128)S(1)} %fusion.25), kind=kOutput, calls=%fused_computation.31 | convolution fusion | flops 394690560 | bytes 6520320 | tf_op jit(solution)/shard_map/ekij,ekjs->eis/dot_general | solution.py:32
  34.3 0.8 collective-permute-start.2
  35.1 3.7 %collective-permute-start.3 = (bf16[4,160,128]{2,1,0:T(8,128)(2,1)S(1)}, bf16[4,160,128]{2,1,0:T(8,128)(2,1)S(1)}, u32[]{:S(2)}, u32[]{:S(2)}) collective-permute-start(bf16[4,160,128]{2,1,0:T(8,128)(2,1)S(1)} %get-tuple-element.10), channel_id=1, source_target_pairs={{2,0},{4,2},{6,4},{8,6},{10,8},{12,10},{14,12},{16,14},{18,16},{20... | collective-permute-start | bytes 491528 | tf_op jit(solution)/shard_map/ppermute | solution.py:22
  38.8 3.1 %collective-permute-done.2 = bf16[4,160,128]{2,1,0:T(8,128)(2,1)S(1)} collective-permute-done((bf16[4,160,128]{2,1,0:T(8,128)(2,1)S(1)}, bf16[4,160,128]{2,1,0:T(8,128)(2,1)S(1)}, u32[]{:S(2)}, u32[]{:S(2)}) %collective-permute-start.2) | collective-permute-done | bytes 163872 | tf_op jit(solution)/shard_map/ppermute | solution.py:19
  41.9 0.0 collective-permute-done.3
  41.9 0.1 pad_maximum_fusion.1
  42.0 2.4 %gather_fusion.1 = bf16[60,160,128]{2,1,0:T(8,128)(2,1)} fusion(bf16[20,160,128]{2,1,0:T(8,128)(2,1)S(1)} %pad_maximum_fusion.1, s32[1024]{0:T(1024)S(1)} %pad_clamp_fusion), kind=kCustom, calls=%fused_computation.1 | custom fusion | bytes 4915440 | tf_op jit(solution)/shard_map/gather | solution.py:59
  44.3 4.4 %fusion.21 = bf16[12,160,128]{2,1,0:T(8,128)(2,1)S(1)} fusion(bf16[12,5,160,160]{3,2,1,0:T(8,128)(2,1)} %param.9, bf16[12,5,160,128]{3,2,1,0:T(8,128)(2,1)} %bitcast.132, bf16[12,160,128]{2,1,0:T(8,128)(2,1)S(1)} %bitcast.130, bf16[12,160,128]{2,1,0:T(8,128)(2,1)S(1)} %fusion.22, f32[12,160]{1,0:T(8,128)S(1)} %fusion.25), kind=kOutput, calls=%fused_computation.30 | convolution fusion | flops 395182080 | bytes 7011840 | tf_op jit(solution)/shard_map/ekij,ekjs->eis/dot_general | solution.py:32
  48.7 0.1 collective-permute-start.4
  48.8 4.4 %collective-permute-start.5 = (bf16[4,160,128]{2,1,0:T(8,128)(2,1)S(1)}, bf16[4,160,128]{2,1,0:T(8,128)(2,1)S(1)}, u32[]{:S(2)}, u32[]{:S(2)}) collective-permute-start(bf16[4,160,128]{2,1,0:T(8,128)(2,1)S(1)} %get-tuple-element.8), channel_id=1, source_target_pairs={{2,0},{4,2},{6,4},{8,6},{10,8},{12,10},{14,12},{16,14},{18,16},{20... | collective-permute-start | bytes 491528 | tf_op jit(solution)/shard_map/ppermute | solution.py:22
  53.2 3.0 %collective-permute-done.4 = bf16[4,160,128]{2,1,0:T(8,128)(2,1)S(1)} collective-permute-done((bf16[4,160,128]{2,1,0:T(8,128)(2,1)S(1)}, bf16[4,160,128]{2,1,0:T(8,128)(2,1)S(1)}, u32[]{:S(2)}, u32[]{:S(2)}) %collective-permute-start.4) | collective-permute-done | bytes 163872 | tf_op jit(solution)/shard_map/ppermute | solution.py:19
  56.2 0.0 collective-permute-done.5
  56.2 0.1 pad_maximum_fusion.2
  56.3 2.4 %gather_fusion.2 = bf16[60,160,128]{2,1,0:T(8,128)(2,1)} fusion(bf16[20,160,128]{2,1,0:T(8,128)(2,1)S(1)} %pad_maximum_fusion.2, s32[1024]{0:T(1024)S(1)} %pad_clamp_fusion), kind=kCustom, calls=%fused_computation.2 | custom fusion | bytes 4915440 | tf_op jit(solution)/shard_map/gather | solution.py:59
  58.7 4.4 %fusion.20 = bf16[12,160,128]{2,1,0:T(8,128)(2,1)S(1)} fusion(bf16[12,5,160,160]{3,2,1,0:T(8,128)(2,1)} %param.9, bf16[12,5,160,128]{3,2,1,0:T(8,128)(2,1)} %bitcast.133, bf16[12,160,128]{2,1,0:T(8,128)(2,1)S(1)} %fusion.22, bf16[12,160,128]{2,1,0:T(8,128)(2,1)S(1)} %fusion.21, f32[12,160]{1,0:T(8,128)S(1)} %fusion.25), kind=kOutput, calls=%fused_computation.29 | convolution fusion | flops 395182080 | bytes 7011840 | tf_op jit(solution)/shard_map/ekij,ekjs->eis/dot_general | solution.py:32
  63.1 0.1 collective-permute-start.6
  63.2 4.5 %collective-permute-start.7 = (bf16[4,160,128]{2,1,0:T(8,128)(2,1)S(1)}, bf16[4,160,128]{2,1,0:T(8,128)(2,1)S(1)}, u32[]{:S(2)}, u32[]{:S(2)}) collective-permute-start(bf16[4,160,128]{2,1,0:T(8,128)(2,1)S(1)} %get-tuple-element.6), channel_id=1, source_target_pairs={{2,0},{4,2},{6,4},{8,6},{10,8},{12,10},{14,12},{16,14},{18,16},{20... | collective-permute-start | bytes 491528 | tf_op jit(solution)/shard_map/ppermute | solution.py:22
  67.7 2.9 %collective-permute-done.6 = bf16[4,160,128]{2,1,0:T(8,128)(2,1)S(1)} collective-permute-done((bf16[4,160,128]{2,1,0:T(8,128)(2,1)S(1)}, bf16[4,160,128]{2,1,0:T(8,128)(2,1)S(1)}, u32[]{:S(2)}, u32[]{:S(2)}) %collective-permute-start.6) | collective-permute-done | bytes 163872 | tf_op jit(solution)/shard_map/ppermute | solution.py:19
  70.6 0.0 collective-permute-done.7
  70.6 0.1 pad_maximum_fusion.3
  70.7 2.4 %gather_fusion.3 = bf16[60,160,128]{2,1,0:T(8,128)(2,1)} fusion(bf16[20,160,128]{2,1,0:T(8,128)(2,1)S(1)} %pad_maximum_fusion.3, s32[1024]{0:T(1024)S(1)} %pad_clamp_fusion), kind=kCustom, calls=%fused_computation.3 | custom fusion | bytes 4915440 | tf_op jit(solution)/shard_map/gather | solution.py:59
  73.1 4.4 %fusion.19 = bf16[12,160,128]{2,1,0:T(8,128)(2,1)S(1)} fusion(bf16[12,5,160,160]{3,2,1,0:T(8,128)(2,1)} %param.9, bf16[12,5,160,128]{3,2,1,0:T(8,128)(2,1)} %bitcast.131, bf16[12,160,128]{2,1,0:T(8,128)(2,1)S(1)} %fusion.21, bf16[12,160,128]{2,1,0:T(8,128)(2,1)S(1)} %fusion.20, f32[12,160]{1,0:T(8,128)S(1)} %fusion.25), kind=kOutput, calls=%fused_computation.28 | convolution fusion | flops 395182080 | bytes 7011840 | tf_op jit(solution)/shard_map/ekij,ekjs->eis/dot_general | solution.py:32
  77.5 8.8 %all_to_all.36 = bf16[12,160,128]{2,1,0:T(8,128)(2,1)S(1)} all-to-all(bf16[12,160,128]{2,1,0:T(8,128)(2,1)S(1)} %fusion.19), channel_id=1, replica_groups=mesh['elem'=16,'state'=2] {'state'}, dimensions={0} | all-to-all | bytes 983040 | tf_op jit(solution)/shard_map/all_to_all | solution.py:76
  86.3 0.9 copy.22
  (6 shorter events, 0.1 us)
Async XLA Ops:
  0.0 1.0 %copy-start = (bf16[6,160,256]{2,1,0:T(8,128)(2,1)S(1)}, bf16[6,160,256]{2,1,0:T(8,128)(2,1)}, u32[]{:S(2)}) copy-start(bf16[6,160,256]{2,1,0:T(8,128)(2,1)} %param.5) | copy-start | bytes 1474564
  1.0 8.5 %copy-start.2 = (s32[12]{0:T(128)S(1)}, s32[12]{0:T(128)}, u32[]{:S(2)}) copy-start(s32[12]{0:T(128)} %param.7) | copy-start | bytes 148
  5.1 19.2 %copy-start.1 = (s32[12,5]{0,1:T(8,128)S(1)}, s32[12,5]{0,1:T(8,128)}, u32[]{:S(2)}) copy-start(s32[12,5]{0,1:T(8,128)} %param.8) | copy-start | bytes 724
  5.1 12.7 %all-to-all-start = ((bf16[2,2,61440]{2,1,0:T(2,128)(2,1)}), bf16[2,2,61440]{2,1,0:T(2,128)(2,1)S(1)}, u32[]{:S(2)}, u32[]{:S(2)}) async-start(bf16[2,2,61440]{2,1,0:T(2,128)(2,1)} %reshape.97), calls=%async_computation | async-start | bytes 983040 | tf_op jit(solution)/shard_map/all_to_all | solution.py:49
  19.8 7.6 %collective-permute-start = (bf16[4,160,128]{2,1,0:T(8,128)(2,1)S(1)}, bf16[4,160,128]{2,1,0:T(8,128)(2,1)S(1)}, u32[]{:S(2)}, u32[]{:S(2)}) collective-permute-start(bf16[4,160,128]{2,1,0:T(8,128)(2,1)S(1)} %get-tuple-element.11), channel_id=1, source_target_pairs={{0,2},{2,4},{4,6},{6,8},{8,10},{10,12},{12,14},{14,16},{16,18},{18... | collective-permute-start | bytes 491528 | tf_op jit(solution)/shard_map/ppermute | solution.py:19
  19.9 7.5 %collective-permute-start.1 = (bf16[4,160,128]{2,1,0:T(8,128)(2,1)S(1)}, bf16[4,160,128]{2,1,0:T(8,128)(2,1)S(1)}, u32[]{:S(2)}, u32[]{:S(2)}) collective-permute-start(bf16[4,160,128]{2,1,0:T(8,128)(2,1)S(1)} %get-tuple-element.12), channel_id=1, source_target_pairs={{2,0},{4,2},{6,4},{8,6},{10,8},{12,10},{14,12},{16,14},{18,16},{20... | collective-permute-start | bytes 491528 | tf_op jit(solution)/shard_map/ppermute | solution.py:22
  34.3 7.6 %collective-permute-start.2 = (bf16[4,160,128]{2,1,0:T(8,128)(2,1)S(1)}, bf16[4,160,128]{2,1,0:T(8,128)(2,1)S(1)}, u32[]{:S(2)}, u32[]{:S(2)}) collective-permute-start(bf16[4,160,128]{2,1,0:T(8,128)(2,1)S(1)} %get-tuple-element.9), channel_id=1, source_target_pairs={{0,2},{2,4},{4,6},{6,8},{8,10},{10,12},{12,14},{14,16},{16,18},{18... | collective-permute-start | bytes 491528 | tf_op jit(solution)/shard_map/ppermute | solution.py:19
  35.1 6.7 %collective-permute-start.3 = (bf16[4,160,128]{2,1,0:T(8,128)(2,1)S(1)}, bf16[4,160,128]{2,1,0:T(8,128)(2,1)S(1)}, u32[]{:S(2)}, u32[]{:S(2)}) collective-permute-start(bf16[4,160,128]{2,1,0:T(8,128)(2,1)S(1)} %get-tuple-element.10), channel_id=1, source_target_pairs={{2,0},{4,2},{6,4},{8,6},{10,8},{12,10},{14,12},{16,14},{18,16},{20... | collective-permute-start | bytes 491528 | tf_op jit(solution)/shard_map/ppermute | solution.py:22
  48.7 7.5 %collective-permute-start.4 = (bf16[4,160,128]{2,1,0:T(8,128)(2,1)S(1)}, bf16[4,160,128]{2,1,0:T(8,128)(2,1)S(1)}, u32[]{:S(2)}, u32[]{:S(2)}) collective-permute-start(bf16[4,160,128]{2,1,0:T(8,128)(2,1)S(1)} %get-tuple-element.7), channel_id=1, source_target_pairs={{0,2},{2,4},{4,6},{6,8},{8,10},{10,12},{12,14},{14,16},{16,18},{18... | collective-permute-start | bytes 491528 | tf_op jit(solution)/shard_map/ppermute | solution.py:19
  48.8 7.4 %collective-permute-start.5 = (bf16[4,160,128]{2,1,0:T(8,128)(2,1)S(1)}, bf16[4,160,128]{2,1,0:T(8,128)(2,1)S(1)}, u32[]{:S(2)}, u32[]{:S(2)}) collective-permute-start(bf16[4,160,128]{2,1,0:T(8,128)(2,1)S(1)} %get-tuple-element.8), channel_id=1, source_target_pairs={{2,0},{4,2},{6,4},{8,6},{10,8},{12,10},{14,12},{16,14},{18,16},{20... | collective-permute-start | bytes 491528 | tf_op jit(solution)/shard_map/ppermute | solution.py:22
  63.1 7.5 %collective-permute-start.6 = (bf16[4,160,128]{2,1,0:T(8,128)(2,1)S(1)}, bf16[4,160,128]{2,1,0:T(8,128)(2,1)S(1)}, u32[]{:S(2)}, u32[]{:S(2)}) collective-permute-start(bf16[4,160,128]{2,1,0:T(8,128)(2,1)S(1)} %get-tuple-element.5), channel_id=1, source_target_pairs={{0,2},{2,4},{4,6},{6,8},{8,10},{10,12},{12,14},{14,16},{16,18},{18... | collective-permute-start | bytes 491528 | tf_op jit(solution)/shard_map/ppermute | solution.py:19
  63.2 7.4 %collective-permute-start.7 = (bf16[4,160,128]{2,1,0:T(8,128)(2,1)S(1)}, bf16[4,160,128]{2,1,0:T(8,128)(2,1)S(1)}, u32[]{:S(2)}, u32[]{:S(2)}) collective-permute-start(bf16[4,160,128]{2,1,0:T(8,128)(2,1)S(1)} %get-tuple-element.6), channel_id=1, source_target_pairs={{2,0},{4,2},{6,4},{8,6},{10,8},{12,10},{14,12},{16,14},{18,16},{20... | collective-permute-start | bytes 491528 | tf_op jit(solution)/shard_map/ppermute | solution.py:22
where the time goes:
time: 87.4 us; the launch traced here: 87.1 us
  starting transfers between devices  22.4 us (26%)
  waiting for transfers between devices  20.2 us (23%)
  matrix products  18.7 us (21%)
  local copies, waits for them, and re-layouts  16.3 us (19%)
  blocking collectives  8.79 us (10%)
    dot_general x4, matrix products, coupled(): jnp.einsum('ekij,ekjs->eis', block_part, gathered, preferred_element_type...  17.5 us
    ppermute x4, starting transfers between devices, with_halo(): lax.ppermute(lax.slice_in_dim(block, 0, width, axis=dim), axis, backward)  17 us
    ppermute x4, waiting for transfers between devices, with_halo(): lax.ppermute(lax.slice_in_dim(block, block.shape[dim] - width, None, axis...  11.9 us
    gather x4, local copies, waits for them, and re-layouts, image_of(): image = coupled(blocks, padded[local_source])  9.42 us
    all_to_all x1, blocking collectives, on_device(): lax.all_to_all(current, 'state', split_axis=0, concat_axis=2, tiled=True)  8.79 us
    all_to_all x1, waiting for transfers between devices, on_device(): lax.all_to_all(start_rows, 'state', split_axis=2, concat_axis=0, tiled=True)  8.3 us
    all_to_all x1, starting transfers between devices, on_device(): lax.all_to_all(start_rows, 'state', split_axis=2, concat_axis=0, tiled=True)  4.37 us
    unnamed x8, local copies, waits for them, and re-layouts  3.53 us
  transfers between devices with their start and end apart: 9, of which 5 were waited for; matrix products, arithmetic and copies ran while one was open for 0% of the time, Pallas kernels for 0%

commit v1 on v0

v1 whole, which is shorter than its diff:
```python
import functools

import jax
import jax.numpy as jnp
from jax import lax
from jax.experimental import pallas as pl
from jax.experimental.pallas import tpu as pltpu
from jax.sharding import PartitionSpec as P

DEG = 4

center_shift = 0.2
half_span = 1.1

VMEM = pl.BlockSpec(memory_space=pltpu.VMEM)
SMEM = pl.BlockSpec(memory_space=pltpu.SMEM)
HBM = pl.BlockSpec(memory_space=pl.ANY)


def call(kernel, outs, ins, *args, scratch=(), out_specs=None, aliases=None, limit=16 << 20, flops=0, name=None):
    shapes = [jax.ShapeDtypeStruct(shape, jnp.bfloat16) for shape in outs]
    return pl.pallas_call(
        kernel,
        out_shape=shapes,
        in_specs=ins,
        out_specs=out_specs or [VMEM] * len(outs),
        scratch_shapes=list(scratch),
        input_output_aliases=aliases or {},
        compiler_params=pltpu.CompilerParams(vmem_limit_bytes=limit),
        cost_estimate=pl.CostEstimate(flops=flops, bytes_accessed=1 << 19, transcendentals=0),
        name=name,
    )(*args)


def rows_below(count, rows, lanes):
    return lax.broadcasted_iota(jnp.int32, (rows, lanes), 0) < count


def rotate_kernel(shards, orbitals, rotation, counts, *outs):
    me = lax.axis_index("state")
    elems, rows, states = orbitals.shape
    lanes = states // shards
    flat = orbitals[...].reshape(elems * rows, states)
    for k, out in enumerate(outs):
        at = lax.rem(me + k, shards) * lanes
        weights = rotation[:, pl.ds(pl.multiple_of(at, lanes), lanes)]
        turned = jnp.dot(flat, weights, preferred_element_type=jnp.float32).reshape(elems, rows, lanes)
        for e in range(elems):
            keep = rows_below(counts[me * elems + e], rows, lanes)
            out[e] = jnp.where(keep, turned[e], 0.0).astype(jnp.bfloat16)


def gather_kernel(shards, *refs):
    me = lax.axis_index("state")
    parts, groups, whole = refs[:shards], refs[shards : shards + 3], refs[-1]
    elems, width = parts[0].shape[0], groups[0].shape[0]
    for k, part in enumerate(parts):
        whole[pl.ds(lax.rem(me + shards - k, shards) * elems, elems)] = part[...]
    for g, group in enumerate(groups):
        group[...] = whole[g * width : (g + 1) * width]


def level_kernel(first, factor, with_prev, blocks, source, counts, before, here, after, *refs):
    if with_prev:
        previous, out, window = refs
    else:
        out, window = refs
    width, rows, lanes = here.shape
    for g, group in enumerate((before, here, after)):
        window[g * width : (g + 1) * width] = group[...]
    for e in range(width):
        image = jnp.zeros((rows, lanes), jnp.float32)
        for k in range(blocks.shape[1]):
            field = window[source[first + e, k]]
            image += jnp.dot(blocks[first + e, k], field, preferred_element_type=jnp.float32)
        image = jnp.where(rows_below(counts[first + e], rows, lanes), image, 0.0)
        value = factor * (image - center_shift * here[e].astype(jnp.float32)) / half_span
        if with_prev:
            value = value - previous[e].astype(jnp.float32)
        out[e] = value.astype(jnp.bfloat16)


def scatter_kernel(shards, *refs):
    me = lax.axis_index("state")
    groups, parts, whole = refs[:3], refs[3:-1], refs[-1]
    elems, width = parts[0].shape[0], groups[0].shape[0]
    for g, group in enumerate(groups):
        whole[g * width : (g + 1) * width] = group[...]
    for k, part in enumerate(parts):
        part[...] = whole[pl.ds(lax.rem(me + k, shards) * elems, elems)]


def join_kernel(shards, *refs):
    me = lax.axis_index("state")
    parts, out = refs[:shards], refs[shards]
    lanes = parts[0].shape[2]
    for k, part in enumerate(parts):
        at = lax.rem(me + shards - k, shards) * lanes
        out[:, :, pl.ds(pl.multiple_of(at, lanes), lanes)] = part[...]


def on_device(orbitals, rotation, counts, neighbors, blocks):
    row_elems, rows, states = orbitals.shape
    elems = counts.shape[0]
    shards = lax.axis_size("state")
    ring = lax.axis_size("elem")
    width = elems // 3
    lanes = states // shards
    group = (width, rows, lanes)

    def to_right(x):
        return lax.ppermute(x, "elem", [(i, (i + 1) % ring) for i in range(ring)])

    def to_left(x):
        return lax.ppermute(x, "elem", [(i, (i - 1) % ring) for i in range(ring)])

    def swapped(parts):
        return [parts[0]] + [
            lax.ppermute(part, "state", [(i, (i + k) % shards) for i in range(shards)])
            for k, part in enumerate(parts)
            if k > 0
        ]

    total = elems * ring
    mine = lax.axis_index("elem") * elems + jnp.arange(elems, dtype=jnp.int32)
    offset = jnp.mod(neighbors - mine[:, None] + width, total)
    source = offset + jnp.mod(jnp.arange(elems, dtype=jnp.int32), width)[:, None]

    part = (row_elems, rows, lanes)
    parts = call(
        functools.partial(rotate_kernel, shards),
        [part] * shards,
        [VMEM, VMEM, SMEM],
        orbitals,
        rotation,
        counts,
        name="rotate",
    )
    parts = swapped(parts)
    start = call(
        functools.partial(gather_kernel, shards),
        [group] * 3,
        [VMEM] * shards,
        *parts,
        scratch=[pltpu.VMEM((elems, rows, lanes), jnp.bfloat16)],
        name="gather",
    )

    def level(g, factor, before, here, after, previous=None):
        body = functools.partial(level_kernel, g * width, factor, previous is not None)
        args = [blocks, source, counts, before, here, after] + ([] if previous is None else [previous])
        return call(
            body,
            [group],
            [VMEM, SMEM, SMEM] + [VMEM] * (len(args) - 3),
            *args,
            scratch=[pltpu.VMEM((3 * width, rows, lanes), jnp.bfloat16)],
            flops=2 * width * blocks.shape[1] * rows * rows * lanes,
            name=("low", "middle", "high")[g],
        )[0]

    older, (low, middle, high) = (None, None, None), start
    for m in range(DEG):
        factor = 1.0 if m == 0 else 2.0
        from_left, from_right = to_right(high), to_left(low)
        newer = (
            level(0, factor, from_left, low, middle, older[0]),
            level(1, factor, low, middle, high, older[1]),
            level(2, factor, middle, high, from_right, older[2]),
        )
        older, (low, middle, high) = (low, middle, high), newer

    parts = call(
        functools.partial(scatter_kernel, shards),
        [part] * shards,
        [VMEM] * 3,
        low,
        middle,
        high,
        scratch=[pltpu.VMEM((elems, rows, lanes), jnp.bfloat16)],
        name="scatter",
    )
    parts = swapped(parts)
    return call(
        functools.partial(join_kernel, shards), [orbitals.shape], [VMEM] * shards, *parts, name="join"
    )[0]


def solution(mesh):
    in_specs = (
        P(("elem", "state"), None, None),
        P(),
        P("elem"),
        P("elem", None),
        P("elem", None, None, None),
    )
    out_specs = P(("elem", "state"), None, None)
    return jax.shard_map(on_device, mesh=mesh, in_specs=in_specs, out_specs=out_specs, check_vma=False)
```

time: 87.4 us -> 56.2 us (0.64)
  matrix products: 18.7 us -> 0 us
  Pallas kernels: 0 us -> 17.6 us
  starting transfers between devices: 22.4 us -> 10.7 us
  local copies, waits for them, and re-layouts: 16.3 us -> 6.42 us
  blocking collectives: 8.79 us -> 0 us
    dot_general x5 -> x0, matrix products: 18.7 us -> none  [the longest x4 17.5 us: coupled(): jnp.einsum('ekij,ekjs->eis', block_part, gathered, preferred_element_type...]
    pallas_call x0 -> x16, Pallas kernels: none -> 17.6 us  [call(): pl.pallas_call(kernel, out_shape=shapes, in_specs=ins, out_specs=out_spec...]
    gather x4 -> x0, local copies, waits for them, and re-layouts: 9.42 us -> none  [image_of(): image = coupled(blocks, padded[local_source])]
    ppermute x8 -> x10, waiting for transfers between devices: 11.9 us -> 21 us  [the longest x4 11.2 us: to_right(): return lax.ppermute(x, 'elem', [(i, (i + 1) % ring) for i in range(ring)])]
    all_to_all x1 -> x0, blocking collectives: 8.79 us -> none  [on_device(): lax.all_to_all(current, 'state', split_axis=0, concat_axis=2, tiled=True)]
    all_to_all x1 -> x0, waiting for transfers between devices: 8.3 us -> none  [on_device(): lax.all_to_all(start_rows, 'state', split_axis=2, concat_axis=0, tiled=True)]
    ppermute x8 -> x10, starting transfers between devices: 18 us -> 10.7 us  [the longest x4 5.25 us: to_left(): return lax.ppermute(x, 'elem', [(i, (i - 1) % ring) for i in range(ring)])]
    all_to_all x1 -> x0, starting transfers between devices: 4.37 us -> none  [on_device(): lax.all_to_all(start_rows, 'state', split_axis=2, concat_axis=0, tiled=True)]
  transfers between devices with their start and end apart: 9 -> 10, of which waited for: 5 -> 6; matrix products, arithmetic and copies ran while one was open for 0% -> 2% of each run, Pallas kernels for 0% -> 25%
where the time goes in v1:
time: 56.2 us; the launch traced here: 55.9 us
  waiting for transfers between devices  21 us (37%)
  Pallas kernels  17.6 us (31%)
  starting transfers between devices  10.7 us (19%)
  local copies, waits for them, and re-layouts  6.42 us (11%)
    pallas_call x16, Pallas kernels, call(): pl.pallas_call(kernel, out_shape=shapes, in_specs=ins, out_specs=out_spec...  17.6 us
    ppermute x4, waiting for transfers between devices, to_right(): return lax.ppermute(x, 'elem', [(i, (i + 1) % ring) for i in range(ring)])  11.2 us
    ppermute x2, waiting for transfers between devices, swapped(): lax.ppermute(part, 'state', [(i, (i + k) % shards) for i in range(shards)])  9.81 us
    unnamed x15, local copies, waits for them, and re-layouts  6.42 us
    ppermute x4, starting transfers between devices, to_left(): return lax.ppermute(x, 'elem', [(i, (i - 1) % ring) for i in range(ring)])  5.25 us
    ppermute x2, starting transfers between devices, swapped(): lax.ppermute(part, 'state', [(i, (i + k) % shards) for i in range(shards)])  4.66 us
  transfers between devices with their start and end apart: 10, of which 6 were waited for; matrix products, arithmetic and copies ran while one was open for 2% of the time, Pallas kernels for 25%

profile of v1, /device:TPU:0, one launch (start us, length us, event | category | flops | bytes accessed | tf_op | source)
XLA Modules:
  0.0 55.9 jit_solution(9749745360137226930)
XLA Ops:
  0.0 0.0 copy-start.2
  0.0 1.0 %copy-done.2 = bf16[6,160,256]{2,1,0:T(8,128)(2,1)S(1)} copy-done((bf16[6,160,256]{2,1,0:T(8,128)(2,1)S(1)}, bf16[6,160,256]{2,1,0:T(8,128)(2,1)}, u32[]{:S(2)}) %copy-start.2) | copy-done | bytes 491544
  1.0 0.0 copy-start.3
  1.0 0.9 %copy-done.3 = bf16[256,256]{1,0:T(8,128)(2,1)S(1)} copy-done((bf16[256,256]{1,0:T(8,128)(2,1)S(1)}, bf16[256,256]{1,0:T(8,128)(2,1)}, u32[]{:S(2)}) %copy-start.3) | copy-done | bytes 131096
  1.9 0.0 copy-start.4
  1.9 0.7 %copy-done.4 = s32[12]{0:T(128)S(1)} copy-done((s32[12]{0:T(128)S(1)}, s32[12]{0:T(128)}, u32[]{:S(2)}) %copy-start.4) | copy-done | bytes 72
  2.6 1.0 %rotate.1 = (bf16[6,160,128]{2,1,0:T(8,128)(2,1)S(1)}, bf16[6,160,128]{2,1,0:T(8,128)(2,1)S(1)}) custom-call(bf16[6,160,256]{2,1,0:T(8,128)(2,1)S(1)} %copy-done.2, bf16[256,256]{1,0:T(8,128)(2,1)S(1)} %copy-done.3, s32[12]{0:T(128)S(1)} %copy-done.4), custom_call_target="tpu_custom_call" | custom-call | bytes 524288 | tf_op jit(solution)/shard_map/rotate/pallas_call | solution.py:22
  3.6 3.0 %collective-permute-start = (bf16[6,160,128]{2,1,0:T(8,128)(2,1)S(1)}, bf16[6,160,128]{2,1,0:T(8,128)(2,1)S(1)}, u32[]{:S(2)}, u32[]{:S(2)}) collective-permute-start(bf16[6,160,128]{2,1,0:T(8,128)(2,1)S(1)} %get-tuple-element.13), channel_id=1, source_target_pairs={{0,1},{1,0},{2,3},{3,2},{4,5},{5,4},{6,7},{7,6},{8,9},{9,8},{10,11... | collective-permute-start | bytes 737288 | tf_op jit(solution)/shard_map/ppermute | solution.py:119
  6.6 0.8 %copy.6 = s32[12,5]{1,0:T(8,128)S(1)} copy(s32[12,5]{0,1:T(8,128)} %param.8) | data formatting | bytes 480 | tf_op args[3]
  7.4 5.2 %collective-permute-done.refs_1_ = bf16[6,160,128]{2,1,0:T(8,128)(2,1)S(1)} collective-permute-done((bf16[6,160,128]{2,1,0:T(8,128)(2,1)S(1)}, bf16[6,160,128]{2,1,0:T(8,128)(2,1)S(1)}, u32[]{:S(2)}, u32[]{:S(2)}) %collective-permute-start) | collective-permute-done | bytes 245792 | tf_op jit(solution)/shard_map/ppermute | solution.py:119
  12.6 0.1 gather.1
  12.6 0.1 collective-permute-start.1
  12.7 4.4 %collective-permute-start.2 = (bf16[4,160,128]{2,1,0:T(8,128)(2,1)S(1)}, bf16[4,160,128]{2,1,0:T(8,128)(2,1)S(1)}, u32[]{:S(2)}, u32[]{:S(2)}) collective-permute-start(bf16[4,160,128]{2,1,0:T(8,128)(2,1)S(1)} %get-tuple-element.15.here.before.refs_0_), channel_id=1, source_target_pairs={{0,30},{2,0},{4,2},{6,4},{8,6},{10,8},{12,10},{14,12},{16,14},{18,... | collective-permute-start | bytes 491528 | tf_op jit(solution)/shard_map/ppermute | solution.py:115
  17.1 0.1 fusion.source
  17.2 3.0 %collective-permute-done.1.before = bf16[4,160,128]{2,1,0:T(8,128)(2,1)S(1)} collective-permute-done((bf16[4,160,128]{2,1,0:T(8,128)(2,1)S(1)}, bf16[4,160,128]{2,1,0:T(8,128)(2,1)S(1)}, u32[]{:S(2)}, u32[]{:S(2)}) %collective-permute-start.1) | collective-permute-done | bytes 163872 | tf_op jit(solution)/shard_map/ppermute | solution.py:112
  20.2 0.0 copy-start
  20.2 2.4 %copy-done = bf16[12,5,160,160]{3,2,1,0:T(8,128)(2,1)S(1)} copy-done((bf16[12,5,160,160]{3,2,1,0:T(8,128)(2,1)S(1)}, bf16[12,5,160,160]{3,2,1,0:T(8,128)(2,1)}, u32[]{:S(2)}) %copy-start) | copy-done | bytes 3072024
  22.6 0.0 copy-start.5
  22.6 0.7 %copy-done.5 = s32[12]{0:T(128)S(1)} copy-done((s32[12]{0:T(128)S(1)}, s32[12]{0:T(128)}, u32[]{:S(2)}) %copy-start.5) | copy-done | bytes 72
  23.3 0.0 copy-start.1
  23.3 1.3 %low.4.before.here.refs_0_ = bf16[4,160,128]{2,1,0:T(8,128)(2,1)S(1)} custom-call(bf16[12,5,160,160]{3,2,1,0:T(8,128)(2,1)S(1)} %copy-done, s32[12,5]{1,0:T(8,128)S(1)} %fusion.source, s32[12]{0:T(128)S(1)} %copy-done.5, bf16[4,160,128]{2,1,0:T(8,128)(2,1)S(1)} %collective-permute-done.1.before, ...), custom_call_target="tpu_custom_call" | custom-call | flops 131072000 | bytes 524288 | tf_op jit(solution)/shard_map/low/pallas_call | solution.py:22
  24.6 0.1 collective-permute-start.3
  24.6 0.0 collective-permute-done.2.after
  24.7 1.3 %high.4.after.here.refs_0_ = bf16[4,160,128]{2,1,0:T(8,128)(2,1)S(1)} custom-call(bf16[12,5,160,160]{3,2,1,0:T(8,128)(2,1)S(1)} %copy-done, s32[12,5]{1,0:T(8,128)S(1)} %fusion.source, s32[12]{0:T(128)S(1)} %copy-done.5, bf16[4,160,128]{2,1,0:T(8,128)(2,1)S(1)} %get-tuple-element.16.after.here.before.refs_0_, ...), custom_call_target="tpu_custom_call" | custom-call | flops 131072000 | bytes 524288 | tf_op jit(solution)/shard_map/high/pallas_call | solution.py:22
  25.9 0.5 collective-permute-start.4
  26.5 0.0 copy-done.1
  26.5 1.3 %middle.4.here.before.after.refs_0_ = bf16[4,160,128]{2,1,0:T(8,128)(2,1)S(1)} custom-call(bf16[12,5,160,160]{3,2,1,0:T(8,128)(2,1)S(1)} %copy-done.1, s32[12,5]{1,0:T(8,128)S(1)} %fusion.source, s32[12]{0:T(128)S(1)} %copy-done.5, bf16[4,160,128]{2,1,0:T(8,128)(2,1)S(1)} %get-tuple-element.15.here.before.refs_0_, ...), custom_call_target="tpu_custom_call" | custom-call | flops 131072000 | bytes 524288 | tf_op jit(solution)/shard_map/middle/pallas_call | solution.py:22
  27.8 0.0 copy-start.6
  27.8 0.0 collective-permute-done.3.after
  27.8 1.3 %high.5.here.after.refs_0_ = bf16[4,160,128]{2,1,0:T(8,128)(2,1)S(1)} custom-call(bf16[12,5,160,160]{3,2,1,0:T(8,128)(2,1)S(1)} %copy-done.1, s32[12,5]{1,0:T(8,128)S(1)} %fusion.source, s32[12]{0:T(128)S(1)} %copy-done.5, bf16[4,160,128]{2,1,0:T(8,128)(2,1)S(1)} %middle.4.here.before.after.refs_0_, bf16[4,160,128]{2,1,0:T(8,128)(2,1)S(1)} %high.4.after.here.refs_0_, ...), custom_call_target="tpu_custom_call" | custom-call | flops 131072000 | bytes 524288 | tf_op jit(solution)/shard_map/high/pallas_call | solution.py:22
  29.1 0.1 collective-permute-start.7
  29.2 4.2 %collective-permute-done.4.before = bf16[4,160,128]{2,1,0:T(8,128)(2,1)S(1)} collective-permute-done((bf16[4,160,128]{2,1,0:T(8,128)(2,1)S(1)}, bf16[4,160,128]{2,1,0:T(8,128)(2,1)S(1)}, u32[]{:S(2)}, u32[]{:S(2)}) %collective-permute-start.4) | collective-permute-done | bytes 163872 | tf_op jit(solution)/shard_map/ppermute | solution.py:112
  33.4 1.3 %low.5.here.before.refs_0_ = bf16[4,160,128]{2,1,0:T(8,128)(2,1)S(1)} custom-call(bf16[12,5,160,160]{3,2,1,0:T(8,128)(2,1)S(1)} %copy-done.1, s32[12,5]{1,0:T(8,128)S(1)} %fusion.source, s32[12]{0:T(128)S(1)} %copy-done.5, bf16[4,160,128]{2,1,0:T(8,128)(2,1)S(1)} %collective-permute-done.4.before, bf16[4,160,128]{2,1,0:T(8,128)(2,1)S(1)} %low.4.before.here.refs_0_, ...), custom_call_target="tpu_custom_call" | custom-call | flops 131072000 | bytes 524288 | tf_op jit(solution)/shard_map/low/pallas_call | solution.py:22
  34.7 0.2 collective-permute-start.5
  35.0 0.0 copy-done.6
  35.0 1.3 %middle.5.before.after.here.refs_0_ = bf16[4,160,128]{2,1,0:T(8,128)(2,1)S(1)} custom-call(bf16[12,5,160,160]{3,2,1,0:T(8,128)(2,1)S(1)} %copy-done.1, s32[12,5]{1,0:T(8,128)S(1)} %fusion.source, s32[12]{0:T(128)S(1)} %copy-done.6, bf16[4,160,128]{2,1,0:T(8,128)(2,1)S(1)} %low.4.before.here.refs_0_, ...), custom_call_target="tpu_custom_call" | custom-call | flops 131072000 | bytes 524288 | tf_op jit(solution)/shard_map/middle/pallas_call | solution.py:22
  36.3 0.4 collective-permute-done.7.before
  36.7 1.3 %low.6.here.before = bf16[4,160,128]{2,1,0:T(8,128)(2,1)S(1)} custom-call(bf16[12,5,160,160]{3,2,1,0:T(8,128)(2,1)S(1)} %copy-done.1, s32[12,5]{1,0:T(8,128)S(1)} %fusion.source, s32[12]{0:T(128)S(1)} %copy-done.6, bf16[4,160,128]{2,1,0:T(8,128)(2,1)S(1)} %collective-permute-done.7.before, bf16[4,160,128]{2,1,0:T(8,128)(2,1)S(1)} %low.5.here.before.refs_0_, ...), custom_call_target="tpu_custom_call" | custom-call | flops 131072000 | bytes 524288 | tf_op jit(solution)/shard_map/low/pallas_call | solution.py:22
  38.0 0.5 collective-permute-start.8
  38.6 0.0 collective-permute-done.5.after
  38.6 1.3 %high.6.after.here = bf16[4,160,128]{2,1,0:T(8,128)(2,1)S(1)} custom-call(bf16[12,5,160,160]{3,2,1,0:T(8,128)(2,1)S(1)} %copy-done.1, s32[12,5]{1,0:T(8,128)S(1)} %fusion.source, s32[12]{0:T(128)S(1)} %copy-done.6, bf16[4,160,128]{2,1,0:T(8,128)(2,1)S(1)} %middle.5.before.after.here.refs_0_, bf16[4,160,128]{2,1,0:T(8,128)(2,1)S(1)} %high.5.here.after.refs_0_, ...), custom_call_target="tpu_custom_call" | custom-call | flops 131072000 | bytes 524288 | tf_op jit(solution)/shard_map/high/pallas_call | solution.py:22
  39.9 0.1 collective-permute-start.6
  39.9 1.3 %middle.6.after.here.before = bf16[4,160,128]{2,1,0:T(8,128)(2,1)S(1)} custom-call(bf16[12,5,160,160]{3,2,1,0:T(8,128)(2,1)S(1)} %copy-done.1, s32[12,5]{1,0:T(8,128)S(1)} %fusion.source, s32[12]{0:T(128)S(1)} %copy-done.6, bf16[4,160,128]{2,1,0:T(8,128)(2,1)S(1)} %low.5.here.before.refs_0_, bf16[4,160,128]{2,1,0:T(8,128)(2,1)S(1)} %middle.5.before.after.here.refs_0_, ...), custom_call_target="tpu_custom_call" | custom-call | flops 131072000 | bytes 524288 | tf_op jit(solution)/shard_map/middle/pallas_call | solution.py:22
  41.2 1.3 %middle.7.refs_1_ = bf16[4,160,128]{2,1,0:T(8,128)(2,1)S(1)} custom-call(bf16[12,5,160,160]{3,2,1,0:T(8,128)(2,1)S(1)} %copy-done.1, s32[12,5]{1,0:T(8,128)S(1)} %fusion.source, s32[12]{0:T(128)S(1)} %copy-done.6, bf16[4,160,128]{2,1,0:T(8,128)(2,1)S(1)} %low.6.here.before, bf16[4,160,128]{2,1,0:T(8,128)(2,1)S(1)} %middle.6.after.here.before, ...), custom_call_target="tpu_custom_call" | custom-call | flops 131072000 | bytes 524288 | tf_op jit(solution)/shard_map/middle/pallas_call | solution.py:22
  42.6 0.0 collective-permute-done.8.after
  42.6 1.3 %high.7.refs_2_ = bf16[4,160,128]{2,1,0:T(8,128)(2,1)S(1)} custom-call(bf16[12,5,160,160]{3,2,1,0:T(8,128)(2,1)S(1)} %copy-done.1, s32[12,5]{1,0:T(8,128)S(1)} %fusion.source, s32[12]{0:T(128)S(1)} %copy-done.6, bf16[4,160,128]{2,1,0:T(8,128)(2,1)S(1)} %middle.6.after.here.before, bf16[4,160,128]{2,1,0:T(8,128)(2,1)S(1)} %high.6.after.here, ...), custom_call_target="tpu_custom_call" | custom-call | flops 131072000 | bytes 524288 | tf_op jit(solution)/shard_map/high/pallas_call | solution.py:22
  43.9 3.5 %collective-permute-done.6.before = bf16[4,160,128]{2,1,0:T(8,128)(2,1)S(1)} collective-permute-done((bf16[4,160,128]{2,1,0:T(8,128)(2,1)S(1)}, bf16[4,160,128]{2,1,0:T(8,128)(2,1)S(1)}, u32[]{:S(2)}, u32[]{:S(2)}) %collective-permute-start.6) | collective-permute-done | bytes 163872 | tf_op jit(solution)/shard_map/ppermute | solution.py:112
  47.4 1.3 %low.7.refs_0_ = bf16[4,160,128]{2,1,0:T(8,128)(2,1)S(1)} custom-call(bf16[12,5,160,160]{3,2,1,0:T(8,128)(2,1)S(1)} %copy-done.1, s32[12,5]{1,0:T(8,128)S(1)} %fusion.source, s32[12]{0:T(128)S(1)} %copy-done.6, bf16[4,160,128]{2,1,0:T(8,128)(2,1)S(1)} %collective-permute-done.6.before, bf16[4,160,128]{2,1,0:T(8,128)(2,1)S(1)} %low.6.here.before, ...), custom_call_target="tpu_custom_call" | custom-call | flops 131072000 | bytes 524288 | tf_op jit(solution)/shard_map/low/pallas_call | solution.py:22
  48.7 0.1 scatter.1
  48.8 1.6 %collective-permute-start.9 = (bf16[6,160,128]{2,1,0:T(8,128)(2,1)S(1)}, bf16[6,160,128]{2,1,0:T(8,128)(2,1)S(1)}, u32[]{:S(2)}, u32[]{:S(2)}) collective-permute-start(bf16[6,160,128]{2,1,0:T(8,128)(2,1)S(1)} %get-tuple-element.18), channel_id=1, source_target_pairs={{0,1},{1,0},{2,3},{3,2},{4,5},{5,4},{6,7},{7,6},{8,9},{9,8},{10,11... | collective-permute-start | bytes 737288 | tf_op jit(solution)/shard_map/ppermute | solution.py:119
  50.4 4.6 %collective-permute-done.9.refs_1_ = bf16[6,160,128]{2,1,0:T(8,128)(2,1)S(1)} collective-permute-done((bf16[6,160,128]{2,1,0:T(8,128)(2,1)S(1)}, bf16[6,160,128]{2,1,0:T(8,128)(2,1)S(1)}, u32[]{:S(2)}, u32[]{:S(2)}) %collective-permute-start.9) | collective-permute-done | bytes 245792 | tf_op jit(solution)/shard_map/ppermute | solution.py:119
  55.0 0.9 %join.1 = bf16[6,160,256]{2,1,0:T(8,128)(2,1)} custom-call(bf16[6,160,128]{2,1,0:T(8,128)(2,1)S(1)} %get-tuple-element.17.refs_0_, bf16[6,160,128]{2,1,0:T(8,128)(2,1)S(1)} %collective-permute-done.9.refs_1_), custom_call_target="tpu_custom_call" | custom-call | bytes 524288 | tf_op jit(solution)/shard_map/join/pallas_call | solution.py:22
  (1 shorter events, 0.0 us)
Async XLA Ops:
  0.0 1.0 %copy-start.2 = (bf16[6,160,256]{2,1,0:T(8,128)(2,1)S(1)}, bf16[6,160,256]{2,1,0:T(8,128)(2,1)}, u32[]{:S(2)}) copy-start(bf16[6,160,256]{2,1,0:T(8,128)(2,1)} %orbitals.1) | copy-start | bytes 1474564
  1.0 0.9 %copy-start.3 = (bf16[256,256]{1,0:T(8,128)(2,1)S(1)}, bf16[256,256]{1,0:T(8,128)(2,1)}, u32[]{:S(2)}) copy-start(bf16[256,256]{1,0:T(8,128)(2,1)} %rotation.1) | copy-start | bytes 393220
  1.9 0.7 %copy-start.4 = (s32[12]{0:T(128)S(1)}, s32[12]{0:T(128)}, u32[]{:S(2)}) copy-start(s32[12]{0:T(128)} %counts.25) | copy-start | bytes 148
  3.6 9.0 %collective-permute-start = (bf16[6,160,128]{2,1,0:T(8,128)(2,1)S(1)}, bf16[6,160,128]{2,1,0:T(8,128)(2,1)S(1)}, u32[]{:S(2)}, u32[]{:S(2)}) collective-permute-start(bf16[6,160,128]{2,1,0:T(8,128)(2,1)S(1)} %get-tuple-element.13), channel_id=1, source_target_pairs={{0,1},{1,0},{2,3},{3,2},{4,5},{5,4},{6,7},{7,6},{8,9},{9,8},{10,11... | collective-permute-start | bytes 737288 | tf_op jit(solution)/shard_map/ppermute | solution.py:119
  12.6 7.6 %collective-permute-start.1 = (bf16[4,160,128]{2,1,0:T(8,128)(2,1)S(1)}, bf16[4,160,128]{2,1,0:T(8,128)(2,1)S(1)}, u32[]{:S(2)}, u32[]{:S(2)}) collective-permute-start(bf16[4,160,128]{2,1,0:T(8,128)(2,1)S(1)} %get-tuple-element.14.after.here.refs_0_), channel_id=1, source_target_pairs={{0,2},{2,4},{4,6},{6,8},{8,10},{10,12},{12,14},{14,16},{16,18},{18... | collective-permute-start | bytes 491528 | tf_op jit(solution)/shard_map/ppermute | solution.py:112
  12.7 11.9 %collective-permute-start.2 = (bf16[4,160,128]{2,1,0:T(8,128)(2,1)S(1)}, bf16[4,160,128]{2,1,0:T(8,128)(2,1)S(1)}, u32[]{:S(2)}, u32[]{:S(2)}) collective-permute-start(bf16[4,160,128]{2,1,0:T(8,128)(2,1)S(1)} %get-tuple-element.15.here.before.refs_0_), channel_id=1, source_target_pairs={{0,30},{2,0},{4,2},{6,4},{8,6},{10,8},{12,10},{14,12},{16,14},{18,... | collective-permute-start | bytes 491528 | tf_op jit(solution)/shard_map/ppermute | solution.py:115
  20.2 2.4 %copy-start = (bf16[12,5,160,160]{3,2,1,0:T(8,128)(2,1)S(1)}, bf16[12,5,160,160]{3,2,1,0:T(8,128)(2,1)}, u32[]{:S(2)}) copy-start(bf16[12,5,160,160]{3,2,1,0:T(8,128)(2,1)} %blocks.23) | copy-start | bytes 9216004
  22.6 0.7 %copy-start.5 = (s32[12]{0:T(128)S(1)}, s32[12]{0:T(128)}, u32[]{:S(2)}) copy-start(s32[12]{0:T(128)} %counts.25) | copy-start | bytes 148
  23.3 3.2 %copy-start.1 = (bf16[12,5,160,160]{3,2,1,0:T(8,128)(2,1)S(1)}, bf16[12,5,160,160]{3,2,1,0:T(8,128)(2,1)}, u32[]{:S(2)}) copy-start(bf16[12,5,160,160]{3,2,1,0:T(8,128)(2,1)} %blocks.23) | copy-start | bytes 9216004
  24.6 3.2 %collective-permute-start.3 = (bf16[4,160,128]{2,1,0:T(8,128)(2,1)S(1)}, bf16[4,160,128]{2,1,0:T(8,128)(2,1)S(1)}, u32[]{:S(2)}, u32[]{:S(2)}) collective-permute-start(bf16[4,160,128]{2,1,0:T(8,128)(2,1)S(1)} %low.4.before.here.refs_0_), channel_id=1, source_target_pairs={{0,30},{2,0},{4,2},{6,4},{8,6},{10,8},{12,10},{14,12},{16,14},{18,... | collective-permute-start | bytes 491528 | tf_op jit(solution)/shard_map/ppermute | solution.py:115
  25.9 7.5 %collective-permute-start.4 = (bf16[4,160,128]{2,1,0:T(8,128)(2,1)S(1)}, bf16[4,160,128]{2,1,0:T(8,128)(2,1)S(1)}, u32[]{:S(2)}, u32[]{:S(2)}) collective-permute-start(bf16[4,160,128]{2,1,0:T(8,128)(2,1)S(1)} %high.4.after.here.refs_0_), channel_id=1, source_target_pairs={{0,2},{2,4},{4,6},{6,8},{8,10},{10,12},{12,14},{14,16},{16,18},{18... | collective-permute-start | bytes 491528 | tf_op jit(solution)/shard_map/ppermute | solution.py:112
  27.8 7.2 %copy-start.6 = (s32[12]{0:T(128)S(1)}, s32[12]{0:T(128)}, u32[]{:S(2)}) copy-start(s32[12]{0:T(128)} %counts.25) | copy-start | bytes 148
  29.1 7.6 %collective-permute-start.7 = (bf16[4,160,128]{2,1,0:T(8,128)(2,1)S(1)}, bf16[4,160,128]{2,1,0:T(8,128)(2,1)S(1)}, u32[]{:S(2)}, u32[]{:S(2)}) collective-permute-start(bf16[4,160,128]{2,1,0:T(8,128)(2,1)S(1)} %high.5.here.after.refs_0_), channel_id=1, source_target_pairs={{0,2},{2,4},{4,6},{6,8},{8,10},{10,12},{12,14},{14,16},{16,18},{18... | collective-permute-start | bytes 491528 | tf_op jit(solution)/shard_map/ppermute | solution.py:112
  34.7 3.8 %collective-permute-start.5 = (bf16[4,160,128]{2,1,0:T(8,128)(2,1)S(1)}, bf16[4,160,128]{2,1,0:T(8,128)(2,1)S(1)}, u32[]{:S(2)}, u32[]{:S(2)}) collective-permute-start(bf16[4,160,128]{2,1,0:T(8,128)(2,1)S(1)} %low.5.here.before.refs_0_), channel_id=1, source_target_pairs={{0,30},{2,0},{4,2},{6,4},{8,6},{10,8},{12,10},{14,12},{16,14},{18,... | collective-permute-start | bytes 491528 | tf_op jit(solution)/shard_map/ppermute | solution.py:115
  38.0 4.5 %collective-permute-start.8 = (bf16[4,160,128]{2,1,0:T(8,128)(2,1)S(1)}, bf16[4,160,128]{2,1,0:T(8,128)(2,1)S(1)}, u32[]{:S(2)}, u32[]{:S(2)}) collective-permute-start(bf16[4,160,128]{2,1,0:T(8,128)(2,1)S(1)} %low.6.here.before), channel_id=1, source_target_pairs={{0,30},{2,0},{4,2},{6,4},{8,6},{10,8},{12,10},{14,12},{16,14},{18,... | collective-permute-start | bytes 491528 | tf_op jit(solution)/shard_map/ppermute | solution.py:115
  39.9 7.5 %collective-permute-start.6 = (bf16[4,160,128]{2,1,0:T(8,128)(2,1)S(1)}, bf16[4,160,128]{2,1,0:T(8,128)(2,1)S(1)}, u32[]{:S(2)}, u32[]{:S(2)}) collective-permute-start(bf16[4,160,128]{2,1,0:T(8,128)(2,1)S(1)} %high.6.after.here), channel_id=1, source_target_pairs={{0,2},{2,4},{4,6},{6,8},{8,10},{10,12},{12,14},{14,16},{16,18},{18... | collective-permute-start | bytes 491528 | tf_op jit(solution)/shard_map/ppermute | solution.py:112
  48.8 6.3 %collective-permute-start.9 = (bf16[6,160,128]{2,1,0:T(8,128)(2,1)S(1)}, bf16[6,160,128]{2,1,0:T(8,128)(2,1)S(1)}, u32[]{:S(2)}, u32[]{:S(2)}) collective-permute-start(bf16[6,160,128]{2,1,0:T(8,128)(2,1)S(1)} %get-tuple-element.18), channel_id=1, source_target_pairs={{0,1},{1,0},{2,3},{3,2},{4,5},{5,4},{6,7},{7,6},{8,9},{9,8},{10,11... | collective-permute-start | bytes 737288 | tf_op jit(solution)/shard_map/ppermute | solution.py:119

commit v2 on v1

v2 whole, which is shorter than its diff:
```python
import functools

import jax
import jax.numpy as jnp
from jax import lax
from jax.experimental import pallas as pl
from jax.experimental.pallas import tpu as pltpu
from jax.sharding import PartitionSpec as P

DEG = 4
FULL = 128

center_shift = 0.2
half_span = 1.1

VMEM = pl.BlockSpec(memory_space=pltpu.VMEM)
HBM = pl.BlockSpec(memory_space=pltpu.HBM)
ANY = pl.BlockSpec(memory_space=pl.ANY)


def call(kernel, outs, ins, *args, out_specs=None, scratch=(), aliases=None, limit=4 << 20, flops=0, name=None):
    return pl.pallas_call(
        kernel,
        out_shape=outs,
        in_specs=ins,
        out_specs=out_specs or [VMEM] * len(outs),
        scratch_shapes=list(scratch),
        input_output_aliases=aliases or {},
        compiler_params=pltpu.CompilerParams(vmem_limit_bytes=limit),
        cost_estimate=pl.CostEstimate(flops=flops, bytes_accessed=1 << 20, transcendentals=0),
        name=name,
    )(*args)


def bf16(*shape):
    return jax.ShapeDtypeStruct(shape, jnp.bfloat16)


def rows_below(count, rows, lanes):
    return lax.broadcasted_iota(jnp.int32, (rows, lanes), 0) < count


def turn(shards, k, element, weights, count):
    rows, lanes = element.shape[0], weights.shape[1] // shards
    at = lax.rem(lax.axis_index("state") + k, shards) * lanes
    turned = jnp.dot(element, weights[:, pl.ds(pl.multiple_of(at, lanes), lanes)], preferred_element_type=jnp.float32)
    return jnp.where(rows_below(count, rows, lanes), turned, 0.0).astype(jnp.bfloat16)


def rotate_out_kernel(shards, orbitals, rotation, counts, *refs):
    outs, (held, weights, limits, sems) = refs[: shards - 1], refs[shards - 1 :]
    elems = orbitals.shape[0]
    me = lax.axis_index("state")
    copies = [
        pltpu.make_async_copy(rotation, weights, sems.at[0]),
        pltpu.make_async_copy(counts, limits, sems.at[1]),
    ]
    copies += [pltpu.make_async_copy(orbitals.at[e], held.at[e], sems.at[2 + e]) for e in range(elems)]
    for copy in copies:
        copy.start()
    copies[0].wait()
    copies[1].wait()
    for e in range(elems):
        copies[2 + e].wait()
        for k, out in enumerate(outs):
            out[e] = turn(shards, k + 1, held[e], weights, limits[me * elems + e])


def local_kernel(reach, total, shards, blocks, neighbors, counts, held, weights, kept, packed, source, limits, raw, scalars, sems):
    elems, couplings, rows, _ = blocks.shape
    copies = [pltpu.make_async_copy(blocks.at[e], raw.at[e], sems.at[e]) for e in range(elems)]
    more = [
        pltpu.make_async_copy(counts, scalars, sems.at[elems]),
        pltpu.make_async_copy(counts, limits, sems.at[elems + 1]),
    ]
    for copy in more + copies:
        copy.start()
    row = lax.broadcasted_iota(jnp.int32, neighbors.shape, 0)
    offset = neighbors[...] - (row + lax.axis_index("elem") * elems)
    offset = jnp.where(offset > reach, offset - total, jnp.where(offset < -reach, offset + total, offset))
    within = row
    for g in range(1, elems // reach):
        within = jnp.where(row >= g * reach, row - g * reach, within)
    source[...] = offset + within + reach
    for copy in more:
        copy.wait()
    mine = held.shape[0]
    for e in range(mine):
        kept[e] = turn(shards, 0, held[e], weights, scalars[lax.axis_index("state") * mine + e])
    for e in range(elems):
        copies[e].wait()
        for k in range(couplings):
            packed[e, :, k * FULL : (k + 1) * FULL] = raw[e, k, :, :FULL]
        packed[e, :, couplings * FULL :] = jnp.concatenate([raw[e, k, :, FULL:] for k in range(couplings)], axis=1)


def gather_kernel(shards, *refs):
    me = lax.axis_index("state")
    parts, groups, whole = refs[:shards], refs[shards : shards + 3], refs[-1]
    elems, width = parts[0].shape[0], groups[0].shape[0]
    for k, part in enumerate(parts):
        whole[pl.ds(lax.rem(me + shards - k, shards) * elems, elems)] = part[...]
    for g, group in enumerate(groups):
        group[...] = whole[g * width : (g + 1) * width]


def level_kernel(first, factor, with_prev, packed, source, limits, before, here, after, *refs):
    out, window = refs[-2:]
    width, rows, lanes = here.shape
    for g, group in enumerate((before, here, after)):
        window[g * width : (g + 1) * width] = group[...]
    places, ends = source[...], limits[...]
    for e in range(width):
        at = [places[first + e, k] for k in range(places.shape[1])]
        fields = [window[i, :FULL] for i in at] + [window[i, FULL:] for i in at]
        image = jnp.dot(packed[first + e], jnp.concatenate(fields, axis=0), preferred_element_type=jnp.float32)
        image = jnp.where(rows_below(ends[first + e], rows, lanes), image, 0.0)
        value = factor * (image - center_shift * here[e].astype(jnp.float32)) / half_span
        if with_prev:
            value = value - refs[0][e].astype(jnp.float32)
        out[e] = value.astype(jnp.bfloat16)


def scatter_kernel(shards, *refs):
    me = lax.axis_index("state")
    groups, parts, whole = refs[:3], refs[3:-1], refs[-1]
    elems, width = parts[0].shape[0], groups[0].shape[0]
    for g, group in enumerate(groups):
        whole[g * width : (g + 1) * width] = group[...]
    for k, part in enumerate(parts):
        part[...] = whole[pl.ds(lax.rem(me + k, shards) * elems, elems)]


def place(shards, k, part, out, sem):
    lanes = part.shape[2]
    at = lax.rem(lax.axis_index("state") + shards - k, shards) * lanes
    return pltpu.make_async_copy(part, out.at[:, :, pl.ds(pl.multiple_of(at, lanes), lanes)], sem)


def own_kernel(shards, part, out, sem):
    copy = place(shards, 0, part, out, sem)
    copy.start()
    copy.wait()


def others_kernel(shards, *refs):
    parts, out, sems = refs[: shards - 1], refs[-2], refs[-1]
    copies = [place(shards, k + 1, part, out, sems.at[k]) for k, part in enumerate(parts)]
    for copy in copies:
        copy.start()
    for copy in copies:
        copy.wait()


def on_device(orbitals, rotation, counts, neighbors, blocks):
    row_elems, rows, states = orbitals.shape
    elems, couplings = neighbors.shape
    orbitals, rotation, counts, blocks = (
        pltpu.with_memory_space_constraint(x, pltpu.HBM) for x in (orbitals, rotation, counts, blocks)
    )
    shards = lax.axis_size("state")
    ring = lax.axis_size("elem")
    width = elems // 3
    lanes = states // shards
    group, part = bf16(width, rows, lanes), bf16(row_elems, rows, lanes)
    whole = pltpu.VMEM((elems, rows, lanes), jnp.bfloat16)
    scalars = pltpu.SMEM(counts.shape, jnp.int32)
    dma = pltpu.SemaphoreType.DMA

    def to_right(x):
        return lax.ppermute(x, "elem", [(i, (i + 1) % ring) for i in range(ring)])

    def to_left(x):
        return lax.ppermute(x, "elem", [(i, (i - 1) % ring) for i in range(ring)])

    def swapped(parts):
        return [
            lax.ppermute(part, "state", [(i, (i + k + 1) % shards) for i in range(shards)])
            for k, part in enumerate(parts)
        ]

    *parts, held, weights = call(
        functools.partial(rotate_out_kernel, shards),
        [part] * (shards - 1) + [bf16(*orbitals.shape), bf16(*rotation.shape)],
        [HBM] * 3,
        orbitals,
        rotation,
        counts,
        scratch=[scalars, dma((row_elems + 2,))],
        name="rotate_out",
    )
    arrived = swapped(parts)
    kept, packed, source, limits = call(
        functools.partial(local_kernel, width, elems * ring, shards),
        [
            part,
            bf16(elems, rows, couplings * rows),
            jax.ShapeDtypeStruct(neighbors.shape, jnp.int32),
            jax.ShapeDtypeStruct(counts.shape, jnp.int32),
        ],
        [HBM, VMEM, HBM, VMEM, VMEM],
        blocks,
        neighbors,
        counts,
        held,
        weights,
        scratch=[pltpu.VMEM(blocks.shape, jnp.bfloat16), scalars, dma((elems + 2,))],
        limit=16 << 20,
        name="local",
    )
    low, middle, high = call(
        functools.partial(drop_input, functools.partial(gather_kernel, shards), shards),
        [group] * 3,
        [VMEM] * shards + [ANY],
        kept,
        *arrived,
        packed,
        scratch=[whole],
        name="gather",
    )

    def level(g, m, before, here, after, previous, behind=None):
        body = functools.partial(level_kernel, g * width, 1.0 if m == 1 else 2.0, previous is not None)
        if behind is not None:
            body = functools.partial(drop_input, body, 6 + (previous is not None))
        args = [packed, source, limits, before, here, after] + ([] if previous is None else [previous])
        specs = [VMEM] * len(args)
        if behind is not None:
            args, specs = args + [behind], specs + [ANY]
        return call(
            body,
            [group],
            specs,
            *args,
            scratch=[pltpu.VMEM((3 * width, rows, lanes), jnp.bfloat16)],
            flops=2 * width * couplings * rows * rows * lanes,
            name=("low", "middle", "high")[g] + str(m),
        )[0]

    older = (None, None, None)
    from_right, from_left = to_left(low), to_right(high)
    for m in range(1, DEG + 1):
        if m % 2:
            new_high = level(2, m, middle, high, from_right, older[2])
            right_halo = to_right(new_high) if m < DEG else None
            new_low = level(0, m, from_left, low, middle, older[0], new_high)
            left_halo = to_left(new_low) if m < DEG else None
        else:
            new_low = level(0, m, from_left, low, middle, older[0])
            left_halo = to_left(new_low) if m < DEG else None
            new_high = level(2, m, middle, high, from_right, older[2], new_low)
            right_halo = to_right(new_high) if m < DEG else None
        new_middle = level(1, m, low, middle, high, older[1])
        from_left, from_right = right_halo, left_halo
        older, (low, middle, high) = (low, middle, high), (new_low, new_middle, new_high)

    kept, *parts = call(
        functools.partial(scatter_kernel, shards),
        [part] * shards,
        [VMEM] * 3,
        low,
        middle,
        high,
        scratch=[whole],
        name="scatter",
    )
    arrived = swapped(parts)
    out = call(
        functools.partial(own_kernel, shards),
        [bf16(*orbitals.shape)],
        [VMEM],
        kept,
        out_specs=[HBM],
        scratch=[dma],
        name="own",
    )[0]
    return call(
        functools.partial(drop_input, functools.partial(others_kernel, shards), shards - 1),
        [bf16(*orbitals.shape)],
        [VMEM] * (shards - 1) + [HBM],
        *arrived,
        out,
        out_specs=[HBM],
        scratch=[dma((shards - 1,))],
        aliases={shards - 1: 0},
        name="others",
    )[0]


def drop_input(body, at, *refs):
    body(*refs[:at], *refs[at + 1 :])


def solution(mesh):
    in_specs = (
        P(("elem", "state"), None, None),
        P(),
        P("elem"),
        P("elem", None),
        P("elem", None, None, None),
    )
    out_specs = P(("elem", "state"), None, None)
    return jax.shard_map(on_device, mesh=mesh, in_specs=in_specs, out_specs=out_specs, check_vma=False)
```

time: 56.2 us -> 47.3 us (0.84)
  local copies, waits for them, and re-layouts: 6.42 us -> 0.77 us
  Pallas kernels: 17.6 us -> 13.5 us
  waiting for transfers between devices: 21 us -> 23.2 us
  starting transfers between devices: 10.7 us -> 9.48 us
    unnamed x15 -> x1, local copies, waits for them, and re-layouts: 6.42 us -> 0.77 us
    pallas_call x16 -> x18, Pallas kernels: 17.6 us -> 13.5 us  [call(): pl.pallas_call(kernel, out_shape=outs, in_specs=ins, out_specs=out_specs...]
    ppermute x4, waiting for transfers between devices: 0.01 us -> 3.92 us  [to_left(): return lax.ppermute(x, 'elem', [(i, (i - 1) % ring) for i in range(ring)])]
    ppermute x2, waiting for transfers between devices: 9.81 us -> 7.65 us  [swapped(): lax.ppermute(part, 'state', [(i, (i + k + 1) % shards) for i in range(sha...]
    ppermute x4, starting transfers between devices: 5.25 us -> 4.21 us  [to_left(): return lax.ppermute(x, 'elem', [(i, (i - 1) % ring) for i in range(ring)])]
  transfers between devices with their start and end apart: 10 -> 10, of which waited for: 6 -> 8; matrix products, arithmetic and copies ran while one was open for 2% -> 2% of each run, Pallas kernels for 25% -> 21%
where the time goes in v2:
time: 47.3 us; the launch traced here: 47.1 us
  waiting for transfers between devices  23.2 us (49%)
  Pallas kernels  13.5 us (29%)
  starting transfers between devices  9.48 us (20%)
  local copies, waits for them, and re-layouts  0.77 us (2%)
    pallas_call x18, Pallas kernels, call(): pl.pallas_call(kernel, out_shape=outs, in_specs=ins, out_specs=out_specs...  13.5 us
    ppermute x4, waiting for transfers between devices, to_right(): return lax.ppermute(x, 'elem', [(i, (i + 1) % ring) for i in range(ring)])  11.6 us
    ppermute x2, waiting for transfers between devices, swapped(): lax.ppermute(part, 'state', [(i, (i + k + 1) % shards) for i in range(sha...  7.65 us
    ppermute x2, starting transfers between devices, swapped(): lax.ppermute(part, 'state', [(i, (i + k + 1) % shards) for i in range(sha...  4.59 us
    ppermute x4, starting transfers between devices, to_left(): return lax.ppermute(x, 'elem', [(i, (i - 1) % ring) for i in range(ring)])  4.21 us
    ppermute x4, waiting for transfers between devices, to_left(): return lax.ppermute(x, 'elem', [(i, (i - 1) % ring) for i in range(ring)])  3.92 us
  transfers between devices with their start and end apart: 10, of which 8 were waited for; matrix products, arithmetic and copies ran while one was open for 2% of the time, Pallas kernels for 21%

profile of v2, /device:TPU:0, one launch (start us, length us, event | category | flops | bytes accessed | tf_op | source)
XLA Modules:
  0.0 47.1 jit_solution(7409607003922095003)
XLA Ops:
  0.0 2.1 %rotate_out.1 = (bf16[6,160,128]{2,1,0:T(8,128)(2,1)S(1)}, bf16[6,160,256]{2,1,0:T(8,128)(2,1)S(1)}, bf16[256,256]{1,0:T(8,128)(2,1)S(1)}) custom-call(bf16[6,160,256]{2,1,0:T(8,128)(2,1)} %orbitals.1, bf16[256,256]{1,0:T(8,128)(2,1)} %rotation.1, s32[12]{0:T(128)} %counts.3), custom_call_target="tpu_custom_call" | custom-call | bytes 1048576 | tf_op jit(solution)/shard_map/rotate_out/pallas_call | solution.py:22
  2.1 3.0 %collective-permute-start = (bf16[6,160,128]{2,1,0:T(8,128)(2,1)S(1)}, bf16[6,160,128]{2,1,0:T(8,128)(2,1)S(1)}, u32[]{:S(2)}, u32[]{:S(2)}) collective-permute-start(bf16[6,160,128]{2,1,0:T(8,128)(2,1)S(1)} %get-tuple-element.23), channel_id=1, source_target_pairs={{0,1},{1,0},{2,3},{3,2},{4,5},{5,4},{6,7},{7,6},{8,9},{9,8},{10,11... | collective-permute-start | bytes 737288 | tf_op jit(solution)/shard_map/ppermute | solution.py:178
  5.1 0.8 %copy.7.neighbors = s32[12,5]{1,0:T(8,128)S(1)} copy(s32[12,5]{0,1:T(8,128)} %param.8) | data formatting | bytes 480 | tf_op args[3]
  5.9 2.8 %local.1 = (bf16[6,160,128]{2,1,0:T(8,128)(2,1)S(1)}, bf16[12,160,800]{2,1,0:T(8,128)(2,1)S(1)}, s32[12,5]{1,0:T(8,128)S(1)}, s32[12]{0:T(128)S(1)}) custom-call(bf16[12,5,160,160]{3,2,1,0:T(8,128)(2,1)} %blocks.1, s32[12,5]{1,0:T(8,128)S(1)} %copy.7.neighbors, s32[12]{0:T(128)} %counts.3, bf16[6,160,256]{2,1,0:T(8,128)(2,1)S(1)} %get-tuple-element.17.held, ...), custom_call_target="tpu_custom_call" | custom-call | bytes 1048576 | tf_op jit(solution)/shard_map/local/pallas_call | solution.py:22
  8.7 2.4 %collective-permute-done.refs_1_ = bf16[6,160,128]{2,1,0:T(8,128)(2,1)S(1)} collective-permute-done((bf16[6,160,128]{2,1,0:T(8,128)(2,1)S(1)}, bf16[6,160,128]{2,1,0:T(8,128)(2,1)S(1)}, u32[]{:S(2)}, u32[]{:S(2)}) %collective-permute-start) | collective-permute-done | bytes 245792 | tf_op jit(solution)/shard_map/ppermute | solution.py:178
  11.1 0.1 gather.1
  11.2 3.4 %collective-permute-start.2 = (bf16[4,160,128]{2,1,0:T(8,128)(2,1)S(1)}, bf16[4,160,128]{2,1,0:T(8,128)(2,1)S(1)}, u32[]{:S(2)}, u32[]{:S(2)}) collective-permute-start(bf16[4,160,128]{2,1,0:T(8,128)(2,1)S(1)} %get-tuple-element.25.refs_4_.before.refs_0_), channel_id=1, source_target_pairs={{0,30},{2,0},{4,2},{6,4},{8,6},{10,8},{12,10},{14,12},{16,14},{18,... | collective-permute-start | bytes 491528 | tf_op jit(solution)/shard_map/ppermute | solution.py:174
  14.6 0.0 collective-permute-start.1
  14.6 2.8 %collective-permute-done.2.after = bf16[4,160,128]{2,1,0:T(8,128)(2,1)S(1)} collective-permute-done((bf16[4,160,128]{2,1,0:T(8,128)(2,1)S(1)}, bf16[4,160,128]{2,1,0:T(8,128)(2,1)S(1)}, u32[]{:S(2)}, u32[]{:S(2)}) %collective-permute-start.2) | collective-permute-done | bytes 163872 | tf_op jit(solution)/shard_map/ppermute | solution.py:174
  17.4 0.6 %high1.1.refs_6_.after.refs_4_.refs_0_ = bf16[4,160,128]{2,1,0:T(8,128)(2,1)S(1)} custom-call(bf16[12,160,800]{2,1,0:T(8,128)(2,1)S(1)} %get-tuple-element.19.refs_2_.packed.refs_0_, s32[12,5]{1,0:T(8,128)S(1)} %get-tuple-element.20.source.refs_1_, s32[12]{0:T(128)S(1)} %get-tuple-element.21.limits.refs_2_, ...), custom_call_target="tpu_custom_call" | custom-call | flops 131072000 | bytes 1048576 | tf_op jit(solution)/shard_map/high1/pallas_call | solution.py:22
  18.0 0.1 collective-permute-start.4
  18.0 4.0 %collective-permute-done.1.refs_3_ = bf16[4,160,128]{2,1,0:T(8,128)(2,1)S(1)} collective-permute-done((bf16[4,160,128]{2,1,0:T(8,128)(2,1)S(1)}, bf16[4,160,128]{2,1,0:T(8,128)(2,1)S(1)}, u32[]{:S(2)}, u32[]{:S(2)}) %collective-permute-start.1) | collective-permute-done | bytes 163872 | tf_op jit(solution)/shard_map/ppermute | solution.py:171
  22.0 0.6 %low1.1.before.here.refs_6_ = bf16[4,160,128]{2,1,0:T(8,128)(2,1)S(1)} custom-call(bf16[12,160,800]{2,1,0:T(8,128)(2,1)S(1)} %get-tuple-element.19.refs_2_.packed.refs_0_, s32[12,5]{1,0:T(8,128)S(1)} %get-tuple-element.20.source.refs_1_, s32[12]{0:T(128)S(1)} %get-tuple-element.21.limits.refs_2_, bf16[4,160,128]{2,1,0:T(8,128)(2,1)S(1)} %collective-permute-done.1.refs_3_, ...), custom_call_target="tpu_custom_call" | custom-call | flops 131072000 | bytes 1048576 | tf_op jit(solution)/shard_map/low1/pallas_call | solution.py:22
  22.6 0.7 %collective-permute-start.3 = (bf16[4,160,128]{2,1,0:T(8,128)(2,1)S(1)}, bf16[4,160,128]{2,1,0:T(8,128)(2,1)S(1)}, u32[]{:S(2)}, u32[]{:S(2)}) collective-permute-start(bf16[4,160,128]{2,1,0:T(8,128)(2,1)S(1)} %low1.1.before.here.refs_6_), channel_id=1, source_target_pairs={{0,30},{2,0},{4,2},{6,4},{8,6},{10,8},{12,10},{14,12},{16,14},{18,... | collective-permute-start | bytes 491528 | tf_op jit(solution)/shard_map/ppermute | solution.py:174
  23.3 0.6 %middle1.1.here.after.refs_3_.refs_0_ = bf16[4,160,128]{2,1,0:T(8,128)(2,1)S(1)} custom-call(bf16[12,160,800]{2,1,0:T(8,128)(2,1)S(1)} %get-tuple-element.19.refs_2_.packed.refs_0_, s32[12,5]{1,0:T(8,128)S(1)} %get-tuple-element.20.source.refs_1_, s32[12]{0:T(128)S(1)} %get-tuple-element.21.limits.refs_2_, ...), custom_call_target="tpu_custom_call" | custom-call | flops 131072000 | bytes 1048576 | tf_op jit(solution)/shard_map/middle1/pallas_call | solution.py:22
  23.9 1.7 %collective-permute-done.4.before = bf16[4,160,128]{2,1,0:T(8,128)(2,1)S(1)} collective-permute-done((bf16[4,160,128]{2,1,0:T(8,128)(2,1)S(1)}, bf16[4,160,128]{2,1,0:T(8,128)(2,1)S(1)}, u32[]{:S(2)}, u32[]{:S(2)}) %collective-permute-start.4) | collective-permute-done | bytes 163872 | tf_op jit(solution)/shard_map/ppermute | solution.py:171
  25.6 0.6 %low2.1.refs_7_.refs_4_.before.refs_0_ = bf16[4,160,128]{2,1,0:T(8,128)(2,1)S(1)} custom-call(bf16[12,160,800]{2,1,0:T(8,128)(2,1)S(1)} %get-tuple-element.19.refs_2_.packed.refs_0_, s32[12,5]{1,0:T(8,128)S(1)} %get-tuple-element.20.source.refs_1_, s32[12]{0:T(128)S(1)} %get-tuple-element.21.limits.refs_2_, ...), custom_call_target="tpu_custom_call" | custom-call | flops 131072000 | bytes 1048576 | tf_op jit(solution)/shard_map/low2/pallas_call | solution.py:22
  26.2 0.1 collective-permute-start.5
  26.3 0.0 collective-permute-done.3.refs_5_
  26.3 0.6 %high2.1.here.after.refs_6_ = bf16[4,160,128]{2,1,0:T(8,128)(2,1)S(1)} custom-call(bf16[12,160,800]{2,1,0:T(8,128)(2,1)S(1)} %get-tuple-element.19.refs_2_.packed.refs_0_, s32[12,5]{1,0:T(8,128)S(1)} %get-tuple-element.20.source.refs_1_, s32[12]{0:T(128)S(1)} %get-tuple-element.21.limits.refs_2_, bf16[4,160,128]{2,1,0:T(8,128)(2,1)S(1)} %middle1.1.here.after.refs_3_.refs_0_, ...), custom_call_target="tpu_custom_call" | custom-call | flops 131072000 | bytes 1048576 | tf_op jit(solution)/shard_map/high2/pallas_call | solution.py:22
  26.9 0.5 %collective-permute-start.7 = (bf16[4,160,128]{2,1,0:T(8,128)(2,1)S(1)}, bf16[4,160,128]{2,1,0:T(8,128)(2,1)S(1)}, u32[]{:S(2)}, u32[]{:S(2)}) collective-permute-start(bf16[4,160,128]{2,1,0:T(8,128)(2,1)S(1)} %high2.1.here.after.refs_6_), channel_id=1, source_target_pairs={{0,2},{2,4},{4,6},{6,8},{8,10},{10,12},{12,14},{14,16},{16,18},{18... | collective-permute-start | bytes 491528 | tf_op jit(solution)/shard_map/ppermute | solution.py:171
  27.5 0.6 %middle2.1.before.refs_5_.here.refs_0_ = bf16[4,160,128]{2,1,0:T(8,128)(2,1)S(1)} custom-call(bf16[12,160,800]{2,1,0:T(8,128)(2,1)S(1)} %get-tuple-element.19.refs_2_.packed.refs_0_, s32[12,5]{1,0:T(8,128)S(1)} %get-tuple-element.20.source.refs_1_, s32[12]{0:T(128)S(1)} %get-tuple-element.21.limits.refs_2_, ...), custom_call_target="tpu_custom_call" | custom-call | flops 131072000 | bytes 1048576 | tf_op jit(solution)/shard_map/middle2/pallas_call | solution.py:22
  28.1 1.1 %collective-permute-done.5.after = bf16[4,160,128]{2,1,0:T(8,128)(2,1)S(1)} collective-permute-done((bf16[4,160,128]{2,1,0:T(8,128)(2,1)S(1)}, bf16[4,160,128]{2,1,0:T(8,128)(2,1)S(1)}, u32[]{:S(2)}, u32[]{:S(2)}) %collective-permute-start.5) | collective-permute-done | bytes 163872 | tf_op jit(solution)/shard_map/ppermute | solution.py:174
  29.1 0.6 %high3.1.refs_7_.after.refs_4_ = bf16[4,160,128]{2,1,0:T(8,128)(2,1)S(1)} custom-call(bf16[12,160,800]{2,1,0:T(8,128)(2,1)S(1)} %get-tuple-element.19.refs_2_.packed.refs_0_, s32[12,5]{1,0:T(8,128)S(1)} %get-tuple-element.20.source.refs_1_, s32[12]{0:T(128)S(1)} %get-tuple-element.21.limits.refs_2_, ...), custom_call_target="tpu_custom_call" | custom-call | flops 131072000 | bytes 1048576 | tf_op jit(solution)/shard_map/high3/pallas_call | solution.py:22
  29.7 0.1 collective-permute-start.6
  29.8 4.7 %collective-permute-done.7.refs_3_ = bf16[4,160,128]{2,1,0:T(8,128)(2,1)S(1)} collective-permute-done((bf16[4,160,128]{2,1,0:T(8,128)(2,1)S(1)}, bf16[4,160,128]{2,1,0:T(8,128)(2,1)S(1)}, u32[]{:S(2)}, u32[]{:S(2)}) %collective-permute-start.7) | collective-permute-done | bytes 163872 | tf_op jit(solution)/shard_map/ppermute | solution.py:171
  34.5 0.6 %low3.1.here.before = bf16[4,160,128]{2,1,0:T(8,128)(2,1)S(1)} custom-call(bf16[12,160,800]{2,1,0:T(8,128)(2,1)S(1)} %get-tuple-element.19.refs_2_.packed.refs_0_, s32[12,5]{1,0:T(8,128)S(1)} %get-tuple-element.20.source.refs_1_, s32[12]{0:T(128)S(1)} %get-tuple-element.21.limits.refs_2_, bf16[4,160,128]{2,1,0:T(8,128)(2,1)S(1)} %collective-permute-done.7.refs_3_, ...), custom_call_target="tpu_custom_call" | custom-call | flops 131072000 | bytes 1048576 | tf_op jit(solution)/shard_map/low3/pallas_call | solution.py:22
  35.1 0.1 collective-permute-start.8
  35.2 0.6 %middle3.1.after.here.refs_3_ = bf16[4,160,128]{2,1,0:T(8,128)(2,1)S(1)} custom-call(bf16[12,160,800]{2,1,0:T(8,128)(2,1)S(1)} %get-tuple-element.19.refs_2_.packed.refs_0_, s32[12,5]{1,0:T(8,128)S(1)} %get-tuple-element.20.source.refs_1_, s32[12]{0:T(128)S(1)} %get-tuple-element.21.limits.refs_2_, ...), custom_call_target="tpu_custom_call" | custom-call | flops 131072000 | bytes 1048576 | tf_op jit(solution)/shard_map/middle3/pallas_call | solution.py:22
  35.8 0.6 %middle4.1.refs_1_ = bf16[4,160,128]{2,1,0:T(8,128)(2,1)S(1)} custom-call(bf16[12,160,800]{2,1,0:T(8,128)(2,1)S(1)} %get-tuple-element.19.refs_2_.packed.refs_0_, s32[12,5]{1,0:T(8,128)S(1)} %get-tuple-element.20.source.refs_1_, s32[12]{0:T(128)S(1)} %get-tuple-element.21.limits.refs_2_, bf16[4,160,128]{2,1,0:T(8,128)(2,1)S(1)} %low3.1.here.before, ...), custom_call_target="tpu_custom_call" | custom-call | flops 131072000 | bytes 1048576 | tf_op jit(solution)/shard_map/middle4/pallas_call | solution.py:22
  36.4 1.2 %collective-permute-done.6.before = bf16[4,160,128]{2,1,0:T(8,128)(2,1)S(1)} collective-permute-done((bf16[4,160,128]{2,1,0:T(8,128)(2,1)S(1)}, bf16[4,160,128]{2,1,0:T(8,128)(2,1)S(1)}, u32[]{:S(2)}, u32[]{:S(2)}) %collective-permute-start.6) | collective-permute-done | bytes 163872 | tf_op jit(solution)/shard_map/ppermute | solution.py:171
  37.6 0.6 %low4.1.refs_7_.refs_0_ = bf16[4,160,128]{2,1,0:T(8,128)(2,1)S(1)} custom-call(bf16[12,160,800]{2,1,0:T(8,128)(2,1)S(1)} %get-tuple-element.19.refs_2_.packed.refs_0_, s32[12,5]{1,0:T(8,128)S(1)} %get-tuple-element.20.source.refs_1_, s32[12]{0:T(128)S(1)} %get-tuple-element.21.limits.refs_2_, bf16[4,160,128]{2,1,0:T(8,128)(2,1)S(1)} %collective-permute-done.6.before, ...), custom_call_target="tpu_custom_call" | custom-call | flops 131072000 | bytes 1048576 | tf_op jit(solution)/shard_map/low4/pallas_call | solution.py:22
  38.2 0.0 collective-permute-done.8.refs_5_
  38.2 0.6 %high4.1.refs_2_ = bf16[4,160,128]{2,1,0:T(8,128)(2,1)S(1)} custom-call(bf16[12,160,800]{2,1,0:T(8,128)(2,1)S(1)} %get-tuple-element.19.refs_2_.packed.refs_0_, s32[12,5]{1,0:T(8,128)S(1)} %get-tuple-element.20.source.refs_1_, s32[12]{0:T(128)S(1)} %get-tuple-element.21.limits.refs_2_, bf16[4,160,128]{2,1,0:T(8,128)(2,1)S(1)} %middle3.1.after.here.refs_3_, ...), custom_call_target="tpu_custom_call" | custom-call | flops 131072000 | bytes 1048576 | tf_op jit(solution)/shard_map/high4/pallas_call | solution.py:22
  38.8 0.1 scatter.1
  38.9 1.6 %collective-permute-start.9 = (bf16[6,160,128]{2,1,0:T(8,128)(2,1)S(1)}, bf16[6,160,128]{2,1,0:T(8,128)(2,1)S(1)}, u32[]{:S(2)}, u32[]{:S(2)}) collective-permute-start(bf16[6,160,128]{2,1,0:T(8,128)(2,1)S(1)} %get-tuple-element.27), channel_id=1, source_target_pairs={{0,1},{1,0},{2,3},{3,2},{4,5},{5,4},{6,7},{7,6},{8,9},{9,8},{10,11... | collective-permute-start | bytes 737288 | tf_op jit(solution)/shard_map/ppermute | solution.py:178
  40.5 0.7 %own.1.refs_1_ = bf16[6,160,256]{2,1,0:T(8,128)(2,1)} custom-call(bf16[6,160,128]{2,1,0:T(8,128)(2,1)S(1)} %get-tuple-element.28.part), custom_call_target="tpu_custom_call" | custom-call | bytes 1048576 | tf_op jit(solution)/shard_map/own/pallas_call | solution.py:22
  41.2 5.3 %collective-permute-done.9.refs_0_ = bf16[6,160,128]{2,1,0:T(8,128)(2,1)S(1)} collective-permute-done((bf16[6,160,128]{2,1,0:T(8,128)(2,1)S(1)}, bf16[6,160,128]{2,1,0:T(8,128)(2,1)S(1)}, u32[]{:S(2)}, u32[]{:S(2)}) %collective-permute-start.9) | collective-permute-done | bytes 245792 | tf_op jit(solution)/shard_map/ppermute | solution.py:178
  46.4 0.7 %others.1 = bf16[6,160,256]{2,1,0:T(8,128)(2,1)} custom-call(bf16[6,160,128]{2,1,0:T(8,128)(2,1)S(1)} %collective-permute-done.9.refs_0_, bf16[6,160,256]{2,1,0:T(8,128)(2,1)} %own.1.refs_1_), custom_call_target="tpu_custom_call", output_to_operand_aliasing={{}: (1, {})} | custom-call | bytes 1048576 | tf_op jit(solution)/shard_map/others/pallas_call | solution.py:22
Async XLA Ops:
  2.1 9.0 %collective-permute-start = (bf16[6,160,128]{2,1,0:T(8,128)(2,1)S(1)}, bf16[6,160,128]{2,1,0:T(8,128)(2,1)S(1)}, u32[]{:S(2)}, u32[]{:S(2)}) collective-permute-start(bf16[6,160,128]{2,1,0:T(8,128)(2,1)S(1)} %get-tuple-element.23), channel_id=1, source_target_pairs={{0,1},{1,0},{2,3},{3,2},{4,5},{5,4},{6,7},{7,6},{8,9},{9,8},{10,11... | collective-permute-start | bytes 737288 | tf_op jit(solution)/shard_map/ppermute | solution.py:178
  11.2 6.2 %collective-permute-start.2 = (bf16[4,160,128]{2,1,0:T(8,128)(2,1)S(1)}, bf16[4,160,128]{2,1,0:T(8,128)(2,1)S(1)}, u32[]{:S(2)}, u32[]{:S(2)}) collective-permute-start(bf16[4,160,128]{2,1,0:T(8,128)(2,1)S(1)} %get-tuple-element.25.refs_4_.before.refs_0_), channel_id=1, source_target_pairs={{0,30},{2,0},{4,2},{6,4},{8,6},{10,8},{12,10},{14,12},{16,14},{18,... | collective-permute-start | bytes 491528 | tf_op jit(solution)/shard_map/ppermute | solution.py:174
  14.6 7.5 %collective-permute-start.1 = (bf16[4,160,128]{2,1,0:T(8,128)(2,1)S(1)}, bf16[4,160,128]{2,1,0:T(8,128)(2,1)S(1)}, u32[]{:S(2)}, u32[]{:S(2)}) collective-permute-start(bf16[4,160,128]{2,1,0:T(8,128)(2,1)S(1)} %get-tuple-element.24.here.after.refs_6_), channel_id=1, source_target_pairs={{0,2},{2,4},{4,6},{6,8},{8,10},{10,12},{12,14},{14,16},{16,18},{18... | collective-permute-start | bytes 491528 | tf_op jit(solution)/shard_map/ppermute | solution.py:171
  18.0 7.7 %collective-permute-start.4 = (bf16[4,160,128]{2,1,0:T(8,128)(2,1)S(1)}, bf16[4,160,128]{2,1,0:T(8,128)(2,1)S(1)}, u32[]{:S(2)}, u32[]{:S(2)}) collective-permute-start(bf16[4,160,128]{2,1,0:T(8,128)(2,1)S(1)} %high1.1.refs_6_.after.refs_4_.refs_0_), channel_id=1, source_target_pairs={{0,2},{2,4},{4,6},{6,8},{8,10},{10,12},{12,14},{14,16},{16,18},{18... | collective-permute-start | bytes 491528 | tf_op jit(solution)/shard_map/ppermute | solution.py:171
  22.6 3.7 %collective-permute-start.3 = (bf16[4,160,128]{2,1,0:T(8,128)(2,1)S(1)}, bf16[4,160,128]{2,1,0:T(8,128)(2,1)S(1)}, u32[]{:S(2)}, u32[]{:S(2)}) collective-permute-start(bf16[4,160,128]{2,1,0:T(8,128)(2,1)S(1)} %low1.1.before.here.refs_6_), channel_id=1, source_target_pairs={{0,30},{2,0},{4,2},{6,4},{8,6},{10,8},{12,10},{14,12},{16,14},{18,... | collective-permute-start | bytes 491528 | tf_op jit(solution)/shard_map/ppermute | solution.py:174
  26.2 2.9 %collective-permute-start.5 = (bf16[4,160,128]{2,1,0:T(8,128)(2,1)S(1)}, bf16[4,160,128]{2,1,0:T(8,128)(2,1)S(1)}, u32[]{:S(2)}, u32[]{:S(2)}) collective-permute-start(bf16[4,160,128]{2,1,0:T(8,128)(2,1)S(1)} %low2.1.refs_7_.refs_4_.before.refs_0_), channel_id=1, source_target_pairs={{0,30},{2,0},{4,2},{6,4},{8,6},{10,8},{12,10},{14,12},{16,14},{18,... | collective-permute-start | bytes 491528 | tf_op jit(solution)/shard_map/ppermute | solution.py:174
  26.9 7.6 %collective-permute-start.7 = (bf16[4,160,128]{2,1,0:T(8,128)(2,1)S(1)}, bf16[4,160,128]{2,1,0:T(8,128)(2,1)S(1)}, u32[]{:S(2)}, u32[]{:S(2)}) collective-permute-start(bf16[4,160,128]{2,1,0:T(8,128)(2,1)S(1)} %high2.1.here.after.refs_6_), channel_id=1, source_target_pairs={{0,2},{2,4},{4,6},{6,8},{8,10},{10,12},{12,14},{14,16},{16,18},{18... | collective-permute-start | bytes 491528 | tf_op jit(solution)/shard_map/ppermute | solution.py:171
  29.7 7.9 %collective-permute-start.6 = (bf16[4,160,128]{2,1,0:T(8,128)(2,1)S(1)}, bf16[4,160,128]{2,1,0:T(8,128)(2,1)S(1)}, u32[]{:S(2)}, u32[]{:S(2)}) collective-permute-start(bf16[4,160,128]{2,1,0:T(8,128)(2,1)S(1)} %high3.1.refs_7_.after.refs_4_), channel_id=1, source_target_pairs={{0,2},{2,4},{4,6},{6,8},{8,10},{10,12},{12,14},{14,16},{16,18},{18... | collective-permute-start | bytes 491528 | tf_op jit(solution)/shard_map/ppermute | solution.py:171
  35.1 3.1 %collective-permute-start.8 = (bf16[4,160,128]{2,1,0:T(8,128)(2,1)S(1)}, bf16[4,160,128]{2,1,0:T(8,128)(2,1)S(1)}, u32[]{:S(2)}, u32[]{:S(2)}) collective-permute-start(bf16[4,160,128]{2,1,0:T(8,128)(2,1)S(1)} %low3.1.here.before), channel_id=1, source_target_pairs={{0,30},{2,0},{4,2},{6,4},{8,6},{10,8},{12,10},{14,12},{16,14},{18,... | collective-permute-start | bytes 491528 | tf_op jit(solution)/shard_map/ppermute | solution.py:174
  38.9 7.5 %collective-permute-start.9 = (bf16[6,160,128]{2,1,0:T(8,128)(2,1)S(1)}, bf16[6,160,128]{2,1,0:T(8,128)(2,1)S(1)}, u32[]{:S(2)}, u32[]{:S(2)}) collective-permute-start(bf16[6,160,128]{2,1,0:T(8,128)(2,1)S(1)} %get-tuple-element.27), channel_id=1, source_target_pairs={{0,1},{1,0},{2,3},{3,2},{4,5},{5,4},{6,7},{7,6},{8,9},{9,8},{10,11... | collective-permute-start | bytes 737288 | tf_op jit(solution)/shard_map/ppermute | solution.py:178

commit v3 on v2

v3 whole, which is shorter than its diff:
```python
import functools

import jax
import jax.numpy as jnp
from jax import lax
from jax.experimental import pallas as pl
from jax.experimental.pallas import tpu as pltpu
from jax.sharding import PartitionSpec as P

DEG = 4
FULL = 128
LONG = 20 * 10**9

center_shift = 0.2
half_span = 1.1

VMEM = pl.BlockSpec(memory_space=pltpu.VMEM)
HBM = pl.BlockSpec(memory_space=pltpu.HBM)
ANY = pl.BlockSpec(memory_space=pl.ANY)


def call(kernel, outs, ins, *args, out_specs=None, scratch=(), aliases=None, limit=4 << 20, flops=0, name=None):
    return pl.pallas_call(
        kernel,
        out_shape=outs,
        in_specs=ins,
        out_specs=out_specs or [VMEM] * len(outs),
        scratch_shapes=list(scratch),
        input_output_aliases=aliases or {},
        compiler_params=pltpu.CompilerParams(vmem_limit_bytes=limit),
        cost_estimate=pl.CostEstimate(flops=flops, bytes_accessed=1024, transcendentals=0),
        name=name,
    )(*args)


def bf16(*shape):
    return jax.ShapeDtypeStruct(shape, jnp.bfloat16)


def without(body, at, *refs):
    body(*refs[:at], *refs[at + 1 :])


def flipped(shards):
    return lax.axis_index("state") == 1 if shards == 2 else False


def choose(flip, yes, no):
    return no if flip is False else jnp.where(flip, yes, no)


def rows_below(count, rows, lanes):
    return lax.broadcasted_iota(jnp.int32, (rows, lanes), 0) < count


def turn(shards, k, element, weights, count):
    rows, lanes = element.shape[0], weights.shape[1] // shards
    at = lax.rem(lax.axis_index("state") + k, shards) * lanes
    turned = jnp.dot(element, weights[:, pl.ds(pl.multiple_of(at, lanes), lanes)], preferred_element_type=jnp.float32)
    return jnp.where(rows_below(count, rows, lanes), turned, 0.0).astype(jnp.bfloat16)


def rotate_out_kernel(shards, reach, orbitals, rotation, counts, *refs):
    outs, (held, weights, limits, scalars, sems) = refs[:-5], refs[-5:]
    elems = orbitals.shape[0]
    me, flip = lax.axis_index("state"), flipped(shards)
    copies = [
        pltpu.make_async_copy(rotation, weights, sems.at[0]),
        pltpu.make_async_copy(counts, scalars, sems.at[1]),
        pltpu.make_async_copy(counts, limits, sems.at[2]),
    ]
    copies += [pltpu.make_async_copy(orbitals.at[e], held.at[e], sems.at[3 + e]) for e in range(elems)]
    for copy in copies:
        copy.start()
    copies[0].wait()
    copies[1].wait()
    for e in range(elems):
        copies[3 + e].wait()
        for k in range(shards - 1):
            spot = choose(flip, (e + reach) % elems, e)
            outs[k][spot] = turn(shards, k + 1, held[e], weights, scalars[me * elems + e])
    if shards == 2:
        outs[1][...] = outs[0][:reach]
    copies[2].wait()


def rotate_in_kernel(shards, reach, held, weights, limits, *outs):
    me, flip = lax.axis_index("state"), flipped(shards)
    elems = held.shape[0]
    ends = limits[...]
    spots = [(out, e) for out in outs for e in range(out.shape[0])]
    for spot, (out, at) in enumerate(spots):
        e = choose(flip, (spot + elems - reach) % elems, spot)
        count = ends[spot]
        for shard in range(shards):
            here = (spot + elems - reach) % elems if shard == 1 and flip is not False else spot
            count = jnp.where(me == shard, ends[shard * elems + here], count)
        out[at] = turn(shards, 0, held[e], weights, count)


def local_kernel(total, shards, reach, blocks, neighbors, limits, *refs):
    packed, (table, raw, beside, sems) = refs[:-4], refs[-4:]
    elems, couplings, _, _ = blocks.shape
    flip, groups = flipped(shards), elems // reach
    spots = [choose(flip, elems - (g + 1) * reach, g * reach) + e for g in range(groups) for e in range(reach)]
    copies = [pltpu.make_async_copy(blocks.at[e], raw.at[i], sems.at[i]) for i, e in enumerate(spots)]
    neighbor_copy = pltpu.make_async_copy(neighbors, beside, sems.at[elems])
    neighbor_copy.start()
    for copy in copies:
        copy.start()
    neighbor_copy.wait()
    column = lax.broadcasted_iota(jnp.int32, beside.shape, 1)
    offset = beside[...] - (column + lax.axis_index("elem") * elems)
    offset = jnp.where(offset > reach, offset - total, jnp.where(offset < -reach, offset + total, offset))
    place = offset + (column - sum(jnp.where(column >= g * reach, reach, 0) for g in range(1, groups))) + reach
    past = sum(jnp.where(place >= g * reach, reach, 0) for g in range(1, groups))
    place = choose(flip, place + (elems - reach) - 2 * past, place)
    ends = limits[...].reshape(1, elems)

    def mirrored(x):
        parts = [x[:, g * reach : (g + 1) * reach] for g in reversed(range(groups))]
        return choose(flip, jnp.concatenate(parts, axis=1), x)

    table[:couplings] = mirrored(place)
    table[couplings:] = mirrored(ends)
    for i in range(elems):
        out, e = packed[i // reach], i % reach
        copies[i].wait()
        for k in range(couplings):
            out[e, :, k * FULL : (k + 1) * FULL] = raw[i, k, :, :FULL]
        tail = [raw[i, k, :, FULL:] for k in range(couplings)]
        out[e, :, couplings * FULL :] = jnp.concatenate(tail, axis=1)


def pair_kernel(reach, arrived, half, far, middle):
    flip, share = flipped(2), half.shape[0]
    far[...] = arrived[:reach]
    middle[pl.ds(choose(flip, share, 0), share)] = half[...]
    middle[pl.ds(choose(flip, 0, share), share)] = arrived[reach:]


def gather_kernel(shards, *refs):
    me = lax.axis_index("state")
    parts, groups, whole = refs[:shards], refs[shards : shards + 3], refs[-1]
    elems, width = parts[0].shape[0], groups[0].shape[0]
    for k, part in enumerate(parts):
        whole[pl.ds(lax.rem(me + shards - k, shards) * elems, elems)] = part[...]
    for g, group in enumerate(groups):
        group[...] = whole[g * width : (g + 1) * width]


def level_kernel(first, factor, with_prev, packed, table, before, here, after, *refs):
    refs, out, window = list(refs[:-2]), refs[-2], refs[-1]
    previous = refs.pop(0) if with_prev else None
    width, rows, lanes = here.shape
    for g, group in enumerate((before, here, after)):
        window[g * width : (g + 1) * width] = group[...]
    places = table[...]
    couplings = places.shape[0] - 1
    for e in range(width):
        at = [places[k, first + e] for k in range(couplings)]
        fields = [window[i, :FULL] for i in at] + [window[i, FULL:] for i in at]
        image = jnp.dot(packed[e], jnp.concatenate(fields, axis=0), preferred_element_type=jnp.float32)
        image = jnp.where(rows_below(places[couplings, first + e], rows, lanes), image, 0.0)
        value = factor * (image - center_shift * here[e].astype(jnp.float32)) / half_span
        if with_prev:
            value = value - previous[e].astype(jnp.float32)
        out[e] = value.astype(jnp.bfloat16)
    if refs:
        share = out.shape[0] - width
        out[width:] = refs[0][pl.ds(choose(flipped(2), 0, width - share), share)]


def scatter_kernel(shards, *refs):
    me = lax.axis_index("state")
    groups, parts, whole = refs[:3], refs[3:-1], refs[-1]
    elems, width = parts[0].shape[0], groups[0].shape[0]
    for g, group in enumerate(groups):
        whole[g * width : (g + 1) * width] = group[...]
    for k, part in enumerate(parts):
        part[...] = whole[pl.ds(lax.rem(me + k, shards) * elems, elems)]


def place(shards, k, first, part, out, sem):
    elems, _, lanes = part.shape
    at = lax.rem(lax.axis_index("state") + shards - k, shards) * lanes
    return pltpu.make_async_copy(part, out.at[pl.ds(first, elems), :, pl.ds(pl.multiple_of(at, lanes), lanes)], sem)


def run(copies):
    for copy in copies:
        copy.start()
    for copy in copies:
        copy.wait()


def rows_copies(k, near, half, out, sems):
    flip, share, width = flipped(2), half.shape[0], near.shape[0]
    return [
        place(2, k, choose(flip, share, 0), near, out, sems.at[0]),
        place(2, k, choose(flip, 0, width), half, out, sems.at[1]),
    ]


def own_kernel(near, middle, out, sems):
    share = out.shape[0] - near.shape[0]
    run(rows_copies(0, near, middle.at[pl.ds(choose(flipped(2), share, 0), share)], out, sems))


def others_kernel(width, part, out, sems):
    run(rows_copies(1, part.at[:width], part.at[width:], out, sems))


def join_kernel(shards, *refs):
    parts, out, sems = refs[:shards], refs[-2], refs[-1]
    run([place(shards, k, 0, part, out, sems.at[k]) for k, part in enumerate(parts)])


def on_device(orbitals, rotation, counts, neighbors, blocks):
    row_elems, rows, states = orbitals.shape
    elems, couplings = neighbors.shape
    orbitals, rotation, counts, neighbors, blocks = (
        pltpu.with_memory_space_constraint(x, pltpu.HBM) for x in (orbitals, rotation, counts, neighbors.T, blocks)
    )
    shards = lax.axis_size("state")
    ring = lax.axis_size("elem")
    width = elems // 3
    lanes = states // shards
    group, part = bf16(width, rows, lanes), bf16(row_elems, rows, lanes)
    half = bf16(row_elems - width, rows, lanes)
    whole = pltpu.VMEM((elems, rows, lanes), jnp.bfloat16)
    scalars = pltpu.SMEM(counts.shape, jnp.int32)
    dma = pltpu.SemaphoreType.DMA
    pair = shards == 2

    def shifted(x, step, across=False):
        moves = []
        for i in range(ring):
            for j in range(shards):
                to = (i + (-step if pair and j == 1 else step)) % ring
                moves.append((i * shards + j, to * shards + (1 - j if across else j)))
        return lax.ppermute(x, ("elem", "state"), moves)

    def to_far_of_neighbor(x):
        return shifted(x, -1)

    def to_near_of_neighbor(x):
        return shifted(x, 1)

    def swapped(parts):
        return [
            lax.ppermute(x, "state", [(i, (i + k + 1) % shards) for i in range(shards)]) for k, x in enumerate(parts)
        ]

    *parts, held, weights, limits = call(
        functools.partial(rotate_out_kernel, shards, width),
        [part] * (shards - 1)
        + [group] * pair
        + [bf16(*orbitals.shape), bf16(*rotation.shape), jax.ShapeDtypeStruct(counts.shape, jnp.int32)],
        [HBM] * 3,
        orbitals,
        rotation,
        counts,
        scratch=[scalars, dma((row_elems + 3,))],
        name="rotate_out",
    )
    arrived = swapped(parts[: shards - 1])
    if pair:
        near_halo = shifted(parts[1], -1, across=True)
    kept = call(
        functools.partial(rotate_in_kernel, shards, width),
        [group, half] if pair else [part],
        [VMEM] * 3,
        held,
        weights,
        limits,
        name="rotate_in",
    )
    if pair:
        far_halo = to_far_of_neighbor(kept[0])
    *packed, table = call(
        functools.partial(without, functools.partial(local_kernel, elems * ring, shards, width), 3),
        [bf16(width, rows, couplings * rows)] * 3 + [jax.ShapeDtypeStruct((couplings + 1, elems), jnp.int32)],
        [HBM, HBM, VMEM, ANY],
        blocks,
        neighbors,
        limits,
        kept[0],
        scratch=[pltpu.VMEM(blocks.shape, jnp.bfloat16), pltpu.VMEM(neighbors.shape, jnp.int32), dma((elems + 1,))],
        limit=16 << 20,
        name="local",
    )
    if pair:
        near = kept[0]
        far, middle = call(
            functools.partial(without, functools.partial(pair_kernel, width), 2),
            [group] * 2,
            [VMEM, VMEM, ANY],
            *arrived,
            kept[1],
            table,
            name="gather",
        )
    else:
        near, middle, far = call(
            functools.partial(without, functools.partial(gather_kernel, shards), shards),
            [group] * 3,
            [VMEM] * shards + [ANY],
            *kept,
            *arrived,
            table,
            scratch=[whole],
            name="gather",
        )
        near_halo, far_halo = to_near_of_neighbor(far), to_far_of_neighbor(near)

    def level(g, m, before, here, after, previous, leaving=None, behind=None, flops=0):
        body = functools.partial(level_kernel, g * width, 1.0 if m == 1 else 2.0, previous is not None)
        args = [packed[g], table, before, here, after] + [x for x in (previous, leaving) if x is not None]
        specs = [VMEM] * len(args)
        if behind is not None:
            body = functools.partial(without, body, len(args))
            args, specs = args + [behind], specs + [ANY]
        return call(
            body,
            [group if leaving is None else part],
            specs,
            *args,
            scratch=[pltpu.VMEM((3 * width, rows, lanes), jnp.bfloat16)],
            flops=flops,
            name=("near", "middle", "far")[g] + str(m),
        )[0]

    older = (None, None, None)
    for m in range(1, DEG + 1):
        last = m == DEG
        if last:
            new_middle = level(1, m, near, middle, far, older[1])
        if m % 2:
            new_near = level(0, m, near_halo, near, middle, older[0])
            next_far_halo = to_far_of_neighbor(new_near)
            new_far = level(2, m, middle, far, far_halo, older[2], behind=new_near)
            next_near_halo = to_near_of_neighbor(new_far)
        else:
            new_far = level(2, m, middle, far, far_halo, older[2], new_middle if last and pair else None)
            if last and pair:
                arrived = swapped([new_far])[0]
            else:
                next_near_halo = to_near_of_neighbor(new_far)
            new_near = level(0, m, near_halo, near, middle, older[0], behind=None if last else new_far, flops=LONG * last)
            if not last:
                next_far_halo = to_far_of_neighbor(new_near)
        if not last:
            new_middle = level(1, m, near, middle, far, older[1])
            near_halo, far_halo = next_near_halo, next_far_halo
        older, (near, middle, far) = (near, middle, far), (new_near, new_middle, new_far)

    whole_out = [bf16(*orbitals.shape)]
    if pair:
        out = call(
            own_kernel, whole_out, [VMEM] * 2, near, middle, out_specs=[HBM], scratch=[dma((2,))], name="own"
        )[0]
        return call(
            functools.partial(without, functools.partial(others_kernel, width), 1),
            whole_out,
            [VMEM, HBM],
            arrived,
            out,
            out_specs=[HBM],
            scratch=[dma((2,))],
            aliases={1: 0},
            name="others",
        )[0]
    kept, *parts = call(
        functools.partial(scatter_kernel, shards),
        [part] * shards,
        [VMEM] * 3,
        near,
        middle,
        far,
        scratch=[whole],
        name="scatter",
    )
    return call(
        functools.partial(join_kernel, shards),
        whole_out,
        [VMEM] * shards,
        kept,
        *swapped(parts),
        out_specs=[HBM],
        scratch=[dma((shards,))],
        name="join",
    )[0]


def solution(mesh):
    in_specs = (
        P(("elem", "state"), None, None),
        P(),
        P("elem"),
        P("elem", None),
        P("elem", None, None, None),
    )
    out_specs = P(("elem", "state"), None, None)
    return jax.shard_map(on_device, mesh=mesh, in_specs=in_specs, out_specs=out_specs, check_vma=False)
```

time: 47.3 us -> 44.1 us (0.932)
  waiting for transfers between devices: 23.2 us -> 13.9 us
  starting transfers between devices: 9.48 us -> 16.2 us
  local copies, waits for them, and re-layouts: 0.77 us -> 0 us
    ppermute x10, waiting for transfers between devices: 23.2 us -> 13.9 us  [the longest x8 11.2 us: shifted(): return lax.ppermute(x, ('elem', 'state'), moves)]
    ppermute x10, starting transfers between devices: 9.48 us -> 16.2 us  [the longest x8 10.8 us: shifted(): return lax.ppermute(x, ('elem', 'state'), moves)]
    unnamed x1 -> x0, local copies, waits for them, and re-layouts: 0.77 us -> none
  transfers between devices with their start and end apart: 10 -> 10, of which waited for: 8 -> 8; matrix products, arithmetic and copies ran while one was open for 2% -> 0% of each run, Pallas kernels for 21% -> 25%
where the time goes in v3:
time: 44.1 us; the launch traced here: 43.9 us
  starting transfers between devices  16.2 us (37%)
  waiting for transfers between devices  13.9 us (32%)
  Pallas kernels  13.6 us (31%)
    pallas_call x18, Pallas kernels, call(): pl.pallas_call(kernel, out_shape=outs, in_specs=ins, out_specs=out_specs...  13.6 us
    ppermute x8, waiting for transfers between devices, shifted(): return lax.ppermute(x, ('elem', 'state'), moves)  11.2 us
    ppermute x8, starting transfers between devices, shifted(): return lax.ppermute(x, ('elem', 'state'), moves)  10.8 us
    ppermute x2, starting transfers between devices, swapped(): lax.ppermute(x, 'state', [(i, (i + k + 1) % shards) for i in range(shards)])  5.4 us
    ppermute x2, waiting for transfers between devices, swapped(): lax.ppermute(x, 'state', [(i, (i + k + 1) % shards) for i in range(shards)])  2.73 us
  transfers between devices with their start and end apart: 10, of which 8 were waited for; matrix products, arithmetic and copies ran while one was open for 0% of the time, Pallas kernels for 25%

profile of v3, /device:TPU:0, one launch (start us, length us, event | category | flops | bytes accessed | tf_op | source)
XLA Modules:
  0.0 43.9 jit_solution(17744375921516822930)
XLA Ops:
  0.0 2.1 %rotate_out.1 = (bf16[6,160,128]{2,1,0:T(8,128)(2,1)S(1)}, bf16[4,160,128]{2,1,0:T(8,128)(2,1)S(1)}, bf16[6,160,256]{2,1,0:T(8,128)(2,1)S(1)}, bf16[256,256]{1,0:T(8,128)(2,1)S(1)}, s32[12]{0:T(128)S(1)}) custom-call(bf16[6,160,256]{2,1,0:T(8,128)(2,1)} %orbitals.1, bf16[256,256]{1,0:T(8,128)(2,1)} %rotation.1, s32[12]{0:T(128)} %counts.1), custom_call_target="tpu_custom_call" | custom-call | bytes 1024 | tf_op jit(solution)/shard_map/rotate_out/pallas_call | solution.py:23
  2.1 3.0 %collective-permute-start = (bf16[6,160,128]{2,1,0:T(8,128)(2,1)S(1)}, bf16[6,160,128]{2,1,0:T(8,128)(2,1)S(1)}, u32[]{:S(2)}, u32[]{:S(2)}) collective-permute-start(bf16[6,160,128]{2,1,0:T(8,128)(2,1)S(1)} %get-tuple-element.26), channel_id=1, source_target_pairs={{0,1},{1,0},{2,3},{3,2},{4,5},{5,4},{6,7},{7,6},{8,9},{9,8},{10,11... | collective-permute-start | bytes 737288 | tf_op jit(solution)/shard_map/ppermute | solution.py:252
  5.2 3.6 %collective-permute-start.2 = (bf16[4,160,128]{2,1,0:T(8,128)(2,1)S(1)}, bf16[4,160,128]{2,1,0:T(8,128)(2,1)S(1)}, u32[]{:S(2)}, u32[]{:S(2)}) collective-permute-start(bf16[4,160,128]{2,1,0:T(8,128)(2,1)S(1)} %get-tuple-element.30), channel_id=1, source_target_pairs={{0,31},{1,2},{2,1},{3,4},{4,3},{5,6},{6,5},{7,8},{8,7},{9,10},{10,... | collective-permute-start | bytes 491528 | tf_op jit(solution)/shard_map/ppermute | solution.py:242
  8.8 0.3 rotate_in.1
  9.1 1.2 %collective-permute-start.1 = (bf16[4,160,128]{2,1,0:T(8,128)(2,1)S(1)}, bf16[4,160,128]{2,1,0:T(8,128)(2,1)S(1)}, u32[]{:S(2)}, u32[]{:S(2)}) collective-permute-start(bf16[4,160,128]{2,1,0:T(8,128)(2,1)S(1)} %get-tuple-element.21.refs_3_.here.before.refs_5_), channel_id=1, source_target_pairs={{0,30},{1,3},{2,0},{3,5},{4,2},{5,7},{6,4},{7,9},{8,6},{9,11},{10,... | collective-permute-start | bytes 491528 | tf_op jit(solution)/shard_map/ppermute | solution.py:242
  10.3 2.8 %local.1 = (bf16[4,160,800]{2,1,0:T(8,128)(2,1)S(1)}, bf16[4,160,800]{2,1,0:T(8,128)(2,1)S(1)}, bf16[4,160,800]{2,1,0:T(8,128)(2,1)S(1)}, s32[6,12]{1,0:T(8,128)S(1)}) custom-call(bf16[12,5,160,160]{3,2,1,0:T(8,128)(2,1)} %refs_0_.1, s32[5,12]{1,0:T(8,128)} %bitcast.1, s32[12]{0:T(128)S(1)} %get-tuple-element.18.limits.refs_2_, ...), custom_call_target="tpu_custom_call" | custom-call | bytes 1024 | tf_op jit(solution)/shard_map/local/pallas_call | solution.py:23
  13.1 0.2 collective-permute-done.refs_0_
  13.3 0.3 collective-permute-done.2.before
  13.6 0.5 %near1.1.refs_5_.refs_3_.before.refs_0_ = bf16[4,160,128]{2,1,0:T(8,128)(2,1)S(1)} custom-call(bf16[4,160,800]{2,1,0:T(8,128)(2,1)S(1)} %get-tuple-element.25.packed.refs_0_, s32[6,12]{1,0:T(8,128)S(1)} %get-tuple-element.23.refs_2_.table.refs_1_, bf16[4,160,128]{2,1,0:T(8,128)(2,1)S(1)} %collective-permute-done.2.before, ...), custom_call_target="tpu_custom_call" | custom-call | bytes 1024 | tf_op jit(solution)/shard_map/near1/pallas_call | solution.py:23
  14.2 5.2 %collective-permute-start.4 = (bf16[4,160,128]{2,1,0:T(8,128)(2,1)S(1)}, bf16[4,160,128]{2,1,0:T(8,128)(2,1)S(1)}, u32[]{:S(2)}, u32[]{:S(2)}) collective-permute-start(bf16[4,160,128]{2,1,0:T(8,128)(2,1)S(1)} %near1.1.refs_5_.refs_3_.before.refs_0_), channel_id=1, source_target_pairs={{0,30},{1,3},{2,0},{3,5},{4,2},{5,7},{6,4},{7,9},{8,6},{9,11},{10,... | collective-permute-start | bytes 491528 | tf_op jit(solution)/shard_map/ppermute | solution.py:242
  19.4 0.0 collective-permute-done.1.refs_4_
  19.4 0.6 %far1.1.here.after.refs_5_ = bf16[4,160,128]{2,1,0:T(8,128)(2,1)S(1)} custom-call(bf16[4,160,800]{2,1,0:T(8,128)(2,1)S(1)} %get-tuple-element.22.refs_0_.packed, s32[6,12]{1,0:T(8,128)S(1)} %get-tuple-element.23.refs_2_.table.refs_1_, bf16[4,160,128]{2,1,0:T(8,128)(2,1)S(1)} %get-tuple-element.28.after.refs_2_.here.refs_0_, ...), custom_call_target="tpu_custom_call" | custom-call | bytes 1024 | tf_op jit(solution)/shard_map/far1/pallas_call | solution.py:23
  20.0 0.1 collective-permute-start.3
  20.1 0.6 %middle1.1.before.refs_4_.here.refs_0_ = bf16[4,160,128]{2,1,0:T(8,128)(2,1)S(1)} custom-call(bf16[4,160,800]{2,1,0:T(8,128)(2,1)S(1)} %get-tuple-element.24.packed, s32[6,12]{1,0:T(8,128)S(1)} %get-tuple-element.23.refs_2_.table.refs_1_, bf16[4,160,128]{2,1,0:T(8,128)(2,1)S(1)} %get-tuple-element.21.refs_3_.here.before.refs_5_, ...), custom_call_target="tpu_custom_call" | custom-call | bytes 1024 | tf_op jit(solution)/shard_map/middle1/pallas_call | solution.py:23
  20.7 1.6 %collective-permute-done.4.after = bf16[4,160,128]{2,1,0:T(8,128)(2,1)S(1)} collective-permute-done((bf16[4,160,128]{2,1,0:T(8,128)(2,1)S(1)}, bf16[4,160,128]{2,1,0:T(8,128)(2,1)S(1)}, u32[]{:S(2)}, u32[]{:S(2)}) %collective-permute-start.4) | collective-permute-done | bytes 163872 | tf_op jit(solution)/shard_map/ppermute | solution.py:242
  22.2 0.6 %far2.1.refs_6_.after.refs_3_.refs_0_ = bf16[4,160,128]{2,1,0:T(8,128)(2,1)S(1)} custom-call(bf16[4,160,800]{2,1,0:T(8,128)(2,1)S(1)} %get-tuple-element.22.refs_0_.packed, s32[6,12]{1,0:T(8,128)S(1)} %get-tuple-element.23.refs_2_.table.refs_1_, bf16[4,160,128]{2,1,0:T(8,128)(2,1)S(1)} %middle1.1.before.refs_4_.here.refs_0_, ...), custom_call_target="tpu_custom_call" | custom-call | bytes 1024 | tf_op jit(solution)/shard_map/far2/pallas_call | solution.py:23
  22.8 0.1 collective-permute-start.6
  22.9 4.7 %collective-permute-done.3.refs_2_ = bf16[4,160,128]{2,1,0:T(8,128)(2,1)S(1)} collective-permute-done((bf16[4,160,128]{2,1,0:T(8,128)(2,1)S(1)}, bf16[4,160,128]{2,1,0:T(8,128)(2,1)S(1)}, u32[]{:S(2)}, u32[]{:S(2)}) %collective-permute-start.3) | collective-permute-done | bytes 163872 | tf_op jit(solution)/shard_map/ppermute | solution.py:242
  27.6 0.5 %near2.1.before.here.refs_0_ = bf16[4,160,128]{2,1,0:T(8,128)(2,1)S(1)} custom-call(bf16[4,160,800]{2,1,0:T(8,128)(2,1)S(1)} %get-tuple-element.25.packed.refs_0_, s32[6,12]{1,0:T(8,128)S(1)} %get-tuple-element.23.refs_2_.table.refs_1_, bf16[4,160,128]{2,1,0:T(8,128)(2,1)S(1)} %collective-permute-done.3.refs_2_, ...), custom_call_target="tpu_custom_call" | custom-call | bytes 1024 | tf_op jit(solution)/shard_map/near2/pallas_call | solution.py:23
  28.1 0.1 collective-permute-start.5
  28.2 0.6 %middle2.1.here.after.refs_2_.refs_0_ = bf16[4,160,128]{2,1,0:T(8,128)(2,1)S(1)} custom-call(bf16[4,160,800]{2,1,0:T(8,128)(2,1)S(1)} %get-tuple-element.24.packed, s32[6,12]{1,0:T(8,128)S(1)} %get-tuple-element.23.refs_2_.table.refs_1_, bf16[4,160,128]{2,1,0:T(8,128)(2,1)S(1)} %near1.1.refs_5_.refs_3_.before.refs_0_, ...), custom_call_target="tpu_custom_call" | custom-call | bytes 1024 | tf_op jit(solution)/shard_map/middle2/pallas_call | solution.py:23
  28.8 1.9 %collective-permute-done.6.before = bf16[4,160,128]{2,1,0:T(8,128)(2,1)S(1)} collective-permute-done((bf16[4,160,128]{2,1,0:T(8,128)(2,1)S(1)}, bf16[4,160,128]{2,1,0:T(8,128)(2,1)S(1)}, u32[]{:S(2)}, u32[]{:S(2)}) %collective-permute-start.6) | collective-permute-done | bytes 163872 | tf_op jit(solution)/shard_map/ppermute | solution.py:242
  30.7 0.5 %near3.1.refs_6_.before.here = bf16[4,160,128]{2,1,0:T(8,128)(2,1)S(1)} custom-call(bf16[4,160,800]{2,1,0:T(8,128)(2,1)S(1)} %get-tuple-element.25.packed.refs_0_, s32[6,12]{1,0:T(8,128)S(1)} %get-tuple-element.23.refs_2_.table.refs_1_, bf16[4,160,128]{2,1,0:T(8,128)(2,1)S(1)} %collective-permute-done.6.before, ...), custom_call_target="tpu_custom_call" | custom-call | bytes 1024 | tf_op jit(solution)/shard_map/near3/pallas_call | solution.py:23
  31.3 0.1 collective-permute-start.7
  31.3 0.0 collective-permute-done.5.refs_4_
  31.3 0.6 %far3.1.after.here = bf16[4,160,128]{2,1,0:T(8,128)(2,1)S(1)} custom-call(bf16[4,160,800]{2,1,0:T(8,128)(2,1)S(1)} %get-tuple-element.22.refs_0_.packed, s32[6,12]{1,0:T(8,128)S(1)} %get-tuple-element.23.refs_2_.table.refs_1_, bf16[4,160,128]{2,1,0:T(8,128)(2,1)S(1)} %middle2.1.here.after.refs_2_.refs_0_, ...), custom_call_target="tpu_custom_call" | custom-call | bytes 1024 | tf_op jit(solution)/shard_map/far3/pallas_call | solution.py:23
  31.9 0.5 %collective-permute-start.9 = (bf16[4,160,128]{2,1,0:T(8,128)(2,1)S(1)}, bf16[4,160,128]{2,1,0:T(8,128)(2,1)S(1)}, u32[]{:S(2)}, u32[]{:S(2)}) collective-permute-start(bf16[4,160,128]{2,1,0:T(8,128)(2,1)S(1)} %far3.1.after.here), channel_id=1, source_target_pairs={{0,2},{1,31},{2,4},{3,1},{4,6},{5,3},{6,8},{7,5},{8,10},{9,7},{10,... | collective-permute-start | bytes 491528 | tf_op jit(solution)/shard_map/ppermute | solution.py:242
  32.5 0.6 %middle3.1.here.before.after = bf16[4,160,128]{2,1,0:T(8,128)(2,1)S(1)} custom-call(bf16[4,160,800]{2,1,0:T(8,128)(2,1)S(1)} %get-tuple-element.24.packed, s32[6,12]{1,0:T(8,128)S(1)} %get-tuple-element.23.refs_2_.table.refs_1_, bf16[4,160,128]{2,1,0:T(8,128)(2,1)S(1)} %near2.1.before.here.refs_0_, ...), custom_call_target="tpu_custom_call" | custom-call | bytes 1024 | tf_op jit(solution)/shard_map/middle3/pallas_call | solution.py:23
  33.1 0.6 %middle4.1.refs_1_.middle = bf16[4,160,128]{2,1,0:T(8,128)(2,1)S(1)} custom-call(bf16[4,160,800]{2,1,0:T(8,128)(2,1)S(1)} %get-tuple-element.24.packed, s32[6,12]{1,0:T(8,128)S(1)} %get-tuple-element.23.refs_2_.table.refs_1_, bf16[4,160,128]{2,1,0:T(8,128)(2,1)S(1)} %near3.1.refs_6_.before.here, bf16[4,160,128]{2,1,0:T(8,128)(2,1)S(1)} %middle3.1.here.before.after, ...), custom_call_target="tpu_custom_call" | custom-call | bytes 1024 | tf_op jit(solution)/shard_map/middle4/pallas_call | solution.py:23
  33.7 0.5 %collective-permute-done.7.after = bf16[4,160,128]{2,1,0:T(8,128)(2,1)S(1)} collective-permute-done((bf16[4,160,128]{2,1,0:T(8,128)(2,1)S(1)}, bf16[4,160,128]{2,1,0:T(8,128)(2,1)S(1)}, u32[]{:S(2)}, u32[]{:S(2)}) %collective-permute-start.7) | collective-permute-done | bytes 163872 | tf_op jit(solution)/shard_map/ppermute | solution.py:242
  34.1 0.6 %far4.1 = bf16[6,160,128]{2,1,0:T(8,128)(2,1)S(1)} custom-call(bf16[4,160,800]{2,1,0:T(8,128)(2,1)S(1)} %get-tuple-element.22.refs_0_.packed, s32[6,12]{1,0:T(8,128)S(1)} %get-tuple-element.23.refs_2_.table.refs_1_, bf16[4,160,128]{2,1,0:T(8,128)(2,1)S(1)} %middle3.1.here.before.after, bf16[4,160,128]{2,1,0:T(8,128)(2,1)S(1)} %far3.1.after.here, ...), custom_call_target="tpu_custom_call" | custom-call | bytes 1024 | tf_op jit(solution)/shard_map/far4/pallas_call | solution.py:23
  34.8 2.4 %collective-permute-start.8 = (bf16[6,160,128]{2,1,0:T(8,128)(2,1)S(1)}, bf16[6,160,128]{2,1,0:T(8,128)(2,1)S(1)}, u32[]{:S(2)}, u32[]{:S(2)}) collective-permute-start(bf16[6,160,128]{2,1,0:T(8,128)(2,1)S(1)} %far4.1), channel_id=1, source_target_pairs={{0,1},{1,0},{2,3},{3,2},{4,5},{5,4},{6,7},{7,6},{8,9},{9,8},{10,11... | collective-permute-start | bytes 737288 | tf_op jit(solution)/shard_map/ppermute | solution.py:252
  37.1 2.3 %collective-permute-done.9.before = bf16[4,160,128]{2,1,0:T(8,128)(2,1)S(1)} collective-permute-done((bf16[4,160,128]{2,1,0:T(8,128)(2,1)S(1)}, bf16[4,160,128]{2,1,0:T(8,128)(2,1)S(1)}, u32[]{:S(2)}, u32[]{:S(2)}) %collective-permute-start.9) | collective-permute-done | bytes 163872 | tf_op jit(solution)/shard_map/ppermute | solution.py:242
  39.4 0.5 %near4.1.near = bf16[4,160,128]{2,1,0:T(8,128)(2,1)S(1)} custom-call(bf16[4,160,800]{2,1,0:T(8,128)(2,1)S(1)} %get-tuple-element.25.packed.refs_0_, s32[6,12]{1,0:T(8,128)S(1)} %get-tuple-element.23.refs_2_.table.refs_1_, bf16[4,160,128]{2,1,0:T(8,128)(2,1)S(1)} %collective-permute-done.9.before, bf16[4,160,128]{2,1,0:T(8,128)(2,1)S(1)} %near3.1.refs_6_.before.here, ...), custom_call_target="tpu_custom_call" | custom-call | flops 20000000000 | bytes 1024 | tf_op jit(solution)/shard_map/near4/pallas_call | solution.py:23
  40.0 0.7 %own.1.refs_1_ = bf16[6,160,256]{2,1,0:T(8,128)(2,1)} custom-call(bf16[4,160,128]{2,1,0:T(8,128)(2,1)S(1)} %near4.1.near, bf16[4,160,128]{2,1,0:T(8,128)(2,1)S(1)} %middle4.1.refs_1_.middle), custom_call_target="tpu_custom_call" | custom-call | bytes 1024 | tf_op jit(solution)/shard_map/own/pallas_call | solution.py:23
  40.7 2.5 %collective-permute-done.8.refs_0_ = bf16[6,160,128]{2,1,0:T(8,128)(2,1)S(1)} collective-permute-done((bf16[6,160,128]{2,1,0:T(8,128)(2,1)S(1)}, bf16[6,160,128]{2,1,0:T(8,128)(2,1)S(1)}, u32[]{:S(2)}, u32[]{:S(2)}) %collective-permute-start.8) | collective-permute-done | bytes 245792 | tf_op jit(solution)/shard_map/ppermute | solution.py:252
  43.2 0.7 %others.1 = bf16[6,160,256]{2,1,0:T(8,128)(2,1)} custom-call(bf16[6,160,128]{2,1,0:T(8,128)(2,1)S(1)} %collective-permute-done.8.refs_0_, bf16[6,160,256]{2,1,0:T(8,128)(2,1)} %own.1.refs_1_), custom_call_target="tpu_custom_call", output_to_operand_aliasing={{}: (1, {})} | custom-call | bytes 1024 | tf_op jit(solution)/shard_map/others/pallas_call | solution.py:23
  (1 shorter events, 0.0 us)
Async XLA Ops:
  2.1 11.2 %collective-permute-start = (bf16[6,160,128]{2,1,0:T(8,128)(2,1)S(1)}, bf16[6,160,128]{2,1,0:T(8,128)(2,1)S(1)}, u32[]{:S(2)}, u32[]{:S(2)}) collective-permute-start(bf16[6,160,128]{2,1,0:T(8,128)(2,1)S(1)} %get-tuple-element.26), channel_id=1, source_target_pairs={{0,1},{1,0},{2,3},{3,2},{4,5},{5,4},{6,7},{7,6},{8,9},{9,8},{10,11... | collective-permute-start | bytes 737288 | tf_op jit(solution)/shard_map/ppermute | solution.py:252
  5.2 8.4 %collective-permute-start.2 = (bf16[4,160,128]{2,1,0:T(8,128)(2,1)S(1)}, bf16[4,160,128]{2,1,0:T(8,128)(2,1)S(1)}, u32[]{:S(2)}, u32[]{:S(2)}) collective-permute-start(bf16[4,160,128]{2,1,0:T(8,128)(2,1)S(1)} %get-tuple-element.30), channel_id=1, source_target_pairs={{0,31},{1,2},{2,1},{3,4},{4,3},{5,6},{6,5},{7,8},{8,7},{9,10},{10,... | collective-permute-start | bytes 491528 | tf_op jit(solution)/shard_map/ppermute | solution.py:242
  9.1 10.3 %collective-permute-start.1 = (bf16[4,160,128]{2,1,0:T(8,128)(2,1)S(1)}, bf16[4,160,128]{2,1,0:T(8,128)(2,1)S(1)}, u32[]{:S(2)}, u32[]{:S(2)}) collective-permute-start(bf16[4,160,128]{2,1,0:T(8,128)(2,1)S(1)} %get-tuple-element.21.refs_3_.here.before.refs_5_), channel_id=1, source_target_pairs={{0,30},{1,3},{2,0},{3,5},{4,2},{5,7},{6,4},{7,9},{8,6},{9,11},{10,... | collective-permute-start | bytes 491528 | tf_op jit(solution)/shard_map/ppermute | solution.py:242
  14.2 8.1 %collective-permute-start.4 = (bf16[4,160,128]{2,1,0:T(8,128)(2,1)S(1)}, bf16[4,160,128]{2,1,0:T(8,128)(2,1)S(1)}, u32[]{:S(2)}, u32[]{:S(2)}) collective-permute-start(bf16[4,160,128]{2,1,0:T(8,128)(2,1)S(1)} %near1.1.refs_5_.refs_3_.before.refs_0_), channel_id=1, source_target_pairs={{0,30},{1,3},{2,0},{3,5},{4,2},{5,7},{6,4},{7,9},{8,6},{9,11},{10,... | collective-permute-start | bytes 491528 | tf_op jit(solution)/shard_map/ppermute | solution.py:242
  20.0 7.6 %collective-permute-start.3 = (bf16[4,160,128]{2,1,0:T(8,128)(2,1)S(1)}, bf16[4,160,128]{2,1,0:T(8,128)(2,1)S(1)}, u32[]{:S(2)}, u32[]{:S(2)}) collective-permute-start(bf16[4,160,128]{2,1,0:T(8,128)(2,1)S(1)} %far1.1.here.after.refs_5_), channel_id=1, source_target_pairs={{0,2},{1,31},{2,4},{3,1},{4,6},{5,3},{6,8},{7,5},{8,10},{9,7},{10,... | collective-permute-start | bytes 491528 | tf_op jit(solution)/shard_map/ppermute | solution.py:242
  22.8 7.9 %collective-permute-start.6 = (bf16[4,160,128]{2,1,0:T(8,128)(2,1)S(1)}, bf16[4,160,128]{2,1,0:T(8,128)(2,1)S(1)}, u32[]{:S(2)}, u32[]{:S(2)}) collective-permute-start(bf16[4,160,128]{2,1,0:T(8,128)(2,1)S(1)} %far2.1.refs_6_.after.refs_3_.refs_0_), channel_id=1, source_target_pairs={{0,2},{1,31},{2,4},{3,1},{4,6},{5,3},{6,8},{7,5},{8,10},{9,7},{10,... | collective-permute-start | bytes 491528 | tf_op jit(solution)/shard_map/ppermute | solution.py:242
  28.1 3.2 %collective-permute-start.5 = (bf16[4,160,128]{2,1,0:T(8,128)(2,1)S(1)}, bf16[4,160,128]{2,1,0:T(8,128)(2,1)S(1)}, u32[]{:S(2)}, u32[]{:S(2)}) collective-permute-start(bf16[4,160,128]{2,1,0:T(8,128)(2,1)S(1)} %near2.1.before.here.refs_0_), channel_id=1, source_target_pairs={{0,30},{1,3},{2,0},{3,5},{4,2},{5,7},{6,4},{7,9},{8,6},{9,11},{10,... | collective-permute-start | bytes 491528 | tf_op jit(solution)/shard_map/ppermute | solution.py:242
  31.3 2.9 %collective-permute-start.7 = (bf16[4,160,128]{2,1,0:T(8,128)(2,1)S(1)}, bf16[4,160,128]{2,1,0:T(8,128)(2,1)S(1)}, u32[]{:S(2)}, u32[]{:S(2)}) collective-permute-start(bf16[4,160,128]{2,1,0:T(8,128)(2,1)S(1)} %near3.1.refs_6_.before.here), channel_id=1, source_target_pairs={{0,30},{1,3},{2,0},{3,5},{4,2},{5,7},{6,4},{7,9},{8,6},{9,11},{10,... | collective-permute-start | bytes 491528 | tf_op jit(solution)/shard_map/ppermute | solution.py:242
  31.9 7.5 %collective-permute-start.9 = (bf16[4,160,128]{2,1,0:T(8,128)(2,1)S(1)}, bf16[4,160,128]{2,1,0:T(8,128)(2,1)S(1)}, u32[]{:S(2)}, u32[]{:S(2)}) collective-permute-start(bf16[4,160,128]{2,1,0:T(8,128)(2,1)S(1)} %far3.1.after.here), channel_id=1, source_target_pairs={{0,2},{1,31},{2,4},{3,1},{4,6},{5,3},{6,8},{7,5},{8,10},{9,7},{10,... | collective-permute-start | bytes 491528 | tf_op jit(solution)/shard_map/ppermute | solution.py:242
  34.8 8.5 %collective-permute-start.8 = (bf16[6,160,128]{2,1,0:T(8,128)(2,1)S(1)}, bf16[6,160,128]{2,1,0:T(8,128)(2,1)S(1)}, u32[]{:S(2)}, u32[]{:S(2)}) collective-permute-start(bf16[6,160,128]{2,1,0:T(8,128)(2,1)S(1)} %far4.1), channel_id=1, source_target_pairs={{0,1},{1,0},{2,3},{3,2},{4,5},{5,4},{6,7},{7,6},{8,9},{9,8},{10,11... | collective-permute-start | bytes 737288 | tf_op jit(solution)/shard_map/ppermute | solution.py:252

commit v4 on v3

--- a/solution.py
+++ b/solution.py
@@ -60,31 +60,30 @@
     return jnp.where(rows_below(count, rows, lanes), turned, 0.0).astype(jnp.bfloat16)
 
 
-def rotate_out_kernel(shards, reach, orbitals, rotation, counts, *refs):
-    outs, (held, weights, limits, scalars, sems) = refs[:-5], refs[-5:]
+def fetch_kernel(shards, reach, orbitals, rotation, counts, neighbors, *refs):
+    outs, (held, weights, limits, beside, scalars, sems) = refs[:-6], refs[-6:]
     elems = orbitals.shape[0]
     me, flip = lax.axis_index("state"), flipped(shards)
     copies = [
-        pltpu.make_async_copy(rotation, weights, sems.at[0]),
-        pltpu.make_async_copy(counts, scalars, sems.at[1]),
-        pltpu.make_async_copy(counts, limits, sems.at[2]),
+        pltpu.make_async_copy(source, target, sems.at[i])
+        for i, (source, target) in enumerate(
+            [(rotation, weights), (counts, scalars), (orbitals, held), (counts, limits), (neighbors, beside)]
+        )
     ]
-    copies += [pltpu.make_async_copy(orbitals.at[e], held.at[e], sems.at[3 + e]) for e in range(elems)]
     for copy in copies:
         copy.start()
-    copies[0].wait()
-    copies[1].wait()
-    for e in range(elems):
-        copies[3 + e].wait()
-        for k in range(shards - 1):
-            spot = choose(flip, (e + reach) % elems, e)
-            outs[k][spot] = turn(shards, k + 1, held[e], weights, scalars[me * elems + e])
-    if shards == 2:
-        outs[1][...] = outs[0][:reach]
-    copies[2].wait()
-
-
-def rotate_in_kernel(shards, reach, held, weights, limits, *outs):
+    for copy in copies[:3]:
+        copy.wait()
+    first = reach if shards == 2 else 0
+    for k, out in enumerate(outs):
+        for at in range(out.shape[0]):
+            e = choose(flip, (first + at + elems - reach) % elems, first + at)
+            out[at] = turn(shards, k + 1, held[e], weights, scalars[me * elems + e])
+    for copy in copies[3:]:
+        copy.wait()
+
+
+def rotate_kernel(shards, reach, k, held, weights, limits, *outs):
     me, flip = lax.axis_index("state"), flipped(shards)
     elems = held.shape[0]
     ends = limits[...]
@@ -95,20 +94,12 @@
         for shard in range(shards):
             here = (spot + elems - reach) % elems if shard == 1 and flip is not False else spot
             count = jnp.where(me == shard, ends[shard * elems + here], count)
-        out[at] = turn(shards, 0, held[e], weights, count)
-
-
-def local_kernel(total, shards, reach, blocks, neighbors, limits, *refs):
-    packed, (table, raw, beside, sems) = refs[:-4], refs[-4:]
-    elems, couplings, _, _ = blocks.shape
+        out[at] = turn(shards, k, held[e], weights, count)
+
+
+def table_kernel(total, shards, reach, beside, limits, table):
+    couplings, elems = beside.shape
     flip, groups = flipped(shards), elems // reach
-    spots = [choose(flip, elems - (g + 1) * reach, g * reach) + e for g in range(groups) for e in range(reach)]
-    copies = [pltpu.make_async_copy(blocks.at[e], raw.at[i], sems.at[i]) for i, e in enumerate(spots)]
-    neighbor_copy = pltpu.make_async_copy(neighbors, beside, sems.at[elems])
-    neighbor_copy.start()
-    for copy in copies:
-        copy.start()
-    neighbor_copy.wait()
     column = lax.broadcasted_iota(jnp.int32, beside.shape, 1)
     offset = beside[...] - (column + lax.axis_index("elem") * elems)
     offset = jnp.where(offset > reach, offset - total, jnp.where(offset < -reach, offset + total, offset))
@@ -123,20 +114,24 @@
 
     table[:couplings] = mirrored(place)
     table[couplings:] = mirrored(ends)
-    for i in range(elems):
-        out, e = packed[i // reach], i % reach
-        copies[i].wait()
+
+
+def pack_kernel(shards, group, blocks, packed):
+    elems, couplings, _, _ = blocks.shape
+    width = packed.shape[0]
+    first = choose(flipped(shards), elems - (group + 1) * width, group * width)
+    for e in range(width):
         for k in range(couplings):
-            out[e, :, k * FULL : (k + 1) * FULL] = raw[i, k, :, :FULL]
-        tail = [raw[i, k, :, FULL:] for k in range(couplings)]
-        out[e, :, couplings * FULL :] = jnp.concatenate(tail, axis=1)
-
-
-def pair_kernel(reach, arrived, half, far, middle):
+            packed[e, :, k * FULL : (k + 1) * FULL] = blocks[first + e, k, :, :FULL]
+        tail = [blocks[first + e, k, :, FULL:] for k in range(couplings)]
+        packed[e, :, couplings * FULL :] = jnp.concatenate(tail, axis=1)
+
+
+def middle_kernel(half, arrived, leaving, middle, copied):
     flip, share = flipped(2), half.shape[0]
-    far[...] = arrived[:reach]
+    copied[...] = leaving[...]
     middle[pl.ds(choose(flip, share, 0), share)] = half[...]
-    middle[pl.ds(choose(flip, 0, share), share)] = arrived[reach:]
+    middle[pl.ds(choose(flip, 0, share), share)] = arrived[...]
 
 
 def gather_kernel(shards, *refs):
@@ -219,9 +214,9 @@
 def on_device(orbitals, rotation, counts, neighbors, blocks):
     row_elems, rows, states = orbitals.shape
     elems, couplings = neighbors.shape
-    orbitals, rotation, counts, neighbors, blocks = (
-        pltpu.with_memory_space_constraint(x, pltpu.HBM) for x in (orbitals, rotation, counts, neighbors.T, blocks)
-    )
+    inputs = [
+        pltpu.with_memory_space_constraint(x, pltpu.HBM) for x in (orbitals, rotation, counts, neighbors.T)
+    ]
     shards = lax.axis_size("state")
     ring = lax.axis_size("elem")
     width = elems // 3
@@ -252,55 +247,63 @@
             lax.ppermute(x, "state", [(i, (i + k + 1) % shards) for i in range(shards)]) for k, x in enumerate(parts)
         ]
 
-    *parts, held, weights, limits = call(
-        functools.partial(rotate_out_kernel, shards, width),
-        [part] * (shards - 1)
-        + [group] * pair
-        + [bf16(*orbitals.shape), bf16(*rotation.shape), jax.ShapeDtypeStruct(counts.shape, jnp.int32)],
-        [HBM] * 3,
-        orbitals,
-        rotation,
-        counts,
-        scratch=[scalars, dma((row_elems + 3,))],
-        name="rotate_out",
-    )
-    arrived = swapped(parts[: shards - 1])
-    if pair:
-        near_halo = shifted(parts[1], -1, across=True)
-    kept = call(
-        functools.partial(rotate_in_kernel, shards, width),
-        [group, half] if pair else [part],
-        [VMEM] * 3,
-        held,
-        weights,
-        limits,
-        name="rotate_in",
+    *parts, held, weights, limits, beside = call(
+        functools.partial(fetch_kernel, shards, width),
+        ([half] if pair else [part] * (shards - 1)) + [jax.ShapeDtypeStruct(x.shape, x.dtype) for x in inputs],
+        [HBM] * len(inputs),
+        *inputs,
+        scratch=[scalars, dma((5,))],
+        flops=LONG,
+        name="fetch",
     )
     if pair:
+        arrived_half = swapped(parts)[0]
+        leaving = call(
+            functools.partial(rotate_kernel, shards, width, 1), [group], [VMEM] * 3, held, weights, limits, name="rotate_out"
+        )[0]
+        near_halo = shifted(leaving, -1, across=True)
+        kept = call(
+            functools.partial(rotate_kernel, shards, width, 0),
+            [group, half],
+            [VMEM] * 3,
+            held,
+            weights,
+            limits,
+            name="rotate_in",
+        )
         far_halo = to_far_of_neighbor(kept[0])
-    *packed, table = call(
-        functools.partial(without, functools.partial(local_kernel, elems * ring, shards, width), 3),
-        [bf16(width, rows, couplings * rows)] * 3 + [jax.ShapeDtypeStruct((couplings + 1, elems), jnp.int32)],
-        [HBM, HBM, VMEM, ANY],
-        blocks,
-        neighbors,
+        middle, leaving = call(
+            middle_kernel, [group] * 2, [VMEM] * 3, kept[1], arrived_half, leaving, name="gather"
+        )
+        far = swapped([leaving])[0]
+    else:
+        arrived = swapped(parts)
+        kept = call(
+            functools.partial(rotate_kernel, shards, width, 0), [part], [VMEM] * 3, held, weights, limits, name="rotate_in"
+        )
+    table = call(
+        functools.partial(without, functools.partial(table_kernel, elems * ring, shards, width), 2),
+        [jax.ShapeDtypeStruct((couplings + 1, elems), jnp.int32)],
+        [VMEM, VMEM, ANY],
+        beside,
         limits,
         kept[0],
-        scratch=[pltpu.VMEM(blocks.shape, jnp.bfloat16), pltpu.VMEM(neighbors.shape, jnp.int32), dma((elems + 1,))],
-        limit=16 << 20,
-        name="local",
-    )
+        name="table",
+    )[0]
+
+    def pack(g, behind):
+        return call(
+            functools.partial(without, functools.partial(pack_kernel, shards, g), 1),
+            [bf16(width, rows, couplings * rows)],
+            [VMEM, ANY],
+            blocks,
+            behind,
+            name="pack",
+        )[0]
+
+    packed = {0: pack(0, table)}
     if pair:
         near = kept[0]
-        far, middle = call(
-            functools.partial(without, functools.partial(pair_kernel, width), 2),
-            [group] * 2,
-            [VMEM, VMEM, ANY],
-            *arrived,
-            kept[1],
-            table,
-            name="gather",
-        )
     else:
         near, middle, far = call(
             functools.partial(without, functools.partial(gather_kernel, shards), shards),
@@ -308,7 +311,7 @@
             [VMEM] * shards + [ANY],
             *kept,
             *arrived,
-            table,
+            packed[0],
             scratch=[whole],
             name="gather",
         )
@@ -339,6 +342,8 @@
         if m % 2:
             new_near = level(0, m, near_halo, near, middle, older[0])
             next_far_halo = to_far_of_neighbor(new_near)
+            if m == 1:
+                packed[2] = pack(2, new_near)
             new_far = level(2, m, middle, far, far_halo, older[2], behind=new_near)
             next_near_halo = to_near_of_neighbor(new_far)
         else:
@@ -350,6 +355,8 @@
             new_near = level(0, m, near_halo, near, middle, older[0], behind=None if last else new_far, flops=LONG * last)
             if not last:
                 next_far_halo = to_far_of_neighbor(new_near)
+        if m == 1:
+            packed[1] = pack(1, new_far)
         if not last:
             new_middle = level(1, m, near, middle, far, older[1])
             near_halo, far_halo = next_near_halo, next_far_halo

time: 44.1 us -> 41.3 us (0.937)
  Pallas kernels: 13.6 us -> 11.3 us
  starting transfers between devices: 16.2 us -> 15.6 us
    ppermute x8, starting transfers between devices: 10.8 us -> 7.64 us  [shifted(): return lax.ppermute(x, ('elem', 'state'), moves)]
    ppermute x2 -> x3, starting transfers between devices: 5.4 us -> 8 us  [swapped(): lax.ppermute(x, 'state', [(i, (i + k + 1) % shards) for i in range(shards)])]
    pallas_call x18 -> x22, Pallas kernels: 13.6 us -> 11.3 us  [call(): pl.pallas_call(kernel, out_shape=outs, in_specs=ins, out_specs=out_specs...]
    ppermute x2 -> x3, waiting for transfers between devices: 2.73 us -> 2.9 us  [swapped(): lax.ppermute(x, 'state', [(i, (i + k + 1) % shards) for i in range(shards)])]
  transfers between devices with their start and end apart: 10 -> 11, of which waited for: 8 -> 9; matrix products, arithmetic and copies ran while one was open for 0% -> 0% of each run, Pallas kernels for 25% -> 22%
where the time goes in v4:
time: 41.3 us; the launch traced here: 41.2 us
  starting transfers between devices  15.6 us (38%)
  waiting for transfers between devices  14 us (34%)
  Pallas kernels  11.3 us (27%)
    pallas_call x22, Pallas kernels, call(): pl.pallas_call(kernel, out_shape=outs, in_specs=ins, out_specs=out_specs...  11.3 us
    ppermute x8, waiting for transfers between devices, shifted(): return lax.ppermute(x, ('elem', 'state'), moves)  11.1 us
    ppermute x3, starting transfers between devices, swapped(): lax.ppermute(x, 'state', [(i, (i + k + 1) % shards) for i in range(shards)])  8 us
    ppermute x8, starting transfers between devices, shifted(): return lax.ppermute(x, ('elem', 'state'), moves)  7.64 us
    ppermute x3, waiting for transfers between devices, swapped(): lax.ppermute(x, 'state', [(i, (i + k + 1) % shards) for i in range(shards)])  2.9 us
  transfers between devices with their start and end apart: 11, of which 9 were waited for; matrix products, arithmetic and copies ran while one was open for 0% of the time, Pallas kernels for 22%

profile of v4, /device:TPU:0, one launch (start us, length us, event | category | flops | bytes accessed | tf_op | source)
XLA Modules:
  0.0 41.2 jit_solution(9117134846249617708)
XLA Ops:
  0.0 0.0 slice-start
  0.0 0.0 slice-start.1
  0.0 1.5 %fetch.1 = (bf16[2,160,128]{2,1,0:T(8,128)(2,1)S(1)}, bf16[6,160,256]{2,1,0:T(8,128)(2,1)S(1)}, bf16[256,256]{1,0:T(8,128)(2,1)S(1)}, s32[12]{0:T(128)S(1)}, s32[5,12]{1,0:T(8,128)S(1)}) custom-call(bf16[6,160,256]{2,1,0:T(8,128)(2,1)} %orbitals.1, bf16[256,256]{1,0:T(8,128)(2,1)} %rotation.1, s32[12]{0:T(128)} %counts.1, s32[5,12]{1,0:T(8,128)} %bitcast.3), custom_call_target="tpu_custom_call" | custom-call | flops 20000000000 | bytes 1024 | tf_op jit(solution)/shard_map/fetch/pallas_call | solution.py:23
  1.5 3.0 %collective-permute-start.1 = (bf16[2,160,128]{2,1,0:T(8,128)(2,1)S(1)}, bf16[2,160,128]{2,1,0:T(8,128)(2,1)S(1)}, u32[]{:S(2)}, u32[]{:S(2)}) collective-permute-start(bf16[2,160,128]{2,1,0:T(8,128)(2,1)S(1)} %get-tuple-element.20), channel_id=1, source_target_pairs={{0,1},{1,0},{2,3},{3,2},{4,5},{5,4},{6,7},{7,6},{8,9},{9,8},{10,11... | collective-permute-start | bytes 245768 | tf_op jit(solution)/shard_map/ppermute | solution.py:247
  4.5 0.3 rotate_out.1.leaving
  4.8 3.7 %collective-permute-start = (bf16[4,160,128]{2,1,0:T(8,128)(2,1)S(1)}, bf16[4,160,128]{2,1,0:T(8,128)(2,1)S(1)}, u32[]{:S(2)}, u32[]{:S(2)}) collective-permute-start(bf16[4,160,128]{2,1,0:T(8,128)(2,1)S(1)} %rotate_out.1.leaving), channel_id=1, source_target_pairs={{0,31},{1,2},{2,1},{3,4},{4,3},{5,6},{6,5},{7,8},{8,7},{9,10},{10,... | collective-permute-start | bytes 491528 | tf_op jit(solution)/shard_map/ppermute | solution.py:237
  8.5 0.3 rotate_in.1
  8.8 1.2 %collective-permute-start.3 = (bf16[4,160,128]{2,1,0:T(8,128)(2,1)S(1)}, bf16[4,160,128]{2,1,0:T(8,128)(2,1)S(1)}, u32[]{:S(2)}, u32[]{:S(2)}) collective-permute-start(bf16[4,160,128]{2,1,0:T(8,128)(2,1)S(1)} %get-tuple-element.18.refs_2_.here.before.refs_5_), channel_id=1, source_target_pairs={{0,30},{1,3},{2,0},{3,5},{4,2},{5,7},{6,4},{7,9},{8,6},{9,11},{10,... | collective-permute-start | bytes 491528 | tf_op jit(solution)/shard_map/ppermute | solution.py:237
  10.0 0.0 collective-permute-done.1.arrived
  10.0 1.7 %collective-permute-start.2 = (bf16[4,160,128]{2,1,0:T(8,128)(2,1)S(1)}, bf16[4,160,128]{2,1,0:T(8,128)(2,1)S(1)}, u32[]{:S(2)}, u32[]{:S(2)}) collective-permute-start(bf16[4,160,128]{2,1,0:T(8,128)(2,1)S(1)} %get-tuple-element.22), channel_id=1, source_target_pairs={{0,1},{1,0},{2,3},{3,2},{4,5},{5,4},{6,7},{7,6},{8,9},{9,8},{10,11... | collective-permute-start | bytes 491528 | tf_op jit(solution)/shard_map/ppermute | solution.py:247
  11.7 0.1 table.1.refs_1_
  11.8 0.0 slice-done
  11.8 0.0 slice-done.1
  11.8 0.3 pack.3.packed.refs_0_
  12.1 1.2 %collective-permute-done.before = bf16[4,160,128]{2,1,0:T(8,128)(2,1)S(1)} collective-permute-done((bf16[4,160,128]{2,1,0:T(8,128)(2,1)S(1)}, bf16[4,160,128]{2,1,0:T(8,128)(2,1)S(1)}, u32[]{:S(2)}, u32[]{:S(2)}) %collective-permute-start) | collective-permute-done | bytes 163872 | tf_op jit(solution)/shard_map/ppermute | solution.py:237
  13.3 0.5 %near1.1.refs_1_.refs_5_.refs_3_.before.refs_0_ = bf16[4,160,128]{2,1,0:T(8,128)(2,1)S(1)} custom-call(bf16[4,160,800]{2,1,0:T(8,128)(2,1)S(1)} %pack.3.packed.refs_0_, s32[6,12]{1,0:T(8,128)S(1)} %table.1.refs_1_, bf16[4,160,128]{2,1,0:T(8,128)(2,1)S(1)} %collective-permute-done.before, ...), custom_call_target="tpu_custom_call" | custom-call | bytes 1024 | tf_op jit(solution)/shard_map/near1/pallas_call | solution.py:23
  13.8 2.3 %collective-permute-start.5 = (bf16[4,160,128]{2,1,0:T(8,128)(2,1)S(1)}, bf16[4,160,128]{2,1,0:T(8,128)(2,1)S(1)}, u32[]{:S(2)}, u32[]{:S(2)}) collective-permute-start(bf16[4,160,128]{2,1,0:T(8,128)(2,1)S(1)} %near1.1.refs_1_.refs_5_.refs_3_.before.refs_0_), channel_id=1, source_target_pairs={{0,30},{1,3},{2,0},{3,5},{4,2},{5,7},{6,4},{7,9},{8,6},{9,11},{10,... | collective-permute-start | bytes 491528 | tf_op jit(solution)/shard_map/ppermute | solution.py:237
  16.1 0.3 pack.4.refs_0_.packed
  16.4 0.0 collective-permute-done.3.refs_4_
  16.4 0.3 collective-permute-done.2.refs_3_.after.refs_0_
  16.7 0.6 %far1.1.refs_1_.here.after.refs_5_ = bf16[4,160,128]{2,1,0:T(8,128)(2,1)S(1)} custom-call(bf16[4,160,800]{2,1,0:T(8,128)(2,1)S(1)} %pack.4.refs_0_.packed, s32[6,12]{1,0:T(8,128)S(1)} %table.1.refs_1_, bf16[4,160,128]{2,1,0:T(8,128)(2,1)S(1)} %get-tuple-element.21.after.refs_2_.here.refs_0_, ...), custom_call_target="tpu_custom_call" | custom-call | bytes 1024 | tf_op jit(solution)/shard_map/far1/pallas_call | solution.py:23
  17.3 0.1 collective-permute-start.4
  17.4 0.3 pack.5.packed
  17.6 0.6 %middle1.1.before.refs_4_.here.refs_0_ = bf16[4,160,128]{2,1,0:T(8,128)(2,1)S(1)} custom-call(bf16[4,160,800]{2,1,0:T(8,128)(2,1)S(1)} %pack.5.packed, s32[6,12]{1,0:T(8,128)S(1)} %table.1.refs_1_, bf16[4,160,128]{2,1,0:T(8,128)(2,1)S(1)} %get-tuple-element.18.refs_2_.here.before.refs_5_, ...), custom_call_target="tpu_custom_call" | custom-call | bytes 1024 | tf_op jit(solution)/shard_map/middle1/pallas_call | solution.py:23
  18.2 0.7 %collective-permute-done.5.after = bf16[4,160,128]{2,1,0:T(8,128)(2,1)S(1)} collective-permute-done((bf16[4,160,128]{2,1,0:T(8,128)(2,1)S(1)}, bf16[4,160,128]{2,1,0:T(8,128)(2,1)S(1)}, u32[]{:S(2)}, u32[]{:S(2)}) %collective-permute-start.5) | collective-permute-done | bytes 163872 | tf_op jit(solution)/shard_map/ppermute | solution.py:237
  18.9 0.6 %far2.1.refs_6_.after.refs_3_.refs_0_ = bf16[4,160,128]{2,1,0:T(8,128)(2,1)S(1)} custom-call(bf16[4,160,800]{2,1,0:T(8,128)(2,1)S(1)} %pack.4.refs_0_.packed, s32[6,12]{1,0:T(8,128)S(1)} %table.1.refs_1_, bf16[4,160,128]{2,1,0:T(8,128)(2,1)S(1)} %middle1.1.before.refs_4_.here.refs_0_, bf16[4,160,128]{2,1,0:T(8,128)(2,1)S(1)} %far1.1.refs_1_.here.after.refs_5_, ...), custom_call_target="tpu_custom_call" | custom-call | bytes 1024 | tf_op jit(solution)/shard_map/far2/pallas_call | solution.py:23
  19.6 0.1 collective-permute-start.7
  19.6 5.3 %collective-permute-done.4.refs_2_ = bf16[4,160,128]{2,1,0:T(8,128)(2,1)S(1)} collective-permute-done((bf16[4,160,128]{2,1,0:T(8,128)(2,1)S(1)}, bf16[4,160,128]{2,1,0:T(8,128)(2,1)S(1)}, u32[]{:S(2)}, u32[]{:S(2)}) %collective-permute-start.4) | collective-permute-done | bytes 163872 | tf_op jit(solution)/shard_map/ppermute | solution.py:237
  24.9 0.5 %near2.1.before.here.refs_0_ = bf16[4,160,128]{2,1,0:T(8,128)(2,1)S(1)} custom-call(bf16[4,160,800]{2,1,0:T(8,128)(2,1)S(1)} %pack.3.packed.refs_0_, s32[6,12]{1,0:T(8,128)S(1)} %table.1.refs_1_, bf16[4,160,128]{2,1,0:T(8,128)(2,1)S(1)} %collective-permute-done.4.refs_2_, bf16[4,160,128]{2,1,0:T(8,128)(2,1)S(1)} %near1.1.refs_1_.refs_5_.refs_3_.before.refs_0_, ...), custom_call_target="tpu_custom_call" | custom-call | bytes 1024 | tf_op jit(solution)/shard_map/near2/pallas_call | solution.py:23
  25.4 0.1 collective-permute-start.6
  25.5 0.6 %middle2.1.here.after.refs_2_.refs_0_ = bf16[4,160,128]{2,1,0:T(8,128)(2,1)S(1)} custom-call(bf16[4,160,800]{2,1,0:T(8,128)(2,1)S(1)} %pack.5.packed, s32[6,12]{1,0:T(8,128)S(1)} %table.1.refs_1_, bf16[4,160,128]{2,1,0:T(8,128)(2,1)S(1)} %near1.1.refs_1_.refs_5_.refs_3_.before.refs_0_, bf16[4,160,128]{2,1,0:T(8,128)(2,1)S(1)} %middle1.1.before.refs_4_.here.refs_0_, ...), custom_call_target="tpu_custom_call" | custom-call | bytes 1024 | tf_op jit(solution)/shard_map/middle2/pallas_call | solution.py:23
  26.1 1.3 %collective-permute-done.7.before = bf16[4,160,128]{2,1,0:T(8,128)(2,1)S(1)} collective-permute-done((bf16[4,160,128]{2,1,0:T(8,128)(2,1)S(1)}, bf16[4,160,128]{2,1,0:T(8,128)(2,1)S(1)}, u32[]{:S(2)}, u32[]{:S(2)}) %collective-permute-start.7) | collective-permute-done | bytes 163872 | tf_op jit(solution)/shard_map/ppermute | solution.py:237
  27.4 0.5 %near3.1.refs_6_.before.here = bf16[4,160,128]{2,1,0:T(8,128)(2,1)S(1)} custom-call(bf16[4,160,800]{2,1,0:T(8,128)(2,1)S(1)} %pack.3.packed.refs_0_, s32[6,12]{1,0:T(8,128)S(1)} %table.1.refs_1_, bf16[4,160,128]{2,1,0:T(8,128)(2,1)S(1)} %collective-permute-done.7.before, bf16[4,160,128]{2,1,0:T(8,128)(2,1)S(1)} %near2.1.before.here.refs_0_, ...), custom_call_target="tpu_custom_call" | custom-call | bytes 1024 | tf_op jit(solution)/shard_map/near3/pallas_call | solution.py:23
  28.0 0.1 collective-permute-start.8
  28.0 0.3 collective-permute-done.6.refs_4_
  28.3 0.6 %far3.1.after.here = bf16[4,160,128]{2,1,0:T(8,128)(2,1)S(1)} custom-call(bf16[4,160,800]{2,1,0:T(8,128)(2,1)S(1)} %pack.4.refs_0_.packed, s32[6,12]{1,0:T(8,128)S(1)} %table.1.refs_1_, bf16[4,160,128]{2,1,0:T(8,128)(2,1)S(1)} %middle2.1.here.after.refs_2_.refs_0_, bf16[4,160,128]{2,1,0:T(8,128)(2,1)S(1)} %far2.1.refs_6_.after.refs_3_.refs_0_, ...), custom_call_target="tpu_custom_call" | custom-call | bytes 1024 | tf_op jit(solution)/shard_map/far3/pallas_call | solution.py:23
  28.9 0.3 collective-permute-start.10
  29.2 0.6 %middle3.1.here.before.after = bf16[4,160,128]{2,1,0:T(8,128)(2,1)S(1)} custom-call(bf16[4,160,800]{2,1,0:T(8,128)(2,1)S(1)} %pack.5.packed, s32[6,12]{1,0:T(8,128)S(1)} %table.1.refs_1_, bf16[4,160,128]{2,1,0:T(8,128)(2,1)S(1)} %near2.1.before.here.refs_0_, bf16[4,160,128]{2,1,0:T(8,128)(2,1)S(1)} %middle2.1.here.after.refs_2_.refs_0_, ...), custom_call_target="tpu_custom_call" | custom-call | bytes 1024 | tf_op jit(solution)/shard_map/middle3/pallas_call | solution.py:23
  29.8 0.6 %middle4.1.refs_1_.middle = bf16[4,160,128]{2,1,0:T(8,128)(2,1)S(1)} custom-call(bf16[4,160,800]{2,1,0:T(8,128)(2,1)S(1)} %pack.5.packed, s32[6,12]{1,0:T(8,128)S(1)} %table.1.refs_1_, bf16[4,160,128]{2,1,0:T(8,128)(2,1)S(1)} %near3.1.refs_6_.before.here, bf16[4,160,128]{2,1,0:T(8,128)(2,1)S(1)} %middle3.1.here.before.after, ...), custom_call_target="tpu_custom_call" | custom-call | bytes 1024 | tf_op jit(solution)/shard_map/middle4/pallas_call | solution.py:23
  30.4 0.5 %collective-permute-done.8.after = bf16[4,160,128]{2,1,0:T(8,128)(2,1)S(1)} collective-permute-done((bf16[4,160,128]{2,1,0:T(8,128)(2,1)S(1)}, bf16[4,160,128]{2,1,0:T(8,128)(2,1)S(1)}, u32[]{:S(2)}, u32[]{:S(2)}) %collective-permute-start.8) | collective-permute-done | bytes 163872 | tf_op jit(solution)/shard_map/ppermute | solution.py:237
  30.9 0.6 %far4.1 = bf16[6,160,128]{2,1,0:T(8,128)(2,1)S(1)} custom-call(bf16[4,160,800]{2,1,0:T(8,128)(2,1)S(1)} %pack.4.refs_0_.packed, s32[6,12]{1,0:T(8,128)S(1)} %table.1.refs_1_, bf16[4,160,128]{2,1,0:T(8,128)(2,1)S(1)} %middle3.1.here.before.after, bf16[4,160,128]{2,1,0:T(8,128)(2,1)S(1)} %far3.1.after.here, ...), custom_call_target="tpu_custom_call" | custom-call | bytes 1024 | tf_op jit(solution)/shard_map/far4/pallas_call | solution.py:23
  31.5 3.3 %collective-permute-start.9 = (bf16[6,160,128]{2,1,0:T(8,128)(2,1)S(1)}, bf16[6,160,128]{2,1,0:T(8,128)(2,1)S(1)}, u32[]{:S(2)}, u32[]{:S(2)}) collective-permute-start(bf16[6,160,128]{2,1,0:T(8,128)(2,1)S(1)} %far4.1), channel_id=1, source_target_pairs={{0,1},{1,0},{2,3},{3,2},{4,5},{5,4},{6,7},{7,6},{8,9},{9,8},{10,11... | collective-permute-start | bytes 737288 | tf_op jit(solution)/shard_map/ppermute | solution.py:247
  34.7 1.9 %collective-permute-done.10.before = bf16[4,160,128]{2,1,0:T(8,128)(2,1)S(1)} collective-permute-done((bf16[4,160,128]{2,1,0:T(8,128)(2,1)S(1)}, bf16[4,160,128]{2,1,0:T(8,128)(2,1)S(1)}, u32[]{:S(2)}, u32[]{:S(2)}) %collective-permute-start.10) | collective-permute-done | bytes 163872 | tf_op jit(solution)/shard_map/ppermute | solution.py:237
  36.6 0.5 %near4.1.near = bf16[4,160,128]{2,1,0:T(8,128)(2,1)S(1)} custom-call(bf16[4,160,800]{2,1,0:T(8,128)(2,1)S(1)} %pack.3.packed.refs_0_, s32[6,12]{1,0:T(8,128)S(1)} %table.1.refs_1_, bf16[4,160,128]{2,1,0:T(8,128)(2,1)S(1)} %collective-permute-done.10.before, bf16[4,160,128]{2,1,0:T(8,128)(2,1)S(1)} %near3.1.refs_6_.before.here, ...), custom_call_target="tpu_custom_call" | custom-call | flops 20000000000 | bytes 1024 | tf_op jit(solution)/shard_map/near4/pallas_call | solution.py:23
  37.2 0.7 %own.1.refs_1_ = bf16[6,160,256]{2,1,0:T(8,128)(2,1)} custom-call(bf16[4,160,128]{2,1,0:T(8,128)(2,1)S(1)} %near4.1.near, bf16[4,160,128]{2,1,0:T(8,128)(2,1)S(1)} %middle4.1.refs_1_.middle), custom_call_target="tpu_custom_call" | custom-call | bytes 1024 | tf_op jit(solution)/shard_map/own/pallas_call | solution.py:23
  37.9 2.6 %collective-permute-done.9.refs_0_ = bf16[6,160,128]{2,1,0:T(8,128)(2,1)S(1)} collective-permute-done((bf16[6,160,128]{2,1,0:T(8,128)(2,1)S(1)}, bf16[6,160,128]{2,1,0:T(8,128)(2,1)S(1)}, u32[]{:S(2)}, u32[]{:S(2)}) %collective-permute-start.9) | collective-permute-done | bytes 245792 | tf_op jit(solution)/shard_map/ppermute | solution.py:247
  40.5 0.7 %others.1 = bf16[6,160,256]{2,1,0:T(8,128)(2,1)} custom-call(bf16[6,160,128]{2,1,0:T(8,128)(2,1)S(1)} %collective-permute-done.9.refs_0_, bf16[6,160,256]{2,1,0:T(8,128)(2,1)} %own.1.refs_1_), custom_call_target="tpu_custom_call", output_to_operand_aliasing={{}: (1, {})} | custom-call | bytes 1024 | tf_op jit(solution)/shard_map/others/pallas_call | solution.py:23
  (2 shorter events, 0.0 us)
Async XLA Ops:
  0.0 11.8 %slice-start = ((s8[4915200]{0:T(1024)(128)(4,1)}), s8[4194304]{0:T(1024)(128)(4,1)S(1)}, s32[]{:S(2)}) async-start(s8[4915200]{0:T(1024)(128)(4,1)} %bitcast.1), calls=%async_computation | async-start | bytes 8388608
  0.0 11.8 %slice-start.1 = ((s8[4915200]{0:T(1024)(128)(4,1)}), s8[720896]{0:T(1024)(128)(4,1)S(1)}, s32[]{:S(2)}) async-start(s8[4915200]{0:T(1024)(128)(4,1)} %bitcast.1), calls=%async_computation.1 | async-start | bytes 1441792
  1.5 8.5 %collective-permute-start.1 = (bf16[2,160,128]{2,1,0:T(8,128)(2,1)S(1)}, bf16[2,160,128]{2,1,0:T(8,128)(2,1)S(1)}, u32[]{:S(2)}, u32[]{:S(2)}) collective-permute-start(bf16[2,160,128]{2,1,0:T(8,128)(2,1)S(1)} %get-tuple-element.20), channel_id=1, source_target_pairs={{0,1},{1,0},{2,3},{3,2},{4,5},{5,4},{6,7},{7,6},{8,9},{9,8},{10,11... | collective-permute-start | bytes 245768 | tf_op jit(solution)/shard_map/ppermute | solution.py:247
  4.8 8.5 %collective-permute-start = (bf16[4,160,128]{2,1,0:T(8,128)(2,1)S(1)}, bf16[4,160,128]{2,1,0:T(8,128)(2,1)S(1)}, u32[]{:S(2)}, u32[]{:S(2)}) collective-permute-start(bf16[4,160,128]{2,1,0:T(8,128)(2,1)S(1)} %rotate_out.1.leaving), channel_id=1, source_target_pairs={{0,31},{1,2},{2,1},{3,4},{4,3},{5,6},{6,5},{7,8},{8,7},{9,10},{10,... | collective-permute-start | bytes 491528 | tf_op jit(solution)/shard_map/ppermute | solution.py:237
  8.8 7.6 %collective-permute-start.3 = (bf16[4,160,128]{2,1,0:T(8,128)(2,1)S(1)}, bf16[4,160,128]{2,1,0:T(8,128)(2,1)S(1)}, u32[]{:S(2)}, u32[]{:S(2)}) collective-permute-start(bf16[4,160,128]{2,1,0:T(8,128)(2,1)S(1)} %get-tuple-element.18.refs_2_.here.before.refs_5_), channel_id=1, source_target_pairs={{0,30},{1,3},{2,0},{3,5},{4,2},{5,7},{6,4},{7,9},{8,6},{9,11},{10,... | collective-permute-start | bytes 491528 | tf_op jit(solution)/shard_map/ppermute | solution.py:237
  10.0 6.7 %collective-permute-start.2 = (bf16[4,160,128]{2,1,0:T(8,128)(2,1)S(1)}, bf16[4,160,128]{2,1,0:T(8,128)(2,1)S(1)}, u32[]{:S(2)}, u32[]{:S(2)}) collective-permute-start(bf16[4,160,128]{2,1,0:T(8,128)(2,1)S(1)} %get-tuple-element.22), channel_id=1, source_target_pairs={{0,1},{1,0},{2,3},{3,2},{4,5},{5,4},{6,7},{7,6},{8,9},{9,8},{10,11... | collective-permute-start | bytes 491528 | tf_op jit(solution)/shard_map/ppermute | solution.py:247
  13.8 5.1 %collective-permute-start.5 = (bf16[4,160,128]{2,1,0:T(8,128)(2,1)S(1)}, bf16[4,160,128]{2,1,0:T(8,128)(2,1)S(1)}, u32[]{:S(2)}, u32[]{:S(2)}) collective-permute-start(bf16[4,160,128]{2,1,0:T(8,128)(2,1)S(1)} %near1.1.refs_1_.refs_5_.refs_3_.before.refs_0_), channel_id=1, source_target_pairs={{0,30},{1,3},{2,0},{3,5},{4,2},{5,7},{6,4},{7,9},{8,6},{9,11},{10,... | collective-permute-start | bytes 491528 | tf_op jit(solution)/shard_map/ppermute | solution.py:237
  17.3 7.6 %collective-permute-start.4 = (bf16[4,160,128]{2,1,0:T(8,128)(2,1)S(1)}, bf16[4,160,128]{2,1,0:T(8,128)(2,1)S(1)}, u32[]{:S(2)}, u32[]{:S(2)}) collective-permute-start(bf16[4,160,128]{2,1,0:T(8,128)(2,1)S(1)} %far1.1.refs_1_.here.after.refs_5_), channel_id=1, source_target_pairs={{0,2},{1,31},{2,4},{3,1},{4,6},{5,3},{6,8},{7,5},{8,10},{9,7},{10,... | collective-permute-start | bytes 491528 | tf_op jit(solution)/shard_map/ppermute | solution.py:237
  19.6 7.9 %collective-permute-start.7 = (bf16[4,160,128]{2,1,0:T(8,128)(2,1)S(1)}, bf16[4,160,128]{2,1,0:T(8,128)(2,1)S(1)}, u32[]{:S(2)}, u32[]{:S(2)}) collective-permute-start(bf16[4,160,128]{2,1,0:T(8,128)(2,1)S(1)} %far2.1.refs_6_.after.refs_3_.refs_0_), channel_id=1, source_target_pairs={{0,2},{1,31},{2,4},{3,1},{4,6},{5,3},{6,8},{7,5},{8,10},{9,7},{10,... | collective-permute-start | bytes 491528 | tf_op jit(solution)/shard_map/ppermute | solution.py:237
  25.4 2.9 %collective-permute-start.6 = (bf16[4,160,128]{2,1,0:T(8,128)(2,1)S(1)}, bf16[4,160,128]{2,1,0:T(8,128)(2,1)S(1)}, u32[]{:S(2)}, u32[]{:S(2)}) collective-permute-start(bf16[4,160,128]{2,1,0:T(8,128)(2,1)S(1)} %near2.1.before.here.refs_0_), channel_id=1, source_target_pairs={{0,30},{1,3},{2,0},{3,5},{4,2},{5,7},{6,4},{7,9},{8,6},{9,11},{10,... | collective-permute-start | bytes 491528 | tf_op jit(solution)/shard_map/ppermute | solution.py:237
  28.0 2.9 %collective-permute-start.8 = (bf16[4,160,128]{2,1,0:T(8,128)(2,1)S(1)}, bf16[4,160,128]{2,1,0:T(8,128)(2,1)S(1)}, u32[]{:S(2)}, u32[]{:S(2)}) collective-permute-start(bf16[4,160,128]{2,1,0:T(8,128)(2,1)S(1)} %near3.1.refs_6_.before.here), channel_id=1, source_target_pairs={{0,30},{1,3},{2,0},{3,5},{4,2},{5,7},{6,4},{7,9},{8,6},{9,11},{10,... | collective-permute-start | bytes 491528 | tf_op jit(solution)/shard_map/ppermute | solution.py:237
  28.9 7.7 %collective-permute-start.10 = (bf16[4,160,128]{2,1,0:T(8,128)(2,1)S(1)}, bf16[4,160,128]{2,1,0:T(8,128)(2,1)S(1)}, u32[]{:S(2)}, u32[]{:S(2)}) collective-permute-start(bf16[4,160,128]{2,1,0:T(8,128)(2,1)S(1)} %far3.1.after.here), channel_id=1, source_target_pairs={{0,2},{1,31},{2,4},{3,1},{4,6},{5,3},{6,8},{7,5},{8,10},{9,7},{10,... | collective-permute-start | bytes 491528 | tf_op jit(solution)/shard_map/ppermute | solution.py:237
  31.5 9.0 %collective-permute-start.9 = (bf16[6,160,128]{2,1,0:T(8,128)(2,1)S(1)}, bf16[6,160,128]{2,1,0:T(8,128)(2,1)S(1)}, u32[]{:S(2)}, u32[]{:S(2)}) collective-permute-start(bf16[6,160,128]{2,1,0:T(8,128)(2,1)S(1)} %far4.1), channel_id=1, source_target_pairs={{0,1},{1,0},{2,3},{3,2},{4,5},{5,4},{6,7},{7,6},{8,9},{9,8},{10,11... | collective-permute-start | bytes 737288 | tf_op jit(solution)/shard_map/ppermute | solution.py:247

commit v5 on v4

--- a/solution.py
+++ b/solution.py
@@ -145,8 +145,9 @@
 
 
 def level_kernel(first, factor, with_prev, packed, table, before, here, after, *refs):
-    refs, out, window = list(refs[:-2]), refs[-2], refs[-1]
+    refs, window = list(refs[:-1]), refs[-1]
     previous = refs.pop(0) if with_prev else None
+    out = refs[0]
     width, rows, lanes = here.shape
     for g, group in enumerate((before, here, after)):
         window[g * width : (g + 1) * width] = group[...]
@@ -161,9 +162,9 @@
         if with_prev:
             value = value - previous[e].astype(jnp.float32)
         out[e] = value.astype(jnp.bfloat16)
-    if refs:
-        share = out.shape[0] - width
-        out[width:] = refs[0][pl.ds(choose(flipped(2), 0, width - share), share)]
+    if len(refs) > 1:
+        share = refs[1].shape[0]
+        refs[1][...] = out[pl.ds(choose(flipped(2), 0, width - share), share)]
 
 
 def scatter_kernel(shards, *refs):
@@ -189,21 +190,22 @@
         copy.wait()
 
 
-def rows_copies(k, near, half, out, sems):
-    flip, share, width = flipped(2), half.shape[0], near.shape[0]
-    return [
-        place(2, k, choose(flip, share, 0), near, out, sems.at[0]),
-        place(2, k, choose(flip, 0, width), half, out, sems.at[1]),
-    ]
-
-
-def own_kernel(near, middle, out, sems):
-    share = out.shape[0] - near.shape[0]
-    run(rows_copies(0, near, middle.at[pl.ds(choose(flipped(2), share, 0), share)], out, sems))
-
-
-def others_kernel(width, part, out, sems):
-    run(rows_copies(1, part.at[:width], part.at[width:], out, sems))
+def near_copy(k, near, out, sem):
+    return place(2, k, choose(flipped(2), out.shape[0] - near.shape[0], 0), near, out, sem)
+
+
+def half_copy(k, half, out, sem):
+    return place(2, k, choose(flipped(2), 0, out.shape[0] - half.shape[0]), half, out, sem)
+
+
+def own_kernel(near, middle, half, out, sems):
+    share = half.shape[0]
+    kept = middle.at[pl.ds(choose(flipped(2), share, 0), share)]
+    run([near_copy(0, near, out, sems.at[0]), half_copy(0, kept, out, sems.at[1]), half_copy(1, half, out, sems.at[2])])
+
+
+def others_kernel(far, out, sem):
+    run([near_copy(1, far, out, sem)])
 
 
 def join_kernel(shards, *refs):
@@ -263,19 +265,16 @@
         )[0]
         near_halo = shifted(leaving, -1, across=True)
         kept = call(
-            functools.partial(rotate_kernel, shards, width, 0),
+            functools.partial(without, functools.partial(rotate_kernel, shards, width, 0), 3),
             [group, half],
-            [VMEM] * 3,
+            [VMEM] * 3 + [ANY],
             held,
             weights,
             limits,
+            leaving,
             name="rotate_in",
         )
         far_halo = to_far_of_neighbor(kept[0])
-        middle, leaving = call(
-            middle_kernel, [group] * 2, [VMEM] * 3, kept[1], arrived_half, leaving, name="gather"
-        )
-        far = swapped([leaving])[0]
     else:
         arrived = swapped(parts)
         kept = call(
@@ -302,8 +301,21 @@
         )[0]
 
     packed = {0: pack(0, table)}
+    packed[2] = pack(2, packed[0])
+    packed[1] = pack(1, packed[2])
     if pair:
         near = kept[0]
+        middle, leaving = call(
+            functools.partial(without, middle_kernel, 3),
+            [group] * 2,
+            [VMEM] * 3 + [ANY],
+            kept[1],
+            arrived_half,
+            leaving,
+            packed[1],
+            name="gather",
+        )
+        far = swapped([leaving])[0]
     else:
         near, middle, far = call(
             functools.partial(without, functools.partial(gather_kernel, shards), shards),
@@ -311,70 +323,83 @@
             [VMEM] * shards + [ANY],
             *kept,
             *arrived,
-            packed[0],
+            packed[1],
             scratch=[whole],
             name="gather",
         )
         near_halo, far_halo = to_near_of_neighbor(far), to_far_of_neighbor(near)
 
-    def level(g, m, before, here, after, previous, leaving=None, behind=None, flops=0):
+    def level(g, m, before, here, after, previous, split=False, behind=None, flops=0):
         body = functools.partial(level_kernel, g * width, 1.0 if m == 1 else 2.0, previous is not None)
-        args = [packed[g], table, before, here, after] + [x for x in (previous, leaving) if x is not None]
+        args = [packed[g], table, before, here, after] + ([] if previous is None else [previous])
         specs = [VMEM] * len(args)
         if behind is not None:
             body = functools.partial(without, body, len(args))
             args, specs = args + [behind], specs + [ANY]
-        return call(
+        outs = call(
             body,
-            [group if leaving is None else part],
+            [group] + [half] * split,
             specs,
             *args,
             scratch=[pltpu.VMEM((3 * width, rows, lanes), jnp.bfloat16)],
             flops=flops,
             name=("near", "middle", "far")[g] + str(m),
-        )[0]
+        )
+        return outs if split else outs[0]
 
     older = (None, None, None)
     for m in range(1, DEG + 1):
         last = m == DEG
-        if last:
-            new_middle = level(1, m, near, middle, far, older[1])
+        behind = half_arrived = None
+        if m > 2:
+            new_middle = behind = level(1, m, near, middle, far, older[1], split=pair and last)
+            if pair and last:
+                new_middle, half_leaving = new_middle
+                behind, half_arrived = None, swapped([half_leaving])[0]
         if m % 2:
-            new_near = level(0, m, near_halo, near, middle, older[0])
+            new_near = level(0, m, near_halo, near, middle, older[0], behind=behind)
             next_far_halo = to_far_of_neighbor(new_near)
-            if m == 1:
-                packed[2] = pack(2, new_near)
             new_far = level(2, m, middle, far, far_halo, older[2], behind=new_near)
             next_near_halo = to_near_of_neighbor(new_far)
         else:
-            new_far = level(2, m, middle, far, far_halo, older[2], new_middle if last and pair else None)
+            new_far = level(2, m, middle, far, far_halo, older[2], behind=behind)
+            if m == 2:
+                new_middle = level(1, m, near, middle, far, older[1], behind=new_far)
             if last and pair:
                 arrived = swapped([new_far])[0]
             else:
                 next_near_halo = to_near_of_neighbor(new_far)
-            new_near = level(0, m, near_halo, near, middle, older[0], behind=None if last else new_far, flops=LONG * last)
+            behind = half_arrived if last else new_middle
+            new_near = level(0, m, near_halo, near, middle, older[0], behind=behind, flops=LONG * last)
             if not last:
                 next_far_halo = to_far_of_neighbor(new_near)
         if m == 1:
-            packed[1] = pack(1, new_far)
+            new_middle = level(1, m, near, middle, far, older[1])
         if not last:
-            new_middle = level(1, m, near, middle, far, older[1])
             near_halo, far_halo = next_near_halo, next_far_halo
         older, (near, middle, far) = (near, middle, far), (new_near, new_middle, new_far)
 
     whole_out = [bf16(*orbitals.shape)]
     if pair:
         out = call(
-            own_kernel, whole_out, [VMEM] * 2, near, middle, out_specs=[HBM], scratch=[dma((2,))], name="own"
+            own_kernel,
+            whole_out,
+            [VMEM] * 3,
+            near,
+            middle,
+            half_arrived,
+            out_specs=[HBM],
+            scratch=[dma((3,))],
+            name="own",
         )[0]
         return call(
-            functools.partial(without, functools.partial(others_kernel, width), 1),
+            functools.partial(without, others_kernel, 1),
             whole_out,
             [VMEM, HBM],
             arrived,
             out,
             out_specs=[HBM],
-            scratch=[dma((2,))],
+            scratch=[dma],
             aliases={1: 0},
             name="others",
         )[0]

time: 41.3 us -> 40.4 us (0.978)
  waiting for transfers between devices: 14 us -> 13.3 us
    ppermute x8, waiting for transfers between devices: 11.1 us -> 9.68 us  [shifted(): return lax.ppermute(x, ('elem', 'state'), moves)]
    ppermute x3 -> x4, waiting for transfers between devices: 2.9 us -> 3.6 us  [swapped(): lax.ppermute(x, 'state', [(i, (i + k + 1) % shards) for i in range(shards)])]
    ppermute x3 -> x4, starting transfers between devices: 8 us -> 7.86 us  [swapped(): lax.ppermute(x, 'state', [(i, (i + k + 1) % shards) for i in range(shards)])]
  transfers between devices with their start and end apart: 11 -> 12, of which waited for: 9 -> 9; matrix products, arithmetic and copies ran while one was open for 0% -> 0% of each run, Pallas kernels for 22% -> 23%
where the time goes in v5:
time: 40.4 us; the launch traced here: 40.3 us
  starting transfers between devices  15.5 us (38%)
  waiting for transfers between devices  13.3 us (33%)
  Pallas kernels  11.4 us (28%)
    pallas_call x22, Pallas kernels, call(): pl.pallas_call(kernel, out_shape=outs, in_specs=ins, out_specs=out_specs...  11.4 us
    ppermute x8, waiting for transfers between devices, shifted(): return lax.ppermute(x, ('elem', 'state'), moves)  9.68 us
    ppermute x4, starting transfers between devices, swapped(): lax.ppermute(x, 'state', [(i, (i + k + 1) % shards) for i in range(shards)])  7.86 us
    ppermute x8, starting transfers between devices, shifted(): return lax.ppermute(x, ('elem', 'state'), moves)  7.61 us
    ppermute x4, waiting for transfers between devices, swapped(): lax.ppermute(x, 'state', [(i, (i + k + 1) % shards) for i in range(shards)])  3.6 us
  transfers between devices with their start and end apart: 12, of which 9 were waited for; matrix products, arithmetic and copies ran while one was open for 0% of the time, Pallas kernels for 23%

profile of v5, /device:TPU:0, one launch (start us, length us, event | category | flops | bytes accessed | tf_op | source)
XLA Modules:
  0.0 40.3 jit_solution(11219280919636074128)
XLA Ops:
  0.0 0.0 slice-start
  0.0 0.0 slice-start.1
  0.0 1.5 %fetch.1 = (bf16[2,160,128]{2,1,0:T(8,128)(2,1)S(1)}, bf16[6,160,256]{2,1,0:T(8,128)(2,1)S(1)}, bf16[256,256]{1,0:T(8,128)(2,1)S(1)}, s32[12]{0:T(128)S(1)}, s32[5,12]{1,0:T(8,128)S(1)}) custom-call(bf16[6,160,256]{2,1,0:T(8,128)(2,1)} %orbitals.1, bf16[256,256]{1,0:T(8,128)(2,1)} %rotation.1, s32[12]{0:T(128)} %counts.1, s32[5,12]{1,0:T(8,128)} %bitcast.3), custom_call_target="tpu_custom_call" | custom-call | flops 20000000000 | bytes 1024 | tf_op jit(solution)/shard_map/fetch/pallas_call | solution.py:23
  1.5 3.0 %collective-permute-start = (bf16[2,160,128]{2,1,0:T(8,128)(2,1)S(1)}, bf16[2,160,128]{2,1,0:T(8,128)(2,1)S(1)}, u32[]{:S(2)}, u32[]{:S(2)}) collective-permute-start(bf16[2,160,128]{2,1,0:T(8,128)(2,1)S(1)} %get-tuple-element.22), channel_id=1, source_target_pairs={{0,1},{1,0},{2,3},{3,2},{4,5},{5,4},{6,7},{7,6},{8,9},{9,8},{10,11... | collective-permute-start | bytes 245768 | tf_op jit(solution)/shard_map/ppermute | solution.py:249
  4.5 0.3 rotate_out.1.refs_3_.refs_2_
  4.8 3.7 %collective-permute-start.3 = (bf16[4,160,128]{2,1,0:T(8,128)(2,1)S(1)}, bf16[4,160,128]{2,1,0:T(8,128)(2,1)S(1)}, u32[]{:S(2)}, u32[]{:S(2)}) collective-permute-start(bf16[4,160,128]{2,1,0:T(8,128)(2,1)S(1)} %rotate_out.1.refs_3_.refs_2_), channel_id=1, source_target_pairs={{0,31},{1,2},{2,1},{3,4},{4,3},{5,6},{6,5},{7,8},{8,7},{9,10},{10,... | collective-permute-start | bytes 491528 | tf_op jit(solution)/shard_map/ppermute | solution.py:239
  8.5 0.3 rotate_in.1
  8.8 1.2 %collective-permute-start.2 = (bf16[4,160,128]{2,1,0:T(8,128)(2,1)S(1)}, bf16[4,160,128]{2,1,0:T(8,128)(2,1)S(1)}, u32[]{:S(2)}, u32[]{:S(2)}) collective-permute-start(bf16[4,160,128]{2,1,0:T(8,128)(2,1)S(1)} %get-tuple-element.20.refs_2_.here.before.refs_5_), channel_id=1, source_target_pairs={{0,30},{1,3},{2,0},{3,5},{4,2},{5,7},{6,4},{7,9},{8,6},{9,11},{10,... | collective-permute-start | bytes 491528 | tf_op jit(solution)/shard_map/ppermute | solution.py:239
  10.0 0.1 table.1.refs_1_
  10.0 0.0 slice-done
  10.0 0.0 slice-done.1
  10.1 0.3 pack.3.refs_1_.packed.refs_0_
  10.3 0.3 pack.4.refs_1_.refs_0_.packed
  10.6 0.3 pack.5.refs_3_.packed.refs_0_
  10.9 0.0 collective-permute-done.refs_1_
  11.0 0.7 %collective-permute-start.1 = (bf16[4,160,128]{2,1,0:T(8,128)(2,1)S(1)}, bf16[4,160,128]{2,1,0:T(8,128)(2,1)S(1)}, u32[]{:S(2)}, u32[]{:S(2)}) collective-permute-start(bf16[4,160,128]{2,1,0:T(8,128)(2,1)S(1)} %get-tuple-element.24), channel_id=1, source_target_pairs={{0,1},{1,0},{2,3},{3,2},{4,5},{5,4},{6,7},{7,6},{8,9},{9,8},{10,11... | collective-permute-start | bytes 491528 | tf_op jit(solution)/shard_map/ppermute | solution.py:249
  11.7 1.5 %collective-permute-done.3.before = bf16[4,160,128]{2,1,0:T(8,128)(2,1)S(1)} collective-permute-done((bf16[4,160,128]{2,1,0:T(8,128)(2,1)S(1)}, bf16[4,160,128]{2,1,0:T(8,128)(2,1)S(1)}, u32[]{:S(2)}, u32[]{:S(2)}) %collective-permute-start.3) | collective-permute-done | bytes 163872 | tf_op jit(solution)/shard_map/ppermute | solution.py:239
  13.2 0.5 %near1.1.refs_5_.refs_2_.refs_3_ = bf16[4,160,128]{2,1,0:T(8,128)(2,1)S(1)} custom-call(bf16[4,160,800]{2,1,0:T(8,128)(2,1)S(1)} %pack.3.refs_1_.packed.refs_0_, s32[6,12]{1,0:T(8,128)S(1)} %table.1.refs_1_, bf16[4,160,128]{2,1,0:T(8,128)(2,1)S(1)} %collective-permute-done.3.before, bf16[4,160,128]{2,1,0:T(8,128)(2,1)S(1)} %get-tuple-element.20.refs_2_.here.before.refs_5_, ...), custom_call_target="tpu_custom_call" | custom-call | bytes 1024 | tf_op jit(solution)/shard_map/near1/pallas_call | solution.py:23
  13.7 2.3 %collective-permute-start.5 = (bf16[4,160,128]{2,1,0:T(8,128)(2,1)S(1)}, bf16[4,160,128]{2,1,0:T(8,128)(2,1)S(1)}, u32[]{:S(2)}, u32[]{:S(2)}) collective-permute-start(bf16[4,160,128]{2,1,0:T(8,128)(2,1)S(1)} %near1.1.refs_5_.refs_2_.refs_3_), channel_id=1, source_target_pairs={{0,30},{1,3},{2,0},{3,5},{4,2},{5,7},{6,4},{7,9},{8,6},{9,11},{10,... | collective-permute-start | bytes 491528 | tf_op jit(solution)/shard_map/ppermute | solution.py:239
  16.0 0.0 collective-permute-done.2.refs_4_
  16.1 0.6 %collective-permute-done.1.refs_3_.after.refs_0_ = bf16[4,160,128]{2,1,0:T(8,128)(2,1)S(1)} collective-permute-done((bf16[4,160,128]{2,1,0:T(8,128)(2,1)S(1)}, bf16[4,160,128]{2,1,0:T(8,128)(2,1)S(1)}, u32[]{:S(2)}, u32[]{:S(2)}) %collective-permute-start.1) | collective-permute-done | bytes 163872 | tf_op jit(solution)/shard_map/ppermute | solution.py:249
  16.7 0.6 %far1.1.here.refs_4_.refs_5_ = bf16[4,160,128]{2,1,0:T(8,128)(2,1)S(1)} custom-call(bf16[4,160,800]{2,1,0:T(8,128)(2,1)S(1)} %pack.4.refs_1_.refs_0_.packed, s32[6,12]{1,0:T(8,128)S(1)} %table.1.refs_1_, bf16[4,160,128]{2,1,0:T(8,128)(2,1)S(1)} %get-tuple-element.23.after.refs_2_.here.refs_5_, ...), custom_call_target="tpu_custom_call" | custom-call | bytes 1024 | tf_op jit(solution)/shard_map/far1/pallas_call | solution.py:23
  17.3 0.1 collective-permute-start.4
  17.4 0.6 %middle1.1.before.refs_3_.refs_4_.refs_0_ = bf16[4,160,128]{2,1,0:T(8,128)(2,1)S(1)} custom-call(bf16[4,160,800]{2,1,0:T(8,128)(2,1)S(1)} %pack.5.refs_3_.packed.refs_0_, s32[6,12]{1,0:T(8,128)S(1)} %table.1.refs_1_, bf16[4,160,128]{2,1,0:T(8,128)(2,1)S(1)} %get-tuple-element.20.refs_2_.here.before.refs_5_, ...), custom_call_target="tpu_custom_call" | custom-call | bytes 1024 | tf_op jit(solution)/shard_map/middle1/pallas_call | solution.py:23
  17.9 0.9 %collective-permute-done.5.after = bf16[4,160,128]{2,1,0:T(8,128)(2,1)S(1)} collective-permute-done((bf16[4,160,128]{2,1,0:T(8,128)(2,1)S(1)}, bf16[4,160,128]{2,1,0:T(8,128)(2,1)S(1)}, u32[]{:S(2)}, u32[]{:S(2)}) %collective-permute-start.5) | collective-permute-done | bytes 163872 | tf_op jit(solution)/shard_map/ppermute | solution.py:239
  18.9 0.6 %far2.1.refs_6_.after.refs_3_.refs_0_ = bf16[4,160,128]{2,1,0:T(8,128)(2,1)S(1)} custom-call(bf16[4,160,800]{2,1,0:T(8,128)(2,1)S(1)} %pack.4.refs_1_.refs_0_.packed, s32[6,12]{1,0:T(8,128)S(1)} %table.1.refs_1_, bf16[4,160,128]{2,1,0:T(8,128)(2,1)S(1)} %middle1.1.before.refs_3_.refs_4_.refs_0_, bf16[4,160,128]{2,1,0:T(8,128)(2,1)S(1)} %far1.1.here.refs_4_.refs_5_, ...), custom_call_target="tpu_custom_call" | custom-call | bytes 1024 | tf_op jit(solution)/shard_map/far2/pallas_call | solution.py:23
  19.5 0.1 collective-permute-start.7
  19.6 0.6 %middle2.1.refs_6_.here.refs_4_.refs_2_.refs_0_ = bf16[4,160,128]{2,1,0:T(8,128)(2,1)S(1)} custom-call(bf16[4,160,800]{2,1,0:T(8,128)(2,1)S(1)} %pack.5.refs_3_.packed.refs_0_, s32[6,12]{1,0:T(8,128)S(1)} %table.1.refs_1_, bf16[4,160,128]{2,1,0:T(8,128)(2,1)S(1)} %near1.1.refs_5_.refs_2_.refs_3_, ...), custom_call_target="tpu_custom_call" | custom-call | bytes 1024 | tf_op jit(solution)/shard_map/middle2/pallas_call | solution.py:23
  20.2 4.7 %collective-permute-done.4.refs_2_ = bf16[4,160,128]{2,1,0:T(8,128)(2,1)S(1)} collective-permute-done((bf16[4,160,128]{2,1,0:T(8,128)(2,1)S(1)}, bf16[4,160,128]{2,1,0:T(8,128)(2,1)S(1)}, u32[]{:S(2)}, u32[]{:S(2)}) %collective-permute-start.4) | collective-permute-done | bytes 163872 | tf_op jit(solution)/shard_map/ppermute | solution.py:239
  24.9 0.5 %near2.1.before.refs_3_.refs_5_ = bf16[4,160,128]{2,1,0:T(8,128)(2,1)S(1)} custom-call(bf16[4,160,800]{2,1,0:T(8,128)(2,1)S(1)} %pack.3.refs_1_.packed.refs_0_, s32[6,12]{1,0:T(8,128)S(1)} %table.1.refs_1_, bf16[4,160,128]{2,1,0:T(8,128)(2,1)S(1)} %collective-permute-done.4.refs_2_, bf16[4,160,128]{2,1,0:T(8,128)(2,1)S(1)} %near1.1.refs_5_.refs_2_.refs_3_, ...), custom_call_target="tpu_custom_call" | custom-call | bytes 1024 | tf_op jit(solution)/shard_map/near2/pallas_call | solution.py:23
  25.4 0.1 collective-permute-start.6
  25.5 0.6 %middle3.1.refs_6_.before.here.refs_4_ = bf16[4,160,128]{2,1,0:T(8,128)(2,1)S(1)} custom-call(bf16[4,160,800]{2,1,0:T(8,128)(2,1)S(1)} %pack.5.refs_3_.packed.refs_0_, s32[6,12]{1,0:T(8,128)S(1)} %table.1.refs_1_, bf16[4,160,128]{2,1,0:T(8,128)(2,1)S(1)} %near2.1.before.refs_3_.refs_5_, bf16[4,160,128]{2,1,0:T(8,128)(2,1)S(1)} %middle2.1.refs_6_.here.refs_4_.refs_2_.refs_0_, ...), custom_call_target="tpu_custom_call" | custom-call | bytes 1024 | tf_op jit(solution)/shard_map/middle3/pallas_call | solution.py:23
  26.1 1.3 %collective-permute-done.7.refs_2_ = bf16[4,160,128]{2,1,0:T(8,128)(2,1)S(1)} collective-permute-done((bf16[4,160,128]{2,1,0:T(8,128)(2,1)S(1)}, bf16[4,160,128]{2,1,0:T(8,128)(2,1)S(1)}, u32[]{:S(2)}, u32[]{:S(2)}) %collective-permute-start.7) | collective-permute-done | bytes 163872 | tf_op jit(solution)/shard_map/ppermute | solution.py:239
  27.4 0.5 %near3.1.refs_6_.before.refs_3_ = bf16[4,160,128]{2,1,0:T(8,128)(2,1)S(1)} custom-call(bf16[4,160,800]{2,1,0:T(8,128)(2,1)S(1)} %pack.3.refs_1_.packed.refs_0_, s32[6,12]{1,0:T(8,128)S(1)} %table.1.refs_1_, bf16[4,160,128]{2,1,0:T(8,128)(2,1)S(1)} %collective-permute-done.7.refs_2_, bf16[4,160,128]{2,1,0:T(8,128)(2,1)S(1)} %near2.1.before.refs_3_.refs_5_, ...), custom_call_target="tpu_custom_call" | custom-call | bytes 1024 | tf_op jit(solution)/shard_map/near3/pallas_call | solution.py:23
  27.9 0.1 collective-permute-start.8
  28.0 0.4 collective-permute-done.6.refs_4_
  28.3 0.6 %far3.1.here.after = bf16[4,160,128]{2,1,0:T(8,128)(2,1)S(1)} custom-call(bf16[4,160,800]{2,1,0:T(8,128)(2,1)S(1)} %pack.4.refs_1_.refs_0_.packed, s32[6,12]{1,0:T(8,128)S(1)} %table.1.refs_1_, bf16[4,160,128]{2,1,0:T(8,128)(2,1)S(1)} %middle2.1.refs_6_.here.refs_4_.refs_2_.refs_0_, bf16[4,160,128]{2,1,0:T(8,128)(2,1)S(1)} %far2.1.refs_6_.after.refs_3_.refs_0_, ...), custom_call_target="tpu_custom_call" | custom-call | bytes 1024 | tf_op jit(solution)/shard_map/far3/pallas_call | solution.py:23
  28.9 0.2 collective-permute-start.10
  29.1 0.6 %middle4.1 = (bf16[4,160,128]{2,1,0:T(8,128)(2,1)S(1)}, bf16[2,160,128]{2,1,0:T(8,128)(2,1)S(1)}) custom-call(bf16[4,160,800]{2,1,0:T(8,128)(2,1)S(1)} %pack.5.refs_3_.packed.refs_0_, s32[6,12]{1,0:T(8,128)S(1)} %table.1.refs_1_, bf16[4,160,128]{2,1,0:T(8,128)(2,1)S(1)} %near3.1.refs_6_.before.refs_3_, ...), custom_call_target="tpu_custom_call" | custom-call | bytes 1024 | tf_op jit(solution)/shard_map/middle4/pallas_call | solution.py:23
  29.8 2.9 %collective-permute-start.11 = (bf16[2,160,128]{2,1,0:T(8,128)(2,1)S(1)}, bf16[2,160,128]{2,1,0:T(8,128)(2,1)S(1)}, u32[]{:S(2)}, u32[]{:S(2)}) collective-permute-start(bf16[2,160,128]{2,1,0:T(8,128)(2,1)S(1)} %get-tuple-element.25), channel_id=1, source_target_pairs={{0,1},{1,0},{2,3},{3,2},{4,5},{5,4},{6,7},{7,6},{8,9},{9,8},{10,11... | collective-permute-start | bytes 245768 | tf_op jit(solution)/shard_map/ppermute | solution.py:249
  32.6 0.0 collective-permute-done.8.after
  32.6 0.6 %far4.1 = bf16[4,160,128]{2,1,0:T(8,128)(2,1)S(1)} custom-call(bf16[4,160,800]{2,1,0:T(8,128)(2,1)S(1)} %pack.4.refs_1_.refs_0_.packed, s32[6,12]{1,0:T(8,128)S(1)} %table.1.refs_1_, bf16[4,160,128]{2,1,0:T(8,128)(2,1)S(1)} %middle3.1.refs_6_.before.here.refs_4_, bf16[4,160,128]{2,1,0:T(8,128)(2,1)S(1)} %far3.1.here.after, ...), custom_call_target="tpu_custom_call" | custom-call | bytes 1024 | tf_op jit(solution)/shard_map/far4/pallas_call | solution.py:23
  33.3 1.2 %collective-permute-start.9 = (bf16[4,160,128]{2,1,0:T(8,128)(2,1)S(1)}, bf16[4,160,128]{2,1,0:T(8,128)(2,1)S(1)}, u32[]{:S(2)}, u32[]{:S(2)}) collective-permute-start(bf16[4,160,128]{2,1,0:T(8,128)(2,1)S(1)} %far4.1), channel_id=1, source_target_pairs={{0,1},{1,0},{2,3},{3,2},{4,5},{5,4},{6,7},{7,6},{8,9},{9,8},{10,11... | collective-permute-start | bytes 491528 | tf_op jit(solution)/shard_map/ppermute | solution.py:249
  34.5 1.3 %collective-permute-done.11.refs_6_.half = bf16[2,160,128]{2,1,0:T(8,128)(2,1)S(1)} collective-permute-done((bf16[2,160,128]{2,1,0:T(8,128)(2,1)S(1)}, bf16[2,160,128]{2,1,0:T(8,128)(2,1)S(1)}, u32[]{:S(2)}, u32[]{:S(2)}) %collective-permute-start.11) | collective-permute-done | bytes 81952 | tf_op jit(solution)/shard_map/ppermute | solution.py:249
  35.7 0.9 %collective-permute-done.10.refs_2_ = bf16[4,160,128]{2,1,0:T(8,128)(2,1)S(1)} collective-permute-done((bf16[4,160,128]{2,1,0:T(8,128)(2,1)S(1)}, bf16[4,160,128]{2,1,0:T(8,128)(2,1)S(1)}, u32[]{:S(2)}, u32[]{:S(2)}) %collective-permute-start.10) | collective-permute-done | bytes 163872 | tf_op jit(solution)/shard_map/ppermute | solution.py:239
  36.6 0.5 %near4.1.near = bf16[4,160,128]{2,1,0:T(8,128)(2,1)S(1)} custom-call(bf16[4,160,800]{2,1,0:T(8,128)(2,1)S(1)} %pack.3.refs_1_.packed.refs_0_, s32[6,12]{1,0:T(8,128)S(1)} %table.1.refs_1_, bf16[4,160,128]{2,1,0:T(8,128)(2,1)S(1)} %collective-permute-done.10.refs_2_, bf16[4,160,128]{2,1,0:T(8,128)(2,1)S(1)} %near3.1.refs_6_.before.refs_3_, ...), custom_call_target="tpu_custom_call" | custom-call | flops 20000000000 | bytes 1024 | tf_op jit(solution)/shard_map/near4/pallas_call | solution.py:23
  37.2 0.8 %own.1.refs_1_ = bf16[6,160,256]{2,1,0:T(8,128)(2,1)} custom-call(bf16[4,160,128]{2,1,0:T(8,128)(2,1)S(1)} %near4.1.near, bf16[4,160,128]{2,1,0:T(8,128)(2,1)S(1)} %get-tuple-element.26.middle, bf16[2,160,128]{2,1,0:T(8,128)(2,1)S(1)} %collective-permute-done.11.refs_6_.half), custom_call_target="tpu_custom_call" | custom-call | bytes 1024 | tf_op jit(solution)/shard_map/own/pallas_call | solution.py:23
  38.0 1.7 %collective-permute-done.9.refs_0_ = bf16[4,160,128]{2,1,0:T(8,128)(2,1)S(1)} collective-permute-done((bf16[4,160,128]{2,1,0:T(8,128)(2,1)S(1)}, bf16[4,160,128]{2,1,0:T(8,128)(2,1)S(1)}, u32[]{:S(2)}, u32[]{:S(2)}) %collective-permute-start.9) | collective-permute-done | bytes 163872 | tf_op jit(solution)/shard_map/ppermute | solution.py:249
  39.6 0.7 %others.1 = bf16[6,160,256]{2,1,0:T(8,128)(2,1)} custom-call(bf16[4,160,128]{2,1,0:T(8,128)(2,1)S(1)} %collective-permute-done.9.refs_0_, bf16[6,160,256]{2,1,0:T(8,128)(2,1)} %own.1.refs_1_), custom_call_target="tpu_custom_call", output_to_operand_aliasing={{}: (1, {})} | custom-call | bytes 1024 | tf_op jit(solution)/shard_map/others/pallas_call | solution.py:23
  (2 shorter events, 0.0 us)
Async XLA Ops:
  0.0 10.0 %slice-start = ((s8[4915200]{0:T(1024)(128)(4,1)}), s8[4194304]{0:T(1024)(128)(4,1)S(1)}, s32[]{:S(2)}) async-start(s8[4915200]{0:T(1024)(128)(4,1)} %bitcast.1), calls=%async_computation | async-start | bytes 8388608
  0.0 10.0 %slice-start.1 = ((s8[4915200]{0:T(1024)(128)(4,1)}), s8[720896]{0:T(1024)(128)(4,1)S(1)}, s32[]{:S(2)}) async-start(s8[4915200]{0:T(1024)(128)(4,1)} %bitcast.1), calls=%async_computation.1 | async-start | bytes 1441792
  1.5 9.4 %collective-permute-start = (bf16[2,160,128]{2,1,0:T(8,128)(2,1)S(1)}, bf16[2,160,128]{2,1,0:T(8,128)(2,1)S(1)}, u32[]{:S(2)}, u32[]{:S(2)}) collective-permute-start(bf16[2,160,128]{2,1,0:T(8,128)(2,1)S(1)} %get-tuple-element.22), channel_id=1, source_target_pairs={{0,1},{1,0},{2,3},{3,2},{4,5},{5,4},{6,7},{7,6},{8,9},{9,8},{10,11... | collective-permute-start | bytes 245768 | tf_op jit(solution)/shard_map/ppermute | solution.py:249
  4.8 8.4 %collective-permute-start.3 = (bf16[4,160,128]{2,1,0:T(8,128)(2,1)S(1)}, bf16[4,160,128]{2,1,0:T(8,128)(2,1)S(1)}, u32[]{:S(2)}, u32[]{:S(2)}) collective-permute-start(bf16[4,160,128]{2,1,0:T(8,128)(2,1)S(1)} %rotate_out.1.refs_3_.refs_2_), channel_id=1, source_target_pairs={{0,31},{1,2},{2,1},{3,4},{4,3},{5,6},{6,5},{7,8},{8,7},{9,10},{10,... | collective-permute-start | bytes 491528 | tf_op jit(solution)/shard_map/ppermute | solution.py:239
  8.8 7.3 %collective-permute-start.2 = (bf16[4,160,128]{2,1,0:T(8,128)(2,1)S(1)}, bf16[4,160,128]{2,1,0:T(8,128)(2,1)S(1)}, u32[]{:S(2)}, u32[]{:S(2)}) collective-permute-start(bf16[4,160,128]{2,1,0:T(8,128)(2,1)S(1)} %get-tuple-element.20.refs_2_.here.before.refs_5_), channel_id=1, source_target_pairs={{0,30},{1,3},{2,0},{3,5},{4,2},{5,7},{6,4},{7,9},{8,6},{9,11},{10,... | collective-permute-start | bytes 491528 | tf_op jit(solution)/shard_map/ppermute | solution.py:239
  11.0 5.7 %collective-permute-start.1 = (bf16[4,160,128]{2,1,0:T(8,128)(2,1)S(1)}, bf16[4,160,128]{2,1,0:T(8,128)(2,1)S(1)}, u32[]{:S(2)}, u32[]{:S(2)}) collective-permute-start(bf16[4,160,128]{2,1,0:T(8,128)(2,1)S(1)} %get-tuple-element.24), channel_id=1, source_target_pairs={{0,1},{1,0},{2,3},{3,2},{4,5},{5,4},{6,7},{7,6},{8,9},{9,8},{10,11... | collective-permute-start | bytes 491528 | tf_op jit(solution)/shard_map/ppermute | solution.py:249
  13.7 5.1 %collective-permute-start.5 = (bf16[4,160,128]{2,1,0:T(8,128)(2,1)S(1)}, bf16[4,160,128]{2,1,0:T(8,128)(2,1)S(1)}, u32[]{:S(2)}, u32[]{:S(2)}) collective-permute-start(bf16[4,160,128]{2,1,0:T(8,128)(2,1)S(1)} %near1.1.refs_5_.refs_2_.refs_3_), channel_id=1, source_target_pairs={{0,30},{1,3},{2,0},{3,5},{4,2},{5,7},{6,4},{7,9},{8,6},{9,11},{10,... | collective-permute-start | bytes 491528 | tf_op jit(solution)/shard_map/ppermute | solution.py:239
  17.3 7.6 %collective-permute-start.4 = (bf16[4,160,128]{2,1,0:T(8,128)(2,1)S(1)}, bf16[4,160,128]{2,1,0:T(8,128)(2,1)S(1)}, u32[]{:S(2)}, u32[]{:S(2)}) collective-permute-start(bf16[4,160,128]{2,1,0:T(8,128)(2,1)S(1)} %far1.1.here.refs_4_.refs_5_), channel_id=1, source_target_pairs={{0,2},{1,31},{2,4},{3,1},{4,6},{5,3},{6,8},{7,5},{8,10},{9,7},{10,... | collective-permute-start | bytes 491528 | tf_op jit(solution)/shard_map/ppermute | solution.py:239
  19.5 7.9 %collective-permute-start.7 = (bf16[4,160,128]{2,1,0:T(8,128)(2,1)S(1)}, bf16[4,160,128]{2,1,0:T(8,128)(2,1)S(1)}, u32[]{:S(2)}, u32[]{:S(2)}) collective-permute-start(bf16[4,160,128]{2,1,0:T(8,128)(2,1)S(1)} %far2.1.refs_6_.after.refs_3_.refs_0_), channel_id=1, source_target_pairs={{0,2},{1,31},{2,4},{3,1},{4,6},{5,3},{6,8},{7,5},{8,10},{9,7},{10,... | collective-permute-start | bytes 491528 | tf_op jit(solution)/shard_map/ppermute | solution.py:239
  25.4 2.9 %collective-permute-start.6 = (bf16[4,160,128]{2,1,0:T(8,128)(2,1)S(1)}, bf16[4,160,128]{2,1,0:T(8,128)(2,1)S(1)}, u32[]{:S(2)}, u32[]{:S(2)}) collective-permute-start(bf16[4,160,128]{2,1,0:T(8,128)(2,1)S(1)} %near2.1.before.refs_3_.refs_5_), channel_id=1, source_target_pairs={{0,30},{1,3},{2,0},{3,5},{4,2},{5,7},{6,4},{7,9},{8,6},{9,11},{10,... | collective-permute-start | bytes 491528 | tf_op jit(solution)/shard_map/ppermute | solution.py:239
  27.9 4.7 %collective-permute-start.8 = (bf16[4,160,128]{2,1,0:T(8,128)(2,1)S(1)}, bf16[4,160,128]{2,1,0:T(8,128)(2,1)S(1)}, u32[]{:S(2)}, u32[]{:S(2)}) collective-permute-start(bf16[4,160,128]{2,1,0:T(8,128)(2,1)S(1)} %near3.1.refs_6_.before.refs_3_), channel_id=1, source_target_pairs={{0,30},{1,3},{2,0},{3,5},{4,2},{5,7},{6,4},{7,9},{8,6},{9,11},{10,... | collective-permute-start | bytes 491528 | tf_op jit(solution)/shard_map/ppermute | solution.py:239
  28.9 7.7 %collective-permute-start.10 = (bf16[4,160,128]{2,1,0:T(8,128)(2,1)S(1)}, bf16[4,160,128]{2,1,0:T(8,128)(2,1)S(1)}, u32[]{:S(2)}, u32[]{:S(2)}) collective-permute-start(bf16[4,160,128]{2,1,0:T(8,128)(2,1)S(1)} %far3.1.here.after), channel_id=1, source_target_pairs={{0,2},{1,31},{2,4},{3,1},{4,6},{5,3},{6,8},{7,5},{8,10},{9,7},{10,... | collective-permute-start | bytes 491528 | tf_op jit(solution)/shard_map/ppermute | solution.py:239
  29.8 6.0 %collective-permute-start.11 = (bf16[2,160,128]{2,1,0:T(8,128)(2,1)S(1)}, bf16[2,160,128]{2,1,0:T(8,128)(2,1)S(1)}, u32[]{:S(2)}, u32[]{:S(2)}) collective-permute-start(bf16[2,160,128]{2,1,0:T(8,128)(2,1)S(1)} %get-tuple-element.25), channel_id=1, source_target_pairs={{0,1},{1,0},{2,3},{3,2},{4,5},{5,4},{6,7},{7,6},{8,9},{9,8},{10,11... | collective-permute-start | bytes 245768 | tf_op jit(solution)/shard_map/ppermute | solution.py:249
  33.3 6.4 %collective-permute-start.9 = (bf16[4,160,128]{2,1,0:T(8,128)(2,1)S(1)}, bf16[4,160,128]{2,1,0:T(8,128)(2,1)S(1)}, u32[]{:S(2)}, u32[]{:S(2)}) collective-permute-start(bf16[4,160,128]{2,1,0:T(8,128)(2,1)S(1)} %far4.1), channel_id=1, source_target_pairs={{0,1},{1,0},{2,3},{3,2},{4,5},{5,4},{6,7},{7,6},{8,9},{9,8},{10,11... | collective-permute-start | bytes 491528 | tf_op jit(solution)/shard_map/ppermute | solution.py:249

commit v6 on v5

--- a/solution.py
+++ b/solution.py
@@ -37,8 +37,8 @@
     return jax.ShapeDtypeStruct(shape, jnp.bfloat16)
 
 
-def without(body, at, *refs):
-    body(*refs[:at], *refs[at + 1 :])
+def without(body, at, count, *refs):
+    body(*refs[:at], *refs[at + count :])
 
 
 def flipped(shards):
@@ -60,41 +60,35 @@
     return jnp.where(rows_below(count, rows, lanes), turned, 0.0).astype(jnp.bfloat16)
 
 
-def fetch_kernel(shards, reach, orbitals, rotation, counts, neighbors, *refs):
-    outs, (held, weights, limits, beside, scalars, sems) = refs[:-6], refs[-6:]
-    elems = orbitals.shape[0]
-    me, flip = lax.axis_index("state"), flipped(shards)
-    copies = [
-        pltpu.make_async_copy(source, target, sems.at[i])
-        for i, (source, target) in enumerate(
-            [(rotation, weights), (counts, scalars), (orbitals, held), (counts, limits), (neighbors, beside)]
-        )
-    ]
-    for copy in copies:
-        copy.start()
-    for copy in copies[:3]:
-        copy.wait()
-    first = reach if shards == 2 else 0
-    for k, out in enumerate(outs):
-        for at in range(out.shape[0]):
-            e = choose(flip, (first + at + elems - reach) % elems, first + at)
-            out[at] = turn(shards, k + 1, held[e], weights, scalars[me * elems + e])
-    for copy in copies[3:]:
-        copy.wait()
-
-
-def rotate_kernel(shards, reach, k, held, weights, limits, *outs):
+def rotate_kernel(shards, reach, k, first, held, weights, limits, *outs):
     me, flip = lax.axis_index("state"), flipped(shards)
     elems = held.shape[0]
     ends = limits[...]
     spots = [(out, e) for out in outs for e in range(out.shape[0])]
-    for spot, (out, at) in enumerate(spots):
+    for spot, (out, at) in enumerate(spots, first):
         e = choose(flip, (spot + elems - reach) % elems, spot)
         count = ends[spot]
         for shard in range(shards):
             here = (spot + elems - reach) % elems if shard == 1 and flip is not False else spot
             count = jnp.where(me == shard, ends[shard * elems + here], count)
         out[at] = turn(shards, k, held[e], weights, count)
+
+
+def fetch_kernel(shards, reach, orbitals, rotation, counts, neighbors, *refs):
+    outs, (held, weights, limits, beside, sems) = refs[:-5], refs[-5:]
+    copies = [
+        pltpu.make_async_copy(source, target, sems.at[i])
+        for i, (source, target) in enumerate(
+            [(rotation, weights), (counts, limits), (orbitals, held), (neighbors, beside)]
+        )
+    ]
+    for copy in copies:
+        copy.start()
+    for copy in copies[:3]:
+        copy.wait()
+    for k, out in enumerate(outs):
+        rotate_kernel(shards, reach, k + 1, reach if shards == 2 else 0, held, weights, limits, out)
+    copies[3].wait()
 
 
 def table_kernel(total, shards, reach, beside, limits, table):
@@ -112,8 +106,10 @@
         parts = [x[:, g * reach : (g + 1) * reach] for g in reversed(range(groups))]
         return choose(flip, jnp.concatenate(parts, axis=1), x)
 
-    table[:couplings] = mirrored(place)
-    table[couplings:] = mirrored(ends)
+    rows = jnp.concatenate([mirrored(place), mirrored(ends)], axis=0)
+    for e in range(elems):
+        for k in range(couplings + 1):
+            table[e, k] = jnp.full(table.shape[2:], rows[k, e], jnp.int32)
 
 
 def pack_kernel(shards, group, blocks, packed):
@@ -144,6 +140,21 @@
         group[...] = whole[g * width : (g + 1) * width]
 
 
+def hard():
+    return lax.rem(lax.axis_index("elem") + lax.axis_index("state"), 2)
+
+
+def level_if_kernel(which, instead, body, at, *refs):
+    if instead:
+        other, refs = refs[at], refs[:at] + refs[at + 1 :]
+
+        @pl.when(hard() != which)
+        def _():
+            refs[-2][...] = other[...]
+
+    pl.when(hard() == which)(functools.partial(body, *refs))
+
+
 def level_kernel(first, factor, with_prev, packed, table, before, here, after, *refs):
     refs, window = list(refs[:-1]), refs[-1]
     previous = refs.pop(0) if with_prev else None
@@ -151,13 +162,12 @@
     width, rows, lanes = here.shape
     for g, group in enumerate((before, here, after)):
         window[g * width : (g + 1) * width] = group[...]
-    places = table[...]
-    couplings = places.shape[0] - 1
+    couplings = table.shape[1] - 1
     for e in range(width):
-        at = [places[k, first + e] for k in range(couplings)]
+        *at, end = [table[first + e, k, 0, 0] for k in range(couplings + 1)]
         fields = [window[i, :FULL] for i in at] + [window[i, FULL:] for i in at]
         image = jnp.dot(packed[e], jnp.concatenate(fields, axis=0), preferred_element_type=jnp.float32)
-        image = jnp.where(rows_below(places[couplings, first + e], rows, lanes), image, 0.0)
+        image = jnp.where(rows_below(end, rows, lanes), image, 0.0)
         value = factor * (image - center_shift * here[e].astype(jnp.float32)) / half_span
         if with_prev:
             value = value - previous[e].astype(jnp.float32)
@@ -226,17 +236,19 @@
     group, part = bf16(width, rows, lanes), bf16(row_elems, rows, lanes)
     half = bf16(row_elems - width, rows, lanes)
     whole = pltpu.VMEM((elems, rows, lanes), jnp.bfloat16)
-    scalars = pltpu.SMEM(counts.shape, jnp.int32)
     dma = pltpu.SemaphoreType.DMA
     pair = shards == 2
 
-    def shifted(x, step, across=False):
+    def permuted(x, target):
         moves = []
         for i in range(ring):
             for j in range(shards):
-                to = (i + (-step if pair and j == 1 else step)) % ring
-                moves.append((i * shards + j, to * shards + (1 - j if across else j)))
+                to_i, to_j = target(i, j)
+                moves.append((i * shards + j, to_i % ring * shards + to_j))
         return lax.ppermute(x, ("elem", "state"), moves)
+
+    def shifted(x, step, across=False):
+        return permuted(x, lambda i, j: (i + (-step if pair and j == 1 else step), 1 - j if across else j))
 
     def to_far_of_neighbor(x):
         return shifted(x, -1)
@@ -254,18 +266,17 @@
         ([half] if pair else [part] * (shards - 1)) + [jax.ShapeDtypeStruct(x.shape, x.dtype) for x in inputs],
         [HBM] * len(inputs),
         *inputs,
-        scratch=[scalars, dma((5,))],
-        flops=LONG,
+        scratch=[dma((4,))],
         name="fetch",
     )
     if pair:
         arrived_half = swapped(parts)[0]
         leaving = call(
-            functools.partial(rotate_kernel, shards, width, 1), [group], [VMEM] * 3, held, weights, limits, name="rotate_out"
+            functools.partial(rotate_kernel, shards, width, 1, 0), [group], [VMEM] * 3, held, weights, limits, flops=LONG, name="rotate_out"
         )[0]
         near_halo = shifted(leaving, -1, across=True)
         kept = call(
-            functools.partial(without, functools.partial(rotate_kernel, shards, width, 0), 3),
+            functools.partial(without, functools.partial(rotate_kernel, shards, width, 0, 0), 3, 1),
             [group, half],
             [VMEM] * 3 + [ANY],
             held,
@@ -278,11 +289,11 @@
     else:
         arrived = swapped(parts)
         kept = call(
-            functools.partial(rotate_kernel, shards, width, 0), [part], [VMEM] * 3, held, weights, limits, name="rotate_in"
+            functools.partial(rotate_kernel, shards, width, 0, 0), [part], [VMEM] * 3, held, weights, limits, name="rotate_in"
         )
     table = call(
-        functools.partial(without, functools.partial(table_kernel, elems * ring, shards, width), 2),
-        [jax.ShapeDtypeStruct((couplings + 1, elems), jnp.int32)],
+        functools.partial(without, functools.partial(table_kernel, elems * ring, shards, width), 2, 1),
+        [jax.ShapeDtypeStruct((elems, couplings + 1, 8, 128), jnp.int32)],
         [VMEM, VMEM, ANY],
         beside,
         limits,
@@ -292,7 +303,7 @@
 
     def pack(g, behind):
         return call(
-            functools.partial(without, functools.partial(pack_kernel, shards, g), 1),
+            functools.partial(without, functools.partial(pack_kernel, shards, g), 1, 1),
             [bf16(width, rows, couplings * rows)],
             [VMEM, ANY],
             blocks,
@@ -306,7 +317,7 @@
     if pair:
         near = kept[0]
         middle, leaving = call(
-            functools.partial(without, middle_kernel, 3),
+            functools.partial(without, middle_kernel, 3, 1),
             [group] * 2,
             [VMEM] * 3 + [ANY],
             kept[1],
@@ -318,7 +329,7 @@
         far = swapped([leaving])[0]
     else:
         near, middle, far = call(
-            functools.partial(without, functools.partial(gather_kernel, shards), shards),
+            functools.partial(without, functools.partial(gather_kernel, shards), shards, 1),
             [group] * 3,
             [VMEM] * shards + [ANY],
             *kept,
@@ -329,13 +340,16 @@
         )
         near_halo, far_halo = to_near_of_neighbor(far), to_far_of_neighbor(near)
 
-    def level(g, m, before, here, after, previous, split=False, behind=None, flops=0):
+    def level(g, m, before, here, after, previous, which=None, instead=None, split=False, behind=(), flops=0):
         body = functools.partial(level_kernel, g * width, 1.0 if m == 1 else 2.0, previous is not None)
         args = [packed[g], table, before, here, after] + ([] if previous is None else [previous])
+        if which is not None:
+            body = functools.partial(level_if_kernel, which, instead is not None, body, len(args))
+            args += [] if instead is None else [instead]
         specs = [VMEM] * len(args)
-        if behind is not None:
-            body = functools.partial(without, body, len(args))
-            args, specs = args + [behind], specs + [ANY]
+        if behind:
+            body = functools.partial(without, body, len(args), len(behind))
+            args, specs = args + list(behind), specs + [ANY] * len(behind)
         outs = call(
             body,
             [group] + [half] * split,
@@ -350,31 +364,37 @@
     older = (None, None, None)
     for m in range(1, DEG + 1):
         last = m == DEG
-        behind = half_arrived = None
-        if m > 2:
-            new_middle = behind = level(1, m, near, middle, far, older[1], split=pair and last)
-            if pair and last:
-                new_middle, half_leaving = new_middle
-                behind, half_arrived = None, swapped([half_leaving])[0]
-        if m % 2:
-            new_near = level(0, m, near_halo, near, middle, older[0], behind=behind)
+        if m == 1:
+            new_near = level(0, m, near_halo, near, middle, older[0])
             next_far_halo = to_far_of_neighbor(new_near)
-            new_far = level(2, m, middle, far, far_halo, older[2], behind=new_near)
+            new_far = level(2, m, middle, far, far_halo, older[2], behind=[new_near])
             next_near_halo = to_near_of_neighbor(new_far)
+            new_middle = level(1, m, near, middle, far, older[1])
+        elif m % 2:
+            new_middle = level(1, m, near, middle, far, older[1])
+            new_near = level(0, m, near_halo, near, middle, older[0], behind=[new_middle])
+            next_far_halo = to_far_of_neighbor(new_near)
+            new_far = level(2, m, middle, far, far_halo, older[2], behind=[new_near])
+            next_near_halo = to_near_of_neighbor(new_far)
+        elif not last:
+            new_far = level(2, m, middle, far, far_halo, older[2])
+            next_near_halo = to_near_of_neighbor(new_far)
+            new_middle = level(1, m, near, middle, far, older[1], behind=[new_far])
+            new_near = level(0, m, near_halo, near, middle, older[0], behind=[new_middle])
+            next_far_halo = to_far_of_neighbor(new_near)
         else:
-            new_far = level(2, m, middle, far, far_halo, older[2], behind=behind)
-            if m == 2:
-                new_middle = level(1, m, near, middle, far, older[1], behind=new_far)
-            if last and pair:
+            if pair:
+                mate_halo = permuted(near, lambda i, j: (i ^ 1, j))
+                early = level(2, m, middle, far, mate_halo, older[2], which=0)
+                new_middle, half_leaving = level(1, m, near, middle, far, older[1], split=True, behind=[early])
+                half_arrived = swapped([half_leaving])[0]
+                new_far = level(2, m, middle, far, far_halo, older[2], which=1, instead=early)
                 arrived = swapped([new_far])[0]
             else:
-                next_near_halo = to_near_of_neighbor(new_far)
-            behind = half_arrived if last else new_middle
-            new_near = level(0, m, near_halo, near, middle, older[0], behind=behind, flops=LONG * last)
-            if not last:
-                next_far_halo = to_far_of_neighbor(new_near)
-        if m == 1:
-            new_middle = level(1, m, near, middle, far, older[1])
+                new_middle = level(1, m, near, middle, far, older[1])
+                new_far = level(2, m, middle, far, far_halo, older[2])
+            behind = [half_arrived] if pair else []
+            new_near = level(0, m, near_halo, near, middle, older[0], behind=behind, flops=LONG)
         if not last:
             near_halo, far_halo = next_near_halo, next_far_halo
         older, (near, middle, far) = (near, middle, far), (new_near, new_middle, new_far)
@@ -393,7 +413,7 @@
             name="own",
         )[0]
         return call(
-            functools.partial(without, others_kernel, 1),
+            functools.partial(without, others_kernel, 1, 1),
             whole_out,
             [VMEM, HBM],
             arrived,

time: 40.4 us -> 39.9 us (0.988)
  Pallas kernels: 11.4 us -> 10.8 us
    ppermute x4, waiting for transfers between devices: 3.6 us -> 2.11 us  [swapped(): lax.ppermute(x, 'state', [(i, (i + k + 1) % shards) for i in range(shards)])]
    ppermute x8 -> x9, waiting for transfers between devices: 9.68 us -> 11 us  [permuted(): return lax.ppermute(x, ('elem', 'state'), moves)]
    pallas_call x22 -> x23, Pallas kernels: 11.4 us -> 10.8 us  [call(): pl.pallas_call(kernel, out_shape=outs, in_specs=ins, out_specs=out_specs...]
    ppermute x8 -> x9, starting transfers between devices: 7.61 us -> 8.05 us  [permuted(): return lax.ppermute(x, ('elem', 'state'), moves)]
  transfers between devices with their start and end apart: 12 -> 13, of which waited for: 9 -> 8; matrix products, arithmetic and copies ran while one was open for 0% -> 0% of each run, Pallas kernels for 23% -> 22%
where the time goes in v6:
time: 39.9 us; the launch traced here: 39.8 us
  starting transfers between devices  15.6 us (39%)
  waiting for transfers between devices  13.1 us (33%)
  Pallas kernels  10.8 us (27%)
    ppermute x9, waiting for transfers between devices, permuted(): return lax.ppermute(x, ('elem', 'state'), moves)  11 us
    pallas_call x23, Pallas kernels, call(): pl.pallas_call(kernel, out_shape=outs, in_specs=ins, out_specs=out_specs...  10.8 us
    ppermute x9, starting transfers between devices, permuted(): return lax.ppermute(x, ('elem', 'state'), moves)  8.05 us
    ppermute x4, starting transfers between devices, swapped(): lax.ppermute(x, 'state', [(i, (i + k + 1) % shards) for i in range(shards)])  7.56 us
    ppermute x4, waiting for transfers between devices, swapped(): lax.ppermute(x, 'state', [(i, (i + k + 1) % shards) for i in range(shards)])  2.11 us
  transfers between devices with their start and end apart: 13, of which 8 were waited for; matrix products, arithmetic and copies ran while one was open for 0% of the time, Pallas kernels for 22%

profile of v6, /device:TPU:0, one launch (start us, length us, event | category | flops | bytes accessed | tf_op | source)
XLA Modules:
  0.0 39.8 jit_solution(11985512846091405760)
XLA Ops:
  0.0 1.3 %fetch.1 = (bf16[2,160,128]{2,1,0:T(8,128)(2,1)S(1)}, bf16[6,160,256]{2,1,0:T(8,128)(2,1)S(1)}, bf16[256,256]{1,0:T(8,128)(2,1)S(1)}, s32[12]{0:T(128)S(1)}, s32[5,12]{1,0:T(8,128)S(1)}) custom-call(bf16[6,160,256]{2,1,0:T(8,128)(2,1)} %orbitals.1, bf16[256,256]{1,0:T(8,128)(2,1)} %rotation.1, s32[12]{0:T(128)} %counts.1, s32[5,12]{1,0:T(8,128)} %bitcast.3), custom_call_target="tpu_custom_call" | custom-call | bytes 1024 | tf_op jit(solution)/shard_map/fetch/pallas_call | solution.py:23
  1.4 3.0 %collective-permute-start = (bf16[2,160,128]{2,1,0:T(8,128)(2,1)S(1)}, bf16[2,160,128]{2,1,0:T(8,128)(2,1)S(1)}, u32[]{:S(2)}, u32[]{:S(2)}) collective-permute-start(bf16[2,160,128]{2,1,0:T(8,128)(2,1)S(1)} %get-tuple-element.22), channel_id=1, source_target_pairs={{0,1},{1,0},{2,3},{3,2},{4,5},{5,4},{6,7},{7,6},{8,9},{9,8},{10,11... | collective-permute-start | bytes 245768 | tf_op jit(solution)/shard_map/ppermute | solution.py:261
  4.4 0.0 slice-start
  4.4 0.0 slice-start.1
  4.4 0.2 rotate_out.1.refs_3_.refs_2_
  4.6 3.7 %collective-permute-start.3 = (bf16[4,160,128]{2,1,0:T(8,128)(2,1)S(1)}, bf16[4,160,128]{2,1,0:T(8,128)(2,1)S(1)}, u32[]{:S(2)}, u32[]{:S(2)}) collective-permute-start(bf16[4,160,128]{2,1,0:T(8,128)(2,1)S(1)} %rotate_out.1.refs_3_.refs_2_), channel_id=1, source_target_pairs={{0,31},{1,2},{2,1},{3,4},{4,3},{5,6},{6,5},{7,8},{8,7},{9,10},{10,... | collective-permute-start | bytes 491528 | tf_op jit(solution)/shard_map/ppermute | solution.py:248
  8.3 0.3 rotate_in.1
  8.6 1.2 %collective-permute-start.2 = (bf16[4,160,128]{2,1,0:T(8,128)(2,1)S(1)}, bf16[4,160,128]{2,1,0:T(8,128)(2,1)S(1)}, u32[]{:S(2)}, u32[]{:S(2)}) collective-permute-start(bf16[4,160,128]{2,1,0:T(8,128)(2,1)S(1)} %get-tuple-element.20.refs_2_.here.before.refs_5_), channel_id=1, source_target_pairs={{0,30},{1,3},{2,0},{3,5},{4,2},{5,7},{6,4},{7,9},{8,6},{9,11},{10,... | collective-permute-start | bytes 491528 | tf_op jit(solution)/shard_map/ppermute | solution.py:248
  9.8 0.3 table.1.refs_1_
  10.1 0.0 slice-done
  10.1 0.0 slice-done.1
  10.1 0.3 pack.3.refs_1_.packed.refs_0_
  10.4 0.3 pack.4.refs_1_.refs_0_.packed
  10.7 0.3 pack.5.refs_3_.packed.refs_0_
  11.0 0.0 collective-permute-done.refs_1_
  11.0 0.5 %collective-permute-start.1 = (bf16[4,160,128]{2,1,0:T(8,128)(2,1)S(1)}, bf16[4,160,128]{2,1,0:T(8,128)(2,1)S(1)}, u32[]{:S(2)}, u32[]{:S(2)}) collective-permute-start(bf16[4,160,128]{2,1,0:T(8,128)(2,1)S(1)} %get-tuple-element.24), channel_id=1, source_target_pairs={{0,1},{1,0},{2,3},{3,2},{4,5},{5,4},{6,7},{7,6},{8,9},{9,8},{10,11... | collective-permute-start | bytes 491528 | tf_op jit(solution)/shard_map/ppermute | solution.py:261
  11.6 1.5 %collective-permute-done.3.before = bf16[4,160,128]{2,1,0:T(8,128)(2,1)S(1)} collective-permute-done((bf16[4,160,128]{2,1,0:T(8,128)(2,1)S(1)}, bf16[4,160,128]{2,1,0:T(8,128)(2,1)S(1)}, u32[]{:S(2)}, u32[]{:S(2)}) %collective-permute-start.3) | collective-permute-done | bytes 163872 | tf_op jit(solution)/shard_map/ppermute | solution.py:248
  13.1 0.5 %near1.1.refs_5_.refs_2_.refs_3_ = bf16[4,160,128]{2,1,0:T(8,128)(2,1)S(1)} custom-call(bf16[4,160,800]{2,1,0:T(8,128)(2,1)S(1)} %pack.3.refs_1_.packed.refs_0_, s32[12,6,8,128]{3,2,1,0:T(8,128)S(1)} %table.1.refs_1_, bf16[4,160,128]{2,1,0:T(8,128)(2,1)S(1)} %collective-permute-done.3.before, ...), custom_call_target="tpu_custom_call" | custom-call | bytes 1024 | tf_op jit(solution)/shard_map/near1/pallas_call | solution.py:23
  13.6 2.3 %collective-permute-start.5 = (bf16[4,160,128]{2,1,0:T(8,128)(2,1)S(1)}, bf16[4,160,128]{2,1,0:T(8,128)(2,1)S(1)}, u32[]{:S(2)}, u32[]{:S(2)}) collective-permute-start(bf16[4,160,128]{2,1,0:T(8,128)(2,1)S(1)} %near1.1.refs_5_.refs_2_.refs_3_), channel_id=1, source_target_pairs={{0,30},{1,3},{2,0},{3,5},{4,2},{5,7},{6,4},{7,9},{8,6},{9,11},{10,... | collective-permute-start | bytes 491528 | tf_op jit(solution)/shard_map/ppermute | solution.py:248
  15.9 0.0 collective-permute-done.2.refs_4_
  15.9 0.7 %collective-permute-done.1.refs_3_.after.refs_0_ = bf16[4,160,128]{2,1,0:T(8,128)(2,1)S(1)} collective-permute-done((bf16[4,160,128]{2,1,0:T(8,128)(2,1)S(1)}, bf16[4,160,128]{2,1,0:T(8,128)(2,1)S(1)}, u32[]{:S(2)}, u32[]{:S(2)}) %collective-permute-start.1) | collective-permute-done | bytes 163872 | tf_op jit(solution)/shard_map/ppermute | solution.py:261
  16.6 0.5 %far1.1.here.refs_4_.refs_5_ = bf16[4,160,128]{2,1,0:T(8,128)(2,1)S(1)} custom-call(bf16[4,160,800]{2,1,0:T(8,128)(2,1)S(1)} %pack.4.refs_1_.refs_0_.packed, s32[12,6,8,128]{3,2,1,0:T(8,128)S(1)} %table.1.refs_1_, bf16[4,160,128]{2,1,0:T(8,128)(2,1)S(1)} %get-tuple-element.23.after.refs_2_.here.refs_5_, ...), custom_call_target="tpu_custom_call" | custom-call | bytes 1024 | tf_op jit(solution)/shard_map/far1/pallas_call | solution.py:23
  17.1 0.1 collective-permute-start.4
  17.2 0.5 %middle1.1.before.refs_3_.refs_4_.refs_0_ = bf16[4,160,128]{2,1,0:T(8,128)(2,1)S(1)} custom-call(bf16[4,160,800]{2,1,0:T(8,128)(2,1)S(1)} %pack.5.refs_3_.packed.refs_0_, s32[12,6,8,128]{3,2,1,0:T(8,128)S(1)} %table.1.refs_1_, bf16[4,160,128]{2,1,0:T(8,128)(2,1)S(1)} %get-tuple-element.20.refs_2_.here.before.refs_5_, ...), custom_call_target="tpu_custom_call" | custom-call | bytes 1024 | tf_op jit(solution)/shard_map/middle1/pallas_call | solution.py:23
  17.7 1.0 %collective-permute-done.5.after = bf16[4,160,128]{2,1,0:T(8,128)(2,1)S(1)} collective-permute-done((bf16[4,160,128]{2,1,0:T(8,128)(2,1)S(1)}, bf16[4,160,128]{2,1,0:T(8,128)(2,1)S(1)}, u32[]{:S(2)}, u32[]{:S(2)}) %collective-permute-start.5) | collective-permute-done | bytes 163872 | tf_op jit(solution)/shard_map/ppermute | solution.py:248
  18.7 0.5 %far2.1.refs_6_.after.refs_3_.refs_5_ = bf16[4,160,128]{2,1,0:T(8,128)(2,1)S(1)} custom-call(bf16[4,160,800]{2,1,0:T(8,128)(2,1)S(1)} %pack.4.refs_1_.refs_0_.packed, s32[12,6,8,128]{3,2,1,0:T(8,128)S(1)} %table.1.refs_1_, bf16[4,160,128]{2,1,0:T(8,128)(2,1)S(1)} %middle1.1.before.refs_3_.refs_4_.refs_0_, bf16[4,160,128]{2,1,0:T(8,128)(2,1)S(1)} %far1.1.here.refs_4_.refs_5_, ...), custom_call_target="tpu_custom_call" | custom-call | bytes 1024 | tf_op jit(solution)/shard_map/far2/pallas_call | solution.py:23
  19.3 0.1 collective-permute-start.7
  19.3 0.5 %middle2.1.refs_6_.here.refs_4_.refs_2_.refs_5_ = bf16[4,160,128]{2,1,0:T(8,128)(2,1)S(1)} custom-call(bf16[4,160,800]{2,1,0:T(8,128)(2,1)S(1)} %pack.5.refs_3_.packed.refs_0_, s32[12,6,8,128]{3,2,1,0:T(8,128)S(1)} %table.1.refs_1_, bf16[4,160,128]{2,1,0:T(8,128)(2,1)S(1)} %near1.1.refs_5_.refs_2_.refs_3_, ...), custom_call_target="tpu_custom_call" | custom-call | bytes 1024 | tf_op jit(solution)/shard_map/middle2/pallas_call | solution.py:23
  19.9 4.8 %collective-permute-done.4.refs_2_ = bf16[4,160,128]{2,1,0:T(8,128)(2,1)S(1)} collective-permute-done((bf16[4,160,128]{2,1,0:T(8,128)(2,1)S(1)}, bf16[4,160,128]{2,1,0:T(8,128)(2,1)S(1)}, u32[]{:S(2)}, u32[]{:S(2)}) %collective-permute-start.4) | collective-permute-done | bytes 163872 | tf_op jit(solution)/shard_map/ppermute | solution.py:248
  24.7 0.5 %near2.1.before.refs_3_.refs_5_ = bf16[4,160,128]{2,1,0:T(8,128)(2,1)S(1)} custom-call(bf16[4,160,800]{2,1,0:T(8,128)(2,1)S(1)} %pack.3.refs_1_.packed.refs_0_, s32[12,6,8,128]{3,2,1,0:T(8,128)S(1)} %table.1.refs_1_, bf16[4,160,128]{2,1,0:T(8,128)(2,1)S(1)} %collective-permute-done.4.refs_2_, bf16[4,160,128]{2,1,0:T(8,128)(2,1)S(1)} %near1.1.refs_5_.refs_2_.refs_3_, ...), custom_call_target="tpu_custom_call" | custom-call | bytes 1024 | tf_op jit(solution)/shard_map/near2/pallas_call | solution.py:23
  25.2 0.1 collective-permute-start.6
  25.3 0.5 %middle3.1.refs_6_.refs_2_.refs_3_.refs_4_ = bf16[4,160,128]{2,1,0:T(8,128)(2,1)S(1)} custom-call(bf16[4,160,800]{2,1,0:T(8,128)(2,1)S(1)} %pack.5.refs_3_.packed.refs_0_, s32[12,6,8,128]{3,2,1,0:T(8,128)S(1)} %table.1.refs_1_, bf16[4,160,128]{2,1,0:T(8,128)(2,1)S(1)} %near2.1.before.refs_3_.refs_5_, ...), custom_call_target="tpu_custom_call" | custom-call | bytes 1024 | tf_op jit(solution)/shard_map/middle3/pallas_call | solution.py:23
  25.8 1.3 %collective-permute-done.7.refs_2_ = bf16[4,160,128]{2,1,0:T(8,128)(2,1)S(1)} collective-permute-done((bf16[4,160,128]{2,1,0:T(8,128)(2,1)S(1)}, bf16[4,160,128]{2,1,0:T(8,128)(2,1)S(1)}, u32[]{:S(2)}, u32[]{:S(2)}) %collective-permute-start.7) | collective-permute-done | bytes 163872 | tf_op jit(solution)/shard_map/ppermute | solution.py:248
  27.1 0.5 %near3.1.refs_6_.refs_2_.refs_3_ = bf16[4,160,128]{2,1,0:T(8,128)(2,1)S(1)} custom-call(bf16[4,160,800]{2,1,0:T(8,128)(2,1)S(1)} %pack.3.refs_1_.packed.refs_0_, s32[12,6,8,128]{3,2,1,0:T(8,128)S(1)} %table.1.refs_1_, bf16[4,160,128]{2,1,0:T(8,128)(2,1)S(1)} %collective-permute-done.7.refs_2_, bf16[4,160,128]{2,1,0:T(8,128)(2,1)S(1)} %near2.1.before.refs_3_.refs_5_, ...), custom_call_target="tpu_custom_call" | custom-call | bytes 1024 | tf_op jit(solution)/shard_map/near3/pallas_call | solution.py:23
  27.7 0.1 collective-permute-start.9
  27.7 0.4 collective-permute-start.8
  28.1 0.0 collective-permute-done.6.refs_4_
  28.1 0.5 %far3.1.refs_3_.refs_4_ = bf16[4,160,128]{2,1,0:T(8,128)(2,1)S(1)} custom-call(bf16[4,160,800]{2,1,0:T(8,128)(2,1)S(1)} %pack.4.refs_1_.refs_0_.packed, s32[12,6,8,128]{3,2,1,0:T(8,128)S(1)} %table.1.refs_1_, bf16[4,160,128]{2,1,0:T(8,128)(2,1)S(1)} %middle2.1.refs_6_.here.refs_4_.refs_2_.refs_5_, ...), custom_call_target="tpu_custom_call" | custom-call | bytes 1024 | tf_op jit(solution)/shard_map/far3/pallas_call | solution.py:23
  28.7 0.2 collective-permute-start.11
  28.9 0.2 collective-permute-done.9.refs_4_
  29.1 0.5 %far4.2.refs_6_ = bf16[4,160,128]{2,1,0:T(8,128)(2,1)S(1)} custom-call(bf16[4,160,800]{2,1,0:T(8,128)(2,1)S(1)} %pack.4.refs_1_.refs_0_.packed, s32[12,6,8,128]{3,2,1,0:T(8,128)S(1)} %table.1.refs_1_, bf16[4,160,128]{2,1,0:T(8,128)(2,1)S(1)} %middle3.1.refs_6_.refs_2_.refs_3_.refs_4_, bf16[4,160,128]{2,1,0:T(8,128)(2,1)S(1)} %far3.1.refs_3_.refs_4_, ...), custom_call_target="tpu_custom_call" | custom-call | bytes 1024 | tf_op jit(solution)/shard_map/far4/pallas_call | solution.py:23
  29.7 0.6 %middle4.1 = (bf16[4,160,128]{2,1,0:T(8,128)(2,1)S(1)}, bf16[2,160,128]{2,1,0:T(8,128)(2,1)S(1)}) custom-call(bf16[4,160,800]{2,1,0:T(8,128)(2,1)S(1)} %pack.5.refs_3_.packed.refs_0_, s32[12,6,8,128]{3,2,1,0:T(8,128)S(1)} %table.1.refs_1_, bf16[4,160,128]{2,1,0:T(8,128)(2,1)S(1)} %near3.1.refs_6_.refs_2_.refs_3_, ...), custom_call_target="tpu_custom_call" | custom-call | bytes 1024 | tf_op jit(solution)/shard_map/middle4/pallas_call | solution.py:23
  30.2 2.0 %collective-permute-start.12 = (bf16[2,160,128]{2,1,0:T(8,128)(2,1)S(1)}, bf16[2,160,128]{2,1,0:T(8,128)(2,1)S(1)}, u32[]{:S(2)}, u32[]{:S(2)}) collective-permute-start(bf16[2,160,128]{2,1,0:T(8,128)(2,1)S(1)} %get-tuple-element.25), channel_id=1, source_target_pairs={{0,1},{1,0},{2,3},{3,2},{4,5},{5,4},{6,7},{7,6},{8,9},{9,8},{10,11... | collective-permute-start | bytes 245768 | tf_op jit(solution)/shard_map/ppermute | solution.py:261
  32.2 0.0 collective-permute-done.8.refs_4_
  32.3 2.0 %collective-permute-start.10 = (bf16[4,160,128]{2,1,0:T(8,128)(2,1)S(1)}, bf16[4,160,128]{2,1,0:T(8,128)(2,1)S(1)}, u32[]{:S(2)}, u32[]{:S(2)}) collective-permute-start(bf16[4,160,128]{2,1,0:T(8,128)(2,1)S(1)} %far4.3), channel_id=1, source_target_pairs={{0,1},{1,0},{2,3},{3,2},{4,5},{5,4},{6,7},{7,6},{8,9},{9,8},{10,11... | collective-permute-start | bytes 491528 | tf_op jit(solution)/shard_map/ppermute | solution.py:261
  34.3 2.1 %collective-permute-done.11.refs_2_ = bf16[4,160,128]{2,1,0:T(8,128)(2,1)S(1)} collective-permute-done((bf16[4,160,128]{2,1,0:T(8,128)(2,1)S(1)}, bf16[4,160,128]{2,1,0:T(8,128)(2,1)S(1)}, u32[]{:S(2)}, u32[]{:S(2)}) %collective-permute-start.11) | collective-permute-done | bytes 163872 | tf_op jit(solution)/shard_map/ppermute | solution.py:248
  36.4 0.0 collective-permute-done.12.refs_6_.half
  36.4 0.5 %near4.1.near = bf16[4,160,128]{2,1,0:T(8,128)(2,1)S(1)} custom-call(bf16[4,160,800]{2,1,0:T(8,128)(2,1)S(1)} %pack.3.refs_1_.packed.refs_0_, s32[12,6,8,128]{3,2,1,0:T(8,128)S(1)} %table.1.refs_1_, bf16[4,160,128]{2,1,0:T(8,128)(2,1)S(1)} %collective-permute-done.11.refs_2_, bf16[4,160,128]{2,1,0:T(8,128)(2,1)S(1)} %near3.1.refs_6_.refs_2_.refs_3_, ...), custom_call_target="tpu_custom_call" | custom-call | flops 20000000000 | bytes 1024 | tf_op jit(solution)/shard_map/near4/pallas_call | solution.py:23
  36.9 0.8 %own.1.refs_1_ = bf16[6,160,256]{2,1,0:T(8,128)(2,1)} custom-call(bf16[4,160,128]{2,1,0:T(8,128)(2,1)S(1)} %near4.1.near, bf16[4,160,128]{2,1,0:T(8,128)(2,1)S(1)} %get-tuple-element.26.middle, bf16[2,160,128]{2,1,0:T(8,128)(2,1)S(1)} %collective-permute-done.12.refs_6_.half), custom_call_target="tpu_custom_call" | custom-call | bytes 1024 | tf_op jit(solution)/shard_map/own/pallas_call | solution.py:23
  37.7 1.4 %collective-permute-done.10.refs_0_ = bf16[4,160,128]{2,1,0:T(8,128)(2,1)S(1)} collective-permute-done((bf16[4,160,128]{2,1,0:T(8,128)(2,1)S(1)}, bf16[4,160,128]{2,1,0:T(8,128)(2,1)S(1)}, u32[]{:S(2)}, u32[]{:S(2)}) %collective-permute-start.10) | collective-permute-done | bytes 163872 | tf_op jit(solution)/shard_map/ppermute | solution.py:261
  39.1 0.7 %others.1 = bf16[6,160,256]{2,1,0:T(8,128)(2,1)} custom-call(bf16[4,160,128]{2,1,0:T(8,128)(2,1)S(1)} %collective-permute-done.10.refs_0_, bf16[6,160,256]{2,1,0:T(8,128)(2,1)} %own.1.refs_1_), custom_call_target="tpu_custom_call", output_to_operand_aliasing={{}: (1, {})} | custom-call | bytes 1024 | tf_op jit(solution)/shard_map/others/pallas_call | solution.py:23
  (3 shorter events, 0.0 us)
Async XLA Ops:
  1.4 9.6 %collective-permute-start = (bf16[2,160,128]{2,1,0:T(8,128)(2,1)S(1)}, bf16[2,160,128]{2,1,0:T(8,128)(2,1)S(1)}, u32[]{:S(2)}, u32[]{:S(2)}) collective-permute-start(bf16[2,160,128]{2,1,0:T(8,128)(2,1)S(1)} %get-tuple-element.22), channel_id=1, source_target_pairs={{0,1},{1,0},{2,3},{3,2},{4,5},{5,4},{6,7},{7,6},{8,9},{9,8},{10,11... | collective-permute-start | bytes 245768 | tf_op jit(solution)/shard_map/ppermute | solution.py:261
  4.4 5.7 %slice-start = ((s8[4915200]{0:T(1024)(128)(4,1)}), s8[4194304]{0:T(1024)(128)(4,1)S(1)}, s32[]{:S(2)}) async-start(s8[4915200]{0:T(1024)(128)(4,1)} %bitcast.1), calls=%async_computation | async-start | bytes 8388608
  4.4 5.7 %slice-start.1 = ((s8[4915200]{0:T(1024)(128)(4,1)}), s8[720896]{0:T(1024)(128)(4,1)S(1)}, s32[]{:S(2)}) async-start(s8[4915200]{0:T(1024)(128)(4,1)} %bitcast.1), calls=%async_computation.1 | async-start | bytes 1441792
  4.6 8.4 %collective-permute-start.3 = (bf16[4,160,128]{2,1,0:T(8,128)(2,1)S(1)}, bf16[4,160,128]{2,1,0:T(8,128)(2,1)S(1)}, u32[]{:S(2)}, u32[]{:S(2)}) collective-permute-start(bf16[4,160,128]{2,1,0:T(8,128)(2,1)S(1)} %rotate_out.1.refs_3_.refs_2_), channel_id=1, source_target_pairs={{0,31},{1,2},{2,1},{3,4},{4,3},{5,6},{6,5},{7,8},{8,7},{9,10},{10,... | collective-permute-start | bytes 491528 | tf_op jit(solution)/shard_map/ppermute | solution.py:248
  8.6 7.3 %collective-permute-start.2 = (bf16[4,160,128]{2,1,0:T(8,128)(2,1)S(1)}, bf16[4,160,128]{2,1,0:T(8,128)(2,1)S(1)}, u32[]{:S(2)}, u32[]{:S(2)}) collective-permute-start(bf16[4,160,128]{2,1,0:T(8,128)(2,1)S(1)} %get-tuple-element.20.refs_2_.here.before.refs_5_), channel_id=1, source_target_pairs={{0,30},{1,3},{2,0},{3,5},{4,2},{5,7},{6,4},{7,9},{8,6},{9,11},{10,... | collective-permute-start | bytes 491528 | tf_op jit(solution)/shard_map/ppermute | solution.py:248
  11.0 5.6 %collective-permute-start.1 = (bf16[4,160,128]{2,1,0:T(8,128)(2,1)S(1)}, bf16[4,160,128]{2,1,0:T(8,128)(2,1)S(1)}, u32[]{:S(2)}, u32[]{:S(2)}) collective-permute-start(bf16[4,160,128]{2,1,0:T(8,128)(2,1)S(1)} %get-tuple-element.24), channel_id=1, source_target_pairs={{0,1},{1,0},{2,3},{3,2},{4,5},{5,4},{6,7},{7,6},{8,9},{9,8},{10,11... | collective-permute-start | bytes 491528 | tf_op jit(solution)/shard_map/ppermute | solution.py:261
  13.6 5.2 %collective-permute-start.5 = (bf16[4,160,128]{2,1,0:T(8,128)(2,1)S(1)}, bf16[4,160,128]{2,1,0:T(8,128)(2,1)S(1)}, u32[]{:S(2)}, u32[]{:S(2)}) collective-permute-start(bf16[4,160,128]{2,1,0:T(8,128)(2,1)S(1)} %near1.1.refs_5_.refs_2_.refs_3_), channel_id=1, source_target_pairs={{0,30},{1,3},{2,0},{3,5},{4,2},{5,7},{6,4},{7,9},{8,6},{9,11},{10,... | collective-permute-start | bytes 491528 | tf_op jit(solution)/shard_map/ppermute | solution.py:248
  17.1 7.6 %collective-permute-start.4 = (bf16[4,160,128]{2,1,0:T(8,128)(2,1)S(1)}, bf16[4,160,128]{2,1,0:T(8,128)(2,1)S(1)}, u32[]{:S(2)}, u32[]{:S(2)}) collective-permute-start(bf16[4,160,128]{2,1,0:T(8,128)(2,1)S(1)} %far1.1.here.refs_4_.refs_5_), channel_id=1, source_target_pairs={{0,2},{1,31},{2,4},{3,1},{4,6},{5,3},{6,8},{7,5},{8,10},{9,7},{10,... | collective-permute-start | bytes 491528 | tf_op jit(solution)/shard_map/ppermute | solution.py:248
  19.3 7.9 %collective-permute-start.7 = (bf16[4,160,128]{2,1,0:T(8,128)(2,1)S(1)}, bf16[4,160,128]{2,1,0:T(8,128)(2,1)S(1)}, u32[]{:S(2)}, u32[]{:S(2)}) collective-permute-start(bf16[4,160,128]{2,1,0:T(8,128)(2,1)S(1)} %far2.1.refs_6_.after.refs_3_.refs_5_), channel_id=1, source_target_pairs={{0,2},{1,31},{2,4},{3,1},{4,6},{5,3},{6,8},{7,5},{8,10},{9,7},{10,... | collective-permute-start | bytes 491528 | tf_op jit(solution)/shard_map/ppermute | solution.py:248
  25.2 2.9 %collective-permute-start.6 = (bf16[4,160,128]{2,1,0:T(8,128)(2,1)S(1)}, bf16[4,160,128]{2,1,0:T(8,128)(2,1)S(1)}, u32[]{:S(2)}, u32[]{:S(2)}) collective-permute-start(bf16[4,160,128]{2,1,0:T(8,128)(2,1)S(1)} %near2.1.before.refs_3_.refs_5_), channel_id=1, source_target_pairs={{0,30},{1,3},{2,0},{3,5},{4,2},{5,7},{6,4},{7,9},{8,6},{9,11},{10,... | collective-permute-start | bytes 491528 | tf_op jit(solution)/shard_map/ppermute | solution.py:248
  27.7 1.5 %collective-permute-start.9 = (bf16[4,160,128]{2,1,0:T(8,128)(2,1)S(1)}, bf16[4,160,128]{2,1,0:T(8,128)(2,1)S(1)}, u32[]{:S(2)}, u32[]{:S(2)}) collective-permute-start(bf16[4,160,128]{2,1,0:T(8,128)(2,1)S(1)} %near3.1.refs_6_.refs_2_.refs_3_), channel_id=1, source_target_pairs={{0,2},{1,3},{2,0},{3,1},{4,6},{5,7},{6,4},{7,5},{8,10},{9,11},{10,... | collective-permute-start | bytes 491528 | tf_op jit(solution)/shard_map/ppermute | solution.py:248
  27.7 4.5 %collective-permute-start.8 = (bf16[4,160,128]{2,1,0:T(8,128)(2,1)S(1)}, bf16[4,160,128]{2,1,0:T(8,128)(2,1)S(1)}, u32[]{:S(2)}, u32[]{:S(2)}) collective-permute-start(bf16[4,160,128]{2,1,0:T(8,128)(2,1)S(1)} %near3.1.refs_6_.refs_2_.refs_3_), channel_id=1, source_target_pairs={{0,30},{1,3},{2,0},{3,5},{4,2},{5,7},{6,4},{7,9},{8,6},{9,11},{10,... | collective-permute-start | bytes 491528 | tf_op jit(solution)/shard_map/ppermute | solution.py:248
  28.7 7.7 %collective-permute-start.11 = (bf16[4,160,128]{2,1,0:T(8,128)(2,1)S(1)}, bf16[4,160,128]{2,1,0:T(8,128)(2,1)S(1)}, u32[]{:S(2)}, u32[]{:S(2)}) collective-permute-start(bf16[4,160,128]{2,1,0:T(8,128)(2,1)S(1)} %far3.1.refs_3_.refs_4_), channel_id=1, source_target_pairs={{0,2},{1,31},{2,4},{3,1},{4,6},{5,3},{6,8},{7,5},{8,10},{9,7},{10,... | collective-permute-start | bytes 491528 | tf_op jit(solution)/shard_map/ppermute | solution.py:248
  30.2 6.1 %collective-permute-start.12 = (bf16[2,160,128]{2,1,0:T(8,128)(2,1)S(1)}, bf16[2,160,128]{2,1,0:T(8,128)(2,1)S(1)}, u32[]{:S(2)}, u32[]{:S(2)}) collective-permute-start(bf16[2,160,128]{2,1,0:T(8,128)(2,1)S(1)} %get-tuple-element.25), channel_id=1, source_target_pairs={{0,1},{1,0},{2,3},{3,2},{4,5},{5,4},{6,7},{7,6},{8,9},{9,8},{10,11... | collective-permute-start | bytes 245768 | tf_op jit(solution)/shard_map/ppermute | solution.py:261
  32.3 6.8 %collective-permute-start.10 = (bf16[4,160,128]{2,1,0:T(8,128)(2,1)S(1)}, bf16[4,160,128]{2,1,0:T(8,128)(2,1)S(1)}, u32[]{:S(2)}, u32[]{:S(2)}) collective-permute-start(bf16[4,160,128]{2,1,0:T(8,128)(2,1)S(1)} %far4.3), channel_id=1, source_target_pairs={{0,1},{1,0},{2,3},{3,2},{4,5},{5,4},{6,7},{7,6},{8,9},{9,8},{10,11... | collective-permute-start | bytes 491528 | tf_op jit(solution)/shard_map/ppermute | solution.py:261

commit v7 on v6

--- a/solution.py
+++ b/solution.py
@@ -9,7 +9,7 @@
 
 DEG = 4
 FULL = 128
-LONG = 20 * 10**9
+LONG, SHORT = 20 * 10**9, 10**9
 
 center_shift = 0.2
 half_span = 1.1
@@ -86,8 +86,13 @@
         copy.start()
     for copy in copies[:3]:
         copy.wait()
-    for k, out in enumerate(outs):
-        rotate_kernel(shards, reach, k + 1, reach if shards == 2 else 0, held, weights, limits, out)
+    if shards == 2:
+        near, half = outs
+        rotate_kernel(shards, reach, 1, reach, held, weights, limits, half)
+        rotate_kernel(shards, reach, 1, 0, held, weights, limits, near)
+    else:
+        for k, out in enumerate(outs):
+            rotate_kernel(shards, reach, k + 1, 0, held, weights, limits, out)
     copies[3].wait()
 
 
@@ -263,17 +268,16 @@
 
     *parts, held, weights, limits, beside = call(
         functools.partial(fetch_kernel, shards, width),
-        ([half] if pair else [part] * (shards - 1)) + [jax.ShapeDtypeStruct(x.shape, x.dtype) for x in inputs],
+        ([group, half] if pair else [part] * (shards - 1)) + [jax.ShapeDtypeStruct(x.shape, x.dtype) for x in inputs],
         [HBM] * len(inputs),
         *inputs,
         scratch=[dma((4,))],
+        flops=LONG,
         name="fetch",
     )
     if pair:
-        arrived_half = swapped(parts)[0]
-        leaving = call(
-            functools.partial(rotate_kernel, shards, width, 1, 0), [group], [VMEM] * 3, held, weights, limits, flops=LONG, name="rotate_out"
-        )[0]
+        leaving = parts[0]
+        arrived_half = swapped(parts[1:])[0]
         near_halo = shifted(leaving, -1, across=True)
         kept = call(
             functools.partial(without, functools.partial(rotate_kernel, shards, width, 0, 0), 3, 1),
@@ -324,6 +328,7 @@
             arrived_half,
             leaving,
             packed[1],
+            flops=SHORT,
             name="gather",
         )
         far = swapped([leaving])[0]

time: 39.9 us -> 39.6 us (level)
  waiting for transfers between devices: 13.1 us -> 12 us
  starting transfers between devices: 15.6 us -> 16.4 us
    ppermute x4, waiting for transfers between devices: 2.11 us -> 1.09 us  [swapped(): lax.ppermute(x, 'state', [(i, (i + k + 1) % shards) for i in range(shards)])]
    ppermute x9, starting transfers between devices: 8.05 us -> 8.74 us  [permuted(): return lax.ppermute(x, ('elem', 'state'), moves)]
    pallas_call x23 -> x22, Pallas kernels: 10.8 us -> 10.8 us  [call(): pl.pallas_call(kernel, out_shape=outs, in_specs=ins, out_specs=out_specs...]
where the time goes in v7:
time: 39.6 us; the launch traced here: 39.4 us
  starting transfers between devices  16.4 us (41%)
  waiting for transfers between devices  12 us (30%)
  Pallas kernels  10.8 us (27%)
    ppermute x9, waiting for transfers between devices, permuted(): return lax.ppermute(x, ('elem', 'state'), moves)  10.9 us
    pallas_call x22, Pallas kernels, call(): pl.pallas_call(kernel, out_shape=outs, in_specs=ins, out_specs=out_specs...  10.8 us
    ppermute x9, starting transfers between devices, permuted(): return lax.ppermute(x, ('elem', 'state'), moves)  8.74 us
    ppermute x4, starting transfers between devices, swapped(): lax.ppermute(x, 'state', [(i, (i + k + 1) % shards) for i in range(shards)])  7.62 us
    ppermute x4, waiting for transfers between devices, swapped(): lax.ppermute(x, 'state', [(i, (i + k + 1) % shards) for i in range(shards)])  1.09 us
  transfers between devices with their start and end apart: 13, of which 8 were waited for; matrix products, arithmetic and copies ran while one was open for 0% of the time, Pallas kernels for 22%

profile of v7, /device:TPU:0, one launch (start us, length us, event | category | flops | bytes accessed | tf_op | source)
XLA Modules:
  0.0 39.4 jit_solution(3363899685909452103)
XLA Ops:
  0.0 0.0 slice-start
  0.0 0.0 slice-start.1
  0.0 1.6 %fetch.1 = (bf16[4,160,128]{2,1,0:T(8,128)(2,1)S(1)}, bf16[2,160,128]{2,1,0:T(8,128)(2,1)S(1)}, bf16[6,160,256]{2,1,0:T(8,128)(2,1)S(1)}, bf16[256,256]{1,0:T(8,...) custom-call(bf16[6,160,256]{2,1,0:T(8,128)(2,1)} %orbitals.1, bf16[256,256]{1,0:T(8,128)(2,1)} %rotation.1, s32[12]{0:T(128)} %counts.1, ...), custom_call_target="tpu_custom_call" | custom-call | flops 20000000000 | bytes 1024 | tf_op jit(solution)/shard_map/fetch/pallas_call | solution.py:23
  1.6 3.0 %collective-permute-start = (bf16[2,160,128]{2,1,0:T(8,128)(2,1)S(1)}, bf16[2,160,128]{2,1,0:T(8,128)(2,1)S(1)}, u32[]{:S(2)}, u32[]{:S(2)}) collective-permute-start(bf16[2,160,128]{2,1,0:T(8,128)(2,1)S(1)} %get-tuple-element.24), channel_id=1, source_target_pairs={{0,1},{1,0},{2,3},{3,2},{4,5},{5,4},{6,7},{7,6},{8,9},{9,8},{10,11... | collective-permute-start | bytes 245768 | tf_op jit(solution)/shard_map/ppermute | solution.py:266
  4.6 3.6 %collective-permute-start.3 = (bf16[4,160,128]{2,1,0:T(8,128)(2,1)S(1)}, bf16[4,160,128]{2,1,0:T(8,128)(2,1)S(1)}, u32[]{:S(2)}, u32[]{:S(2)}) collective-permute-start(bf16[4,160,128]{2,1,0:T(8,128)(2,1)S(1)} %get-tuple-element.21.refs_3_.refs_2_), channel_id=1, source_target_pairs={{0,31},{1,2},{2,1},{3,4},{4,3},{5,6},{6,5},{7,8},{8,7},{9,10},{10,... | collective-permute-start | bytes 491528 | tf_op jit(solution)/shard_map/ppermute | solution.py:253
  8.3 0.3 rotate_in.1
  8.6 1.2 %collective-permute-start.2 = (bf16[4,160,128]{2,1,0:T(8,128)(2,1)S(1)}, bf16[4,160,128]{2,1,0:T(8,128)(2,1)S(1)}, u32[]{:S(2)}, u32[]{:S(2)}) collective-permute-start(bf16[4,160,128]{2,1,0:T(8,128)(2,1)S(1)} %get-tuple-element.22.refs_2_.here.before.refs_5_), channel_id=1, source_target_pairs={{0,30},{1,3},{2,0},{3,5},{4,2},{5,7},{6,4},{7,9},{8,6},{9,11},{10,... | collective-permute-start | bytes 491528 | tf_op jit(solution)/shard_map/ppermute | solution.py:253
  9.7 0.3 table.1.refs_1_
  10.0 0.0 slice-done
  10.0 0.0 slice-done.1
  10.1 0.3 pack.3.refs_1_.packed.refs_0_
  10.3 0.3 pack.4.refs_1_.refs_0_.packed
  10.6 0.3 pack.5.refs_3_.packed.refs_0_
  10.9 0.0 collective-permute-done.refs_1_
  11.0 0.9 %collective-permute-start.1 = (bf16[4,160,128]{2,1,0:T(8,128)(2,1)S(1)}, bf16[4,160,128]{2,1,0:T(8,128)(2,1)S(1)}, u32[]{:S(2)}, u32[]{:S(2)}) collective-permute-start(bf16[4,160,128]{2,1,0:T(8,128)(2,1)S(1)} %get-tuple-element.26), channel_id=1, source_target_pairs={{0,1},{1,0},{2,3},{3,2},{4,5},{5,4},{6,7},{7,6},{8,9},{9,8},{10,11... | collective-permute-start | bytes 491528 | tf_op jit(solution)/shard_map/ppermute | solution.py:266
  11.8 1.2 %collective-permute-done.3.before = bf16[4,160,128]{2,1,0:T(8,128)(2,1)S(1)} collective-permute-done((bf16[4,160,128]{2,1,0:T(8,128)(2,1)S(1)}, bf16[4,160,128]{2,1,0:T(8,128)(2,1)S(1)}, u32[]{:S(2)}, u32[]{:S(2)}) %collective-permute-start.3) | collective-permute-done | bytes 163872 | tf_op jit(solution)/shard_map/ppermute | solution.py:253
  13.0 0.5 %near1.1.refs_5_.refs_2_.refs_3_ = bf16[4,160,128]{2,1,0:T(8,128)(2,1)S(1)} custom-call(bf16[4,160,800]{2,1,0:T(8,128)(2,1)S(1)} %pack.3.refs_1_.packed.refs_0_, s32[12,6,8,128]{3,2,1,0:T(8,128)S(1)} %table.1.refs_1_, bf16[4,160,128]{2,1,0:T(8,128)(2,1)S(1)} %collective-permute-done.3.before, ...), custom_call_target="tpu_custom_call" | custom-call | bytes 1024 | tf_op jit(solution)/shard_map/near1/pallas_call | solution.py:23
  13.5 2.7 %collective-permute-start.5 = (bf16[4,160,128]{2,1,0:T(8,128)(2,1)S(1)}, bf16[4,160,128]{2,1,0:T(8,128)(2,1)S(1)}, u32[]{:S(2)}, u32[]{:S(2)}) collective-permute-start(bf16[4,160,128]{2,1,0:T(8,128)(2,1)S(1)} %near1.1.refs_5_.refs_2_.refs_3_), channel_id=1, source_target_pairs={{0,30},{1,3},{2,0},{3,5},{4,2},{5,7},{6,4},{7,9},{8,6},{9,11},{10,... | collective-permute-start | bytes 491528 | tf_op jit(solution)/shard_map/ppermute | solution.py:253
  16.2 0.0 collective-permute-done.2.refs_4_
  16.2 0.3 collective-permute-done.1.refs_3_.after.refs_0_
  16.5 0.5 %far1.1.here.refs_4_.refs_5_ = bf16[4,160,128]{2,1,0:T(8,128)(2,1)S(1)} custom-call(bf16[4,160,800]{2,1,0:T(8,128)(2,1)S(1)} %pack.4.refs_1_.refs_0_.packed, s32[12,6,8,128]{3,2,1,0:T(8,128)S(1)} %table.1.refs_1_, bf16[4,160,128]{2,1,0:T(8,128)(2,1)S(1)} %get-tuple-element.25.after.refs_2_.here.refs_5_, ...), custom_call_target="tpu_custom_call" | custom-call | bytes 1024 | tf_op jit(solution)/shard_map/far1/pallas_call | solution.py:23
  17.0 0.1 collective-permute-start.4
  17.1 0.5 %middle1.1.before.refs_3_.refs_4_.refs_0_ = bf16[4,160,128]{2,1,0:T(8,128)(2,1)S(1)} custom-call(bf16[4,160,800]{2,1,0:T(8,128)(2,1)S(1)} %pack.5.refs_3_.packed.refs_0_, s32[12,6,8,128]{3,2,1,0:T(8,128)S(1)} %table.1.refs_1_, bf16[4,160,128]{2,1,0:T(8,128)(2,1)S(1)} %get-tuple-element.22.refs_2_.here.before.refs_5_, ...), custom_call_target="tpu_custom_call" | custom-call | bytes 1024 | tf_op jit(solution)/shard_map/middle1/pallas_call | solution.py:23
  17.6 1.4 %collective-permute-done.5.after = bf16[4,160,128]{2,1,0:T(8,128)(2,1)S(1)} collective-permute-done((bf16[4,160,128]{2,1,0:T(8,128)(2,1)S(1)}, bf16[4,160,128]{2,1,0:T(8,128)(2,1)S(1)}, u32[]{:S(2)}, u32[]{:S(2)}) %collective-permute-start.5) | collective-permute-done | bytes 163872 | tf_op jit(solution)/shard_map/ppermute | solution.py:253
  19.1 0.5 %far2.1.refs_6_.after.refs_3_.refs_5_ = bf16[4,160,128]{2,1,0:T(8,128)(2,1)S(1)} custom-call(bf16[4,160,800]{2,1,0:T(8,128)(2,1)S(1)} %pack.4.refs_1_.refs_0_.packed, s32[12,6,8,128]{3,2,1,0:T(8,128)S(1)} %table.1.refs_1_, bf16[4,160,128]{2,1,0:T(8,128)(2,1)S(1)} %middle1.1.before.refs_3_.refs_4_.refs_0_, bf16[4,160,128]{2,1,0:T(8,128)(2,1)S(1)} %far1.1.here.refs_4_.refs_5_, ...), custom_call_target="tpu_custom_call" | custom-call | bytes 1024 | tf_op jit(solution)/shard_map/far2/pallas_call | solution.py:23
  19.6 0.1 collective-permute-start.7
  19.7 0.5 %middle2.1.refs_6_.here.refs_4_.refs_2_.refs_5_ = bf16[4,160,128]{2,1,0:T(8,128)(2,1)S(1)} custom-call(bf16[4,160,800]{2,1,0:T(8,128)(2,1)S(1)} %pack.5.refs_3_.packed.refs_0_, s32[12,6,8,128]{3,2,1,0:T(8,128)S(1)} %table.1.refs_1_, bf16[4,160,128]{2,1,0:T(8,128)(2,1)S(1)} %near1.1.refs_5_.refs_2_.refs_3_, ...), custom_call_target="tpu_custom_call" | custom-call | bytes 1024 | tf_op jit(solution)/shard_map/middle2/pallas_call | solution.py:23
  20.2 4.4 %collective-permute-done.4.refs_2_ = bf16[4,160,128]{2,1,0:T(8,128)(2,1)S(1)} collective-permute-done((bf16[4,160,128]{2,1,0:T(8,128)(2,1)S(1)}, bf16[4,160,128]{2,1,0:T(8,128)(2,1)S(1)}, u32[]{:S(2)}, u32[]{:S(2)}) %collective-permute-start.4) | collective-permute-done | bytes 163872 | tf_op jit(solution)/shard_map/ppermute | solution.py:253
  24.6 0.5 %near2.1.before.refs_3_.refs_5_ = bf16[4,160,128]{2,1,0:T(8,128)(2,1)S(1)} custom-call(bf16[4,160,800]{2,1,0:T(8,128)(2,1)S(1)} %pack.3.refs_1_.packed.refs_0_, s32[12,6,8,128]{3,2,1,0:T(8,128)S(1)} %table.1.refs_1_, bf16[4,160,128]{2,1,0:T(8,128)(2,1)S(1)} %collective-permute-done.4.refs_2_, bf16[4,160,128]{2,1,0:T(8,128)(2,1)S(1)} %near1.1.refs_5_.refs_2_.refs_3_, ...), custom_call_target="tpu_custom_call" | custom-call | bytes 1024 | tf_op jit(solution)/shard_map/near2/pallas_call | solution.py:23
  25.1 0.4 %collective-permute-start.6 = (bf16[4,160,128]{2,1,0:T(8,128)(2,1)S(1)}, bf16[4,160,128]{2,1,0:T(8,128)(2,1)S(1)}, u32[]{:S(2)}, u32[]{:S(2)}) collective-permute-start(bf16[4,160,128]{2,1,0:T(8,128)(2,1)S(1)} %near2.1.before.refs_3_.refs_5_), channel_id=1, source_target_pairs={{0,30},{1,3},{2,0},{3,5},{4,2},{5,7},{6,4},{7,9},{8,6},{9,11},{10,... | collective-permute-start | bytes 491528 | tf_op jit(solution)/shard_map/ppermute | solution.py:253
  25.5 0.5 %middle3.1.refs_6_.refs_2_.refs_3_.refs_4_ = bf16[4,160,128]{2,1,0:T(8,128)(2,1)S(1)} custom-call(bf16[4,160,800]{2,1,0:T(8,128)(2,1)S(1)} %pack.5.refs_3_.packed.refs_0_, s32[12,6,8,128]{3,2,1,0:T(8,128)S(1)} %table.1.refs_1_, bf16[4,160,128]{2,1,0:T(8,128)(2,1)S(1)} %near2.1.before.refs_3_.refs_5_, ...), custom_call_target="tpu_custom_call" | custom-call | bytes 1024 | tf_op jit(solution)/shard_map/middle3/pallas_call | solution.py:23
  26.0 1.4 %collective-permute-done.7.refs_2_ = bf16[4,160,128]{2,1,0:T(8,128)(2,1)S(1)} collective-permute-done((bf16[4,160,128]{2,1,0:T(8,128)(2,1)S(1)}, bf16[4,160,128]{2,1,0:T(8,128)(2,1)S(1)}, u32[]{:S(2)}, u32[]{:S(2)}) %collective-permute-start.7) | collective-permute-done | bytes 163872 | tf_op jit(solution)/shard_map/ppermute | solution.py:253
  27.5 0.5 %near3.1.refs_6_.refs_2_.refs_3_ = bf16[4,160,128]{2,1,0:T(8,128)(2,1)S(1)} custom-call(bf16[4,160,800]{2,1,0:T(8,128)(2,1)S(1)} %pack.3.refs_1_.packed.refs_0_, s32[12,6,8,128]{3,2,1,0:T(8,128)S(1)} %table.1.refs_1_, bf16[4,160,128]{2,1,0:T(8,128)(2,1)S(1)} %collective-permute-done.7.refs_2_, bf16[4,160,128]{2,1,0:T(8,128)(2,1)S(1)} %near2.1.before.refs_3_.refs_5_, ...), custom_call_target="tpu_custom_call" | custom-call | bytes 1024 | tf_op jit(solution)/shard_map/near3/pallas_call | solution.py:23
  28.0 0.1 collective-permute-start.9
  28.1 0.4 collective-permute-start.8
  28.5 0.0 collective-permute-done.6.refs_4_
  28.5 0.5 %far3.1.refs_3_.refs_4_ = bf16[4,160,128]{2,1,0:T(8,128)(2,1)S(1)} custom-call(bf16[4,160,800]{2,1,0:T(8,128)(2,1)S(1)} %pack.4.refs_1_.refs_0_.packed, s32[12,6,8,128]{3,2,1,0:T(8,128)S(1)} %table.1.refs_1_, bf16[4,160,128]{2,1,0:T(8,128)(2,1)S(1)} %middle2.1.refs_6_.here.refs_4_.refs_2_.refs_5_, ...), custom_call_target="tpu_custom_call" | custom-call | bytes 1024 | tf_op jit(solution)/shard_map/far3/pallas_call | solution.py:23
  29.0 0.2 collective-permute-start.11
  29.2 0.2 collective-permute-done.9.refs_4_
  29.5 0.5 %far4.2.refs_6_ = bf16[4,160,128]{2,1,0:T(8,128)(2,1)S(1)} custom-call(bf16[4,160,800]{2,1,0:T(8,128)(2,1)S(1)} %pack.4.refs_1_.refs_0_.packed, s32[12,6,8,128]{3,2,1,0:T(8,128)S(1)} %table.1.refs_1_, bf16[4,160,128]{2,1,0:T(8,128)(2,1)S(1)} %middle3.1.refs_6_.refs_2_.refs_3_.refs_4_, bf16[4,160,128]{2,1,0:T(8,128)(2,1)S(1)} %far3.1.refs_3_.refs_4_, ...), custom_call_target="tpu_custom_call" | custom-call | bytes 1024 | tf_op jit(solution)/shard_map/far4/pallas_call | solution.py:23
  30.0 0.6 %middle4.1 = (bf16[4,160,128]{2,1,0:T(8,128)(2,1)S(1)}, bf16[2,160,128]{2,1,0:T(8,128)(2,1)S(1)}) custom-call(bf16[4,160,800]{2,1,0:T(8,128)(2,1)S(1)} %pack.5.refs_3_.packed.refs_0_, s32[12,6,8,128]{3,2,1,0:T(8,128)S(1)} %table.1.refs_1_, bf16[4,160,128]{2,1,0:T(8,128)(2,1)S(1)} %near3.1.refs_6_.refs_2_.refs_3_, ...), custom_call_target="tpu_custom_call" | custom-call | bytes 1024 | tf_op jit(solution)/shard_map/middle4/pallas_call | solution.py:23
  30.6 1.6 %collective-permute-start.12 = (bf16[2,160,128]{2,1,0:T(8,128)(2,1)S(1)}, bf16[2,160,128]{2,1,0:T(8,128)(2,1)S(1)}, u32[]{:S(2)}, u32[]{:S(2)}) collective-permute-start(bf16[2,160,128]{2,1,0:T(8,128)(2,1)S(1)} %get-tuple-element.27), channel_id=1, source_target_pairs={{0,1},{1,0},{2,3},{3,2},{4,5},{5,4},{6,7},{7,6},{8,9},{9,8},{10,11... | collective-permute-start | bytes 245768 | tf_op jit(solution)/shard_map/ppermute | solution.py:266
  32.2 0.0 collective-permute-done.8.refs_4_
  32.2 2.1 %collective-permute-start.10 = (bf16[4,160,128]{2,1,0:T(8,128)(2,1)S(1)}, bf16[4,160,128]{2,1,0:T(8,128)(2,1)S(1)}, u32[]{:S(2)}, u32[]{:S(2)}) collective-permute-start(bf16[4,160,128]{2,1,0:T(8,128)(2,1)S(1)} %far4.3), channel_id=1, source_target_pairs={{0,1},{1,0},{2,3},{3,2},{4,5},{5,4},{6,7},{7,6},{8,9},{9,8},{10,11... | collective-permute-start | bytes 491528 | tf_op jit(solution)/shard_map/ppermute | solution.py:266
  34.3 2.3 %collective-permute-done.11.refs_2_ = bf16[4,160,128]{2,1,0:T(8,128)(2,1)S(1)} collective-permute-done((bf16[4,160,128]{2,1,0:T(8,128)(2,1)S(1)}, bf16[4,160,128]{2,1,0:T(8,128)(2,1)S(1)}, u32[]{:S(2)}, u32[]{:S(2)}) %collective-permute-start.11) | collective-permute-done | bytes 163872 | tf_op jit(solution)/shard_map/ppermute | solution.py:253
  36.6 0.0 collective-permute-done.12.refs_6_.half
  36.6 0.5 %near4.1.near = bf16[4,160,128]{2,1,0:T(8,128)(2,1)S(1)} custom-call(bf16[4,160,800]{2,1,0:T(8,128)(2,1)S(1)} %pack.3.refs_1_.packed.refs_0_, s32[12,6,8,128]{3,2,1,0:T(8,128)S(1)} %table.1.refs_1_, bf16[4,160,128]{2,1,0:T(8,128)(2,1)S(1)} %collective-permute-done.11.refs_2_, bf16[4,160,128]{2,1,0:T(8,128)(2,1)S(1)} %near3.1.refs_6_.refs_2_.refs_3_, ...), custom_call_target="tpu_custom_call" | custom-call | flops 20000000000 | bytes 1024 | tf_op jit(solution)/shard_map/near4/pallas_call | solution.py:23
  37.1 0.8 %own.1.refs_1_ = bf16[6,160,256]{2,1,0:T(8,128)(2,1)} custom-call(bf16[4,160,128]{2,1,0:T(8,128)(2,1)S(1)} %near4.1.near, bf16[4,160,128]{2,1,0:T(8,128)(2,1)S(1)} %get-tuple-element.28.middle, bf16[2,160,128]{2,1,0:T(8,128)(2,1)S(1)} %collective-permute-done.12.refs_6_.half), custom_call_target="tpu_custom_call" | custom-call | bytes 1024 | tf_op jit(solution)/shard_map/own/pallas_call | solution.py:23
  37.9 0.8 %collective-permute-done.10.refs_0_ = bf16[4,160,128]{2,1,0:T(8,128)(2,1)S(1)} collective-permute-done((bf16[4,160,128]{2,1,0:T(8,128)(2,1)S(1)}, bf16[4,160,128]{2,1,0:T(8,128)(2,1)S(1)}, u32[]{:S(2)}, u32[]{:S(2)}) %collective-permute-start.10) | collective-permute-done | bytes 163872 | tf_op jit(solution)/shard_map/ppermute | solution.py:266
  38.7 0.7 %others.1 = bf16[6,160,256]{2,1,0:T(8,128)(2,1)} custom-call(bf16[4,160,128]{2,1,0:T(8,128)(2,1)S(1)} %collective-permute-done.10.refs_0_, bf16[6,160,256]{2,1,0:T(8,128)(2,1)} %own.1.refs_1_), custom_call_target="tpu_custom_call", output_to_operand_aliasing={{}: (1, {})} | custom-call | bytes 1024 | tf_op jit(solution)/shard_map/others/pallas_call | solution.py:23
  (3 shorter events, 0.0 us)
Async XLA Ops:
  0.0 10.0 %slice-start = ((s8[4915200]{0:T(1024)(128)(4,1)}), s8[4194304]{0:T(1024)(128)(4,1)S(1)}, s32[]{:S(2)}) async-start(s8[4915200]{0:T(1024)(128)(4,1)} %bitcast.1), calls=%async_computation | async-start | bytes 8388608
  0.0 10.0 %slice-start.1 = ((s8[4915200]{0:T(1024)(128)(4,1)}), s8[720896]{0:T(1024)(128)(4,1)S(1)}, s32[]{:S(2)}) async-start(s8[4915200]{0:T(1024)(128)(4,1)} %bitcast.1), calls=%async_computation.1 | async-start | bytes 1441792
  1.6 9.3 %collective-permute-start = (bf16[2,160,128]{2,1,0:T(8,128)(2,1)S(1)}, bf16[2,160,128]{2,1,0:T(8,128)(2,1)S(1)}, u32[]{:S(2)}, u32[]{:S(2)}) collective-permute-start(bf16[2,160,128]{2,1,0:T(8,128)(2,1)S(1)} %get-tuple-element.24), channel_id=1, source_target_pairs={{0,1},{1,0},{2,3},{3,2},{4,5},{5,4},{6,7},{7,6},{8,9},{9,8},{10,11... | collective-permute-start | bytes 245768 | tf_op jit(solution)/shard_map/ppermute | solution.py:266
  4.6 8.3 %collective-permute-start.3 = (bf16[4,160,128]{2,1,0:T(8,128)(2,1)S(1)}, bf16[4,160,128]{2,1,0:T(8,128)(2,1)S(1)}, u32[]{:S(2)}, u32[]{:S(2)}) collective-permute-start(bf16[4,160,128]{2,1,0:T(8,128)(2,1)S(1)} %get-tuple-element.21.refs_3_.refs_2_), channel_id=1, source_target_pairs={{0,31},{1,2},{2,1},{3,4},{4,3},{5,6},{6,5},{7,8},{8,7},{9,10},{10,... | collective-permute-start | bytes 491528 | tf_op jit(solution)/shard_map/ppermute | solution.py:253
  8.6 7.7 %collective-permute-start.2 = (bf16[4,160,128]{2,1,0:T(8,128)(2,1)S(1)}, bf16[4,160,128]{2,1,0:T(8,128)(2,1)S(1)}, u32[]{:S(2)}, u32[]{:S(2)}) collective-permute-start(bf16[4,160,128]{2,1,0:T(8,128)(2,1)S(1)} %get-tuple-element.22.refs_2_.here.before.refs_5_), channel_id=1, source_target_pairs={{0,30},{1,3},{2,0},{3,5},{4,2},{5,7},{6,4},{7,9},{8,6},{9,11},{10,... | collective-permute-start | bytes 491528 | tf_op jit(solution)/shard_map/ppermute | solution.py:253
  11.0 5.6 %collective-permute-start.1 = (bf16[4,160,128]{2,1,0:T(8,128)(2,1)S(1)}, bf16[4,160,128]{2,1,0:T(8,128)(2,1)S(1)}, u32[]{:S(2)}, u32[]{:S(2)}) collective-permute-start(bf16[4,160,128]{2,1,0:T(8,128)(2,1)S(1)} %get-tuple-element.26), channel_id=1, source_target_pairs={{0,1},{1,0},{2,3},{3,2},{4,5},{5,4},{6,7},{7,6},{8,9},{9,8},{10,11... | collective-permute-start | bytes 491528 | tf_op jit(solution)/shard_map/ppermute | solution.py:266
  13.5 5.6 %collective-permute-start.5 = (bf16[4,160,128]{2,1,0:T(8,128)(2,1)S(1)}, bf16[4,160,128]{2,1,0:T(8,128)(2,1)S(1)}, u32[]{:S(2)}, u32[]{:S(2)}) collective-permute-start(bf16[4,160,128]{2,1,0:T(8,128)(2,1)S(1)} %near1.1.refs_5_.refs_2_.refs_3_), channel_id=1, source_target_pairs={{0,30},{1,3},{2,0},{3,5},{4,2},{5,7},{6,4},{7,9},{8,6},{9,11},{10,... | collective-permute-start | bytes 491528 | tf_op jit(solution)/shard_map/ppermute | solution.py:253
  17.0 7.5 %collective-permute-start.4 = (bf16[4,160,128]{2,1,0:T(8,128)(2,1)S(1)}, bf16[4,160,128]{2,1,0:T(8,128)(2,1)S(1)}, u32[]{:S(2)}, u32[]{:S(2)}) collective-permute-start(bf16[4,160,128]{2,1,0:T(8,128)(2,1)S(1)} %far1.1.here.refs_4_.refs_5_), channel_id=1, source_target_pairs={{0,2},{1,31},{2,4},{3,1},{4,6},{5,3},{6,8},{7,5},{8,10},{9,7},{10,... | collective-permute-start | bytes 491528 | tf_op jit(solution)/shard_map/ppermute | solution.py:253
  19.6 7.9 %collective-permute-start.7 = (bf16[4,160,128]{2,1,0:T(8,128)(2,1)S(1)}, bf16[4,160,128]{2,1,0:T(8,128)(2,1)S(1)}, u32[]{:S(2)}, u32[]{:S(2)}) collective-permute-start(bf16[4,160,128]{2,1,0:T(8,128)(2,1)S(1)} %far2.1.refs_6_.after.refs_3_.refs_5_), channel_id=1, source_target_pairs={{0,2},{1,31},{2,4},{3,1},{4,6},{5,3},{6,8},{7,5},{8,10},{9,7},{10,... | collective-permute-start | bytes 491528 | tf_op jit(solution)/shard_map/ppermute | solution.py:253
  25.1 3.4 %collective-permute-start.6 = (bf16[4,160,128]{2,1,0:T(8,128)(2,1)S(1)}, bf16[4,160,128]{2,1,0:T(8,128)(2,1)S(1)}, u32[]{:S(2)}, u32[]{:S(2)}) collective-permute-start(bf16[4,160,128]{2,1,0:T(8,128)(2,1)S(1)} %near2.1.before.refs_3_.refs_5_), channel_id=1, source_target_pairs={{0,30},{1,3},{2,0},{3,5},{4,2},{5,7},{6,4},{7,9},{8,6},{9,11},{10,... | collective-permute-start | bytes 491528 | tf_op jit(solution)/shard_map/ppermute | solution.py:253
  28.0 1.5 %collective-permute-start.9 = (bf16[4,160,128]{2,1,0:T(8,128)(2,1)S(1)}, bf16[4,160,128]{2,1,0:T(8,128)(2,1)S(1)}, u32[]{:S(2)}, u32[]{:S(2)}) collective-permute-start(bf16[4,160,128]{2,1,0:T(8,128)(2,1)S(1)} %near3.1.refs_6_.refs_2_.refs_3_), channel_id=1, source_target_pairs={{0,2},{1,3},{2,0},{3,1},{4,6},{5,7},{6,4},{7,5},{8,10},{9,11},{10,... | collective-permute-start | bytes 491528 | tf_op jit(solution)/shard_map/ppermute | solution.py:253
  28.1 4.1 %collective-permute-start.8 = (bf16[4,160,128]{2,1,0:T(8,128)(2,1)S(1)}, bf16[4,160,128]{2,1,0:T(8,128)(2,1)S(1)}, u32[]{:S(2)}, u32[]{:S(2)}) collective-permute-start(bf16[4,160,128]{2,1,0:T(8,128)(2,1)S(1)} %near3.1.refs_6_.refs_2_.refs_3_), channel_id=1, source_target_pairs={{0,30},{1,3},{2,0},{3,5},{4,2},{5,7},{6,4},{7,9},{8,6},{9,11},{10,... | collective-permute-start | bytes 491528 | tf_op jit(solution)/shard_map/ppermute | solution.py:253
  29.0 7.6 %collective-permute-start.11 = (bf16[4,160,128]{2,1,0:T(8,128)(2,1)S(1)}, bf16[4,160,128]{2,1,0:T(8,128)(2,1)S(1)}, u32[]{:S(2)}, u32[]{:S(2)}) collective-permute-start(bf16[4,160,128]{2,1,0:T(8,128)(2,1)S(1)} %far3.1.refs_3_.refs_4_), channel_id=1, source_target_pairs={{0,2},{1,31},{2,4},{3,1},{4,6},{5,3},{6,8},{7,5},{8,10},{9,7},{10,... | collective-permute-start | bytes 491528 | tf_op jit(solution)/shard_map/ppermute | solution.py:253
  30.6 6.0 %collective-permute-start.12 = (bf16[2,160,128]{2,1,0:T(8,128)(2,1)S(1)}, bf16[2,160,128]{2,1,0:T(8,128)(2,1)S(1)}, u32[]{:S(2)}, u32[]{:S(2)}) collective-permute-start(bf16[2,160,128]{2,1,0:T(8,128)(2,1)S(1)} %get-tuple-element.27), channel_id=1, source_target_pairs={{0,1},{1,0},{2,3},{3,2},{4,5},{5,4},{6,7},{7,6},{8,9},{9,8},{10,11... | collective-permute-start | bytes 245768 | tf_op jit(solution)/shard_map/ppermute | solution.py:266
  32.2 6.5 %collective-permute-start.10 = (bf16[4,160,128]{2,1,0:T(8,128)(2,1)S(1)}, bf16[4,160,128]{2,1,0:T(8,128)(2,1)S(1)}, u32[]{:S(2)}, u32[]{:S(2)}) collective-permute-start(bf16[4,160,128]{2,1,0:T(8,128)(2,1)S(1)} %far4.3), channel_id=1, source_target_pairs={{0,1},{1,0},{2,3},{3,2},{4,5},{5,4},{6,7},{7,6},{8,9},{9,8},{10,11... | collective-permute-start | bytes 491528 | tf_op jit(solution)/shard_map/ppermute | solution.py:266

commit v8 on v7

--- a/solution.py
+++ b/solution.py
@@ -9,6 +9,7 @@
 
 DEG = 4
 FULL = 128
+DEPTH = 512
 LONG, SHORT = 20 * 10**9, 10**9
 
 center_shift = 0.2
@@ -170,8 +171,11 @@
     couplings = table.shape[1] - 1
     for e in range(width):
         *at, end = [table[first + e, k, 0, 0] for k in range(couplings + 1)]
-        fields = [window[i, :FULL] for i in at] + [window[i, FULL:] for i in at]
-        image = jnp.dot(packed[e], jnp.concatenate(fields, axis=0), preferred_element_type=jnp.float32)
+        fields = jnp.concatenate([window[i, :FULL] for i in at] + [window[i, FULL:] for i in at], axis=0)
+        image = jnp.zeros((rows, lanes), jnp.float32)
+        for k in range(0, fields.shape[0], DEPTH):
+            part = packed[e, :, k : k + DEPTH]
+            image += jnp.dot(part, fields[k : k + DEPTH], preferred_element_type=jnp.float32)
         image = jnp.where(rows_below(end, rows, lanes), image, 0.0)
         value = factor * (image - center_shift * here[e].astype(jnp.float32)) / half_span
         if with_prev:

time: 39.6 us -> 39.5 us (level)
  transfers between devices with their start and end apart: 13 -> 13, of which waited for: 8 -> 8; matrix products, arithmetic and copies ran while one was open for 0% -> 0% of each run, Pallas kernels for 22% -> 21%
where the time goes in v8:
time: 39.5 us; the launch traced here: 39.3 us
  starting transfers between devices  16.3 us (41%)
  waiting for transfers between devices  12.2 us (31%)
  Pallas kernels  10.6 us (27%)
    ppermute x9, waiting for transfers between devices, permuted(): return lax.ppermute(x, ('elem', 'state'), moves)  11.1 us
    pallas_call x22, Pallas kernels, call(): pl.pallas_call(kernel, out_shape=outs, in_specs=ins, out_specs=out_specs...  10.6 us
    ppermute x9, starting transfers between devices, permuted(): return lax.ppermute(x, ('elem', 'state'), moves)  8.67 us
    ppermute x4, starting transfers between devices, swapped(): lax.ppermute(x, 'state', [(i, (i + k + 1) % shards) for i in range(shards)])  7.61 us
    ppermute x4, waiting for transfers between devices, swapped(): lax.ppermute(x, 'state', [(i, (i + k + 1) % shards) for i in range(shards)])  1.17 us
  transfers between devices with their start and end apart: 13, of which 8 were waited for; matrix products, arithmetic and copies ran while one was open for 0% of the time, Pallas kernels for 21%

profile of v8, /device:TPU:0, one launch (start us, length us, event | category | flops | bytes accessed | tf_op | source)
XLA Modules:
  0.0 39.3 jit_solution(8487768483868031756)
XLA Ops:
  0.0 0.0 slice-start
  0.0 0.0 slice-start.1
  0.0 1.6 %fetch.1 = (bf16[4,160,128]{2,1,0:T(8,128)(2,1)S(1)}, bf16[2,160,128]{2,1,0:T(8,128)(2,1)S(1)}, bf16[6,160,256]{2,1,0:T(8,128)(2,1)S(1)}, bf16[256,256]{1,0:T(8,...) custom-call(bf16[6,160,256]{2,1,0:T(8,128)(2,1)} %orbitals.1, bf16[256,256]{1,0:T(8,128)(2,1)} %rotation.1, s32[12]{0:T(128)} %counts.1, ...), custom_call_target="tpu_custom_call" | custom-call | flops 20000000000 | bytes 1024 | tf_op jit(solution)/shard_map/fetch/pallas_call | solution.py:24
  1.6 3.0 %collective-permute-start = (bf16[2,160,128]{2,1,0:T(8,128)(2,1)S(1)}, bf16[2,160,128]{2,1,0:T(8,128)(2,1)S(1)}, u32[]{:S(2)}, u32[]{:S(2)}) collective-permute-start(bf16[2,160,128]{2,1,0:T(8,128)(2,1)S(1)} %get-tuple-element.24), channel_id=1, source_target_pairs={{0,1},{1,0},{2,3},{3,2},{4,5},{5,4},{6,7},{7,6},{8,9},{9,8},{10,11... | collective-permute-start | bytes 245768 | tf_op jit(solution)/shard_map/ppermute | solution.py:270
  4.6 3.6 %collective-permute-start.3 = (bf16[4,160,128]{2,1,0:T(8,128)(2,1)S(1)}, bf16[4,160,128]{2,1,0:T(8,128)(2,1)S(1)}, u32[]{:S(2)}, u32[]{:S(2)}) collective-permute-start(bf16[4,160,128]{2,1,0:T(8,128)(2,1)S(1)} %get-tuple-element.21.refs_3_.refs_2_), channel_id=1, source_target_pairs={{0,31},{1,2},{2,1},{3,4},{4,3},{5,6},{6,5},{7,8},{8,7},{9,10},{10,... | collective-permute-start | bytes 491528 | tf_op jit(solution)/shard_map/ppermute | solution.py:257
  8.3 0.3 rotate_in.1
  8.6 1.2 %collective-permute-start.2 = (bf16[4,160,128]{2,1,0:T(8,128)(2,1)S(1)}, bf16[4,160,128]{2,1,0:T(8,128)(2,1)S(1)}, u32[]{:S(2)}, u32[]{:S(2)}) collective-permute-start(bf16[4,160,128]{2,1,0:T(8,128)(2,1)S(1)} %get-tuple-element.22.refs_2_.here.before.refs_5_), channel_id=1, source_target_pairs={{0,30},{1,3},{2,0},{3,5},{4,2},{5,7},{6,4},{7,9},{8,6},{9,11},{10,... | collective-permute-start | bytes 491528 | tf_op jit(solution)/shard_map/ppermute | solution.py:257
  9.7 0.3 table.1.refs_1_
  10.0 0.0 slice-done
  10.0 0.0 slice-done.1
  10.1 0.3 pack.3.refs_1_.packed.refs_0_
  10.3 0.3 pack.4.refs_1_.refs_0_.packed
  10.6 0.3 pack.5.refs_3_.packed.refs_0_
  10.9 0.0 collective-permute-done.refs_1_
  11.0 0.9 %collective-permute-start.1 = (bf16[4,160,128]{2,1,0:T(8,128)(2,1)S(1)}, bf16[4,160,128]{2,1,0:T(8,128)(2,1)S(1)}, u32[]{:S(2)}, u32[]{:S(2)}) collective-permute-start(bf16[4,160,128]{2,1,0:T(8,128)(2,1)S(1)} %get-tuple-element.26), channel_id=1, source_target_pairs={{0,1},{1,0},{2,3},{3,2},{4,5},{5,4},{6,7},{7,6},{8,9},{9,8},{10,11... | collective-permute-start | bytes 491528 | tf_op jit(solution)/shard_map/ppermute | solution.py:270
  11.8 1.2 %collective-permute-done.3.before = bf16[4,160,128]{2,1,0:T(8,128)(2,1)S(1)} collective-permute-done((bf16[4,160,128]{2,1,0:T(8,128)(2,1)S(1)}, bf16[4,160,128]{2,1,0:T(8,128)(2,1)S(1)}, u32[]{:S(2)}, u32[]{:S(2)}) %collective-permute-start.3) | collective-permute-done | bytes 163872 | tf_op jit(solution)/shard_map/ppermute | solution.py:257
  13.0 0.5 %near1.1.refs_5_.refs_2_.refs_3_ = bf16[4,160,128]{2,1,0:T(8,128)(2,1)S(1)} custom-call(bf16[4,160,800]{2,1,0:T(8,128)(2,1)S(1)} %pack.3.refs_1_.packed.refs_0_, s32[12,6,8,128]{3,2,1,0:T(8,128)S(1)} %table.1.refs_1_, bf16[4,160,128]{2,1,0:T(8,128)(2,1)S(1)} %collective-permute-done.3.before, ...), custom_call_target="tpu_custom_call" | custom-call | bytes 1024 | tf_op jit(solution)/shard_map/near1/pallas_call | solution.py:24
  13.5 2.7 %collective-permute-start.5 = (bf16[4,160,128]{2,1,0:T(8,128)(2,1)S(1)}, bf16[4,160,128]{2,1,0:T(8,128)(2,1)S(1)}, u32[]{:S(2)}, u32[]{:S(2)}) collective-permute-start(bf16[4,160,128]{2,1,0:T(8,128)(2,1)S(1)} %near1.1.refs_5_.refs_2_.refs_3_), channel_id=1, source_target_pairs={{0,30},{1,3},{2,0},{3,5},{4,2},{5,7},{6,4},{7,9},{8,6},{9,11},{10,... | collective-permute-start | bytes 491528 | tf_op jit(solution)/shard_map/ppermute | solution.py:257
  16.2 0.0 collective-permute-done.2.refs_4_
  16.2 0.3 collective-permute-done.1.refs_3_.after.refs_0_
  16.5 0.5 %far1.1.here.refs_4_.refs_5_ = bf16[4,160,128]{2,1,0:T(8,128)(2,1)S(1)} custom-call(bf16[4,160,800]{2,1,0:T(8,128)(2,1)S(1)} %pack.4.refs_1_.refs_0_.packed, s32[12,6,8,128]{3,2,1,0:T(8,128)S(1)} %table.1.refs_1_, bf16[4,160,128]{2,1,0:T(8,128)(2,1)S(1)} %get-tuple-element.25.after.refs_2_.here.refs_5_, ...), custom_call_target="tpu_custom_call" | custom-call | bytes 1024 | tf_op jit(solution)/shard_map/far1/pallas_call | solution.py:24
  17.0 0.1 collective-permute-start.4
  17.1 0.5 %middle1.1.before.refs_3_.refs_4_.refs_0_ = bf16[4,160,128]{2,1,0:T(8,128)(2,1)S(1)} custom-call(bf16[4,160,800]{2,1,0:T(8,128)(2,1)S(1)} %pack.5.refs_3_.packed.refs_0_, s32[12,6,8,128]{3,2,1,0:T(8,128)S(1)} %table.1.refs_1_, bf16[4,160,128]{2,1,0:T(8,128)(2,1)S(1)} %get-tuple-element.22.refs_2_.here.before.refs_5_, ...), custom_call_target="tpu_custom_call" | custom-call | bytes 1024 | tf_op jit(solution)/shard_map/middle1/pallas_call | solution.py:24
  17.6 1.5 %collective-permute-done.5.after = bf16[4,160,128]{2,1,0:T(8,128)(2,1)S(1)} collective-permute-done((bf16[4,160,128]{2,1,0:T(8,128)(2,1)S(1)}, bf16[4,160,128]{2,1,0:T(8,128)(2,1)S(1)}, u32[]{:S(2)}, u32[]{:S(2)}) %collective-permute-start.5) | collective-permute-done | bytes 163872 | tf_op jit(solution)/shard_map/ppermute | solution.py:257
  19.0 0.5 %far2.1.refs_6_.after.refs_3_.refs_5_ = bf16[4,160,128]{2,1,0:T(8,128)(2,1)S(1)} custom-call(bf16[4,160,800]{2,1,0:T(8,128)(2,1)S(1)} %pack.4.refs_1_.refs_0_.packed, s32[12,6,8,128]{3,2,1,0:T(8,128)S(1)} %table.1.refs_1_, bf16[4,160,128]{2,1,0:T(8,128)(2,1)S(1)} %middle1.1.before.refs_3_.refs_4_.refs_0_, bf16[4,160,128]{2,1,0:T(8,128)(2,1)S(1)} %far1.1.here.refs_4_.refs_5_, ...), custom_call_target="tpu_custom_call" | custom-call | bytes 1024 | tf_op jit(solution)/shard_map/far2/pallas_call | solution.py:24
  19.6 0.1 collective-permute-start.7
  19.6 0.5 %middle2.1.refs_6_.here.refs_4_.refs_2_.refs_5_ = bf16[4,160,128]{2,1,0:T(8,128)(2,1)S(1)} custom-call(bf16[4,160,800]{2,1,0:T(8,128)(2,1)S(1)} %pack.5.refs_3_.packed.refs_0_, s32[12,6,8,128]{3,2,1,0:T(8,128)S(1)} %table.1.refs_1_, bf16[4,160,128]{2,1,0:T(8,128)(2,1)S(1)} %near1.1.refs_5_.refs_2_.refs_3_, ...), custom_call_target="tpu_custom_call" | custom-call | bytes 1024 | tf_op jit(solution)/shard_map/middle2/pallas_call | solution.py:24
  20.1 4.4 %collective-permute-done.4.refs_2_ = bf16[4,160,128]{2,1,0:T(8,128)(2,1)S(1)} collective-permute-done((bf16[4,160,128]{2,1,0:T(8,128)(2,1)S(1)}, bf16[4,160,128]{2,1,0:T(8,128)(2,1)S(1)}, u32[]{:S(2)}, u32[]{:S(2)}) %collective-permute-start.4) | collective-permute-done | bytes 163872 | tf_op jit(solution)/shard_map/ppermute | solution.py:257
  24.6 0.5 %near2.1.before.refs_3_.refs_5_ = bf16[4,160,128]{2,1,0:T(8,128)(2,1)S(1)} custom-call(bf16[4,160,800]{2,1,0:T(8,128)(2,1)S(1)} %pack.3.refs_1_.packed.refs_0_, s32[12,6,8,128]{3,2,1,0:T(8,128)S(1)} %table.1.refs_1_, bf16[4,160,128]{2,1,0:T(8,128)(2,1)S(1)} %collective-permute-done.4.refs_2_, bf16[4,160,128]{2,1,0:T(8,128)(2,1)S(1)} %near1.1.refs_5_.refs_2_.refs_3_, ...), custom_call_target="tpu_custom_call" | custom-call | bytes 1024 | tf_op jit(solution)/shard_map/near2/pallas_call | solution.py:24
  25.1 0.3 collective-permute-start.6
  25.4 0.5 %middle3.1.refs_6_.refs_2_.refs_3_.refs_4_ = bf16[4,160,128]{2,1,0:T(8,128)(2,1)S(1)} custom-call(bf16[4,160,800]{2,1,0:T(8,128)(2,1)S(1)} %pack.5.refs_3_.packed.refs_0_, s32[12,6,8,128]{3,2,1,0:T(8,128)S(1)} %table.1.refs_1_, bf16[4,160,128]{2,1,0:T(8,128)(2,1)S(1)} %near2.1.before.refs_3_.refs_5_, ...), custom_call_target="tpu_custom_call" | custom-call | bytes 1024 | tf_op jit(solution)/shard_map/middle3/pallas_call | solution.py:24
  25.9 1.5 %collective-permute-done.7.refs_2_ = bf16[4,160,128]{2,1,0:T(8,128)(2,1)S(1)} collective-permute-done((bf16[4,160,128]{2,1,0:T(8,128)(2,1)S(1)}, bf16[4,160,128]{2,1,0:T(8,128)(2,1)S(1)}, u32[]{:S(2)}, u32[]{:S(2)}) %collective-permute-start.7) | collective-permute-done | bytes 163872 | tf_op jit(solution)/shard_map/ppermute | solution.py:257
  27.4 0.5 %near3.1.refs_6_.refs_2_.refs_3_ = bf16[4,160,128]{2,1,0:T(8,128)(2,1)S(1)} custom-call(bf16[4,160,800]{2,1,0:T(8,128)(2,1)S(1)} %pack.3.refs_1_.packed.refs_0_, s32[12,6,8,128]{3,2,1,0:T(8,128)S(1)} %table.1.refs_1_, bf16[4,160,128]{2,1,0:T(8,128)(2,1)S(1)} %collective-permute-done.7.refs_2_, bf16[4,160,128]{2,1,0:T(8,128)(2,1)S(1)} %near2.1.before.refs_3_.refs_5_, ...), custom_call_target="tpu_custom_call" | custom-call | bytes 1024 | tf_op jit(solution)/shard_map/near3/pallas_call | solution.py:24
  27.9 0.1 collective-permute-start.9
  28.0 0.4 %collective-permute-start.8 = (bf16[4,160,128]{2,1,0:T(8,128)(2,1)S(1)}, bf16[4,160,128]{2,1,0:T(8,128)(2,1)S(1)}, u32[]{:S(2)}, u32[]{:S(2)}) collective-permute-start(bf16[4,160,128]{2,1,0:T(8,128)(2,1)S(1)} %near3.1.refs_6_.refs_2_.refs_3_), channel_id=1, source_target_pairs={{0,30},{1,3},{2,0},{3,5},{4,2},{5,7},{6,4},{7,9},{8,6},{9,11},{10,... | collective-permute-start | bytes 491528 | tf_op jit(solution)/shard_map/ppermute | solution.py:257
  28.4 0.0 collective-permute-done.6.refs_4_
  28.4 0.5 %far3.1.refs_3_.refs_4_ = bf16[4,160,128]{2,1,0:T(8,128)(2,1)S(1)} custom-call(bf16[4,160,800]{2,1,0:T(8,128)(2,1)S(1)} %pack.4.refs_1_.refs_0_.packed, s32[12,6,8,128]{3,2,1,0:T(8,128)S(1)} %table.1.refs_1_, bf16[4,160,128]{2,1,0:T(8,128)(2,1)S(1)} %middle2.1.refs_6_.here.refs_4_.refs_2_.refs_5_, ...), custom_call_target="tpu_custom_call" | custom-call | bytes 1024 | tf_op jit(solution)/shard_map/far3/pallas_call | solution.py:24
  28.9 0.2 collective-permute-start.11
  29.1 0.3 collective-permute-done.9.refs_4_
  29.4 0.5 %far4.2.refs_6_ = bf16[4,160,128]{2,1,0:T(8,128)(2,1)S(1)} custom-call(bf16[4,160,800]{2,1,0:T(8,128)(2,1)S(1)} %pack.4.refs_1_.refs_0_.packed, s32[12,6,8,128]{3,2,1,0:T(8,128)S(1)} %table.1.refs_1_, bf16[4,160,128]{2,1,0:T(8,128)(2,1)S(1)} %middle3.1.refs_6_.refs_2_.refs_3_.refs_4_, bf16[4,160,128]{2,1,0:T(8,128)(2,1)S(1)} %far3.1.refs_3_.refs_4_, ...), custom_call_target="tpu_custom_call" | custom-call | bytes 1024 | tf_op jit(solution)/shard_map/far4/pallas_call | solution.py:24
  29.9 0.6 %middle4.1 = (bf16[4,160,128]{2,1,0:T(8,128)(2,1)S(1)}, bf16[2,160,128]{2,1,0:T(8,128)(2,1)S(1)}) custom-call(bf16[4,160,800]{2,1,0:T(8,128)(2,1)S(1)} %pack.5.refs_3_.packed.refs_0_, s32[12,6,8,128]{3,2,1,0:T(8,128)S(1)} %table.1.refs_1_, bf16[4,160,128]{2,1,0:T(8,128)(2,1)S(1)} %near3.1.refs_6_.refs_2_.refs_3_, ...), custom_call_target="tpu_custom_call" | custom-call | bytes 1024 | tf_op jit(solution)/shard_map/middle4/pallas_call | solution.py:24
  30.5 1.6 %collective-permute-start.12 = (bf16[2,160,128]{2,1,0:T(8,128)(2,1)S(1)}, bf16[2,160,128]{2,1,0:T(8,128)(2,1)S(1)}, u32[]{:S(2)}, u32[]{:S(2)}) collective-permute-start(bf16[2,160,128]{2,1,0:T(8,128)(2,1)S(1)} %get-tuple-element.27), channel_id=1, source_target_pairs={{0,1},{1,0},{2,3},{3,2},{4,5},{5,4},{6,7},{7,6},{8,9},{9,8},{10,11... | collective-permute-start | bytes 245768 | tf_op jit(solution)/shard_map/ppermute | solution.py:270
  32.0 0.0 collective-permute-done.8.refs_4_
  32.1 2.1 %collective-permute-start.10 = (bf16[4,160,128]{2,1,0:T(8,128)(2,1)S(1)}, bf16[4,160,128]{2,1,0:T(8,128)(2,1)S(1)}, u32[]{:S(2)}, u32[]{:S(2)}) collective-permute-start(bf16[4,160,128]{2,1,0:T(8,128)(2,1)S(1)} %far4.3), channel_id=1, source_target_pairs={{0,1},{1,0},{2,3},{3,2},{4,5},{5,4},{6,7},{7,6},{8,9},{9,8},{10,11... | collective-permute-start | bytes 491528 | tf_op jit(solution)/shard_map/ppermute | solution.py:270
  34.2 2.3 %collective-permute-done.11.refs_2_ = bf16[4,160,128]{2,1,0:T(8,128)(2,1)S(1)} collective-permute-done((bf16[4,160,128]{2,1,0:T(8,128)(2,1)S(1)}, bf16[4,160,128]{2,1,0:T(8,128)(2,1)S(1)}, u32[]{:S(2)}, u32[]{:S(2)}) %collective-permute-start.11) | collective-permute-done | bytes 163872 | tf_op jit(solution)/shard_map/ppermute | solution.py:257
  36.4 0.0 collective-permute-done.12.refs_6_.half
  36.5 0.5 %near4.1.near = bf16[4,160,128]{2,1,0:T(8,128)(2,1)S(1)} custom-call(bf16[4,160,800]{2,1,0:T(8,128)(2,1)S(1)} %pack.3.refs_1_.packed.refs_0_, s32[12,6,8,128]{3,2,1,0:T(8,128)S(1)} %table.1.refs_1_, bf16[4,160,128]{2,1,0:T(8,128)(2,1)S(1)} %collective-permute-done.11.refs_2_, bf16[4,160,128]{2,1,0:T(8,128)(2,1)S(1)} %near3.1.refs_6_.refs_2_.refs_3_, ...), custom_call_target="tpu_custom_call" | custom-call | flops 20000000000 | bytes 1024 | tf_op jit(solution)/shard_map/near4/pallas_call | solution.py:24
  37.0 0.8 %own.1.refs_1_ = bf16[6,160,256]{2,1,0:T(8,128)(2,1)} custom-call(bf16[4,160,128]{2,1,0:T(8,128)(2,1)S(1)} %near4.1.near, bf16[4,160,128]{2,1,0:T(8,128)(2,1)S(1)} %get-tuple-element.28.middle, bf16[2,160,128]{2,1,0:T(8,128)(2,1)S(1)} %collective-permute-done.12.refs_6_.half), custom_call_target="tpu_custom_call" | custom-call | bytes 1024 | tf_op jit(solution)/shard_map/own/pallas_call | solution.py:24
  37.7 0.9 %collective-permute-done.10.refs_0_ = bf16[4,160,128]{2,1,0:T(8,128)(2,1)S(1)} collective-permute-done((bf16[4,160,128]{2,1,0:T(8,128)(2,1)S(1)}, bf16[4,160,128]{2,1,0:T(8,128)(2,1)S(1)}, u32[]{:S(2)}, u32[]{:S(2)}) %collective-permute-start.10) | collective-permute-done | bytes 163872 | tf_op jit(solution)/shard_map/ppermute | solution.py:270
  38.6 0.7 %others.1 = bf16[6,160,256]{2,1,0:T(8,128)(2,1)} custom-call(bf16[4,160,128]{2,1,0:T(8,128)(2,1)S(1)} %collective-permute-done.10.refs_0_, bf16[6,160,256]{2,1,0:T(8,128)(2,1)} %own.1.refs_1_), custom_call_target="tpu_custom_call", output_to_operand_aliasing={{}: (1, {})} | custom-call | bytes 1024 | tf_op jit(solution)/shard_map/others/pallas_call | solution.py:24
  (3 shorter events, 0.0 us)
Async XLA Ops:
  0.0 10.0 %slice-start = ((s8[4915200]{0:T(1024)(128)(4,1)}), s8[4194304]{0:T(1024)(128)(4,1)S(1)}, s32[]{:S(2)}) async-start(s8[4915200]{0:T(1024)(128)(4,1)} %bitcast.1), calls=%async_computation | async-start | bytes 8388608
  0.0 10.0 %slice-start.1 = ((s8[4915200]{0:T(1024)(128)(4,1)}), s8[720896]{0:T(1024)(128)(4,1)S(1)}, s32[]{:S(2)}) async-start(s8[4915200]{0:T(1024)(128)(4,1)} %bitcast.1), calls=%async_computation.1 | async-start | bytes 1441792
  1.6 9.3 %collective-permute-start = (bf16[2,160,128]{2,1,0:T(8,128)(2,1)S(1)}, bf16[2,160,128]{2,1,0:T(8,128)(2,1)S(1)}, u32[]{:S(2)}, u32[]{:S(2)}) collective-permute-start(bf16[2,160,128]{2,1,0:T(8,128)(2,1)S(1)} %get-tuple-element.24), channel_id=1, source_target_pairs={{0,1},{1,0},{2,3},{3,2},{4,5},{5,4},{6,7},{7,6},{8,9},{9,8},{10,11... | collective-permute-start | bytes 245768 | tf_op jit(solution)/shard_map/ppermute | solution.py:270
  4.6 8.3 %collective-permute-start.3 = (bf16[4,160,128]{2,1,0:T(8,128)(2,1)S(1)}, bf16[4,160,128]{2,1,0:T(8,128)(2,1)S(1)}, u32[]{:S(2)}, u32[]{:S(2)}) collective-permute-start(bf16[4,160,128]{2,1,0:T(8,128)(2,1)S(1)} %get-tuple-element.21.refs_3_.refs_2_), channel_id=1, source_target_pairs={{0,31},{1,2},{2,1},{3,4},{4,3},{5,6},{6,5},{7,8},{8,7},{9,10},{10,... | collective-permute-start | bytes 491528 | tf_op jit(solution)/shard_map/ppermute | solution.py:257
  8.6 7.7 %collective-permute-start.2 = (bf16[4,160,128]{2,1,0:T(8,128)(2,1)S(1)}, bf16[4,160,128]{2,1,0:T(8,128)(2,1)S(1)}, u32[]{:S(2)}, u32[]{:S(2)}) collective-permute-start(bf16[4,160,128]{2,1,0:T(8,128)(2,1)S(1)} %get-tuple-element.22.refs_2_.here.before.refs_5_), channel_id=1, source_target_pairs={{0,30},{1,3},{2,0},{3,5},{4,2},{5,7},{6,4},{7,9},{8,6},{9,11},{10,... | collective-permute-start | bytes 491528 | tf_op jit(solution)/shard_map/ppermute | solution.py:257
  11.0 5.6 %collective-permute-start.1 = (bf16[4,160,128]{2,1,0:T(8,128)(2,1)S(1)}, bf16[4,160,128]{2,1,0:T(8,128)(2,1)S(1)}, u32[]{:S(2)}, u32[]{:S(2)}) collective-permute-start(bf16[4,160,128]{2,1,0:T(8,128)(2,1)S(1)} %get-tuple-element.26), channel_id=1, source_target_pairs={{0,1},{1,0},{2,3},{3,2},{4,5},{5,4},{6,7},{7,6},{8,9},{9,8},{10,11... | collective-permute-start | bytes 491528 | tf_op jit(solution)/shard_map/ppermute | solution.py:270
  13.5 5.6 %collective-permute-start.5 = (bf16[4,160,128]{2,1,0:T(8,128)(2,1)S(1)}, bf16[4,160,128]{2,1,0:T(8,128)(2,1)S(1)}, u32[]{:S(2)}, u32[]{:S(2)}) collective-permute-start(bf16[4,160,128]{2,1,0:T(8,128)(2,1)S(1)} %near1.1.refs_5_.refs_2_.refs_3_), channel_id=1, source_target_pairs={{0,30},{1,3},{2,0},{3,5},{4,2},{5,7},{6,4},{7,9},{8,6},{9,11},{10,... | collective-permute-start | bytes 491528 | tf_op jit(solution)/shard_map/ppermute | solution.py:257
  17.0 7.5 %collective-permute-start.4 = (bf16[4,160,128]{2,1,0:T(8,128)(2,1)S(1)}, bf16[4,160,128]{2,1,0:T(8,128)(2,1)S(1)}, u32[]{:S(2)}, u32[]{:S(2)}) collective-permute-start(bf16[4,160,128]{2,1,0:T(8,128)(2,1)S(1)} %far1.1.here.refs_4_.refs_5_), channel_id=1, source_target_pairs={{0,2},{1,31},{2,4},{3,1},{4,6},{5,3},{6,8},{7,5},{8,10},{9,7},{10,... | collective-permute-start | bytes 491528 | tf_op jit(solution)/shard_map/ppermute | solution.py:257
  19.6 7.9 %collective-permute-start.7 = (bf16[4,160,128]{2,1,0:T(8,128)(2,1)S(1)}, bf16[4,160,128]{2,1,0:T(8,128)(2,1)S(1)}, u32[]{:S(2)}, u32[]{:S(2)}) collective-permute-start(bf16[4,160,128]{2,1,0:T(8,128)(2,1)S(1)} %far2.1.refs_6_.after.refs_3_.refs_5_), channel_id=1, source_target_pairs={{0,2},{1,31},{2,4},{3,1},{4,6},{5,3},{6,8},{7,5},{8,10},{9,7},{10,... | collective-permute-start | bytes 491528 | tf_op jit(solution)/shard_map/ppermute | solution.py:257
  25.1 3.4 %collective-permute-start.6 = (bf16[4,160,128]{2,1,0:T(8,128)(2,1)S(1)}, bf16[4,160,128]{2,1,0:T(8,128)(2,1)S(1)}, u32[]{:S(2)}, u32[]{:S(2)}) collective-permute-start(bf16[4,160,128]{2,1,0:T(8,128)(2,1)S(1)} %near2.1.before.refs_3_.refs_5_), channel_id=1, source_target_pairs={{0,30},{1,3},{2,0},{3,5},{4,2},{5,7},{6,4},{7,9},{8,6},{9,11},{10,... | collective-permute-start | bytes 491528 | tf_op jit(solution)/shard_map/ppermute | solution.py:257
  27.9 1.5 %collective-permute-start.9 = (bf16[4,160,128]{2,1,0:T(8,128)(2,1)S(1)}, bf16[4,160,128]{2,1,0:T(8,128)(2,1)S(1)}, u32[]{:S(2)}, u32[]{:S(2)}) collective-permute-start(bf16[4,160,128]{2,1,0:T(8,128)(2,1)S(1)} %near3.1.refs_6_.refs_2_.refs_3_), channel_id=1, source_target_pairs={{0,2},{1,3},{2,0},{3,1},{4,6},{5,7},{6,4},{7,5},{8,10},{9,11},{10,... | collective-permute-start | bytes 491528 | tf_op jit(solution)/shard_map/ppermute | solution.py:257
  28.0 4.0 %collective-permute-start.8 = (bf16[4,160,128]{2,1,0:T(8,128)(2,1)S(1)}, bf16[4,160,128]{2,1,0:T(8,128)(2,1)S(1)}, u32[]{:S(2)}, u32[]{:S(2)}) collective-permute-start(bf16[4,160,128]{2,1,0:T(8,128)(2,1)S(1)} %near3.1.refs_6_.refs_2_.refs_3_), channel_id=1, source_target_pairs={{0,30},{1,3},{2,0},{3,5},{4,2},{5,7},{6,4},{7,9},{8,6},{9,11},{10,... | collective-permute-start | bytes 491528 | tf_op jit(solution)/shard_map/ppermute | solution.py:257
  28.9 7.5 %collective-permute-start.11 = (bf16[4,160,128]{2,1,0:T(8,128)(2,1)S(1)}, bf16[4,160,128]{2,1,0:T(8,128)(2,1)S(1)}, u32[]{:S(2)}, u32[]{:S(2)}) collective-permute-start(bf16[4,160,128]{2,1,0:T(8,128)(2,1)S(1)} %far3.1.refs_3_.refs_4_), channel_id=1, source_target_pairs={{0,2},{1,31},{2,4},{3,1},{4,6},{5,3},{6,8},{7,5},{8,10},{9,7},{10,... | collective-permute-start | bytes 491528 | tf_op jit(solution)/shard_map/ppermute | solution.py:257
  30.5 6.0 %collective-permute-start.12 = (bf16[2,160,128]{2,1,0:T(8,128)(2,1)S(1)}, bf16[2,160,128]{2,1,0:T(8,128)(2,1)S(1)}, u32[]{:S(2)}, u32[]{:S(2)}) collective-permute-start(bf16[2,160,128]{2,1,0:T(8,128)(2,1)S(1)} %get-tuple-element.27), channel_id=1, source_target_pairs={{0,1},{1,0},{2,3},{3,2},{4,5},{5,4},{6,7},{7,6},{8,9},{9,8},{10,11... | collective-permute-start | bytes 245768 | tf_op jit(solution)/shard_map/ppermute | solution.py:270
  32.1 6.5 %collective-permute-start.10 = (bf16[4,160,128]{2,1,0:T(8,128)(2,1)S(1)}, bf16[4,160,128]{2,1,0:T(8,128)(2,1)S(1)}, u32[]{:S(2)}, u32[]{:S(2)}) collective-permute-start(bf16[4,160,128]{2,1,0:T(8,128)(2,1)S(1)} %far4.3), channel_id=1, source_target_pairs={{0,1},{1,0},{2,3},{3,2},{4,5},{5,4},{6,7},{7,6},{8,9},{9,8},{10,11... | collective-permute-start | bytes 491528 | tf_op jit(solution)/shard_map/ppermute | solution.py:270

commit v9 on v8

--- a/solution.py
+++ b/solution.py
@@ -95,6 +95,10 @@
         for k, out in enumerate(outs):
             rotate_kernel(shards, reach, k + 1, 0, held, weights, limits, out)
     copies[3].wait()
+
+
+def copy_kernel(source, target):
+    target[...] = source[...]
 
 
 def table_kernel(total, shards, reach, beside, limits, table):
@@ -276,11 +280,10 @@
         [HBM] * len(inputs),
         *inputs,
         scratch=[dma((4,))],
-        flops=LONG,
         name="fetch",
     )
     if pair:
-        leaving = parts[0]
+        leaving = call(copy_kernel, [group], [VMEM], parts[0], flops=LONG, name="copy")[0]
         arrived_half = swapped(parts[1:])[0]
         near_halo = shifted(leaving, -1, across=True)
         kept = call(

time: 39.5 us -> 39.5 us (level)
  waiting for transfers between devices: 12.2 us -> 12.7 us
    ppermute x4, waiting for transfers between devices: 1.17 us -> 1.65 us  [swapped(): lax.ppermute(x, 'state', [(i, (i + k + 1) % shards) for i in range(shards)])]
    pallas_call x22 -> x23, Pallas kernels: 10.6 us -> 10.5 us  [call(): pl.pallas_call(kernel, out_shape=outs, in_specs=ins, out_specs=out_specs...]
where the time goes in v9:
time: 39.5 us; the launch traced here: 39.4 us
  starting transfers between devices  16.1 us (41%)
  waiting for transfers between devices  12.7 us (32%)
  Pallas kernels  10.5 us (27%)
    ppermute x9, waiting for transfers between devices, permuted(): return lax.ppermute(x, ('elem', 'state'), moves)  11 us
    pallas_call x23, Pallas kernels, call(): pl.pallas_call(kernel, out_shape=outs, in_specs=ins, out_specs=out_specs...  10.5 us
    ppermute x9, starting transfers between devices, permuted(): return lax.ppermute(x, ('elem', 'state'), moves)  8.4 us
    ppermute x4, starting transfers between devices, swapped(): lax.ppermute(x, 'state', [(i, (i + k + 1) % shards) for i in range(shards)])  7.67 us
    ppermute x4, waiting for transfers between devices, swapped(): lax.ppermute(x, 'state', [(i, (i + k + 1) % shards) for i in range(shards)])  1.65 us
  transfers between devices with their start and end apart: 13, of which 8 were waited for; matrix products, arithmetic and copies ran while one was open for 0% of the time, Pallas kernels for 21%

profile of v9, /device:TPU:0, one launch (start us, length us, event | category | flops | bytes accessed | tf_op | source)
XLA Modules:
  0.0 39.4 jit_solution(10246172508606198868)
XLA Ops:
  0.0 1.5 %fetch.1 = (bf16[4,160,128]{2,1,0:T(8,128)(2,1)S(1)}, bf16[2,160,128]{2,1,0:T(8,128)(2,1)S(1)}, bf16[6,160,256]{2,1,0:T(8,128)(2,1)S(1)}, bf16[256,256]{1,0:T(8,...) custom-call(bf16[6,160,256]{2,1,0:T(8,128)(2,1)} %orbitals.1, bf16[256,256]{1,0:T(8,128)(2,1)} %rotation.1, s32[12]{0:T(128)} %counts.1, ...), custom_call_target="tpu_custom_call" | custom-call | bytes 1024 | tf_op jit(solution)/shard_map/fetch/pallas_call | solution.py:24
  1.5 3.0 %collective-permute-start = (bf16[2,160,128]{2,1,0:T(8,128)(2,1)S(1)}, bf16[2,160,128]{2,1,0:T(8,128)(2,1)S(1)}, u32[]{:S(2)}, u32[]{:S(2)}) collective-permute-start(bf16[2,160,128]{2,1,0:T(8,128)(2,1)S(1)} %get-tuple-element.24), channel_id=1, source_target_pairs={{0,1},{1,0},{2,3},{3,2},{4,5},{5,4},{6,7},{7,6},{8,9},{9,8},{10,11... | collective-permute-start | bytes 245768 | tf_op jit(solution)/shard_map/ppermute | solution.py:274
  4.5 0.0 slice-start
  4.5 0.0 slice-start.1
  4.5 3.7 %collective-permute-start.3 = (bf16[4,160,128]{2,1,0:T(8,128)(2,1)S(1)}, bf16[4,160,128]{2,1,0:T(8,128)(2,1)S(1)}, u32[]{:S(2)}, u32[]{:S(2)}) collective-permute-start(bf16[4,160,128]{2,1,0:T(8,128)(2,1)S(1)} %copy.9.refs_3_.refs_2_), channel_id=1, source_target_pairs={{0,31},{1,2},{2,1},{3,4},{4,3},{5,6},{6,5},{7,8},{8,7},{9,10},{10,... | collective-permute-start | bytes 491528 | tf_op jit(solution)/shard_map/ppermute | solution.py:261
  8.2 0.3 rotate_in.1
  8.5 1.2 %collective-permute-start.2 = (bf16[4,160,128]{2,1,0:T(8,128)(2,1)S(1)}, bf16[4,160,128]{2,1,0:T(8,128)(2,1)S(1)}, u32[]{:S(2)}, u32[]{:S(2)}) collective-permute-start(bf16[4,160,128]{2,1,0:T(8,128)(2,1)S(1)} %get-tuple-element.22.refs_2_.here.before.refs_5_), channel_id=1, source_target_pairs={{0,30},{1,3},{2,0},{3,5},{4,2},{5,7},{6,4},{7,9},{8,6},{9,11},{10,... | collective-permute-start | bytes 491528 | tf_op jit(solution)/shard_map/ppermute | solution.py:261
  9.7 0.3 table.1.refs_1_
  10.0 0.0 slice-done
  10.0 0.0 slice-done.1
  10.0 0.3 pack.3.refs_1_.packed.refs_0_
  10.3 0.3 pack.4.refs_1_.refs_0_.packed
  10.6 0.3 pack.5.refs_3_.packed.refs_0_
  10.8 0.0 collective-permute-done.refs_1_
  10.9 0.8 %collective-permute-start.1 = (bf16[4,160,128]{2,1,0:T(8,128)(2,1)S(1)}, bf16[4,160,128]{2,1,0:T(8,128)(2,1)S(1)}, u32[]{:S(2)}, u32[]{:S(2)}) collective-permute-start(bf16[4,160,128]{2,1,0:T(8,128)(2,1)S(1)} %get-tuple-element.26), channel_id=1, source_target_pairs={{0,1},{1,0},{2,3},{3,2},{4,5},{5,4},{6,7},{7,6},{8,9},{9,8},{10,11... | collective-permute-start | bytes 491528 | tf_op jit(solution)/shard_map/ppermute | solution.py:274
  11.7 1.2 %collective-permute-done.3.before = bf16[4,160,128]{2,1,0:T(8,128)(2,1)S(1)} collective-permute-done((bf16[4,160,128]{2,1,0:T(8,128)(2,1)S(1)}, bf16[4,160,128]{2,1,0:T(8,128)(2,1)S(1)}, u32[]{:S(2)}, u32[]{:S(2)}) %collective-permute-start.3) | collective-permute-done | bytes 163872 | tf_op jit(solution)/shard_map/ppermute | solution.py:261
  12.9 0.5 %near1.1.refs_5_.refs_2_.refs_3_ = bf16[4,160,128]{2,1,0:T(8,128)(2,1)S(1)} custom-call(bf16[4,160,800]{2,1,0:T(8,128)(2,1)S(1)} %pack.3.refs_1_.packed.refs_0_, s32[12,6,8,128]{3,2,1,0:T(8,128)S(1)} %table.1.refs_1_, bf16[4,160,128]{2,1,0:T(8,128)(2,1)S(1)} %collective-permute-done.3.before, ...), custom_call_target="tpu_custom_call" | custom-call | bytes 1024 | tf_op jit(solution)/shard_map/near1/pallas_call | solution.py:24
  13.4 2.6 %collective-permute-start.5 = (bf16[4,160,128]{2,1,0:T(8,128)(2,1)S(1)}, bf16[4,160,128]{2,1,0:T(8,128)(2,1)S(1)}, u32[]{:S(2)}, u32[]{:S(2)}) collective-permute-start(bf16[4,160,128]{2,1,0:T(8,128)(2,1)S(1)} %near1.1.refs_5_.refs_2_.refs_3_), channel_id=1, source_target_pairs={{0,30},{1,3},{2,0},{3,5},{4,2},{5,7},{6,4},{7,9},{8,6},{9,11},{10,... | collective-permute-start | bytes 491528 | tf_op jit(solution)/shard_map/ppermute | solution.py:261
  16.0 0.0 collective-permute-done.2.refs_4_
  16.0 0.5 %collective-permute-done.1.refs_3_.after.refs_0_ = bf16[4,160,128]{2,1,0:T(8,128)(2,1)S(1)} collective-permute-done((bf16[4,160,128]{2,1,0:T(8,128)(2,1)S(1)}, bf16[4,160,128]{2,1,0:T(8,128)(2,1)S(1)}, u32[]{:S(2)}, u32[]{:S(2)}) %collective-permute-start.1) | collective-permute-done | bytes 163872 | tf_op jit(solution)/shard_map/ppermute | solution.py:274
  16.4 0.5 %far1.1.here.refs_4_.refs_5_ = bf16[4,160,128]{2,1,0:T(8,128)(2,1)S(1)} custom-call(bf16[4,160,800]{2,1,0:T(8,128)(2,1)S(1)} %pack.4.refs_1_.refs_0_.packed, s32[12,6,8,128]{3,2,1,0:T(8,128)S(1)} %table.1.refs_1_, bf16[4,160,128]{2,1,0:T(8,128)(2,1)S(1)} %get-tuple-element.25.after.refs_2_.here.refs_5_, ...), custom_call_target="tpu_custom_call" | custom-call | bytes 1024 | tf_op jit(solution)/shard_map/far1/pallas_call | solution.py:24
  17.0 0.1 collective-permute-start.4
  17.0 0.5 %middle1.1.before.refs_3_.refs_4_.refs_0_ = bf16[4,160,128]{2,1,0:T(8,128)(2,1)S(1)} custom-call(bf16[4,160,800]{2,1,0:T(8,128)(2,1)S(1)} %pack.5.refs_3_.packed.refs_0_, s32[12,6,8,128]{3,2,1,0:T(8,128)S(1)} %table.1.refs_1_, bf16[4,160,128]{2,1,0:T(8,128)(2,1)S(1)} %get-tuple-element.22.refs_2_.here.before.refs_5_, ...), custom_call_target="tpu_custom_call" | custom-call | bytes 1024 | tf_op jit(solution)/shard_map/middle1/pallas_call | solution.py:24
  17.5 1.3 %collective-permute-done.5.after = bf16[4,160,128]{2,1,0:T(8,128)(2,1)S(1)} collective-permute-done((bf16[4,160,128]{2,1,0:T(8,128)(2,1)S(1)}, bf16[4,160,128]{2,1,0:T(8,128)(2,1)S(1)}, u32[]{:S(2)}, u32[]{:S(2)}) %collective-permute-start.5) | collective-permute-done | bytes 163872 | tf_op jit(solution)/shard_map/ppermute | solution.py:261
  18.8 0.5 %far2.1.refs_6_.after.refs_3_.refs_5_ = bf16[4,160,128]{2,1,0:T(8,128)(2,1)S(1)} custom-call(bf16[4,160,800]{2,1,0:T(8,128)(2,1)S(1)} %pack.4.refs_1_.refs_0_.packed, s32[12,6,8,128]{3,2,1,0:T(8,128)S(1)} %table.1.refs_1_, bf16[4,160,128]{2,1,0:T(8,128)(2,1)S(1)} %middle1.1.before.refs_3_.refs_4_.refs_0_, bf16[4,160,128]{2,1,0:T(8,128)(2,1)S(1)} %far1.1.here.refs_4_.refs_5_, ...), custom_call_target="tpu_custom_call" | custom-call | bytes 1024 | tf_op jit(solution)/shard_map/far2/pallas_call | solution.py:24
  19.3 0.1 collective-permute-start.7
  19.4 0.5 %middle2.1.refs_6_.here.refs_4_.refs_2_.refs_5_ = bf16[4,160,128]{2,1,0:T(8,128)(2,1)S(1)} custom-call(bf16[4,160,800]{2,1,0:T(8,128)(2,1)S(1)} %pack.5.refs_3_.packed.refs_0_, s32[12,6,8,128]{3,2,1,0:T(8,128)S(1)} %table.1.refs_1_, bf16[4,160,128]{2,1,0:T(8,128)(2,1)S(1)} %near1.1.refs_5_.refs_2_.refs_3_, ...), custom_call_target="tpu_custom_call" | custom-call | bytes 1024 | tf_op jit(solution)/shard_map/middle2/pallas_call | solution.py:24
  19.9 4.6 %collective-permute-done.4.refs_2_ = bf16[4,160,128]{2,1,0:T(8,128)(2,1)S(1)} collective-permute-done((bf16[4,160,128]{2,1,0:T(8,128)(2,1)S(1)}, bf16[4,160,128]{2,1,0:T(8,128)(2,1)S(1)}, u32[]{:S(2)}, u32[]{:S(2)}) %collective-permute-start.4) | collective-permute-done | bytes 163872 | tf_op jit(solution)/shard_map/ppermute | solution.py:261
  24.5 0.5 %near2.1.before.refs_3_.refs_5_ = bf16[4,160,128]{2,1,0:T(8,128)(2,1)S(1)} custom-call(bf16[4,160,800]{2,1,0:T(8,128)(2,1)S(1)} %pack.3.refs_1_.packed.refs_0_, s32[12,6,8,128]{3,2,1,0:T(8,128)S(1)} %table.1.refs_1_, bf16[4,160,128]{2,1,0:T(8,128)(2,1)S(1)} %collective-permute-done.4.refs_2_, bf16[4,160,128]{2,1,0:T(8,128)(2,1)S(1)} %near1.1.refs_5_.refs_2_.refs_3_, ...), custom_call_target="tpu_custom_call" | custom-call | bytes 1024 | tf_op jit(solution)/shard_map/near2/pallas_call | solution.py:24
  25.0 0.2 collective-permute-start.6
  25.2 0.5 %middle3.1.refs_6_.refs_2_.refs_3_.refs_4_ = bf16[4,160,128]{2,1,0:T(8,128)(2,1)S(1)} custom-call(bf16[4,160,800]{2,1,0:T(8,128)(2,1)S(1)} %pack.5.refs_3_.packed.refs_0_, s32[12,6,8,128]{3,2,1,0:T(8,128)S(1)} %table.1.refs_1_, bf16[4,160,128]{2,1,0:T(8,128)(2,1)S(1)} %near2.1.before.refs_3_.refs_5_, ...), custom_call_target="tpu_custom_call" | custom-call | bytes 1024 | tf_op jit(solution)/shard_map/middle3/pallas_call | solution.py:24
  25.7 1.5 %collective-permute-done.7.refs_2_ = bf16[4,160,128]{2,1,0:T(8,128)(2,1)S(1)} collective-permute-done((bf16[4,160,128]{2,1,0:T(8,128)(2,1)S(1)}, bf16[4,160,128]{2,1,0:T(8,128)(2,1)S(1)}, u32[]{:S(2)}, u32[]{:S(2)}) %collective-permute-start.7) | collective-permute-done | bytes 163872 | tf_op jit(solution)/shard_map/ppermute | solution.py:261
  27.2 0.5 %near3.1.refs_6_.refs_2_.refs_3_ = bf16[4,160,128]{2,1,0:T(8,128)(2,1)S(1)} custom-call(bf16[4,160,800]{2,1,0:T(8,128)(2,1)S(1)} %pack.3.refs_1_.packed.refs_0_, s32[12,6,8,128]{3,2,1,0:T(8,128)S(1)} %table.1.refs_1_, bf16[4,160,128]{2,1,0:T(8,128)(2,1)S(1)} %collective-permute-done.7.refs_2_, bf16[4,160,128]{2,1,0:T(8,128)(2,1)S(1)} %near2.1.before.refs_3_.refs_5_, ...), custom_call_target="tpu_custom_call" | custom-call | bytes 1024 | tf_op jit(solution)/shard_map/near3/pallas_call | solution.py:24
  27.7 0.1 collective-permute-start.9
  27.8 0.4 %collective-permute-start.8 = (bf16[4,160,128]{2,1,0:T(8,128)(2,1)S(1)}, bf16[4,160,128]{2,1,0:T(8,128)(2,1)S(1)}, u32[]{:S(2)}, u32[]{:S(2)}) collective-permute-start(bf16[4,160,128]{2,1,0:T(8,128)(2,1)S(1)} %near3.1.refs_6_.refs_2_.refs_3_), channel_id=1, source_target_pairs={{0,30},{1,3},{2,0},{3,5},{4,2},{5,7},{6,4},{7,9},{8,6},{9,11},{10,... | collective-permute-start | bytes 491528 | tf_op jit(solution)/shard_map/ppermute | solution.py:261
  28.2 0.0 collective-permute-done.6.refs_4_
  28.2 0.5 %far3.1.refs_3_.refs_4_ = bf16[4,160,128]{2,1,0:T(8,128)(2,1)S(1)} custom-call(bf16[4,160,800]{2,1,0:T(8,128)(2,1)S(1)} %pack.4.refs_1_.refs_0_.packed, s32[12,6,8,128]{3,2,1,0:T(8,128)S(1)} %table.1.refs_1_, bf16[4,160,128]{2,1,0:T(8,128)(2,1)S(1)} %middle2.1.refs_6_.here.refs_4_.refs_2_.refs_5_, ...), custom_call_target="tpu_custom_call" | custom-call | bytes 1024 | tf_op jit(solution)/shard_map/far3/pallas_call | solution.py:24
  28.7 0.2 collective-permute-start.11
  28.9 0.3 collective-permute-done.9.refs_4_
  29.2 0.5 %far4.2.refs_6_ = bf16[4,160,128]{2,1,0:T(8,128)(2,1)S(1)} custom-call(bf16[4,160,800]{2,1,0:T(8,128)(2,1)S(1)} %pack.4.refs_1_.refs_0_.packed, s32[12,6,8,128]{3,2,1,0:T(8,128)S(1)} %table.1.refs_1_, bf16[4,160,128]{2,1,0:T(8,128)(2,1)S(1)} %middle3.1.refs_6_.refs_2_.refs_3_.refs_4_, bf16[4,160,128]{2,1,0:T(8,128)(2,1)S(1)} %far3.1.refs_3_.refs_4_, ...), custom_call_target="tpu_custom_call" | custom-call | bytes 1024 | tf_op jit(solution)/shard_map/far4/pallas_call | solution.py:24
  29.7 0.6 %middle4.1 = (bf16[4,160,128]{2,1,0:T(8,128)(2,1)S(1)}, bf16[2,160,128]{2,1,0:T(8,128)(2,1)S(1)}) custom-call(bf16[4,160,800]{2,1,0:T(8,128)(2,1)S(1)} %pack.5.refs_3_.packed.refs_0_, s32[12,6,8,128]{3,2,1,0:T(8,128)S(1)} %table.1.refs_1_, bf16[4,160,128]{2,1,0:T(8,128)(2,1)S(1)} %near3.1.refs_6_.refs_2_.refs_3_, ...), custom_call_target="tpu_custom_call" | custom-call | bytes 1024 | tf_op jit(solution)/shard_map/middle4/pallas_call | solution.py:24
  30.2 1.7 %collective-permute-start.12 = (bf16[2,160,128]{2,1,0:T(8,128)(2,1)S(1)}, bf16[2,160,128]{2,1,0:T(8,128)(2,1)S(1)}, u32[]{:S(2)}, u32[]{:S(2)}) collective-permute-start(bf16[2,160,128]{2,1,0:T(8,128)(2,1)S(1)} %get-tuple-element.27), channel_id=1, source_target_pairs={{0,1},{1,0},{2,3},{3,2},{4,5},{5,4},{6,7},{7,6},{8,9},{9,8},{10,11... | collective-permute-start | bytes 245768 | tf_op jit(solution)/shard_map/ppermute | solution.py:274
  32.0 0.0 collective-permute-done.8.refs_4_
  32.0 2.1 %collective-permute-start.10 = (bf16[4,160,128]{2,1,0:T(8,128)(2,1)S(1)}, bf16[4,160,128]{2,1,0:T(8,128)(2,1)S(1)}, u32[]{:S(2)}, u32[]{:S(2)}) collective-permute-start(bf16[4,160,128]{2,1,0:T(8,128)(2,1)S(1)} %far4.3), channel_id=1, source_target_pairs={{0,1},{1,0},{2,3},{3,2},{4,5},{5,4},{6,7},{7,6},{8,9},{9,8},{10,11... | collective-permute-start | bytes 491528 | tf_op jit(solution)/shard_map/ppermute | solution.py:274
  34.1 2.1 %collective-permute-done.11.refs_2_ = bf16[4,160,128]{2,1,0:T(8,128)(2,1)S(1)} collective-permute-done((bf16[4,160,128]{2,1,0:T(8,128)(2,1)S(1)}, bf16[4,160,128]{2,1,0:T(8,128)(2,1)S(1)}, u32[]{:S(2)}, u32[]{:S(2)}) %collective-permute-start.11) | collective-permute-done | bytes 163872 | tf_op jit(solution)/shard_map/ppermute | solution.py:261
  36.2 0.0 collective-permute-done.12.refs_6_.half
  36.2 0.5 %near4.1.near = bf16[4,160,128]{2,1,0:T(8,128)(2,1)S(1)} custom-call(bf16[4,160,800]{2,1,0:T(8,128)(2,1)S(1)} %pack.3.refs_1_.packed.refs_0_, s32[12,6,8,128]{3,2,1,0:T(8,128)S(1)} %table.1.refs_1_, bf16[4,160,128]{2,1,0:T(8,128)(2,1)S(1)} %collective-permute-done.11.refs_2_, bf16[4,160,128]{2,1,0:T(8,128)(2,1)S(1)} %near3.1.refs_6_.refs_2_.refs_3_, ...), custom_call_target="tpu_custom_call" | custom-call | flops 20000000000 | bytes 1024 | tf_op jit(solution)/shard_map/near4/pallas_call | solution.py:24
  36.8 0.8 %own.1.refs_1_ = bf16[6,160,256]{2,1,0:T(8,128)(2,1)} custom-call(bf16[4,160,128]{2,1,0:T(8,128)(2,1)S(1)} %near4.1.near, bf16[4,160,128]{2,1,0:T(8,128)(2,1)S(1)} %get-tuple-element.28.middle, bf16[2,160,128]{2,1,0:T(8,128)(2,1)S(1)} %collective-permute-done.12.refs_6_.half), custom_call_target="tpu_custom_call" | custom-call | bytes 1024 | tf_op jit(solution)/shard_map/own/pallas_call | solution.py:24
  37.5 1.2 %collective-permute-done.10.refs_0_ = bf16[4,160,128]{2,1,0:T(8,128)(2,1)S(1)} collective-permute-done((bf16[4,160,128]{2,1,0:T(8,128)(2,1)S(1)}, bf16[4,160,128]{2,1,0:T(8,128)(2,1)S(1)}, u32[]{:S(2)}, u32[]{:S(2)}) %collective-permute-start.10) | collective-permute-done | bytes 163872 | tf_op jit(solution)/shard_map/ppermute | solution.py:274
  38.7 0.7 %others.1 = bf16[6,160,256]{2,1,0:T(8,128)(2,1)} custom-call(bf16[4,160,128]{2,1,0:T(8,128)(2,1)S(1)} %collective-permute-done.10.refs_0_, bf16[6,160,256]{2,1,0:T(8,128)(2,1)} %own.1.refs_1_), custom_call_target="tpu_custom_call", output_to_operand_aliasing={{}: (1, {})} | custom-call | bytes 1024 | tf_op jit(solution)/shard_map/others/pallas_call | solution.py:24
  (4 shorter events, 0.1 us)
Async XLA Ops:
  1.5 9.4 %collective-permute-start = (bf16[2,160,128]{2,1,0:T(8,128)(2,1)S(1)}, bf16[2,160,128]{2,1,0:T(8,128)(2,1)S(1)}, u32[]{:S(2)}, u32[]{:S(2)}) collective-permute-start(bf16[2,160,128]{2,1,0:T(8,128)(2,1)S(1)} %get-tuple-element.24), channel_id=1, source_target_pairs={{0,1},{1,0},{2,3},{3,2},{4,5},{5,4},{6,7},{7,6},{8,9},{9,8},{10,11... | collective-permute-start | bytes 245768 | tf_op jit(solution)/shard_map/ppermute | solution.py:274
  4.5 5.5 %slice-start = ((s8[4915200]{0:T(1024)(128)(4,1)}), s8[4194304]{0:T(1024)(128)(4,1)S(1)}, s32[]{:S(2)}) async-start(s8[4915200]{0:T(1024)(128)(4,1)} %bitcast.1), calls=%async_computation | async-start | bytes 8388608
  4.5 5.5 %slice-start.1 = ((s8[4915200]{0:T(1024)(128)(4,1)}), s8[720896]{0:T(1024)(128)(4,1)S(1)}, s32[]{:S(2)}) async-start(s8[4915200]{0:T(1024)(128)(4,1)} %bitcast.1), calls=%async_computation.1 | async-start | bytes 1441792
  4.5 8.4 %collective-permute-start.3 = (bf16[4,160,128]{2,1,0:T(8,128)(2,1)S(1)}, bf16[4,160,128]{2,1,0:T(8,128)(2,1)S(1)}, u32[]{:S(2)}, u32[]{:S(2)}) collective-permute-start(bf16[4,160,128]{2,1,0:T(8,128)(2,1)S(1)} %copy.9.refs_3_.refs_2_), channel_id=1, source_target_pairs={{0,31},{1,2},{2,1},{3,4},{4,3},{5,6},{6,5},{7,8},{8,7},{9,10},{10,... | collective-permute-start | bytes 491528 | tf_op jit(solution)/shard_map/ppermute | solution.py:261
  8.5 7.5 %collective-permute-start.2 = (bf16[4,160,128]{2,1,0:T(8,128)(2,1)S(1)}, bf16[4,160,128]{2,1,0:T(8,128)(2,1)S(1)}, u32[]{:S(2)}, u32[]{:S(2)}) collective-permute-start(bf16[4,160,128]{2,1,0:T(8,128)(2,1)S(1)} %get-tuple-element.22.refs_2_.here.before.refs_5_), channel_id=1, source_target_pairs={{0,30},{1,3},{2,0},{3,5},{4,2},{5,7},{6,4},{7,9},{8,6},{9,11},{10,... | collective-permute-start | bytes 491528 | tf_op jit(solution)/shard_map/ppermute | solution.py:261
  10.9 5.6 %collective-permute-start.1 = (bf16[4,160,128]{2,1,0:T(8,128)(2,1)S(1)}, bf16[4,160,128]{2,1,0:T(8,128)(2,1)S(1)}, u32[]{:S(2)}, u32[]{:S(2)}) collective-permute-start(bf16[4,160,128]{2,1,0:T(8,128)(2,1)S(1)} %get-tuple-element.26), channel_id=1, source_target_pairs={{0,1},{1,0},{2,3},{3,2},{4,5},{5,4},{6,7},{7,6},{8,9},{9,8},{10,11... | collective-permute-start | bytes 491528 | tf_op jit(solution)/shard_map/ppermute | solution.py:274
  13.4 5.4 %collective-permute-start.5 = (bf16[4,160,128]{2,1,0:T(8,128)(2,1)S(1)}, bf16[4,160,128]{2,1,0:T(8,128)(2,1)S(1)}, u32[]{:S(2)}, u32[]{:S(2)}) collective-permute-start(bf16[4,160,128]{2,1,0:T(8,128)(2,1)S(1)} %near1.1.refs_5_.refs_2_.refs_3_), channel_id=1, source_target_pairs={{0,30},{1,3},{2,0},{3,5},{4,2},{5,7},{6,4},{7,9},{8,6},{9,11},{10,... | collective-permute-start | bytes 491528 | tf_op jit(solution)/shard_map/ppermute | solution.py:261
  17.0 7.6 %collective-permute-start.4 = (bf16[4,160,128]{2,1,0:T(8,128)(2,1)S(1)}, bf16[4,160,128]{2,1,0:T(8,128)(2,1)S(1)}, u32[]{:S(2)}, u32[]{:S(2)}) collective-permute-start(bf16[4,160,128]{2,1,0:T(8,128)(2,1)S(1)} %far1.1.here.refs_4_.refs_5_), channel_id=1, source_target_pairs={{0,2},{1,31},{2,4},{3,1},{4,6},{5,3},{6,8},{7,5},{8,10},{9,7},{10,... | collective-permute-start | bytes 491528 | tf_op jit(solution)/shard_map/ppermute | solution.py:261
  19.3 7.9 %collective-permute-start.7 = (bf16[4,160,128]{2,1,0:T(8,128)(2,1)S(1)}, bf16[4,160,128]{2,1,0:T(8,128)(2,1)S(1)}, u32[]{:S(2)}, u32[]{:S(2)}) collective-permute-start(bf16[4,160,128]{2,1,0:T(8,128)(2,1)S(1)} %far2.1.refs_6_.after.refs_3_.refs_5_), channel_id=1, source_target_pairs={{0,2},{1,31},{2,4},{3,1},{4,6},{5,3},{6,8},{7,5},{8,10},{9,7},{10,... | collective-permute-start | bytes 491528 | tf_op jit(solution)/shard_map/ppermute | solution.py:261
  25.0 3.2 %collective-permute-start.6 = (bf16[4,160,128]{2,1,0:T(8,128)(2,1)S(1)}, bf16[4,160,128]{2,1,0:T(8,128)(2,1)S(1)}, u32[]{:S(2)}, u32[]{:S(2)}) collective-permute-start(bf16[4,160,128]{2,1,0:T(8,128)(2,1)S(1)} %near2.1.before.refs_3_.refs_5_), channel_id=1, source_target_pairs={{0,30},{1,3},{2,0},{3,5},{4,2},{5,7},{6,4},{7,9},{8,6},{9,11},{10,... | collective-permute-start | bytes 491528 | tf_op jit(solution)/shard_map/ppermute | solution.py:261
  27.7 1.5 %collective-permute-start.9 = (bf16[4,160,128]{2,1,0:T(8,128)(2,1)S(1)}, bf16[4,160,128]{2,1,0:T(8,128)(2,1)S(1)}, u32[]{:S(2)}, u32[]{:S(2)}) collective-permute-start(bf16[4,160,128]{2,1,0:T(8,128)(2,1)S(1)} %near3.1.refs_6_.refs_2_.refs_3_), channel_id=1, source_target_pairs={{0,2},{1,3},{2,0},{3,1},{4,6},{5,7},{6,4},{7,5},{8,10},{9,11},{10,... | collective-permute-start | bytes 491528 | tf_op jit(solution)/shard_map/ppermute | solution.py:261
  27.8 4.2 %collective-permute-start.8 = (bf16[4,160,128]{2,1,0:T(8,128)(2,1)S(1)}, bf16[4,160,128]{2,1,0:T(8,128)(2,1)S(1)}, u32[]{:S(2)}, u32[]{:S(2)}) collective-permute-start(bf16[4,160,128]{2,1,0:T(8,128)(2,1)S(1)} %near3.1.refs_6_.refs_2_.refs_3_), channel_id=1, source_target_pairs={{0,30},{1,3},{2,0},{3,5},{4,2},{5,7},{6,4},{7,9},{8,6},{9,11},{10,... | collective-permute-start | bytes 491528 | tf_op jit(solution)/shard_map/ppermute | solution.py:261
  28.7 7.5 %collective-permute-start.11 = (bf16[4,160,128]{2,1,0:T(8,128)(2,1)S(1)}, bf16[4,160,128]{2,1,0:T(8,128)(2,1)S(1)}, u32[]{:S(2)}, u32[]{:S(2)}) collective-permute-start(bf16[4,160,128]{2,1,0:T(8,128)(2,1)S(1)} %far3.1.refs_3_.refs_4_), channel_id=1, source_target_pairs={{0,2},{1,31},{2,4},{3,1},{4,6},{5,3},{6,8},{7,5},{8,10},{9,7},{10,... | collective-permute-start | bytes 491528 | tf_op jit(solution)/shard_map/ppermute | solution.py:261
  30.2 6.0 %collective-permute-start.12 = (bf16[2,160,128]{2,1,0:T(8,128)(2,1)S(1)}, bf16[2,160,128]{2,1,0:T(8,128)(2,1)S(1)}, u32[]{:S(2)}, u32[]{:S(2)}) collective-permute-start(bf16[2,160,128]{2,1,0:T(8,128)(2,1)S(1)} %get-tuple-element.27), channel_id=1, source_target_pairs={{0,1},{1,0},{2,3},{3,2},{4,5},{5,4},{6,7},{7,6},{8,9},{9,8},{10,11... | collective-permute-start | bytes 245768 | tf_op jit(solution)/shard_map/ppermute | solution.py:274
  32.0 6.7 %collective-permute-start.10 = (bf16[4,160,128]{2,1,0:T(8,128)(2,1)S(1)}, bf16[4,160,128]{2,1,0:T(8,128)(2,1)S(1)}, u32[]{:S(2)}, u32[]{:S(2)}) collective-permute-start(bf16[4,160,128]{2,1,0:T(8,128)(2,1)S(1)} %far4.3), channel_id=1, source_target_pairs={{0,1},{1,0},{2,3},{3,2},{4,5},{5,4},{6,7},{7,6},{8,9},{9,8},{10,11... | collective-permute-start | bytes 491528 | tf_op jit(solution)/shard_map/ppermute | solution.py:274

commit v10 on v8

--- a/solution.py
+++ b/solution.py
@@ -169,8 +169,9 @@
     for g, group in enumerate((before, here, after)):
         window[g * width : (g + 1) * width] = group[...]
     couplings = table.shape[1] - 1
+    numbers = [[table[first + e, k, 0, 0] for k in range(couplings + 1)] for e in range(width)]
     for e in range(width):
-        *at, end = [table[first + e, k, 0, 0] for k in range(couplings + 1)]
+        *at, end = numbers[e]
         fields = jnp.concatenate([window[i, :FULL] for i in at] + [window[i, FULL:] for i in at], axis=0)
         image = jnp.zeros((rows, lanes), jnp.float32)
         for k in range(0, fields.shape[0], DEPTH):

time: 39.5 us -> 39.5 us (level)
  no operation moved by 1% of the time
where the time goes in v10:
time: 39.5 us; the launch traced here: 39.3 us
  starting transfers between devices  16.3 us (41%)
  waiting for transfers between devices  12.2 us (31%)
  Pallas kernels  10.6 us (27%)
    ppermute x9, waiting for transfers between devices, permuted(): return lax.ppermute(x, ('elem', 'state'), moves)  11.1 us
    pallas_call x22, Pallas kernels, call(): pl.pallas_call(kernel, out_shape=outs, in_specs=ins, out_specs=out_specs...  10.6 us
    ppermute x9, starting transfers between devices, permuted(): return lax.ppermute(x, ('elem', 'state'), moves)  8.67 us
    ppermute x4, starting transfers between devices, swapped(): lax.ppermute(x, 'state', [(i, (i + k + 1) % shards) for i in range(shards)])  7.61 us
    ppermute x4, waiting for transfers between devices, swapped(): lax.ppermute(x, 'state', [(i, (i + k + 1) % shards) for i in range(shards)])  1.15 us
  transfers between devices with their start and end apart: 13, of which 8 were waited for; matrix products, arithmetic and copies ran while one was open for 0% of the time, Pallas kernels for 21%

profile of v10, /device:TPU:0, one launch (start us, length us, event | category | flops | bytes accessed | tf_op | source)
XLA Modules:
  0.0 39.3 jit_solution(10069567932923636316)
XLA Ops:
  0.0 0.0 slice-start
  0.0 0.0 slice-start.1
  0.0 1.6 %fetch.1 = (bf16[4,160,128]{2,1,0:T(8,128)(2,1)S(1)}, bf16[2,160,128]{2,1,0:T(8,128)(2,1)S(1)}, bf16[6,160,256]{2,1,0:T(8,128)(2,1)S(1)}, bf16[256,256]{1,0:T(8,...) custom-call(bf16[6,160,256]{2,1,0:T(8,128)(2,1)} %orbitals.1, bf16[256,256]{1,0:T(8,128)(2,1)} %rotation.1, s32[12]{0:T(128)} %counts.1, ...), custom_call_target="tpu_custom_call" | custom-call | flops 20000000000 | bytes 1024 | tf_op jit(solution)/shard_map/fetch/pallas_call | solution.py:24
  1.6 3.0 %collective-permute-start = (bf16[2,160,128]{2,1,0:T(8,128)(2,1)S(1)}, bf16[2,160,128]{2,1,0:T(8,128)(2,1)S(1)}, u32[]{:S(2)}, u32[]{:S(2)}) collective-permute-start(bf16[2,160,128]{2,1,0:T(8,128)(2,1)S(1)} %get-tuple-element.24), channel_id=1, source_target_pairs={{0,1},{1,0},{2,3},{3,2},{4,5},{5,4},{6,7},{7,6},{8,9},{9,8},{10,11... | collective-permute-start | bytes 245768 | tf_op jit(solution)/shard_map/ppermute | solution.py:271
  4.6 3.6 %collective-permute-start.3 = (bf16[4,160,128]{2,1,0:T(8,128)(2,1)S(1)}, bf16[4,160,128]{2,1,0:T(8,128)(2,1)S(1)}, u32[]{:S(2)}, u32[]{:S(2)}) collective-permute-start(bf16[4,160,128]{2,1,0:T(8,128)(2,1)S(1)} %get-tuple-element.21.refs_3_.refs_2_), channel_id=1, source_target_pairs={{0,31},{1,2},{2,1},{3,4},{4,3},{5,6},{6,5},{7,8},{8,7},{9,10},{10,... | collective-permute-start | bytes 491528 | tf_op jit(solution)/shard_map/ppermute | solution.py:258
  8.3 0.3 rotate_in.1
  8.6 1.2 %collective-permute-start.2 = (bf16[4,160,128]{2,1,0:T(8,128)(2,1)S(1)}, bf16[4,160,128]{2,1,0:T(8,128)(2,1)S(1)}, u32[]{:S(2)}, u32[]{:S(2)}) collective-permute-start(bf16[4,160,128]{2,1,0:T(8,128)(2,1)S(1)} %get-tuple-element.22.refs_2_.here.before.refs_5_), channel_id=1, source_target_pairs={{0,30},{1,3},{2,0},{3,5},{4,2},{5,7},{6,4},{7,9},{8,6},{9,11},{10,... | collective-permute-start | bytes 491528 | tf_op jit(solution)/shard_map/ppermute | solution.py:258
  9.7 0.3 table.1.refs_1_
  10.0 0.0 slice-done
  10.0 0.0 slice-done.1
  10.1 0.3 pack.3.refs_1_.packed.refs_0_
  10.3 0.3 pack.4.refs_1_.refs_0_.packed
  10.6 0.3 pack.5.refs_3_.packed.refs_0_
  10.9 0.0 collective-permute-done.refs_1_
  11.0 0.9 %collective-permute-start.1 = (bf16[4,160,128]{2,1,0:T(8,128)(2,1)S(1)}, bf16[4,160,128]{2,1,0:T(8,128)(2,1)S(1)}, u32[]{:S(2)}, u32[]{:S(2)}) collective-permute-start(bf16[4,160,128]{2,1,0:T(8,128)(2,1)S(1)} %get-tuple-element.26), channel_id=1, source_target_pairs={{0,1},{1,0},{2,3},{3,2},{4,5},{5,4},{6,7},{7,6},{8,9},{9,8},{10,11... | collective-permute-start | bytes 491528 | tf_op jit(solution)/shard_map/ppermute | solution.py:271
  11.8 1.2 %collective-permute-done.3.before = bf16[4,160,128]{2,1,0:T(8,128)(2,1)S(1)} collective-permute-done((bf16[4,160,128]{2,1,0:T(8,128)(2,1)S(1)}, bf16[4,160,128]{2,1,0:T(8,128)(2,1)S(1)}, u32[]{:S(2)}, u32[]{:S(2)}) %collective-permute-start.3) | collective-permute-done | bytes 163872 | tf_op jit(solution)/shard_map/ppermute | solution.py:258
  13.0 0.5 %near1.1.refs_5_.refs_2_.refs_3_ = bf16[4,160,128]{2,1,0:T(8,128)(2,1)S(1)} custom-call(bf16[4,160,800]{2,1,0:T(8,128)(2,1)S(1)} %pack.3.refs_1_.packed.refs_0_, s32[12,6,8,128]{3,2,1,0:T(8,128)S(1)} %table.1.refs_1_, bf16[4,160,128]{2,1,0:T(8,128)(2,1)S(1)} %collective-permute-done.3.before, ...), custom_call_target="tpu_custom_call" | custom-call | bytes 1024 | tf_op jit(solution)/shard_map/near1/pallas_call | solution.py:24
  13.5 2.7 %collective-permute-start.5 = (bf16[4,160,128]{2,1,0:T(8,128)(2,1)S(1)}, bf16[4,160,128]{2,1,0:T(8,128)(2,1)S(1)}, u32[]{:S(2)}, u32[]{:S(2)}) collective-permute-start(bf16[4,160,128]{2,1,0:T(8,128)(2,1)S(1)} %near1.1.refs_5_.refs_2_.refs_3_), channel_id=1, source_target_pairs={{0,30},{1,3},{2,0},{3,5},{4,2},{5,7},{6,4},{7,9},{8,6},{9,11},{10,... | collective-permute-start | bytes 491528 | tf_op jit(solution)/shard_map/ppermute | solution.py:258
  16.2 0.0 collective-permute-done.2.refs_4_
  16.2 0.3 collective-permute-done.1.refs_3_.after.refs_0_
  16.5 0.5 %far1.1.here.refs_4_.refs_5_ = bf16[4,160,128]{2,1,0:T(8,128)(2,1)S(1)} custom-call(bf16[4,160,800]{2,1,0:T(8,128)(2,1)S(1)} %pack.4.refs_1_.refs_0_.packed, s32[12,6,8,128]{3,2,1,0:T(8,128)S(1)} %table.1.refs_1_, bf16[4,160,128]{2,1,0:T(8,128)(2,1)S(1)} %get-tuple-element.25.after.refs_2_.here.refs_5_, ...), custom_call_target="tpu_custom_call" | custom-call | bytes 1024 | tf_op jit(solution)/shard_map/far1/pallas_call | solution.py:24
  17.0 0.1 collective-permute-start.4
  17.1 0.5 %middle1.1.before.refs_3_.refs_4_.refs_0_ = bf16[4,160,128]{2,1,0:T(8,128)(2,1)S(1)} custom-call(bf16[4,160,800]{2,1,0:T(8,128)(2,1)S(1)} %pack.5.refs_3_.packed.refs_0_, s32[12,6,8,128]{3,2,1,0:T(8,128)S(1)} %table.1.refs_1_, bf16[4,160,128]{2,1,0:T(8,128)(2,1)S(1)} %get-tuple-element.22.refs_2_.here.before.refs_5_, ...), custom_call_target="tpu_custom_call" | custom-call | bytes 1024 | tf_op jit(solution)/shard_map/middle1/pallas_call | solution.py:24
  17.6 1.4 %collective-permute-done.5.after = bf16[4,160,128]{2,1,0:T(8,128)(2,1)S(1)} collective-permute-done((bf16[4,160,128]{2,1,0:T(8,128)(2,1)S(1)}, bf16[4,160,128]{2,1,0:T(8,128)(2,1)S(1)}, u32[]{:S(2)}, u32[]{:S(2)}) %collective-permute-start.5) | collective-permute-done | bytes 163872 | tf_op jit(solution)/shard_map/ppermute | solution.py:258
  19.0 0.5 %far2.1.refs_6_.after.refs_3_.refs_5_ = bf16[4,160,128]{2,1,0:T(8,128)(2,1)S(1)} custom-call(bf16[4,160,800]{2,1,0:T(8,128)(2,1)S(1)} %pack.4.refs_1_.refs_0_.packed, s32[12,6,8,128]{3,2,1,0:T(8,128)S(1)} %table.1.refs_1_, bf16[4,160,128]{2,1,0:T(8,128)(2,1)S(1)} %middle1.1.before.refs_3_.refs_4_.refs_0_, bf16[4,160,128]{2,1,0:T(8,128)(2,1)S(1)} %far1.1.here.refs_4_.refs_5_, ...), custom_call_target="tpu_custom_call" | custom-call | bytes 1024 | tf_op jit(solution)/shard_map/far2/pallas_call | solution.py:24
  19.6 0.1 collective-permute-start.7
  19.6 0.5 %middle2.1.refs_6_.here.refs_4_.refs_2_.refs_5_ = bf16[4,160,128]{2,1,0:T(8,128)(2,1)S(1)} custom-call(bf16[4,160,800]{2,1,0:T(8,128)(2,1)S(1)} %pack.5.refs_3_.packed.refs_0_, s32[12,6,8,128]{3,2,1,0:T(8,128)S(1)} %table.1.refs_1_, bf16[4,160,128]{2,1,0:T(8,128)(2,1)S(1)} %near1.1.refs_5_.refs_2_.refs_3_, ...), custom_call_target="tpu_custom_call" | custom-call | bytes 1024 | tf_op jit(solution)/shard_map/middle2/pallas_call | solution.py:24
  20.1 4.4 %collective-permute-done.4.refs_2_ = bf16[4,160,128]{2,1,0:T(8,128)(2,1)S(1)} collective-permute-done((bf16[4,160,128]{2,1,0:T(8,128)(2,1)S(1)}, bf16[4,160,128]{2,1,0:T(8,128)(2,1)S(1)}, u32[]{:S(2)}, u32[]{:S(2)}) %collective-permute-start.4) | collective-permute-done | bytes 163872 | tf_op jit(solution)/shard_map/ppermute | solution.py:258
  24.6 0.5 %near2.1.before.refs_3_.refs_5_ = bf16[4,160,128]{2,1,0:T(8,128)(2,1)S(1)} custom-call(bf16[4,160,800]{2,1,0:T(8,128)(2,1)S(1)} %pack.3.refs_1_.packed.refs_0_, s32[12,6,8,128]{3,2,1,0:T(8,128)S(1)} %table.1.refs_1_, bf16[4,160,128]{2,1,0:T(8,128)(2,1)S(1)} %collective-permute-done.4.refs_2_, bf16[4,160,128]{2,1,0:T(8,128)(2,1)S(1)} %near1.1.refs_5_.refs_2_.refs_3_, ...), custom_call_target="tpu_custom_call" | custom-call | bytes 1024 | tf_op jit(solution)/shard_map/near2/pallas_call | solution.py:24
  25.1 0.3 collective-permute-start.6
  25.4 0.5 %middle3.1.refs_6_.refs_2_.refs_3_.refs_4_ = bf16[4,160,128]{2,1,0:T(8,128)(2,1)S(1)} custom-call(bf16[4,160,800]{2,1,0:T(8,128)(2,1)S(1)} %pack.5.refs_3_.packed.refs_0_, s32[12,6,8,128]{3,2,1,0:T(8,128)S(1)} %table.1.refs_1_, bf16[4,160,128]{2,1,0:T(8,128)(2,1)S(1)} %near2.1.before.refs_3_.refs_5_, ...), custom_call_target="tpu_custom_call" | custom-call | bytes 1024 | tf_op jit(solution)/shard_map/middle3/pallas_call | solution.py:24
  25.9 1.5 %collective-permute-done.7.refs_2_ = bf16[4,160,128]{2,1,0:T(8,128)(2,1)S(1)} collective-permute-done((bf16[4,160,128]{2,1,0:T(8,128)(2,1)S(1)}, bf16[4,160,128]{2,1,0:T(8,128)(2,1)S(1)}, u32[]{:S(2)}, u32[]{:S(2)}) %collective-permute-start.7) | collective-permute-done | bytes 163872 | tf_op jit(solution)/shard_map/ppermute | solution.py:258
  27.4 0.5 %near3.1.refs_6_.refs_2_.refs_3_ = bf16[4,160,128]{2,1,0:T(8,128)(2,1)S(1)} custom-call(bf16[4,160,800]{2,1,0:T(8,128)(2,1)S(1)} %pack.3.refs_1_.packed.refs_0_, s32[12,6,8,128]{3,2,1,0:T(8,128)S(1)} %table.1.refs_1_, bf16[4,160,128]{2,1,0:T(8,128)(2,1)S(1)} %collective-permute-done.7.refs_2_, bf16[4,160,128]{2,1,0:T(8,128)(2,1)S(1)} %near2.1.before.refs_3_.refs_5_, ...), custom_call_target="tpu_custom_call" | custom-call | bytes 1024 | tf_op jit(solution)/shard_map/near3/pallas_call | solution.py:24
  27.9 0.1 collective-permute-start.9
  28.0 0.4 %collective-permute-start.8 = (bf16[4,160,128]{2,1,0:T(8,128)(2,1)S(1)}, bf16[4,160,128]{2,1,0:T(8,128)(2,1)S(1)}, u32[]{:S(2)}, u32[]{:S(2)}) collective-permute-start(bf16[4,160,128]{2,1,0:T(8,128)(2,1)S(1)} %near3.1.refs_6_.refs_2_.refs_3_), channel_id=1, source_target_pairs={{0,30},{1,3},{2,0},{3,5},{4,2},{5,7},{6,4},{7,9},{8,6},{9,11},{10,... | collective-permute-start | bytes 491528 | tf_op jit(solution)/shard_map/ppermute | solution.py:258
  28.4 0.0 collective-permute-done.6.refs_4_
  28.4 0.5 %far3.1.refs_3_.refs_4_ = bf16[4,160,128]{2,1,0:T(8,128)(2,1)S(1)} custom-call(bf16[4,160,800]{2,1,0:T(8,128)(2,1)S(1)} %pack.4.refs_1_.refs_0_.packed, s32[12,6,8,128]{3,2,1,0:T(8,128)S(1)} %table.1.refs_1_, bf16[4,160,128]{2,1,0:T(8,128)(2,1)S(1)} %middle2.1.refs_6_.here.refs_4_.refs_2_.refs_5_, ...), custom_call_target="tpu_custom_call" | custom-call | bytes 1024 | tf_op jit(solution)/shard_map/far3/pallas_call | solution.py:24
  28.9 0.2 collective-permute-start.11
  29.1 0.3 collective-permute-done.9.refs_4_
  29.4 0.5 %far4.2.refs_6_ = bf16[4,160,128]{2,1,0:T(8,128)(2,1)S(1)} custom-call(bf16[4,160,800]{2,1,0:T(8,128)(2,1)S(1)} %pack.4.refs_1_.refs_0_.packed, s32[12,6,8,128]{3,2,1,0:T(8,128)S(1)} %table.1.refs_1_, bf16[4,160,128]{2,1,0:T(8,128)(2,1)S(1)} %middle3.1.refs_6_.refs_2_.refs_3_.refs_4_, bf16[4,160,128]{2,1,0:T(8,128)(2,1)S(1)} %far3.1.refs_3_.refs_4_, ...), custom_call_target="tpu_custom_call" | custom-call | bytes 1024 | tf_op jit(solution)/shard_map/far4/pallas_call | solution.py:24
  29.9 0.6 %middle4.1 = (bf16[4,160,128]{2,1,0:T(8,128)(2,1)S(1)}, bf16[2,160,128]{2,1,0:T(8,128)(2,1)S(1)}) custom-call(bf16[4,160,800]{2,1,0:T(8,128)(2,1)S(1)} %pack.5.refs_3_.packed.refs_0_, s32[12,6,8,128]{3,2,1,0:T(8,128)S(1)} %table.1.refs_1_, bf16[4,160,128]{2,1,0:T(8,128)(2,1)S(1)} %near3.1.refs_6_.refs_2_.refs_3_, ...), custom_call_target="tpu_custom_call" | custom-call | bytes 1024 | tf_op jit(solution)/shard_map/middle4/pallas_call | solution.py:24
  30.5 1.6 %collective-permute-start.12 = (bf16[2,160,128]{2,1,0:T(8,128)(2,1)S(1)}, bf16[2,160,128]{2,1,0:T(8,128)(2,1)S(1)}, u32[]{:S(2)}, u32[]{:S(2)}) collective-permute-start(bf16[2,160,128]{2,1,0:T(8,128)(2,1)S(1)} %get-tuple-element.27), channel_id=1, source_target_pairs={{0,1},{1,0},{2,3},{3,2},{4,5},{5,4},{6,7},{7,6},{8,9},{9,8},{10,11... | collective-permute-start | bytes 245768 | tf_op jit(solution)/shard_map/ppermute | solution.py:271
  32.0 0.0 collective-permute-done.8.refs_4_
  32.1 2.1 %collective-permute-start.10 = (bf16[4,160,128]{2,1,0:T(8,128)(2,1)S(1)}, bf16[4,160,128]{2,1,0:T(8,128)(2,1)S(1)}, u32[]{:S(2)}, u32[]{:S(2)}) collective-permute-start(bf16[4,160,128]{2,1,0:T(8,128)(2,1)S(1)} %far4.3), channel_id=1, source_target_pairs={{0,1},{1,0},{2,3},{3,2},{4,5},{5,4},{6,7},{7,6},{8,9},{9,8},{10,11... | collective-permute-start | bytes 491528 | tf_op jit(solution)/shard_map/ppermute | solution.py:271
  34.2 2.3 %collective-permute-done.11.refs_2_ = bf16[4,160,128]{2,1,0:T(8,128)(2,1)S(1)} collective-permute-done((bf16[4,160,128]{2,1,0:T(8,128)(2,1)S(1)}, bf16[4,160,128]{2,1,0:T(8,128)(2,1)S(1)}, u32[]{:S(2)}, u32[]{:S(2)}) %collective-permute-start.11) | collective-permute-done | bytes 163872 | tf_op jit(solution)/shard_map/ppermute | solution.py:258
  36.5 0.0 collective-permute-done.12.refs_6_.half
  36.5 0.5 %near4.1.near = bf16[4,160,128]{2,1,0:T(8,128)(2,1)S(1)} custom-call(bf16[4,160,800]{2,1,0:T(8,128)(2,1)S(1)} %pack.3.refs_1_.packed.refs_0_, s32[12,6,8,128]{3,2,1,0:T(8,128)S(1)} %table.1.refs_1_, bf16[4,160,128]{2,1,0:T(8,128)(2,1)S(1)} %collective-permute-done.11.refs_2_, bf16[4,160,128]{2,1,0:T(8,128)(2,1)S(1)} %near3.1.refs_6_.refs_2_.refs_3_, ...), custom_call_target="tpu_custom_call" | custom-call | flops 20000000000 | bytes 1024 | tf_op jit(solution)/shard_map/near4/pallas_call | solution.py:24
  37.0 0.8 %own.1.refs_1_ = bf16[6,160,256]{2,1,0:T(8,128)(2,1)} custom-call(bf16[4,160,128]{2,1,0:T(8,128)(2,1)S(1)} %near4.1.near, bf16[4,160,128]{2,1,0:T(8,128)(2,1)S(1)} %get-tuple-element.28.middle, bf16[2,160,128]{2,1,0:T(8,128)(2,1)S(1)} %collective-permute-done.12.refs_6_.half), custom_call_target="tpu_custom_call" | custom-call | bytes 1024 | tf_op jit(solution)/shard_map/own/pallas_call | solution.py:24
  37.7 0.9 %collective-permute-done.10.refs_0_ = bf16[4,160,128]{2,1,0:T(8,128)(2,1)S(1)} collective-permute-done((bf16[4,160,128]{2,1,0:T(8,128)(2,1)S(1)}, bf16[4,160,128]{2,1,0:T(8,128)(2,1)S(1)}, u32[]{:S(2)}, u32[]{:S(2)}) %collective-permute-start.10) | collective-permute-done | bytes 163872 | tf_op jit(solution)/shard_map/ppermute | solution.py:271
  38.6 0.7 %others.1 = bf16[6,160,256]{2,1,0:T(8,128)(2,1)} custom-call(bf16[4,160,128]{2,1,0:T(8,128)(2,1)S(1)} %collective-permute-done.10.refs_0_, bf16[6,160,256]{2,1,0:T(8,128)(2,1)} %own.1.refs_1_), custom_call_target="tpu_custom_call", output_to_operand_aliasing={{}: (1, {})} | custom-call | bytes 1024 | tf_op jit(solution)/shard_map/others/pallas_call | solution.py:24
  (3 shorter events, 0.0 us)
Async XLA Ops:
  0.0 10.0 %slice-start = ((s8[4915200]{0:T(1024)(128)(4,1)}), s8[4194304]{0:T(1024)(128)(4,1)S(1)}, s32[]{:S(2)}) async-start(s8[4915200]{0:T(1024)(128)(4,1)} %bitcast.1), calls=%async_computation | async-start | bytes 8388608
  0.0 10.0 %slice-start.1 = ((s8[4915200]{0:T(1024)(128)(4,1)}), s8[720896]{0:T(1024)(128)(4,1)S(1)}, s32[]{:S(2)}) async-start(s8[4915200]{0:T(1024)(128)(4,1)} %bitcast.1), calls=%async_computation.1 | async-start | bytes 1441792
  1.6 9.3 %collective-permute-start = (bf16[2,160,128]{2,1,0:T(8,128)(2,1)S(1)}, bf16[2,160,128]{2,1,0:T(8,128)(2,1)S(1)}, u32[]{:S(2)}, u32[]{:S(2)}) collective-permute-start(bf16[2,160,128]{2,1,0:T(8,128)(2,1)S(1)} %get-tuple-element.24), channel_id=1, source_target_pairs={{0,1},{1,0},{2,3},{3,2},{4,5},{5,4},{6,7},{7,6},{8,9},{9,8},{10,11... | collective-permute-start | bytes 245768 | tf_op jit(solution)/shard_map/ppermute | solution.py:271
  4.6 8.3 %collective-permute-start.3 = (bf16[4,160,128]{2,1,0:T(8,128)(2,1)S(1)}, bf16[4,160,128]{2,1,0:T(8,128)(2,1)S(1)}, u32[]{:S(2)}, u32[]{:S(2)}) collective-permute-start(bf16[4,160,128]{2,1,0:T(8,128)(2,1)S(1)} %get-tuple-element.21.refs_3_.refs_2_), channel_id=1, source_target_pairs={{0,31},{1,2},{2,1},{3,4},{4,3},{5,6},{6,5},{7,8},{8,7},{9,10},{10,... | collective-permute-start | bytes 491528 | tf_op jit(solution)/shard_map/ppermute | solution.py:258
  8.6 7.7 %collective-permute-start.2 = (bf16[4,160,128]{2,1,0:T(8,128)(2,1)S(1)}, bf16[4,160,128]{2,1,0:T(8,128)(2,1)S(1)}, u32[]{:S(2)}, u32[]{:S(2)}) collective-permute-start(bf16[4,160,128]{2,1,0:T(8,128)(2,1)S(1)} %get-tuple-element.22.refs_2_.here.before.refs_5_), channel_id=1, source_target_pairs={{0,30},{1,3},{2,0},{3,5},{4,2},{5,7},{6,4},{7,9},{8,6},{9,11},{10,... | collective-permute-start | bytes 491528 | tf_op jit(solution)/shard_map/ppermute | solution.py:258
  11.0 5.6 %collective-permute-start.1 = (bf16[4,160,128]{2,1,0:T(8,128)(2,1)S(1)}, bf16[4,160,128]{2,1,0:T(8,128)(2,1)S(1)}, u32[]{:S(2)}, u32[]{:S(2)}) collective-permute-start(bf16[4,160,128]{2,1,0:T(8,128)(2,1)S(1)} %get-tuple-element.26), channel_id=1, source_target_pairs={{0,1},{1,0},{2,3},{3,2},{4,5},{5,4},{6,7},{7,6},{8,9},{9,8},{10,11... | collective-permute-start | bytes 491528 | tf_op jit(solution)/shard_map/ppermute | solution.py:271
  13.5 5.6 %collective-permute-start.5 = (bf16[4,160,128]{2,1,0:T(8,128)(2,1)S(1)}, bf16[4,160,128]{2,1,0:T(8,128)(2,1)S(1)}, u32[]{:S(2)}, u32[]{:S(2)}) collective-permute-start(bf16[4,160,128]{2,1,0:T(8,128)(2,1)S(1)} %near1.1.refs_5_.refs_2_.refs_3_), channel_id=1, source_target_pairs={{0,30},{1,3},{2,0},{3,5},{4,2},{5,7},{6,4},{7,9},{8,6},{9,11},{10,... | collective-permute-start | bytes 491528 | tf_op jit(solution)/shard_map/ppermute | solution.py:258
  17.0 7.5 %collective-permute-start.4 = (bf16[4,160,128]{2,1,0:T(8,128)(2,1)S(1)}, bf16[4,160,128]{2,1,0:T(8,128)(2,1)S(1)}, u32[]{:S(2)}, u32[]{:S(2)}) collective-permute-start(bf16[4,160,128]{2,1,0:T(8,128)(2,1)S(1)} %far1.1.here.refs_4_.refs_5_), channel_id=1, source_target_pairs={{0,2},{1,31},{2,4},{3,1},{4,6},{5,3},{6,8},{7,5},{8,10},{9,7},{10,... | collective-permute-start | bytes 491528 | tf_op jit(solution)/shard_map/ppermute | solution.py:258
  19.6 7.9 %collective-permute-start.7 = (bf16[4,160,128]{2,1,0:T(8,128)(2,1)S(1)}, bf16[4,160,128]{2,1,0:T(8,128)(2,1)S(1)}, u32[]{:S(2)}, u32[]{:S(2)}) collective-permute-start(bf16[4,160,128]{2,1,0:T(8,128)(2,1)S(1)} %far2.1.refs_6_.after.refs_3_.refs_5_), channel_id=1, source_target_pairs={{0,2},{1,31},{2,4},{3,1},{4,6},{5,3},{6,8},{7,5},{8,10},{9,7},{10,... | collective-permute-start | bytes 491528 | tf_op jit(solution)/shard_map/ppermute | solution.py:258
  25.1 3.3 %collective-permute-start.6 = (bf16[4,160,128]{2,1,0:T(8,128)(2,1)S(1)}, bf16[4,160,128]{2,1,0:T(8,128)(2,1)S(1)}, u32[]{:S(2)}, u32[]{:S(2)}) collective-permute-start(bf16[4,160,128]{2,1,0:T(8,128)(2,1)S(1)} %near2.1.before.refs_3_.refs_5_), channel_id=1, source_target_pairs={{0,30},{1,3},{2,0},{3,5},{4,2},{5,7},{6,4},{7,9},{8,6},{9,11},{10,... | collective-permute-start | bytes 491528 | tf_op jit(solution)/shard_map/ppermute | solution.py:258
  27.9 1.5 %collective-permute-start.9 = (bf16[4,160,128]{2,1,0:T(8,128)(2,1)S(1)}, bf16[4,160,128]{2,1,0:T(8,128)(2,1)S(1)}, u32[]{:S(2)}, u32[]{:S(2)}) collective-permute-start(bf16[4,160,128]{2,1,0:T(8,128)(2,1)S(1)} %near3.1.refs_6_.refs_2_.refs_3_), channel_id=1, source_target_pairs={{0,2},{1,3},{2,0},{3,1},{4,6},{5,7},{6,4},{7,5},{8,10},{9,11},{10,... | collective-permute-start | bytes 491528 | tf_op jit(solution)/shard_map/ppermute | solution.py:258
  28.0 4.0 %collective-permute-start.8 = (bf16[4,160,128]{2,1,0:T(8,128)(2,1)S(1)}, bf16[4,160,128]{2,1,0:T(8,128)(2,1)S(1)}, u32[]{:S(2)}, u32[]{:S(2)}) collective-permute-start(bf16[4,160,128]{2,1,0:T(8,128)(2,1)S(1)} %near3.1.refs_6_.refs_2_.refs_3_), channel_id=1, source_target_pairs={{0,30},{1,3},{2,0},{3,5},{4,2},{5,7},{6,4},{7,9},{8,6},{9,11},{10,... | collective-permute-start | bytes 491528 | tf_op jit(solution)/shard_map/ppermute | solution.py:258
  28.9 7.5 %collective-permute-start.11 = (bf16[4,160,128]{2,1,0:T(8,128)(2,1)S(1)}, bf16[4,160,128]{2,1,0:T(8,128)(2,1)S(1)}, u32[]{:S(2)}, u32[]{:S(2)}) collective-permute-start(bf16[4,160,128]{2,1,0:T(8,128)(2,1)S(1)} %far3.1.refs_3_.refs_4_), channel_id=1, source_target_pairs={{0,2},{1,31},{2,4},{3,1},{4,6},{5,3},{6,8},{7,5},{8,10},{9,7},{10,... | collective-permute-start | bytes 491528 | tf_op jit(solution)/shard_map/ppermute | solution.py:258
  30.5 6.0 %collective-permute-start.12 = (bf16[2,160,128]{2,1,0:T(8,128)(2,1)S(1)}, bf16[2,160,128]{2,1,0:T(8,128)(2,1)S(1)}, u32[]{:S(2)}, u32[]{:S(2)}) collective-permute-start(bf16[2,160,128]{2,1,0:T(8,128)(2,1)S(1)} %get-tuple-element.27), channel_id=1, source_target_pairs={{0,1},{1,0},{2,3},{3,2},{4,5},{5,4},{6,7},{7,6},{8,9},{9,8},{10,11... | collective-permute-start | bytes 245768 | tf_op jit(solution)/shard_map/ppermute | solution.py:271
  32.1 6.5 %collective-permute-start.10 = (bf16[4,160,128]{2,1,0:T(8,128)(2,1)S(1)}, bf16[4,160,128]{2,1,0:T(8,128)(2,1)S(1)}, u32[]{:S(2)}, u32[]{:S(2)}) collective-permute-start(bf16[4,160,128]{2,1,0:T(8,128)(2,1)S(1)} %far4.3), channel_id=1, source_target_pairs={{0,1},{1,0},{2,3},{3,2},{4,5},{5,4},{6,7},{7,6},{8,9},{9,8},{10,11... | collective-permute-start | bytes 491528 | tf_op jit(solution)/shard_map/ppermute | solution.py:271

commit v11 on v10

--- a/solution.py
+++ b/solution.py
@@ -9,7 +9,7 @@
 
 DEG = 4
 FULL = 128
-DEPTH = 512
+DEPTH = 768
 LONG, SHORT = 20 * 10**9, 10**9
 
 center_shift = 0.2

time: 39.5 us -> 39.5 us (level)
  no operation moved by 1% of the time
where the time goes in v11:
time: 39.5 us; the launch traced here: 39.3 us
  starting transfers between devices  16.3 us (41%)
  waiting for transfers between devices  12.2 us (31%)
  Pallas kernels  10.6 us (27%)
    ppermute x9, waiting for transfers between devices, permuted(): return lax.ppermute(x, ('elem', 'state'), moves)  11.1 us
    pallas_call x22, Pallas kernels, call(): pl.pallas_call(kernel, out_shape=outs, in_specs=ins, out_specs=out_specs...  10.6 us
    ppermute x9, starting transfers between devices, permuted(): return lax.ppermute(x, ('elem', 'state'), moves)  8.67 us
    ppermute x4, starting transfers between devices, swapped(): lax.ppermute(x, 'state', [(i, (i + k + 1) % shards) for i in range(shards)])  7.62 us
    ppermute x4, waiting for transfers between devices, swapped(): lax.ppermute(x, 'state', [(i, (i + k + 1) % shards) for i in range(shards)])  1.15 us
  transfers between devices with their start and end apart: 13, of which 8 were waited for; matrix products, arithmetic and copies ran while one was open for 0% of the time, Pallas kernels for 21%

profile of v11, /device:TPU:0, one launch (start us, length us, event | category | flops | bytes accessed | tf_op | source)
XLA Modules:
  0.0 39.3 jit_solution(4848777605648687488)
XLA Ops:
  0.0 0.0 slice-start
  0.0 0.0 slice-start.1
  0.0 1.6 %fetch.1 = (bf16[4,160,128]{2,1,0:T(8,128)(2,1)S(1)}, bf16[2,160,128]{2,1,0:T(8,128)(2,1)S(1)}, bf16[6,160,256]{2,1,0:T(8,128)(2,1)S(1)}, bf16[256,256]{1,0:T(8,...) custom-call(bf16[6,160,256]{2,1,0:T(8,128)(2,1)} %orbitals.1, bf16[256,256]{1,0:T(8,128)(2,1)} %rotation.1, s32[12]{0:T(128)} %counts.1, ...), custom_call_target="tpu_custom_call" | custom-call | flops 20000000000 | bytes 1024 | tf_op jit(solution)/shard_map/fetch/pallas_call | solution.py:24
  1.6 3.0 %collective-permute-start = (bf16[2,160,128]{2,1,0:T(8,128)(2,1)S(1)}, bf16[2,160,128]{2,1,0:T(8,128)(2,1)S(1)}, u32[]{:S(2)}, u32[]{:S(2)}) collective-permute-start(bf16[2,160,128]{2,1,0:T(8,128)(2,1)S(1)} %get-tuple-element.24), channel_id=1, source_target_pairs={{0,1},{1,0},{2,3},{3,2},{4,5},{5,4},{6,7},{7,6},{8,9},{9,8},{10,11... | collective-permute-start | bytes 245768 | tf_op jit(solution)/shard_map/ppermute | solution.py:271
  4.6 3.6 %collective-permute-start.3 = (bf16[4,160,128]{2,1,0:T(8,128)(2,1)S(1)}, bf16[4,160,128]{2,1,0:T(8,128)(2,1)S(1)}, u32[]{:S(2)}, u32[]{:S(2)}) collective-permute-start(bf16[4,160,128]{2,1,0:T(8,128)(2,1)S(1)} %get-tuple-element.21.refs_3_.refs_2_), channel_id=1, source_target_pairs={{0,31},{1,2},{2,1},{3,4},{4,3},{5,6},{6,5},{7,8},{8,7},{9,10},{10,... | collective-permute-start | bytes 491528 | tf_op jit(solution)/shard_map/ppermute | solution.py:258
  8.3 0.3 rotate_in.1
  8.6 1.2 %collective-permute-start.2 = (bf16[4,160,128]{2,1,0:T(8,128)(2,1)S(1)}, bf16[4,160,128]{2,1,0:T(8,128)(2,1)S(1)}, u32[]{:S(2)}, u32[]{:S(2)}) collective-permute-start(bf16[4,160,128]{2,1,0:T(8,128)(2,1)S(1)} %get-tuple-element.22.refs_2_.here.before.refs_5_), channel_id=1, source_target_pairs={{0,30},{1,3},{2,0},{3,5},{4,2},{5,7},{6,4},{7,9},{8,6},{9,11},{10,... | collective-permute-start | bytes 491528 | tf_op jit(solution)/shard_map/ppermute | solution.py:258
  9.7 0.3 table.1.refs_1_
  10.0 0.0 slice-done
  10.0 0.0 slice-done.1
  10.1 0.3 pack.3.refs_1_.packed.refs_0_
  10.3 0.3 pack.4.refs_1_.refs_0_.packed
  10.6 0.3 pack.5.refs_3_.packed.refs_0_
  10.9 0.0 collective-permute-done.refs_1_
  11.0 0.9 %collective-permute-start.1 = (bf16[4,160,128]{2,1,0:T(8,128)(2,1)S(1)}, bf16[4,160,128]{2,1,0:T(8,128)(2,1)S(1)}, u32[]{:S(2)}, u32[]{:S(2)}) collective-permute-start(bf16[4,160,128]{2,1,0:T(8,128)(2,1)S(1)} %get-tuple-element.26), channel_id=1, source_target_pairs={{0,1},{1,0},{2,3},{3,2},{4,5},{5,4},{6,7},{7,6},{8,9},{9,8},{10,11... | collective-permute-start | bytes 491528 | tf_op jit(solution)/shard_map/ppermute | solution.py:271
  11.8 1.2 %collective-permute-done.3.before = bf16[4,160,128]{2,1,0:T(8,128)(2,1)S(1)} collective-permute-done((bf16[4,160,128]{2,1,0:T(8,128)(2,1)S(1)}, bf16[4,160,128]{2,1,0:T(8,128)(2,1)S(1)}, u32[]{:S(2)}, u32[]{:S(2)}) %collective-permute-start.3) | collective-permute-done | bytes 163872 | tf_op jit(solution)/shard_map/ppermute | solution.py:258
  13.0 0.5 %near1.1.refs_5_.refs_2_.refs_3_ = bf16[4,160,128]{2,1,0:T(8,128)(2,1)S(1)} custom-call(bf16[4,160,800]{2,1,0:T(8,128)(2,1)S(1)} %pack.3.refs_1_.packed.refs_0_, s32[12,6,8,128]{3,2,1,0:T(8,128)S(1)} %table.1.refs_1_, bf16[4,160,128]{2,1,0:T(8,128)(2,1)S(1)} %collective-permute-done.3.before, ...), custom_call_target="tpu_custom_call" | custom-call | bytes 1024 | tf_op jit(solution)/shard_map/near1/pallas_call | solution.py:24
  13.5 2.7 %collective-permute-start.5 = (bf16[4,160,128]{2,1,0:T(8,128)(2,1)S(1)}, bf16[4,160,128]{2,1,0:T(8,128)(2,1)S(1)}, u32[]{:S(2)}, u32[]{:S(2)}) collective-permute-start(bf16[4,160,128]{2,1,0:T(8,128)(2,1)S(1)} %near1.1.refs_5_.refs_2_.refs_3_), channel_id=1, source_target_pairs={{0,30},{1,3},{2,0},{3,5},{4,2},{5,7},{6,4},{7,9},{8,6},{9,11},{10,... | collective-permute-start | bytes 491528 | tf_op jit(solution)/shard_map/ppermute | solution.py:258
  16.2 0.0 collective-permute-done.2.refs_4_
  16.2 0.3 collective-permute-done.1.refs_3_.after.refs_0_
  16.5 0.5 %far1.1.here.refs_4_.refs_5_ = bf16[4,160,128]{2,1,0:T(8,128)(2,1)S(1)} custom-call(bf16[4,160,800]{2,1,0:T(8,128)(2,1)S(1)} %pack.4.refs_1_.refs_0_.packed, s32[12,6,8,128]{3,2,1,0:T(8,128)S(1)} %table.1.refs_1_, bf16[4,160,128]{2,1,0:T(8,128)(2,1)S(1)} %get-tuple-element.25.after.refs_2_.here.refs_5_, ...), custom_call_target="tpu_custom_call" | custom-call | bytes 1024 | tf_op jit(solution)/shard_map/far1/pallas_call | solution.py:24
  17.0 0.1 collective-permute-start.4
  17.1 0.5 %middle1.1.before.refs_3_.refs_4_.refs_0_ = bf16[4,160,128]{2,1,0:T(8,128)(2,1)S(1)} custom-call(bf16[4,160,800]{2,1,0:T(8,128)(2,1)S(1)} %pack.5.refs_3_.packed.refs_0_, s32[12,6,8,128]{3,2,1,0:T(8,128)S(1)} %table.1.refs_1_, bf16[4,160,128]{2,1,0:T(8,128)(2,1)S(1)} %get-tuple-element.22.refs_2_.here.before.refs_5_, ...), custom_call_target="tpu_custom_call" | custom-call | bytes 1024 | tf_op jit(solution)/shard_map/middle1/pallas_call | solution.py:24
  17.6 1.4 %collective-permute-done.5.after = bf16[4,160,128]{2,1,0:T(8,128)(2,1)S(1)} collective-permute-done((bf16[4,160,128]{2,1,0:T(8,128)(2,1)S(1)}, bf16[4,160,128]{2,1,0:T(8,128)(2,1)S(1)}, u32[]{:S(2)}, u32[]{:S(2)}) %collective-permute-start.5) | collective-permute-done | bytes 163872 | tf_op jit(solution)/shard_map/ppermute | solution.py:258
  19.0 0.5 %far2.1.refs_6_.after.refs_3_.refs_5_ = bf16[4,160,128]{2,1,0:T(8,128)(2,1)S(1)} custom-call(bf16[4,160,800]{2,1,0:T(8,128)(2,1)S(1)} %pack.4.refs_1_.refs_0_.packed, s32[12,6,8,128]{3,2,1,0:T(8,128)S(1)} %table.1.refs_1_, bf16[4,160,128]{2,1,0:T(8,128)(2,1)S(1)} %middle1.1.before.refs_3_.refs_4_.refs_0_, bf16[4,160,128]{2,1,0:T(8,128)(2,1)S(1)} %far1.1.here.refs_4_.refs_5_, ...), custom_call_target="tpu_custom_call" | custom-call | bytes 1024 | tf_op jit(solution)/shard_map/far2/pallas_call | solution.py:24
  19.6 0.1 collective-permute-start.7
  19.6 0.5 %middle2.1.refs_6_.here.refs_4_.refs_2_.refs_5_ = bf16[4,160,128]{2,1,0:T(8,128)(2,1)S(1)} custom-call(bf16[4,160,800]{2,1,0:T(8,128)(2,1)S(1)} %pack.5.refs_3_.packed.refs_0_, s32[12,6,8,128]{3,2,1,0:T(8,128)S(1)} %table.1.refs_1_, bf16[4,160,128]{2,1,0:T(8,128)(2,1)S(1)} %near1.1.refs_5_.refs_2_.refs_3_, ...), custom_call_target="tpu_custom_call" | custom-call | bytes 1024 | tf_op jit(solution)/shard_map/middle2/pallas_call | solution.py:24
  20.1 4.4 %collective-permute-done.4.refs_2_ = bf16[4,160,128]{2,1,0:T(8,128)(2,1)S(1)} collective-permute-done((bf16[4,160,128]{2,1,0:T(8,128)(2,1)S(1)}, bf16[4,160,128]{2,1,0:T(8,128)(2,1)S(1)}, u32[]{:S(2)}, u32[]{:S(2)}) %collective-permute-start.4) | collective-permute-done | bytes 163872 | tf_op jit(solution)/shard_map/ppermute | solution.py:258
  24.6 0.5 %near2.1.before.refs_3_.refs_5_ = bf16[4,160,128]{2,1,0:T(8,128)(2,1)S(1)} custom-call(bf16[4,160,800]{2,1,0:T(8,128)(2,1)S(1)} %pack.3.refs_1_.packed.refs_0_, s32[12,6,8,128]{3,2,1,0:T(8,128)S(1)} %table.1.refs_1_, bf16[4,160,128]{2,1,0:T(8,128)(2,1)S(1)} %collective-permute-done.4.refs_2_, bf16[4,160,128]{2,1,0:T(8,128)(2,1)S(1)} %near1.1.refs_5_.refs_2_.refs_3_, ...), custom_call_target="tpu_custom_call" | custom-call | bytes 1024 | tf_op jit(solution)/shard_map/near2/pallas_call | solution.py:24
  25.1 0.3 collective-permute-start.6
  25.4 0.5 %middle3.1.refs_6_.refs_2_.refs_3_.refs_4_ = bf16[4,160,128]{2,1,0:T(8,128)(2,1)S(1)} custom-call(bf16[4,160,800]{2,1,0:T(8,128)(2,1)S(1)} %pack.5.refs_3_.packed.refs_0_, s32[12,6,8,128]{3,2,1,0:T(8,128)S(1)} %table.1.refs_1_, bf16[4,160,128]{2,1,0:T(8,128)(2,1)S(1)} %near2.1.before.refs_3_.refs_5_, ...), custom_call_target="tpu_custom_call" | custom-call | bytes 1024 | tf_op jit(solution)/shard_map/middle3/pallas_call | solution.py:24
  25.9 1.5 %collective-permute-done.7.refs_2_ = bf16[4,160,128]{2,1,0:T(8,128)(2,1)S(1)} collective-permute-done((bf16[4,160,128]{2,1,0:T(8,128)(2,1)S(1)}, bf16[4,160,128]{2,1,0:T(8,128)(2,1)S(1)}, u32[]{:S(2)}, u32[]{:S(2)}) %collective-permute-start.7) | collective-permute-done | bytes 163872 | tf_op jit(solution)/shard_map/ppermute | solution.py:258
  27.4 0.5 %near3.1.refs_6_.refs_2_.refs_3_ = bf16[4,160,128]{2,1,0:T(8,128)(2,1)S(1)} custom-call(bf16[4,160,800]{2,1,0:T(8,128)(2,1)S(1)} %pack.3.refs_1_.packed.refs_0_, s32[12,6,8,128]{3,2,1,0:T(8,128)S(1)} %table.1.refs_1_, bf16[4,160,128]{2,1,0:T(8,128)(2,1)S(1)} %collective-permute-done.7.refs_2_, bf16[4,160,128]{2,1,0:T(8,128)(2,1)S(1)} %near2.1.before.refs_3_.refs_5_, ...), custom_call_target="tpu_custom_call" | custom-call | bytes 1024 | tf_op jit(solution)/shard_map/near3/pallas_call | solution.py:24
  27.9 0.1 collective-permute-start.9
  28.0 0.4 %collective-permute-start.8 = (bf16[4,160,128]{2,1,0:T(8,128)(2,1)S(1)}, bf16[4,160,128]{2,1,0:T(8,128)(2,1)S(1)}, u32[]{:S(2)}, u32[]{:S(2)}) collective-permute-start(bf16[4,160,128]{2,1,0:T(8,128)(2,1)S(1)} %near3.1.refs_6_.refs_2_.refs_3_), channel_id=1, source_target_pairs={{0,30},{1,3},{2,0},{3,5},{4,2},{5,7},{6,4},{7,9},{8,6},{9,11},{10,... | collective-permute-start | bytes 491528 | tf_op jit(solution)/shard_map/ppermute | solution.py:258
  28.4 0.0 collective-permute-done.6.refs_4_
  28.4 0.5 %far3.1.refs_3_.refs_4_ = bf16[4,160,128]{2,1,0:T(8,128)(2,1)S(1)} custom-call(bf16[4,160,800]{2,1,0:T(8,128)(2,1)S(1)} %pack.4.refs_1_.refs_0_.packed, s32[12,6,8,128]{3,2,1,0:T(8,128)S(1)} %table.1.refs_1_, bf16[4,160,128]{2,1,0:T(8,128)(2,1)S(1)} %middle2.1.refs_6_.here.refs_4_.refs_2_.refs_5_, ...), custom_call_target="tpu_custom_call" | custom-call | bytes 1024 | tf_op jit(solution)/shard_map/far3/pallas_call | solution.py:24
  28.9 0.2 collective-permute-start.11
  29.2 0.2 collective-permute-done.9.refs_4_
  29.4 0.5 %far4.2.refs_6_ = bf16[4,160,128]{2,1,0:T(8,128)(2,1)S(1)} custom-call(bf16[4,160,800]{2,1,0:T(8,128)(2,1)S(1)} %pack.4.refs_1_.refs_0_.packed, s32[12,6,8,128]{3,2,1,0:T(8,128)S(1)} %table.1.refs_1_, bf16[4,160,128]{2,1,0:T(8,128)(2,1)S(1)} %middle3.1.refs_6_.refs_2_.refs_3_.refs_4_, bf16[4,160,128]{2,1,0:T(8,128)(2,1)S(1)} %far3.1.refs_3_.refs_4_, ...), custom_call_target="tpu_custom_call" | custom-call | bytes 1024 | tf_op jit(solution)/shard_map/far4/pallas_call | solution.py:24
  29.9 0.5 %middle4.1 = (bf16[4,160,128]{2,1,0:T(8,128)(2,1)S(1)}, bf16[2,160,128]{2,1,0:T(8,128)(2,1)S(1)}) custom-call(bf16[4,160,800]{2,1,0:T(8,128)(2,1)S(1)} %pack.5.refs_3_.packed.refs_0_, s32[12,6,8,128]{3,2,1,0:T(8,128)S(1)} %table.1.refs_1_, bf16[4,160,128]{2,1,0:T(8,128)(2,1)S(1)} %near3.1.refs_6_.refs_2_.refs_3_, ...), custom_call_target="tpu_custom_call" | custom-call | bytes 1024 | tf_op jit(solution)/shard_map/middle4/pallas_call | solution.py:24
  30.5 1.6 %collective-permute-start.12 = (bf16[2,160,128]{2,1,0:T(8,128)(2,1)S(1)}, bf16[2,160,128]{2,1,0:T(8,128)(2,1)S(1)}, u32[]{:S(2)}, u32[]{:S(2)}) collective-permute-start(bf16[2,160,128]{2,1,0:T(8,128)(2,1)S(1)} %get-tuple-element.27), channel_id=1, source_target_pairs={{0,1},{1,0},{2,3},{3,2},{4,5},{5,4},{6,7},{7,6},{8,9},{9,8},{10,11... | collective-permute-start | bytes 245768 | tf_op jit(solution)/shard_map/ppermute | solution.py:271
  32.1 0.0 collective-permute-done.8.refs_4_
  32.1 2.1 %collective-permute-start.10 = (bf16[4,160,128]{2,1,0:T(8,128)(2,1)S(1)}, bf16[4,160,128]{2,1,0:T(8,128)(2,1)S(1)}, u32[]{:S(2)}, u32[]{:S(2)}) collective-permute-start(bf16[4,160,128]{2,1,0:T(8,128)(2,1)S(1)} %far4.3), channel_id=1, source_target_pairs={{0,1},{1,0},{2,3},{3,2},{4,5},{5,4},{6,7},{7,6},{8,9},{9,8},{10,11... | collective-permute-start | bytes 491528 | tf_op jit(solution)/shard_map/ppermute | solution.py:271
  34.2 2.3 %collective-permute-done.11.refs_2_ = bf16[4,160,128]{2,1,0:T(8,128)(2,1)S(1)} collective-permute-done((bf16[4,160,128]{2,1,0:T(8,128)(2,1)S(1)}, bf16[4,160,128]{2,1,0:T(8,128)(2,1)S(1)}, u32[]{:S(2)}, u32[]{:S(2)}) %collective-permute-start.11) | collective-permute-done | bytes 163872 | tf_op jit(solution)/shard_map/ppermute | solution.py:258
  36.5 0.0 collective-permute-done.12.refs_6_.half
  36.5 0.5 %near4.1.near = bf16[4,160,128]{2,1,0:T(8,128)(2,1)S(1)} custom-call(bf16[4,160,800]{2,1,0:T(8,128)(2,1)S(1)} %pack.3.refs_1_.packed.refs_0_, s32[12,6,8,128]{3,2,1,0:T(8,128)S(1)} %table.1.refs_1_, bf16[4,160,128]{2,1,0:T(8,128)(2,1)S(1)} %collective-permute-done.11.refs_2_, bf16[4,160,128]{2,1,0:T(8,128)(2,1)S(1)} %near3.1.refs_6_.refs_2_.refs_3_, ...), custom_call_target="tpu_custom_call" | custom-call | flops 20000000000 | bytes 1024 | tf_op jit(solution)/shard_map/near4/pallas_call | solution.py:24
  37.0 0.8 %own.1.refs_1_ = bf16[6,160,256]{2,1,0:T(8,128)(2,1)} custom-call(bf16[4,160,128]{2,1,0:T(8,128)(2,1)S(1)} %near4.1.near, bf16[4,160,128]{2,1,0:T(8,128)(2,1)S(1)} %get-tuple-element.28.middle, bf16[2,160,128]{2,1,0:T(8,128)(2,1)S(1)} %collective-permute-done.12.refs_6_.half), custom_call_target="tpu_custom_call" | custom-call | bytes 1024 | tf_op jit(solution)/shard_map/own/pallas_call | solution.py:24
  37.7 0.9 %collective-permute-done.10.refs_0_ = bf16[4,160,128]{2,1,0:T(8,128)(2,1)S(1)} collective-permute-done((bf16[4,160,128]{2,1,0:T(8,128)(2,1)S(1)}, bf16[4,160,128]{2,1,0:T(8,128)(2,1)S(1)}, u32[]{:S(2)}, u32[]{:S(2)}) %collective-permute-start.10) | collective-permute-done | bytes 163872 | tf_op jit(solution)/shard_map/ppermute | solution.py:271
  38.6 0.7 %others.1 = bf16[6,160,256]{2,1,0:T(8,128)(2,1)} custom-call(bf16[4,160,128]{2,1,0:T(8,128)(2,1)S(1)} %collective-permute-done.10.refs_0_, bf16[6,160,256]{2,1,0:T(8,128)(2,1)} %own.1.refs_1_), custom_call_target="tpu_custom_call", output_to_operand_aliasing={{}: (1, {})} | custom-call | bytes 1024 | tf_op jit(solution)/shard_map/others/pallas_call | solution.py:24
  (3 shorter events, 0.0 us)
Async XLA Ops:
  0.0 10.0 %slice-start = ((s8[4915200]{0:T(1024)(128)(4,1)}), s8[4194304]{0:T(1024)(128)(4,1)S(1)}, s32[]{:S(2)}) async-start(s8[4915200]{0:T(1024)(128)(4,1)} %bitcast.1), calls=%async_computation | async-start | bytes 8388608
  0.0 10.0 %slice-start.1 = ((s8[4915200]{0:T(1024)(128)(4,1)}), s8[720896]{0:T(1024)(128)(4,1)S(1)}, s32[]{:S(2)}) async-start(s8[4915200]{0:T(1024)(128)(4,1)} %bitcast.1), calls=%async_computation.1 | async-start | bytes 1441792
  1.6 9.3 %collective-permute-start = (bf16[2,160,128]{2,1,0:T(8,128)(2,1)S(1)}, bf16[2,160,128]{2,1,0:T(8,128)(2,1)S(1)}, u32[]{:S(2)}, u32[]{:S(2)}) collective-permute-start(bf16[2,160,128]{2,1,0:T(8,128)(2,1)S(1)} %get-tuple-element.24), channel_id=1, source_target_pairs={{0,1},{1,0},{2,3},{3,2},{4,5},{5,4},{6,7},{7,6},{8,9},{9,8},{10,11... | collective-permute-start | bytes 245768 | tf_op jit(solution)/shard_map/ppermute | solution.py:271
  4.6 8.3 %collective-permute-start.3 = (bf16[4,160,128]{2,1,0:T(8,128)(2,1)S(1)}, bf16[4,160,128]{2,1,0:T(8,128)(2,1)S(1)}, u32[]{:S(2)}, u32[]{:S(2)}) collective-permute-start(bf16[4,160,128]{2,1,0:T(8,128)(2,1)S(1)} %get-tuple-element.21.refs_3_.refs_2_), channel_id=1, source_target_pairs={{0,31},{1,2},{2,1},{3,4},{4,3},{5,6},{6,5},{7,8},{8,7},{9,10},{10,... | collective-permute-start | bytes 491528 | tf_op jit(solution)/shard_map/ppermute | solution.py:258
  8.6 7.7 %collective-permute-start.2 = (bf16[4,160,128]{2,1,0:T(8,128)(2,1)S(1)}, bf16[4,160,128]{2,1,0:T(8,128)(2,1)S(1)}, u32[]{:S(2)}, u32[]{:S(2)}) collective-permute-start(bf16[4,160,128]{2,1,0:T(8,128)(2,1)S(1)} %get-tuple-element.22.refs_2_.here.before.refs_5_), channel_id=1, source_target_pairs={{0,30},{1,3},{2,0},{3,5},{4,2},{5,7},{6,4},{7,9},{8,6},{9,11},{10,... | collective-permute-start | bytes 491528 | tf_op jit(solution)/shard_map/ppermute | solution.py:258
  11.0 5.6 %collective-permute-start.1 = (bf16[4,160,128]{2,1,0:T(8,128)(2,1)S(1)}, bf16[4,160,128]{2,1,0:T(8,128)(2,1)S(1)}, u32[]{:S(2)}, u32[]{:S(2)}) collective-permute-start(bf16[4,160,128]{2,1,0:T(8,128)(2,1)S(1)} %get-tuple-element.26), channel_id=1, source_target_pairs={{0,1},{1,0},{2,3},{3,2},{4,5},{5,4},{6,7},{7,6},{8,9},{9,8},{10,11... | collective-permute-start | bytes 491528 | tf_op jit(solution)/shard_map/ppermute | solution.py:271
  13.5 5.6 %collective-permute-start.5 = (bf16[4,160,128]{2,1,0:T(8,128)(2,1)S(1)}, bf16[4,160,128]{2,1,0:T(8,128)(2,1)S(1)}, u32[]{:S(2)}, u32[]{:S(2)}) collective-permute-start(bf16[4,160,128]{2,1,0:T(8,128)(2,1)S(1)} %near1.1.refs_5_.refs_2_.refs_3_), channel_id=1, source_target_pairs={{0,30},{1,3},{2,0},{3,5},{4,2},{5,7},{6,4},{7,9},{8,6},{9,11},{10,... | collective-permute-start | bytes 491528 | tf_op jit(solution)/shard_map/ppermute | solution.py:258
  17.0 7.5 %collective-permute-start.4 = (bf16[4,160,128]{2,1,0:T(8,128)(2,1)S(1)}, bf16[4,160,128]{2,1,0:T(8,128)(2,1)S(1)}, u32[]{:S(2)}, u32[]{:S(2)}) collective-permute-start(bf16[4,160,128]{2,1,0:T(8,128)(2,1)S(1)} %far1.1.here.refs_4_.refs_5_), channel_id=1, source_target_pairs={{0,2},{1,31},{2,4},{3,1},{4,6},{5,3},{6,8},{7,5},{8,10},{9,7},{10,... | collective-permute-start | bytes 491528 | tf_op jit(solution)/shard_map/ppermute | solution.py:258
  19.6 7.9 %collective-permute-start.7 = (bf16[4,160,128]{2,1,0:T(8,128)(2,1)S(1)}, bf16[4,160,128]{2,1,0:T(8,128)(2,1)S(1)}, u32[]{:S(2)}, u32[]{:S(2)}) collective-permute-start(bf16[4,160,128]{2,1,0:T(8,128)(2,1)S(1)} %far2.1.refs_6_.after.refs_3_.refs_5_), channel_id=1, source_target_pairs={{0,2},{1,31},{2,4},{3,1},{4,6},{5,3},{6,8},{7,5},{8,10},{9,7},{10,... | collective-permute-start | bytes 491528 | tf_op jit(solution)/shard_map/ppermute | solution.py:258
  25.1 3.4 %collective-permute-start.6 = (bf16[4,160,128]{2,1,0:T(8,128)(2,1)S(1)}, bf16[4,160,128]{2,1,0:T(8,128)(2,1)S(1)}, u32[]{:S(2)}, u32[]{:S(2)}) collective-permute-start(bf16[4,160,128]{2,1,0:T(8,128)(2,1)S(1)} %near2.1.before.refs_3_.refs_5_), channel_id=1, source_target_pairs={{0,30},{1,3},{2,0},{3,5},{4,2},{5,7},{6,4},{7,9},{8,6},{9,11},{10,... | collective-permute-start | bytes 491528 | tf_op jit(solution)/shard_map/ppermute | solution.py:258
  27.9 1.5 %collective-permute-start.9 = (bf16[4,160,128]{2,1,0:T(8,128)(2,1)S(1)}, bf16[4,160,128]{2,1,0:T(8,128)(2,1)S(1)}, u32[]{:S(2)}, u32[]{:S(2)}) collective-permute-start(bf16[4,160,128]{2,1,0:T(8,128)(2,1)S(1)} %near3.1.refs_6_.refs_2_.refs_3_), channel_id=1, source_target_pairs={{0,2},{1,3},{2,0},{3,1},{4,6},{5,7},{6,4},{7,5},{8,10},{9,11},{10,... | collective-permute-start | bytes 491528 | tf_op jit(solution)/shard_map/ppermute | solution.py:258
  28.0 4.0 %collective-permute-start.8 = (bf16[4,160,128]{2,1,0:T(8,128)(2,1)S(1)}, bf16[4,160,128]{2,1,0:T(8,128)(2,1)S(1)}, u32[]{:S(2)}, u32[]{:S(2)}) collective-permute-start(bf16[4,160,128]{2,1,0:T(8,128)(2,1)S(1)} %near3.1.refs_6_.refs_2_.refs_3_), channel_id=1, source_target_pairs={{0,30},{1,3},{2,0},{3,5},{4,2},{5,7},{6,4},{7,9},{8,6},{9,11},{10,... | collective-permute-start | bytes 491528 | tf_op jit(solution)/shard_map/ppermute | solution.py:258
  28.9 7.5 %collective-permute-start.11 = (bf16[4,160,128]{2,1,0:T(8,128)(2,1)S(1)}, bf16[4,160,128]{2,1,0:T(8,128)(2,1)S(1)}, u32[]{:S(2)}, u32[]{:S(2)}) collective-permute-start(bf16[4,160,128]{2,1,0:T(8,128)(2,1)S(1)} %far3.1.refs_3_.refs_4_), channel_id=1, source_target_pairs={{0,2},{1,31},{2,4},{3,1},{4,6},{5,3},{6,8},{7,5},{8,10},{9,7},{10,... | collective-permute-start | bytes 491528 | tf_op jit(solution)/shard_map/ppermute | solution.py:258
  30.5 6.0 %collective-permute-start.12 = (bf16[2,160,128]{2,1,0:T(8,128)(2,1)S(1)}, bf16[2,160,128]{2,1,0:T(8,128)(2,1)S(1)}, u32[]{:S(2)}, u32[]{:S(2)}) collective-permute-start(bf16[2,160,128]{2,1,0:T(8,128)(2,1)S(1)} %get-tuple-element.27), channel_id=1, source_target_pairs={{0,1},{1,0},{2,3},{3,2},{4,5},{5,4},{6,7},{7,6},{8,9},{9,8},{10,11... | collective-permute-start | bytes 245768 | tf_op jit(solution)/shard_map/ppermute | solution.py:271
  32.1 6.5 %collective-permute-start.10 = (bf16[4,160,128]{2,1,0:T(8,128)(2,1)S(1)}, bf16[4,160,128]{2,1,0:T(8,128)(2,1)S(1)}, u32[]{:S(2)}, u32[]{:S(2)}) collective-permute-start(bf16[4,160,128]{2,1,0:T(8,128)(2,1)S(1)} %far4.3), channel_id=1, source_target_pairs={{0,1},{1,0},{2,3},{3,2},{4,5},{5,4},{6,7},{7,6},{8,9},{9,8},{10,11... | collective-permute-start | bytes 491528 | tf_op jit(solution)/shard_map/ppermute | solution.py:271
